TPU v7x, 256 devices: a whole 4x4x8 slice. The times are simulated.
256 devices in a mesh: pb: 64 (over y, x_hi, z), ka: 4 (over x_lo, core).
Axes of the slice: x: 4 (x_hi: 2, x_lo: 2; x = x_hi * 2 + x_lo), y: 4, z: 8, core: 2. Of those that a mesh axis runs over, the one named last changes fastest.
Arguments:
- queries: bfloat16 [32768, 256], P(('pb', 'ka')), may hold values from -6 to 6
- key_rows: bfloat16 [32768, 256], P(('pb', 'ka')), may hold values from -6 to 6
- value_rows: bfloat16 [32768, 256], P(('pb', 'ka')), may hold values from -6 to 6
- attn_output: bfloat16 [32768, 256], P(('pb', 'ka')), may hold values from -3 to 3
- grad_output: bfloat16 [32768, 256], P(('pb', 'ka')), as said below
- row_lse: float32 [2, 32768], P(None, ('pb', 'ka'))
Outputs:
- grad_query: bfloat16 [32768, 256], P(('pb', 'ka'))
- grad_keys: bfloat16 [32768, 256], P(('pb', 'ka'))
- grad_values: bfloat16 [32768, 256], P(('pb', 'ka'))
Inputs may be any that keep to these rules, and one draw needn't show every extreme that they name: `grad_output`: loss-scaled output gradient, of order sqrt(32768) in magnitude.
All inputs are finite; a program needn't handle non-finite values.
Results may differ from a plain program's by a relative error of at most 0.0051.
Values may be sent and summed in bfloat16 or wider, within the bound.
No kernel may reach another device: no remote copies, remote signals or barrier semaphores. Data moves between devices by JAX's collectives and lax.ppermute only.
A program may use at most 64 MiB of HBM per device.

v0:
```python
import math

import jax
import jax.numpy as jnp
from jax import lax
from jax.sharding import PartitionSpec as P

HEADS = 2


def tile_grads(query_part, grad_part, lse_part, delta_part, key_part, value_part):
    query_count = query_part.shape[0]
    key_count = key_part.shape[0]
    feature_width = query_part.shape[1]
    head_size = feature_width // HEADS
    score_scale = head_size ** (-0.5)
    query_heads = query_part.reshape(query_count, HEADS, head_size)
    grad_heads = grad_part.reshape(query_count, HEADS, head_size)
    key_heads = key_part.reshape(key_count, HEADS, head_size)
    value_heads = value_part.reshape(key_count, HEADS, head_size)
    scores = jnp.einsum("ihd,jhd->hij", query_heads, key_heads, preferred_element_type=jnp.float32)
    attn_probs = jnp.exp(scores * score_scale - lse_part[:, :, None])
    dprobs = jnp.einsum("ihd,jhd->hij", grad_heads, value_heads, preferred_element_type=jnp.float32)
    dscores = (score_scale * attn_probs * (dprobs - delta_part[:, :, None])).astype(jnp.bfloat16)
    grad_q = None
    grad_k = None
    grad_v = None
    grad_q = jnp.einsum(
        "hij,jhd->ihd", dscores, key_heads, preferred_element_type=jnp.float32
    ).reshape(query_count, feature_width)
    probs_low = attn_probs.astype(jnp.bfloat16)
    grad_v = jnp.einsum(
        "hij,ihd->jhd", probs_low, grad_heads, preferred_element_type=jnp.float32
    ).reshape(key_count, feature_width)
    grad_k = jnp.einsum(
        "hij,ihd->jhd", dscores, query_heads, preferred_element_type=jnp.float32
    ).reshape(key_count, feature_width)
    return (grad_q, grad_k, grad_v)


def sweep_keys(query_part, grad_part, lse_part, delta_part, key_set, value_set):
    key_count = key_set.shape[0]
    feature_width = key_set.shape[1]
    block_rows = math.gcd(key_count, 512)
    block_total = key_count // block_rows
    key_blocks = key_set.reshape(block_total, block_rows, feature_width)
    value_blocks = value_set.reshape(block_total, block_rows, feature_width)

    def advance(total_q, blocks):
        grad_q, grad_k, grad_v = tile_grads(
            query_part, grad_part, lse_part, delta_part, blocks[0], blocks[1]
        )
        return (total_q + grad_q, (grad_k, grad_v))

    start_q = jnp.zeros((query_part.shape[0], feature_width), jnp.float32)
    total_q, stacked = lax.scan(advance, start_q, (key_blocks, value_blocks))
    return (
        total_q,
        stacked[0].reshape(key_count, feature_width),
        stacked[1].reshape(key_count, feature_width),
    )


def local(queries, key_rows, value_rows, attn_output, grad_output, row_lse):
    local_rows = queries.shape[0]
    feature_width = queries.shape[1]
    head_size = feature_width // HEADS
    products = grad_output.astype(jnp.float32) * attn_output.astype(jnp.float32)
    row_delta = jnp.sum(products.reshape(local_rows, HEADS, head_size), axis=2).T
    query_block, grad_block = (
        lax.all_gather(queries, "ka", axis=0, tiled=True),
        lax.all_gather(grad_output, "ka", axis=0, tiled=True),
    )
    lse_block, delta_block = (
        lax.all_gather(row_lse, "ka", axis=1, tiled=True),
        lax.all_gather(row_delta, "ka", axis=1, tiled=True),
    )
    key_set, value_set = (
        lax.all_gather(key_rows, "pb", axis=0, tiled=True),
        lax.all_gather(value_rows, "pb", axis=0, tiled=True),
    )
    partial_q, partial_k, partial_v = sweep_keys(
        query_block, grad_block, lse_block, delta_block, key_set, value_set
    )
    summed_k, summed_v = (
        lax.psum_scatter(partial_k, "pb", scatter_dimension=0, tiled=True),
        lax.psum_scatter(partial_v, "pb", scatter_dimension=0, tiled=True),
    )
    summed_q = lax.psum_scatter(partial_q, "ka", scatter_dimension=0, tiled=True)
    return (
        summed_q.astype(jnp.bfloat16),
        summed_k.astype(jnp.bfloat16),
        summed_v.astype(jnp.bfloat16),
    )


def solution(mesh):
    return jax.shard_map(
        local,
        mesh=mesh,
        in_specs=(
            P(("pb", "ka"), None),
            P(("pb", "ka"), None),
            P(("pb", "ka"), None),
            P(("pb", "ka"), None),
            P(("pb", "ka"), None),
            P(None, ("pb", "ka")),
        ),
        out_specs=(P(("pb", "ka"), None), P(("pb", "ka"), None), P(("pb", "ka"), None)),
        check_vma=False,
    )
```

profile of v0, /device:TPU:2, one launch (start us, length us, event | category | flops | bytes accessed | tf_op | source)
XLA Modules:
  0.0 1157.2 jit_solution(15905307768238420565)
XLA Ops:
  11.8 6.5 all_gather.23
  18.5 5.3 all_gather.20
  23.7 5.9 all_gather.22
  29.6 5.9 all_gather.19
  35.5 106.4 %all-gather.3.cloned.1.call-done = bf16[8192,256]{1,0:T(8,128)(2,1)} async-done(((bf16[128,256]{1,0:T(8,128)(2,1)}), bf16[8192,256]{1,0:T(8,128)(2,1)}) %all-gather.3.cloned.1.call-update) | async-done | bytes 4194320 | tf_op jit(solution)/shard_map/all_gather | solution.py:79
  141.9 128.3 %all-gather.5.cloned.1.call-done = bf16[8192,256]{1,0:T(8,128)(2,1)} async-done(((bf16[128,256]{1,0:T(8,128)(2,1)}), bf16[8192,256]{1,0:T(8,128)(2,1)}) %all-gather.5.cloned.1.call-update) | async-done | bytes 4194320 | tf_op jit(solution)/shard_map/all_gather | solution.py:80
  270.2 102.1 %while.15 = (s32[]{:T(128)}, f32[512,256]{0,1:T(8,128)S(1)}, f32[16,512,256]{2,1,0:T(8,128)}, f32[16,512,256]{2,1,0:T(8,128)}, bf16[16,512,256]{2,1,0:T(8,128)(2...) while((s32[]{:T(128)}, f32[512,256]{0,1:T(8,128)S(1)}, ...), condition=%wide.region_2.3_spmd.clone, body=%wide.region_1.2_spmd.clone.sunk | while | flops 676069376 | bytes 20721812 | solution.py:56
  275.6 1.1 constant_dynamic-update-slice_fusion.3
  288.3 1.0 constant_dynamic-update-slice_fusion.3
  301.1 1.0 constant_dynamic-update-slice_fusion.3
  307.5 1.0 constant_dynamic-update-slice_fusion.3
  320.2 1.1 constant_dynamic-update-slice_fusion.3
  326.6 1.1 constant_dynamic-update-slice_fusion.3
  333.0 1.1 constant_dynamic-update-slice_fusion.3
  339.4 1.0 constant_dynamic-update-slice_fusion.3
  352.1 1.1 constant_dynamic-update-slice_fusion.3
  358.5 1.0 constant_dynamic-update-slice_fusion.3
  371.2 1.1 constant_dynamic-update-slice_fusion.3
  374.5 15.8 %reduce-scatter.4.cloned.1.call-done = f32[128,256]{1,0:T(8,128)} async-done(((f32[512,256]{1,0:T(8,128)}), f32[128,256]{1,0:T(8,128)}) %reduce-scatter.4.cloned.1.call-update) | async-done | bytes 131088 | tf_op jit(solution)/shard_map/reduce_scatter | solution.py:89
  390.4 1.5 convert_element_type.24
  391.9 382.6 %reduce-scatter.8.cloned.1.call-done = f32[128,256]{1,0:T(8,128)} async-done(((f32[8192,256]{1,0:T(8,128)}), f32[128,256]{1,0:T(8,128)}) %reduce-scatter.8.cloned.1.call-update) | async-done | bytes 131088 | tf_op jit(solution)/shard_map/reduce_scatter | solution.py:87
  774.5 1.5 convert_element_type.26
  776.1 373.1 %reduce-scatter.6.cloned.1.call-done = f32[128,256]{1,0:T(8,128)} async-done(((f32[8192,256]{1,0:T(8,128)}), f32[128,256]{1,0:T(8,128)}) %reduce-scatter.6.cloned.1.call-update) | async-done | bytes 131088 | tf_op jit(solution)/shard_map/reduce_scatter | solution.py:86
  1149.1 1.5 convert_element_type.25
  (217 shorter events, 96.1 us)
Async XLA Ops:
  7.2 134.8 %all-gather.3.cloned.1.call-start = ((), (), s32[]{:S(2)}) async-start(), calls=%async_computation.3 | async-start | bytes 4259840 | tf_op jit(solution)/shard_map/all_gather | solution.py:79
  7.9 262.3 %all-gather.5.cloned.1.call-start = ((), (), s32[]{:S(2)}) async-start(), calls=%async_computation.4 | async-start | bytes 4259840 | tf_op jit(solution)/shard_map/all_gather | solution.py:80
  8.6 381.7 %reduce-scatter.4.cloned.1.call-start = ((), (), s32[]{:S(2)}) async-start(), calls=%async_computation.5 | async-start | bytes 655360 | tf_op jit(solution)/shard_map/reduce_scatter | solution.py:89
  373.3 401.2 %reduce-scatter.8.cloned.1.call-start = ((), (), s32[]{:S(2)}) async-start(), calls=%async_computation.7 | async-start | bytes 8519680 | tf_op jit(solution)/shard_map/reduce_scatter | solution.py:87
  373.9 775.2 %reduce-scatter.6.cloned.1.call-start = ((), (), s32[]{:S(2)}) async-start(), calls=%async_computation.6 | async-start | bytes 8519680 | tf_op jit(solution)/shard_map/reduce_scatter | solution.py:86
Sparse Core Ops, SparseCore 0:
  11.5 130.3 all-gather.2
  145.4 124.7 all-gather.4
  373.5 16.8 reduce-scatter.3
  392.8 381.7 reduce-scatter.7
  776.9 372.1 reduce-scatter.5
where the time goes:
time: 1160 us
  waiting for transfers between devices  1010 us (87%)
  local copies, waits for them, and re-layouts  61.7 us (5%)
  matrix products  39.7 us (3%)
  blocking collectives  23.6 us (2%)
  between operations  13.8 us (1%)
    reduce_scatter x1, waiting for transfers between devices, local(): lax.psum_scatter(partial_v, 'pb', scatter_dimension=0, tiled=True)  383 us
    reduce_scatter x1, waiting for transfers between devices, local(): lax.psum_scatter(partial_k, 'pb', scatter_dimension=0, tiled=True)  373 us
    all_gather x1, waiting for transfers between devices, local(): lax.all_gather(value_rows, 'pb', axis=0, tiled=True)  128 us
    all_gather x1, waiting for transfers between devices, local(): lax.all_gather(key_rows, 'pb', axis=0, tiled=True)  106 us
    dynamic_slice x64, local copies, waits for them, and re-layouts, sweep_keys(): total_q, stacked = lax.scan(advance, start_q, (key_blocks, value_blocks))  35.6 us
  transfers between devices with their start and end apart: 5, of which 5 were waited for; matrix products, arithmetic and copies ran while one was open for 1% of the time, Pallas kernels for 0%

commit v1 on v0

v1 whole, which is shorter than its diff:
```python
import functools
import math

import jax
import jax.numpy as jnp
from jax import lax
from jax.experimental import pallas as pl
from jax.experimental.pallas import tpu as pltpu
from jax.sharding import Mesh, PartitionSpec as P

HEAD = 128
SCALE = HEAD**-0.5
LOG2E = math.log2(math.e)
AXES = ("y", "xh", "z", "xl", "core")
PLANE = ("y", "xh", "xl")
ROWS = 256
STATS = 16
NT = (((1,), (1,)), ((), ()))
F32, BF16 = jnp.float32, jnp.bfloat16


def split3(x):
    hi = lax.reduce_precision(x, 8, 7)
    mid = lax.reduce_precision(x - hi, 8, 7)
    low = x - hi - mid
    return [term.astype(BF16) for term in (hi, mid, low)]


def tile_kernel(first, last, chips, *refs):
    if first:
        qg_ref, kv1_ref, kv2_ref, dq_ref, d1_ref, d2_ref, acc_k, acc_v, kt_ref = refs
    else:
        qg_ref, kv1_ref, kv2_ref, old_ref, dq_ref, d1_ref, d2_ref, acc_k, acc_v, kt_ref = refs
    step = pl.program_id(0)
    k = jnp.concatenate([kv1_ref[:, :HEAD], kv2_ref[:, :HEAD]], axis=0)
    v = jnp.concatenate([kv1_ref[:, HEAD:], kv2_ref[:, HEAD:]], axis=0)

    @pl.when(step == 0)
    def _():
        acc_k[...] = jnp.zeros_like(acc_k)
        acc_v[...] = jnp.zeros_like(acc_v)
        kt_ref[...] = k.astype(F32).T.astype(BF16)

    kt = kt_ref[...]
    dk = acc_k[...]
    dv = acc_v[...]
    for chip in range(chips):
        q = qg_ref[chip, :ROWS, :HEAD]
        g = qg_ref[chip, :ROWS, HEAD:]
        stats = qg_ref[chip, ROWS:, :].astype(F32)
        lse = stats[0:1] + stats[1:2] + stats[2:3]
        delta = stats[3:4] + stats[4:5] + stats[5:6]
        s = lax.dot_general(k, q, NT, preferred_element_type=F32)
        p = jnp.exp2(s * (SCALE * LOG2E) - lse)
        dp = lax.dot_general(v, g, NT, preferred_element_type=F32)
        ds = (SCALE * p * (dp - delta)).astype(BF16)
        dv = dv + jnp.dot(p.astype(BF16), g, preferred_element_type=F32)
        dk = dk + jnp.dot(ds, q, preferred_element_type=F32)
        dq = jnp.dot(kt, ds, preferred_element_type=F32)
        if not first:
            dq = dq + old_ref[chip]
        dq_ref[chip] = dq.astype(dq_ref.dtype)
    acc_k[...] = dk
    acc_v[...] = dv

    @pl.when(step == pl.num_programs(0) - 1)
    def _():
        d1_ref[:, :HEAD] = dk[:ROWS].astype(BF16)
        d1_ref[:, HEAD:] = dv[:ROWS].astype(BF16)
        d2_ref[:, :HEAD] = dk[ROWS:].astype(BF16)
        d2_ref[:, HEAD:] = dv[ROWS:].astype(BF16)


def tile_call(qg, kv1, kv2, old, last):
    first = old is None
    groups, rows, width = qg.shape
    chips = 4
    q_spec = pl.BlockSpec((chips, rows, width), lambda i: (i, 0, 0))
    kv_spec = pl.BlockSpec((ROWS, width), lambda i: (0, 0))
    dq_spec = pl.BlockSpec((chips, HEAD, ROWS), lambda i: (i, 0, 0))
    pairs = groups * ROWS * 2 * ROWS
    return pl.pallas_call(
        functools.partial(tile_kernel, first, last, chips),
        grid=(groups // chips,),
        in_specs=[q_spec, kv_spec, kv_spec] + ([] if first else [dq_spec]),
        out_specs=[dq_spec, kv_spec, kv_spec],
        out_shape=[
            jax.ShapeDtypeStruct((groups, HEAD, ROWS), BF16 if last else F32),
            jax.ShapeDtypeStruct((ROWS, width), BF16),
            jax.ShapeDtypeStruct((ROWS, width), BF16),
        ],
        scratch_shapes=[
            pltpu.VMEM((2 * ROWS, HEAD), F32),
            pltpu.VMEM((2 * ROWS, HEAD), F32),
            pltpu.VMEM((HEAD, 2 * ROWS), BF16),
        ],
        compiler_params=pltpu.CompilerParams(vmem_limit_bytes=40 * 2**20),
        cost_estimate=pl.CostEstimate(
            flops=pairs * HEAD * 10, bytes_accessed=8 * 2**20, transcendentals=pairs
        ),
        name="tile",
    )(*((qg, kv1, kv2) if first else (qg, kv1, kv2, old)))


def shift(x, axis, by):
    n = lax.axis_size(axis)
    return lax.ppermute(x, axis, [(i, (i + by) % n) for i in range(n)])


def local(queries, key_rows, value_rows, attn_output, grad_output, row_lse):
    core = lax.axis_index("core")
    local_rows = queries.shape[0]
    products = grad_output.astype(F32) * attn_output.astype(F32)
    row_delta = jnp.sum(products.reshape(local_rows, 2, HEAD), axis=2).T
    stats = jnp.stack(split3(row_lse * LOG2E) + split3(row_delta), axis=1)
    stats = jnp.pad(stats, ((0, 0), (0, STATS - stats.shape[1]), (0, 0)))
    rows = jnp.concatenate([queries, grad_output, key_rows, value_rows], axis=0)
    even = core == 0
    heads = [
        jnp.concatenate([rows[:, h * HEAD : (h + 1) * HEAD], stats[h]], axis=0)
        for h in range(2)
    ]
    mine = jnp.where(even, heads[0], heads[1])
    other = shift(jnp.where(even, heads[1], heads[0]), "core", 1)

    def part(x, n):
        return x[n * local_rows : (n + 1) * local_rows]

    def pair(x, n):
        return jnp.concatenate([part(x, n), part(x, n + 1)], axis=1)

    query_pack = jnp.concatenate(
        [
            pair(mine, 0),
            pair(other, 0),
            jnp.concatenate([mine[4 * local_rows :], other[4 * local_rows :]], axis=1),
        ],
        axis=0,
    )
    key_pack = jnp.concatenate([pair(mine, 2), pair(other, 2)], axis=0)

    plane = math.prod(lax.axis_size(a) for a in PLANE)
    depth = lax.axis_size("z")
    spread = jnp.broadcast_to(query_pack[None], (plane,) + query_pack.shape)
    gathered = lax.all_to_all(spread, PLANE, 0, 0, tiled=True)
    keys = {0: key_pack}
    for by in (4, 3, 5, 2, 6, 1, 7):
        keys[by] = shift(key_pack, "z", by)

    total_q = None
    owned = []
    for a, b in ((4, 3), (5, 2), (6, 1), (7, 0)):
        total_q, da, db = tile_call(gathered, keys[a], keys[b], total_q, b == 0)
        for by, d in ((a, da), (b, db)):
            owned.append(shift(d, "z", depth - by) if by else d)
    returned = lax.all_to_all(total_q, PLANE, 0, 0, tiled=True)

    grad_kv = sum(d.astype(F32) for d in owned)
    grad_q = jnp.sum(returned.astype(F32), axis=0).T
    grads = jnp.stack([grad_q, grad_kv[:, :HEAD], grad_kv[:, HEAD:]]).astype(BF16)
    kept = grads[:, :local_rows]
    moved = shift(grads[:, local_rows:], "core", 1)
    out = jnp.concatenate(
        [jnp.where(even, kept, moved), jnp.where(even, moved, kept)], axis=2
    )
    return out[0], out[1], out[2]


def solution(mesh):
    devices = mesh.devices.reshape(4, 2, 8, 2, 2)
    torus = Mesh(devices, AXES)
    rows = P(AXES, None)
    return jax.shard_map(
        local,
        mesh=torus,
        in_specs=(rows, rows, rows, rows, rows, P(None, AXES)),
        out_specs=(rows, rows, rows),
        check_vma=False,
    )
```

time: 1160 us -> 119 us (0.10)
  the two profiles are of different devices: /device:TPU:2 before, /device:TPU:1 now
where the time goes in v1:
time: 119 us; the launch traced here: 118 us
  starting transfers between devices  57.6 us (48%)
  waiting for transfers between devices  26.7 us (22%)
  Pallas kernels  24.9 us (21%)
  local copies, waits for them, and re-layouts  5.28 us (4%)
  other arithmetic  2.9 us (2%)
    ppermute x16, starting transfers between devices, shift(): return lax.ppermute(x, axis, [(i, (i + by) % n) for i in range(n)])  49 us
    pallas_call x4, Pallas kernels, tile_call(): pl.pallas_call(functools.partial(tile_kernel, first, last, chips), grid=(...  24.9 us
    ppermute x16, waiting for transfers between devices, shift(): return lax.ppermute(x, axis, [(i, (i + by) % n) for i in range(n)])  15.9 us
    all_to_all x1, waiting for transfers between devices, local(): gathered = lax.all_to_all(spread, PLANE, 0, 0, tiled=True)  10.8 us
    all_to_all x1, starting transfers between devices, local(): gathered = lax.all_to_all(spread, PLANE, 0, 0, tiled=True)  5.02 us
    all_to_all x1, starting transfers between devices, local(): returned = lax.all_to_all(total_q, PLANE, 0, 0, tiled=True)  3.65 us
    unnamed x3, local copies, waits for them, and re-layouts  2.53 us
  transfers between devices with their start and end apart: 18, of which 6 were waited for; matrix products, arithmetic and copies ran while one was open for 0% of the time, Pallas kernels for 15%

profile of v1, /device:TPU:1, one launch (start us, length us, event | category | flops | bytes accessed | tf_op | source)
XLA Modules:
  0.0 118.4 jit_solution(10866610139829592488)
XLA Ops:
  6.2 3.3 %collective-permute-start = (bf16[528,128]{1,0:T(8,128)(2,1)S(1)}, bf16[528,128]{1,0:T(8,128)(2,1)S(1)}, u32[]{:S(2)}, u32[]{:S(2)}) collective-permute-start(bf16[528,128]{1,0:T(8,128)(2,1)S(1)} %get-tuple-element.30), channel_id=1, source_target_pairs={{0,1},{1,0},{2,3},{3,2},{4,5},{5,4},{6,7},{7,6},{8,9},{9,8},{10,11... | collective-permute-start | bytes 405512 | tf_op jit(solution)/shard_map/ppermute | solution.py:107
  10.5 1.5 %broadcast_in_dim.2 = bf16[16,272,256]{2,1,0:T(8,128)(2,1)} broadcast(bf16[272,256]{1,0:T(8,128)(2,1)S(1)} %maximum_maximum_fusion), dimensions={1,2} | broadcast | bytes 2367488 | tf_op jit(solution)/shard_map/broadcast_in_dim | solution.py:144
  12.1 5.0 %all-to-all-start = ((bf16[16,272,256]{2,1,0:T(8,128)(2,1)}), bf16[16,272,256]{2,1,0:T(8,128)(2,1)S(1)}, u32[]{:S(2)}, u32[]{:S(2)}) async-start(bf16[16,272,256]{2,1,0:T(8,128)(2,1)} %broadcast_in_dim.2), calls=%async_computation | async-start | bytes 4456448 | tf_op jit(solution)/shard_map/all_to_all | solution.py:145
  17.1 7.0 %collective-permute-start.6 = (bf16[256,256]{1,0:T(8,128)(2,1)S(1)}, bf16[256,256]{1,0:T(8,128)(2,1)S(1)}, u32[]{:S(2)}, u32[]{:S(2)}) collective-permute-start(bf16[256,256]{1,0:T(8,128)(2,1)S(1)} %maximum_maximum_fusion.1.refs_2_), channel_id=1, source_target_pairs={{0,16},{4,20},{8,24},{12,28},{16,0},{20,4},{24,8},{28,12},{1,17},{... | collective-permute-start | bytes 393224 | tf_op jit(solution)/shard_map/ppermute | solution.py:107
  24.1 1.6 %collective-permute-start.7 = (bf16[256,256]{1,0:T(8,128)(2,1)S(1)}, bf16[256,256]{1,0:T(8,128)(2,1)S(1)}, u32[]{:S(2)}, u32[]{:S(2)}) collective-permute-start(bf16[256,256]{1,0:T(8,128)(2,1)S(1)} %maximum_maximum_fusion.1.refs_2_), channel_id=1, source_target_pairs={{0,12},{4,16},{8,20},{12,24},{16,28},{20,0},{24,4},{28,8},{1,13},{... | collective-permute-start | bytes 393224 | tf_op jit(solution)/shard_map/ppermute | solution.py:107
  25.8 2.8 %collective-permute-start.4 = (bf16[256,256]{1,0:T(8,128)(2,1)S(1)}, bf16[256,256]{1,0:T(8,128)(2,1)S(1)}, u32[]{:S(2)}, u32[]{:S(2)}) collective-permute-start(bf16[256,256]{1,0:T(8,128)(2,1)S(1)} %maximum_maximum_fusion.1.refs_2_), channel_id=1, source_target_pairs={{0,20},{4,24},{8,28},{12,0},{16,4},{20,8},{24,12},{28,16},{1,21},{... | collective-permute-start | bytes 393224 | tf_op jit(solution)/shard_map/ppermute | solution.py:107
  28.6 1.2 %collective-permute-start.5 = (bf16[256,256]{1,0:T(8,128)(2,1)S(1)}, bf16[256,256]{1,0:T(8,128)(2,1)S(1)}, u32[]{:S(2)}, u32[]{:S(2)}) collective-permute-start(bf16[256,256]{1,0:T(8,128)(2,1)S(1)} %maximum_maximum_fusion.1.refs_2_), channel_id=1, source_target_pairs={{0,8},{4,12},{8,16},{12,20},{16,24},{20,28},{24,0},{28,4},{1,9},{5... | collective-permute-start | bytes 393224 | tf_op jit(solution)/shard_map/ppermute | solution.py:107
  29.8 2.4 %collective-permute-start.2 = (bf16[256,256]{1,0:T(8,128)(2,1)S(1)}, bf16[256,256]{1,0:T(8,128)(2,1)S(1)}, u32[]{:S(2)}, u32[]{:S(2)}) collective-permute-start(bf16[256,256]{1,0:T(8,128)(2,1)S(1)} %maximum_maximum_fusion.1.refs_2_), channel_id=1, source_target_pairs={{0,24},{4,28},{8,0},{12,4},{16,8},{20,12},{24,16},{28,20},{1,25},{... | collective-permute-start | bytes 393224 | tf_op jit(solution)/shard_map/ppermute | solution.py:107
  32.9 7.5 %collective-permute-done.7.refs_2_ = bf16[256,256]{1,0:T(8,128)(2,1)S(1)} collective-permute-done((bf16[256,256]{1,0:T(8,128)(2,1)S(1)}, bf16[256,256]{1,0:T(8,128)(2,1)S(1)}, u32[]{:S(2)}, u32[]{:S(2)}) %collective-permute-start.7) | collective-permute-done | bytes 131104 | tf_op jit(solution)/shard_map/ppermute | solution.py:107
  40.4 10.8 %all-to-all-done.refs_0_ = bf16[16,272,256]{2,1,0:T(8,128)(2,1)S(1)} async-done(((bf16[16,272,256]{2,1,0:T(8,128)(2,1)}), bf16[16,272,256]{2,1,0:T(8,128)(2,1)S(1)}, u32[]{:S(2)}, u32[]{:S(2)}) %all-to-all-start) | async-done | bytes 2228256 | tf_op jit(solution)/shard_map/all_to_all | solution.py:145
  51.3 6.0 %tile.4 = (f32[16,128,256]{2,1,0:T(8,128)S(1)}, bf16[256,256]{1,0:T(8,128)(2,1)S(1)}, bf16[256,256]{1,0:T(8,128)(2,1)S(1)}) custom-call(bf16[16,272,256]{2,1,0:T(8,128)(2,1)S(1)} %all-to-all-done.refs_0_, bf16[256,256]{1,0:T(8,128)(2,1)S(1)} %collective-permute-done.6.refs_1_, bf16[256,256]{1,0:T(8,128)(2,1)S(1)} %collective-permute-done.7.refs_2_), custom_call_target="tpu_custom_call" | custom-call | flops 2684354560 | bytes 8388608 | tf_op jit(solution)/shard_map/tile/pallas_call | solution.py:82
  57.3 6.1 %tile.5 = (f32[16,128,256]{2,1,0:T(8,128)S(1)}, bf16[256,256]{1,0:T(8,128)(2,1)S(1)}, bf16[256,256]{1,0:T(8,128)(2,1)S(1)}) custom-call(bf16[16,272,256]{2,1,0:T(8,128)(2,1)S(1)} %all-to-all-done.refs_0_, bf16[256,256]{1,0:T(8,128)(2,1)S(1)} %collective-permute-done.4.refs_1_, bf16[256,256]{1,0:T(8,128)(2,1)S(1)} %collective-permute-done.5.refs_2_, ...), custom_call_target="tpu_custom_call" | custom-call | flops 2684354560 | bytes 8388608 | tf_op jit(solution)/shard_map/tile/pallas_call | solution.py:82
  63.4 6.1 %tile.6 = (f32[16,128,256]{2,1,0:T(8,128)S(1)}, bf16[256,256]{1,0:T(8,128)(2,1)S(1)}, bf16[256,256]{1,0:T(8,128)(2,1)S(1)}) custom-call(bf16[16,272,256]{2,1,0:T(8,128)(2,1)S(1)} %all-to-all-done.refs_0_, bf16[256,256]{1,0:T(8,128)(2,1)S(1)} %collective-permute-done.2.refs_1_, bf16[256,256]{1,0:T(8,128)(2,1)S(1)} %collective-permute-done.3.refs_2_, ...), custom_call_target="tpu_custom_call" | custom-call | flops 2684354560 | bytes 8388608 | tf_op jit(solution)/shard_map/tile/pallas_call | solution.py:82
  69.5 6.8 %tile.7 = (bf16[16,128,256]{2,1,0:T(8,128)(2,1)}, bf16[256,256]{1,0:T(8,128)(2,1)S(1)}, bf16[256,256]{1,0:T(8,128)(2,1)S(1)}) custom-call(bf16[16,272,256]{2,1,0:T(8,128)(2,1)S(1)} %all-to-all-done.refs_0_, bf16[256,256]{1,0:T(8,128)(2,1)S(1)} %collective-permute-done.1.refs_1_, bf16[256,256]{1,0:T(8,128)(2,1)S(1)} %maximum_maximum_fusion.1.refs_2_, ...), custom_call_target="tpu_custom_call" | custom-call | flops 2684354560 | bytes 8388608 | tf_op jit(solution)/shard_map/tile/pallas_call | solution.py:82
  76.3 3.7 %all-to-all-start.1 = ((bf16[16,128,256]{2,1,0:T(8,128)(2,1)}), bf16[16,128,256]{2,1,0:T(8,128)(2,1)S(1)}, u32[]{:S(2)}, u32[]{:S(2)}) async-start(bf16[16,128,256]{2,1,0:T(8,128)(2,1)} %get-tuple-element.18), calls=%async_computation.1 | async-start | bytes 2097152 | tf_op jit(solution)/shard_map/all_to_all | solution.py:156
  80.0 1.7 %collective-permute-start.14 = (bf16[256,256]{1,0:T(8,128)(2,1)S(1)}, bf16[256,256]{1,0:T(8,128)(2,1)S(1)}, u32[]{:S(2)}, u32[]{:S(2)}) collective-permute-start(bf16[256,256]{1,0:T(8,128)(2,1)S(1)} %get-tuple-element.25), channel_id=1, source_target_pairs={{0,4},{4,8},{8,12},{12,16},{16,20},{20,24},{24,28},{28,0},{1,5},{5... | collective-permute-start | bytes 393224 | tf_op jit(solution)/shard_map/ppermute | solution.py:107
  81.7 3.0 %collective-permute-start.12 = (bf16[256,256]{1,0:T(8,128)(2,1)S(1)}, bf16[256,256]{1,0:T(8,128)(2,1)S(1)}, u32[]{:S(2)}, u32[]{:S(2)}) collective-permute-start(bf16[256,256]{1,0:T(8,128)(2,1)S(1)} %get-tuple-element.23), channel_id=1, source_target_pairs={{0,8},{4,12},{8,16},{12,20},{16,24},{20,28},{24,0},{28,4},{1,9},{5... | collective-permute-start | bytes 393224 | tf_op jit(solution)/shard_map/ppermute | solution.py:107
  85.8 3.4 %collective-permute-start.10 = (bf16[256,256]{1,0:T(8,128)(2,1)S(1)}, bf16[256,256]{1,0:T(8,128)(2,1)S(1)}, u32[]{:S(2)}, u32[]{:S(2)}) collective-permute-start(bf16[256,256]{1,0:T(8,128)(2,1)S(1)} %get-tuple-element.21), channel_id=1, source_target_pairs={{0,12},{4,16},{8,20},{12,24},{16,28},{20,0},{24,4},{28,8},{1,13},{... | collective-permute-start | bytes 393224 | tf_op jit(solution)/shard_map/ppermute | solution.py:107
  89.1 1.7 %collective-permute-start.11 = (bf16[256,256]{1,0:T(8,128)(2,1)S(1)}, bf16[256,256]{1,0:T(8,128)(2,1)S(1)}, u32[]{:S(2)}, u32[]{:S(2)}) collective-permute-start(bf16[256,256]{1,0:T(8,128)(2,1)S(1)} %get-tuple-element.22), channel_id=1, source_target_pairs={{0,24},{4,28},{8,0},{12,4},{16,8},{20,12},{24,16},{28,20},{1,25},{... | collective-permute-start | bytes 393224 | tf_op jit(solution)/shard_map/ppermute | solution.py:107
  90.8 2.8 %collective-permute-start.8 = (bf16[256,256]{1,0:T(8,128)(2,1)S(1)}, bf16[256,256]{1,0:T(8,128)(2,1)S(1)}, u32[]{:S(2)}, u32[]{:S(2)}) collective-permute-start(bf16[256,256]{1,0:T(8,128)(2,1)S(1)} %get-tuple-element.19), channel_id=1, source_target_pairs={{0,16},{4,20},{8,24},{12,28},{16,0},{20,4},{24,8},{28,12},{1,17},{... | collective-permute-start | bytes 393224 | tf_op jit(solution)/shard_map/ppermute | solution.py:107
  93.6 3.4 %collective-permute-start.9 = (bf16[256,256]{1,0:T(8,128)(2,1)S(1)}, bf16[256,256]{1,0:T(8,128)(2,1)S(1)}, u32[]{:S(2)}, u32[]{:S(2)}) collective-permute-start(bf16[256,256]{1,0:T(8,128)(2,1)S(1)} %get-tuple-element.20), channel_id=1, source_target_pairs={{0,20},{4,24},{8,28},{12,0},{16,4},{20,8},{24,12},{28,16},{1,21},{... | collective-permute-start | bytes 393224 | tf_op jit(solution)/shard_map/ppermute | solution.py:107
  97.0 3.8 %collective-permute-done.10 = bf16[256,256]{1,0:T(8,128)(2,1)S(1)} collective-permute-done((bf16[256,256]{1,0:T(8,128)(2,1)S(1)}, bf16[256,256]{1,0:T(8,128)(2,1)S(1)}, u32[]{:S(2)}, u32[]{:S(2)}) %collective-permute-start.10) | collective-permute-done | bytes 131104 | tf_op jit(solution)/shard_map/ppermute | solution.py:107
  100.8 2.6 %collective-permute-done.8 = bf16[256,256]{1,0:T(8,128)(2,1)S(1)} collective-permute-done((bf16[256,256]{1,0:T(8,128)(2,1)S(1)}, bf16[256,256]{1,0:T(8,128)(2,1)S(1)}, u32[]{:S(2)}, u32[]{:S(2)}) %collective-permute-start.8) | collective-permute-done | bytes 131104 | tf_op jit(solution)/shard_map/ppermute | solution.py:107
  103.9 12.8 %collective-permute-start.15 = (bf16[3,128,128]{2,1,0:T(8,128)(2,1)S(1)}, bf16[3,128,128]{2,1,0:T(8,128)(2,1)S(1)}, u32[]{:S(2)}, u32[]{:S(2)}) collective-permute-start(bf16[3,128,128]{2,1,0:T(8,128)(2,1)S(1)} %slice.101), channel_id=1, source_target_pairs={{0,1},{1,0},{2,3},{3,2},{4,5},{5,4},{6,7},{7,6},{8,9},{9,8},{10,11... | collective-permute-start | bytes 294920 | tf_op jit(solution)/shard_map/ppermute | solution.py:107
  (51 shorter events, 10.5 us)
Async XLA Ops:
  6.2 4.3 %collective-permute-start = (bf16[528,128]{1,0:T(8,128)(2,1)S(1)}, bf16[528,128]{1,0:T(8,128)(2,1)S(1)}, u32[]{:S(2)}, u32[]{:S(2)}) collective-permute-start(bf16[528,128]{1,0:T(8,128)(2,1)S(1)} %get-tuple-element.30), channel_id=1, source_target_pairs={{0,1},{1,0},{2,3},{3,2},{4,5},{5,4},{6,7},{7,6},{8,9},{9,8},{10,11... | collective-permute-start | bytes 405512 | tf_op jit(solution)/shard_map/ppermute | solution.py:107
  12.1 39.2 %all-to-all-start = ((bf16[16,272,256]{2,1,0:T(8,128)(2,1)}), bf16[16,272,256]{2,1,0:T(8,128)(2,1)S(1)}, u32[]{:S(2)}, u32[]{:S(2)}) async-start(bf16[16,272,256]{2,1,0:T(8,128)(2,1)} %broadcast_in_dim.2), calls=%async_computation | async-start | bytes 4456448 | tf_op jit(solution)/shard_map/all_to_all | solution.py:145
  17.1 15.1 %collective-permute-start.6 = (bf16[256,256]{1,0:T(8,128)(2,1)S(1)}, bf16[256,256]{1,0:T(8,128)(2,1)S(1)}, u32[]{:S(2)}, u32[]{:S(2)}) collective-permute-start(bf16[256,256]{1,0:T(8,128)(2,1)S(1)} %maximum_maximum_fusion.1.refs_2_), channel_id=1, source_target_pairs={{0,16},{4,20},{8,24},{12,28},{16,0},{20,4},{24,8},{28,12},{1,17},{... | collective-permute-start | bytes 393224 | tf_op jit(solution)/shard_map/ppermute | solution.py:107
  24.1 16.3 %collective-permute-start.7 = (bf16[256,256]{1,0:T(8,128)(2,1)S(1)}, bf16[256,256]{1,0:T(8,128)(2,1)S(1)}, u32[]{:S(2)}, u32[]{:S(2)}) collective-permute-start(bf16[256,256]{1,0:T(8,128)(2,1)S(1)} %maximum_maximum_fusion.1.refs_2_), channel_id=1, source_target_pairs={{0,12},{4,16},{8,20},{12,24},{16,28},{20,0},{24,4},{28,8},{1,13},{... | collective-permute-start | bytes 393224 | tf_op jit(solution)/shard_map/ppermute | solution.py:107
  25.8 31.6 %collective-permute-start.4 = (bf16[256,256]{1,0:T(8,128)(2,1)S(1)}, bf16[256,256]{1,0:T(8,128)(2,1)S(1)}, u32[]{:S(2)}, u32[]{:S(2)}) collective-permute-start(bf16[256,256]{1,0:T(8,128)(2,1)S(1)} %maximum_maximum_fusion.1.refs_2_), channel_id=1, source_target_pairs={{0,20},{4,24},{8,28},{12,0},{16,4},{20,8},{24,12},{28,16},{1,21},{... | collective-permute-start | bytes 393224 | tf_op jit(solution)/shard_map/ppermute | solution.py:107
  28.6 28.8 %collective-permute-start.5 = (bf16[256,256]{1,0:T(8,128)(2,1)S(1)}, bf16[256,256]{1,0:T(8,128)(2,1)S(1)}, u32[]{:S(2)}, u32[]{:S(2)}) collective-permute-start(bf16[256,256]{1,0:T(8,128)(2,1)S(1)} %maximum_maximum_fusion.1.refs_2_), channel_id=1, source_target_pairs={{0,8},{4,12},{8,16},{12,20},{16,24},{20,28},{24,0},{28,4},{1,9},{5... | collective-permute-start | bytes 393224 | tf_op jit(solution)/shard_map/ppermute | solution.py:107
  29.8 33.6 %collective-permute-start.2 = (bf16[256,256]{1,0:T(8,128)(2,1)S(1)}, bf16[256,256]{1,0:T(8,128)(2,1)S(1)}, u32[]{:S(2)}, u32[]{:S(2)}) collective-permute-start(bf16[256,256]{1,0:T(8,128)(2,1)S(1)} %maximum_maximum_fusion.1.refs_2_), channel_id=1, source_target_pairs={{0,24},{4,28},{8,0},{12,4},{16,8},{20,12},{24,16},{28,20},{1,25},{... | collective-permute-start | bytes 393224 | tf_op jit(solution)/shard_map/ppermute | solution.py:107
  32.2 31.3 %collective-permute-start.3 = (bf16[256,256]{1,0:T(8,128)(2,1)S(1)}, bf16[256,256]{1,0:T(8,128)(2,1)S(1)}, u32[]{:S(2)}, u32[]{:S(2)}) collective-permute-start(bf16[256,256]{1,0:T(8,128)(2,1)S(1)} %maximum_maximum_fusion.1.refs_2_), channel_id=1, source_target_pairs={{0,4},{4,8},{8,12},{12,16},{16,20},{20,24},{24,28},{28,0},{1,5},{5... | collective-permute-start | bytes 393224 | tf_op jit(solution)/shard_map/ppermute | solution.py:107
  40.4 29.1 %collective-permute-start.1 = (bf16[256,256]{1,0:T(8,128)(2,1)S(1)}, bf16[256,256]{1,0:T(8,128)(2,1)S(1)}, u32[]{:S(2)}, u32[]{:S(2)}) collective-permute-start(bf16[256,256]{1,0:T(8,128)(2,1)S(1)} %maximum_maximum_fusion.1.refs_2_), channel_id=1, source_target_pairs={{0,28},{4,0},{8,4},{12,8},{16,12},{20,16},{24,20},{28,24},{1,29},{... | collective-permute-start | bytes 393224 | tf_op jit(solution)/shard_map/ppermute | solution.py:107
  76.3 27.3 %all-to-all-start.1 = ((bf16[16,128,256]{2,1,0:T(8,128)(2,1)}), bf16[16,128,256]{2,1,0:T(8,128)(2,1)S(1)}, u32[]{:S(2)}, u32[]{:S(2)}) async-start(bf16[16,128,256]{2,1,0:T(8,128)(2,1)} %get-tuple-element.18), calls=%async_computation.1 | async-start | bytes 2097152 | tf_op jit(solution)/shard_map/all_to_all | solution.py:156
  80.0 10.9 %collective-permute-start.14 = (bf16[256,256]{1,0:T(8,128)(2,1)S(1)}, bf16[256,256]{1,0:T(8,128)(2,1)S(1)}, u32[]{:S(2)}, u32[]{:S(2)}) collective-permute-start(bf16[256,256]{1,0:T(8,128)(2,1)S(1)} %get-tuple-element.25), channel_id=1, source_target_pairs={{0,4},{4,8},{8,12},{12,16},{16,20},{20,24},{24,28},{28,0},{1,5},{5... | collective-permute-start | bytes 393224 | tf_op jit(solution)/shard_map/ppermute | solution.py:107
  81.7 12.0 %collective-permute-start.12 = (bf16[256,256]{1,0:T(8,128)(2,1)S(1)}, bf16[256,256]{1,0:T(8,128)(2,1)S(1)}, u32[]{:S(2)}, u32[]{:S(2)}) collective-permute-start(bf16[256,256]{1,0:T(8,128)(2,1)S(1)} %get-tuple-element.23), channel_id=1, source_target_pairs={{0,8},{4,12},{8,16},{12,20},{16,24},{20,28},{24,0},{28,4},{1,9},{5... | collective-permute-start | bytes 393224 | tf_op jit(solution)/shard_map/ppermute | solution.py:107
  84.7 12.3 %collective-permute-start.13 = (bf16[256,256]{1,0:T(8,128)(2,1)S(1)}, bf16[256,256]{1,0:T(8,128)(2,1)S(1)}, u32[]{:S(2)}, u32[]{:S(2)}) collective-permute-start(bf16[256,256]{1,0:T(8,128)(2,1)S(1)} %get-tuple-element.24), channel_id=1, source_target_pairs={{0,28},{4,0},{8,4},{12,8},{16,12},{20,16},{24,20},{28,24},{1,29},{... | collective-permute-start | bytes 393224 | tf_op jit(solution)/shard_map/ppermute | solution.py:107
  85.8 15.0 %collective-permute-start.10 = (bf16[256,256]{1,0:T(8,128)(2,1)S(1)}, bf16[256,256]{1,0:T(8,128)(2,1)S(1)}, u32[]{:S(2)}, u32[]{:S(2)}) collective-permute-start(bf16[256,256]{1,0:T(8,128)(2,1)S(1)} %get-tuple-element.21), channel_id=1, source_target_pairs={{0,12},{4,16},{8,20},{12,24},{16,28},{20,0},{24,4},{28,8},{1,13},{... | collective-permute-start | bytes 393224 | tf_op jit(solution)/shard_map/ppermute | solution.py:107
  89.1 11.7 %collective-permute-start.11 = (bf16[256,256]{1,0:T(8,128)(2,1)S(1)}, bf16[256,256]{1,0:T(8,128)(2,1)S(1)}, u32[]{:S(2)}, u32[]{:S(2)}) collective-permute-start(bf16[256,256]{1,0:T(8,128)(2,1)S(1)} %get-tuple-element.22), channel_id=1, source_target_pairs={{0,24},{4,28},{8,0},{12,4},{16,8},{20,12},{24,16},{28,20},{1,25},{... | collective-permute-start | bytes 393224 | tf_op jit(solution)/shard_map/ppermute | solution.py:107
  90.8 12.6 %collective-permute-start.8 = (bf16[256,256]{1,0:T(8,128)(2,1)S(1)}, bf16[256,256]{1,0:T(8,128)(2,1)S(1)}, u32[]{:S(2)}, u32[]{:S(2)}) collective-permute-start(bf16[256,256]{1,0:T(8,128)(2,1)S(1)} %get-tuple-element.19), channel_id=1, source_target_pairs={{0,16},{4,20},{8,24},{12,28},{16,0},{20,4},{24,8},{28,12},{1,17},{... | collective-permute-start | bytes 393224 | tf_op jit(solution)/shard_map/ppermute | solution.py:107
  93.6 9.8 %collective-permute-start.9 = (bf16[256,256]{1,0:T(8,128)(2,1)S(1)}, bf16[256,256]{1,0:T(8,128)(2,1)S(1)}, u32[]{:S(2)}, u32[]{:S(2)}) collective-permute-start(bf16[256,256]{1,0:T(8,128)(2,1)S(1)} %get-tuple-element.20), channel_id=1, source_target_pairs={{0,20},{4,24},{8,28},{12,0},{16,4},{20,8},{24,12},{28,16},{1,21},{... | collective-permute-start | bytes 393224 | tf_op jit(solution)/shard_map/ppermute | solution.py:107
  103.9 13.8 %collective-permute-start.15 = (bf16[3,128,128]{2,1,0:T(8,128)(2,1)S(1)}, bf16[3,128,128]{2,1,0:T(8,128)(2,1)S(1)}, u32[]{:S(2)}, u32[]{:S(2)}) collective-permute-start(bf16[3,128,128]{2,1,0:T(8,128)(2,1)S(1)} %slice.101), channel_id=1, source_target_pairs={{0,1},{1,0},{2,3},{3,2},{4,5},{5,4},{6,7},{7,6},{8,9},{9,8},{10,11... | collective-permute-start | bytes 294920 | tf_op jit(solution)/shard_map/ppermute | solution.py:107

commit v2 on v1

v2 whole, which is shorter than its diff:
```python
import functools
import math

import jax
import jax.numpy as jnp
from jax import lax
from jax.experimental import pallas as pl
from jax.experimental.pallas import tpu as pltpu
from jax.sharding import Mesh, PartitionSpec as P

HEAD = 128
SCALE = HEAD**-0.5
LOG2E = math.log2(math.e)
AXES = ("y", "xh", "z", "xl", "core")
PLANE = ("y", "xh", "xl")
ROWS = 256
STATS = 16
HALF = 128
NT = (((1,), (1,)), ((), ()))
F32, BF16 = jnp.float32, jnp.bfloat16


def split3(x):
    hi = x.astype(BF16)
    rest = x - hi.astype(F32)
    mid = rest.astype(BF16)
    low = (rest - mid.astype(F32)).astype(BF16)
    return jnp.concatenate([hi.astype(F32), mid.astype(F32), low.astype(F32)], axis=0)


def pack_kernel(core_ref, q_ref, k_ref, v_ref, o_ref, g_ref, lse_ref, qg_ref, kv_ref, send_ref):
    def fill(head, qg, kv):
        cols = slice(head * HEAD, (head + 1) * HEAD)
        g = g_ref[:, cols]
        products = g.astype(F32) * o_ref[:, cols].astype(F32)
        delta = jnp.sum(products.T, axis=0, keepdims=True)
        lse = lse_ref[head : head + 1, :] * LOG2E
        terms = jnp.concatenate([split3(lse), split3(delta)], axis=1)
        terms = jnp.concatenate([terms, jnp.zeros((STATS - 3, 2 * HALF), F32)], axis=0)
        qg[:HALF, :HEAD] = q_ref[:, cols]
        qg[:HALF, HEAD:] = g
        qg[HALF:, :] = terms.astype(BF16)
        kv[:, :HEAD] = k_ref[:, cols]
        kv[:, HEAD:] = v_ref[:, cols]

    send_qg = send_ref.at[: HALF + STATS]
    send_kv = send_ref.at[HALF + STATS :]
    for core in range(2):

        @pl.when(core_ref[0] == core)
        def _():
            fill(core, qg_ref, kv_ref)
            fill(1 - core, send_qg, send_kv)


def pack_call(core, *args):
    width = 2 * HEAD
    return pl.pallas_call(
        pack_kernel,
        in_specs=[pl.BlockSpec(memory_space=pltpu.SMEM)]
        + [pl.BlockSpec(memory_space=pltpu.VMEM)] * 6,
        out_specs=[pl.BlockSpec(memory_space=pltpu.VMEM)] * 3,
        out_shape=[
            jax.ShapeDtypeStruct((HALF + STATS, width), BF16),
            jax.ShapeDtypeStruct((HALF, width), BF16),
            jax.ShapeDtypeStruct((2 * HALF + STATS, width), BF16),
        ],
        name="pack",
    )(core.reshape(1), *args)


def tile_kernel(first, chips, *refs):
    if first:
        qg_ref, kv1_ref, kv2_ref, dq_ref, d1_ref, d2_ref, acc_k, acc_v, kt_ref = refs
    else:
        qg_ref, kv1_ref, kv2_ref, old_ref, _, dq_ref, d1_ref, d2_ref, acc_k, acc_v, kt_ref = refs
    step = pl.program_id(0)
    k = jnp.concatenate([kv1_ref[:, :HEAD], kv2_ref[:, :HEAD]], axis=0)
    v = jnp.concatenate([kv1_ref[:, HEAD:], kv2_ref[:, HEAD:]], axis=0)

    @pl.when(step == 0)
    def _():
        acc_k[...] = jnp.zeros_like(acc_k)
        acc_v[...] = jnp.zeros_like(acc_v)
        kt_ref[...] = k.astype(F32).T.astype(BF16)

    kt = kt_ref[...]
    dk = acc_k[...]
    dv = acc_v[...]
    for chip in range(chips):
        qs, gs, lses, deltas = [], [], [], []
        for base in (0, HALF + STATS):
            qs.append(qg_ref[chip, base : base + HALF, :HEAD])
            gs.append(qg_ref[chip, base : base + HALF, HEAD:])
            stats = qg_ref[chip, base + HALF : base + HALF + STATS, :].astype(F32)
            stats = stats[0:1] + stats[1:2] + stats[2:3]
            lses.append(stats[:, :HALF])
            deltas.append(stats[:, HALF:])
        q = jnp.concatenate(qs, axis=0)
        g = jnp.concatenate(gs, axis=0)
        lse = jnp.concatenate(lses, axis=1)
        delta = jnp.concatenate(deltas, axis=1)
        s = lax.dot_general(k, q, NT, preferred_element_type=F32)
        p = jnp.exp2(s * (SCALE * LOG2E) - lse)
        dp = lax.dot_general(v, g, NT, preferred_element_type=F32)
        ds = (SCALE * p * (dp - delta)).astype(BF16)
        dv = dv + jnp.dot(p.astype(BF16), g, preferred_element_type=F32)
        dk = dk + jnp.dot(ds, q, preferred_element_type=F32)
        dq = jnp.dot(kt, ds, preferred_element_type=F32)
        if not first:
            dq = dq + old_ref[chip]
        dq_ref[chip] = dq.astype(dq_ref.dtype)
    acc_k[...] = dk
    acc_v[...] = dv

    @pl.when(step == pl.num_programs(0) - 1)
    def _():
        d1_ref[:, :HEAD] = dk[:ROWS]
        d1_ref[:, HEAD:] = dv[:ROWS]
        d2_ref[:, :HEAD] = dk[ROWS:]
        d2_ref[:, HEAD:] = dv[ROWS:]


def tile_call(qg, kv1, kv2, old, after, last):
    first = old is None
    groups, rows, width = qg.shape
    chips = 4
    q_spec = pl.BlockSpec((chips, rows, width), lambda i: (i, 0, 0))
    kv_spec = pl.BlockSpec((ROWS, width), lambda i: (0, 0))
    dq_spec = pl.BlockSpec((chips, HEAD, ROWS), lambda i: (i, 0, 0))
    pairs = groups * ROWS * 2 * ROWS
    return pl.pallas_call(
        functools.partial(tile_kernel, first, chips),
        grid=(groups // chips,),
        in_specs=[q_spec, kv_spec, kv_spec]
        + ([] if first else [dq_spec, pl.BlockSpec(memory_space=pl.ANY)]),
        out_specs=[dq_spec, kv_spec, kv_spec],
        out_shape=[
            jax.ShapeDtypeStruct((groups, HEAD, ROWS), BF16 if last else F32),
            jax.ShapeDtypeStruct((ROWS, width), F32),
            jax.ShapeDtypeStruct((ROWS, width), F32),
        ],
        scratch_shapes=[
            pltpu.VMEM((2 * ROWS, HEAD), F32),
            pltpu.VMEM((2 * ROWS, HEAD), F32),
            pltpu.VMEM((HEAD, 2 * ROWS), BF16),
        ],
        compiler_params=pltpu.CompilerParams(vmem_limit_bytes=40 * 2**20),
        cost_estimate=pl.CostEstimate(
            flops=pairs * HEAD * 20, bytes_accessed=8 * 2**20, transcendentals=pairs
        ),
        name="tile",
    )(*((qg, kv1, kv2) if first else (qg, kv1, kv2, old, after)))


def shift(x, axis, by):
    n = lax.axis_size(axis)
    return lax.ppermute(x, axis, [(i, (i + by) % n) for i in range(n)])


def local(queries, key_rows, value_rows, attn_output, grad_output, row_lse):
    core = lax.axis_index("core")
    even = core == 0
    mine_q, mine_kv, send = pack_call(
        core, queries, key_rows, value_rows, attn_output, grad_output, row_lse
    )
    other = shift(send, "core", 1)
    query_pack = jnp.concatenate([mine_q, other[: HALF + STATS]], axis=0)
    key_pack = jnp.concatenate([mine_kv, other[HALF + STATS :]], axis=0)

    plane = math.prod(lax.axis_size(a) for a in PLANE)
    spread = jnp.broadcast_to(query_pack[None], (plane,) + query_pack.shape)
    gathered = lax.all_to_all(spread, PLANE, 0, 0, tiled=True)
    keys = {0: key_pack}
    for by in (1, 2, 3):
        keys[by] = shift(keys[by - 1], "z", 1)
        keys[-by] = shift(keys[1 - by], "z", -1)
    keys[4] = shift(keys[3], "z", 1)

    def low(x):
        return x.astype(BF16)

    total_q, far, own = tile_call(gathered, keys[4], keys[0], None, None, False)
    up = low(far)
    down = None
    after = up
    for by in (3, 2, 1):
        up_in = shift(up, "z", 1)
        down_in = None if down is None else shift(down, "z", -1)
        total_q, du, dd = tile_call(gathered, keys[-by], keys[by], total_q, after, by == 1)
        up = low(du + up_in.astype(F32))
        down = low(dd if down_in is None else dd + down_in.astype(F32))
        after = up
    returned = lax.all_to_all(total_q, PLANE, 0, 0, tiled=True)
    grad_kv = own + shift(up, "z", 1).astype(F32) + shift(down, "z", -1).astype(F32)

    grad_q = jnp.sum(returned.astype(F32), axis=0).T
    grads = jnp.stack([grad_q, grad_kv[:, :HEAD], grad_kv[:, HEAD:]]).astype(BF16)
    kept = grads[:, :HALF]
    moved = shift(grads[:, HALF:], "core", 1)
    out = jnp.concatenate(
        [jnp.where(even, kept, moved), jnp.where(even, moved, kept)], axis=2
    )
    return out[0], out[1], out[2]


def solution(mesh):
    devices = mesh.devices.reshape(4, 2, 8, 2, 2)
    torus = Mesh(devices, AXES)
    rows = P(AXES, None)
    return jax.shard_map(
        local,
        mesh=torus,
        in_specs=(rows, rows, rows, rows, rows, P(None, AXES)),
        out_specs=(rows, rows, rows),
        check_vma=False,
    )
```

time: 119 us -> 111 us (0.933)
  starting transfers between devices: 57.6 us -> 37.2 us
  waiting for transfers between devices: 26.7 us -> 37.7 us
  local copies, waits for them, and re-layouts: 5.28 us -> 3.36 us
  Pallas kernels: 24.9 us -> 26.7 us
  other arithmetic: 2.9 us -> 4.44 us
    ppermute x16, starting transfers between devices: 49 us -> 28.4 us  [shift(): return lax.ppermute(x, axis, [(i, (i + by) % n) for i in range(n)])]
    ppermute x16, waiting for transfers between devices: 15.9 us -> 22 us  [shift(): return lax.ppermute(x, axis, [(i, (i + by) % n) for i in range(n)])]
    all_to_all x1, waiting for transfers between devices: 0.01 us -> 4.88 us  [local(): returned = lax.all_to_all(total_q, PLANE, 0, 0, tiled=True)]
    convert_element_type x0 -> x7, other arithmetic: none -> 2.62 us  [low(): return x.astype(BF16)]
    pallas_call x4 -> x5, Pallas kernels: 24.9 us -> 26.7 us  [the longest x4 24.9 us: tile_call(): pl.pallas_call(functools.partial(tile_kernel, first, chips), grid=(groups...]
    unnamed x3 -> x6, local copies, waits for them, and re-layouts: 2.53 us -> 1.56 us
  transfers between devices with their start and end apart: 18 -> 18, of which waited for: 6 -> 10; matrix products, arithmetic and copies ran while one was open for 0% -> 2% of each run, Pallas kernels for 15% -> 23%
where the time goes in v2:
time: 111 us; the launch traced here: 110 us
  waiting for transfers between devices  37.7 us (34%)
  starting transfers between devices  37.2 us (34%)
  Pallas kernels  26.7 us (24%)
  other arithmetic  4.44 us (4%)
  local copies, waits for them, and re-layouts  3.36 us (3%)
    ppermute x16, starting transfers between devices, shift(): return lax.ppermute(x, axis, [(i, (i + by) % n) for i in range(n)])  28.4 us
    pallas_call x4, Pallas kernels, tile_call(): pl.pallas_call(functools.partial(tile_kernel, first, chips), grid=(groups...  24.9 us
    ppermute x16, waiting for transfers between devices, shift(): return lax.ppermute(x, axis, [(i, (i + by) % n) for i in range(n)])  22 us
    all_to_all x1, waiting for transfers between devices, local(): gathered = lax.all_to_all(spread, PLANE, 0, 0, tiled=True)  10.8 us
    all_to_all x1, starting transfers between devices, local(): gathered = lax.all_to_all(spread, PLANE, 0, 0, tiled=True)  5.15 us
    all_to_all x1, waiting for transfers between devices, local(): returned = lax.all_to_all(total_q, PLANE, 0, 0, tiled=True)  4.88 us
    all_to_all x1, starting transfers between devices, local(): returned = lax.all_to_all(total_q, PLANE, 0, 0, tiled=True)  3.65 us
    convert_element_type x7, other arithmetic, low(): return x.astype(BF16)  2.62 us
  transfers between devices with their start and end apart: 18, of which 10 were waited for; matrix products, arithmetic and copies ran while one was open for 2% of the time, Pallas kernels for 23%

profile of v2, /device:TPU:1, one launch (start us, length us, event | category | flops | bytes accessed | tf_op | source)
XLA Modules:
  0.0 110.2 jit_solution(6801920797224476528)
XLA Ops:
  0.6 1.8 %pack.1 = (bf16[144,256]{1,0:T(8,128)(2,1)}, bf16[128,256]{1,0:T(8,128)(2,1)}, bf16[272,256]{1,0:T(8,128)(2,1)}) custom-call(s32[1]{0:T(128)} %bitcast.core_ref, bf16[128,256]{1,0:T(8,128)(2,1)} %q_ref.1, bf16[128,256]{1,0:T(8,128)(2,1)} %k_ref.1, bf16[128,256]{1,0:T(8,128)(2,1)} %v_ref.1, bf16[128,256]{1,0:T(8,128)(2,1)} %o_ref.1, bf16[128,256]{1,0:T(8,128)(2,1)} %g_ref.1, ...), custom_call_target="tpu_custom_call" | custom-call | tf_op jit(solution)/shard_map/pack/pallas_call | solution.py:58
  2.4 3.2 %collective-permute-start = (bf16[272,256]{1,0:T(8,128)(2,1)}, bf16[272,256]{1,0:T(8,128)(2,1)S(1)}, u32[]{:S(2)}, u32[]{:S(2)}) collective-permute-start(bf16[272,256]{1,0:T(8,128)(2,1)} %get-tuple-element.19), channel_id=1, source_target_pairs={{0,1},{1,0},{2,3},{3,2},{4,5},{5,4},{6,7},{7,6},{8,9},{9,8},{10,11... | collective-permute-start | bytes 417800 | tf_op jit(solution)/shard_map/ppermute | solution.py:158
  9.5 5.2 %all-to-all-start = ((bf16[16,288,256]{2,1,0:T(8,128)(2,1)}), bf16[16,288,256]{2,1,0:T(8,128)(2,1)S(1)}, u32[]{:S(2)}, u32[]{:S(2)}) async-start(bf16[16,288,256]{2,1,0:T(8,128)(2,1)} %broadcast_in_dim.2), calls=%async_computation | async-start | bytes 4718592 | tf_op jit(solution)/shard_map/all_to_all | solution.py:173
  14.7 1.7 %collective-permute-start.2 = (bf16[256,256]{1,0:T(8,128)(2,1)S(1)}, bf16[256,256]{1,0:T(8,128)(2,1)S(1)}, u32[]{:S(2)}, u32[]{:S(2)}) collective-permute-start(bf16[256,256]{1,0:T(8,128)(2,1)S(1)} %pad_maximum_fusion.2.refs_2_), channel_id=1, source_target_pairs={{0,4},{4,8},{8,12},{12,16},{16,20},{20,24},{24,28},{28,0},{1,5},{5... | collective-permute-start | bytes 393224 | tf_op jit(solution)/shard_map/ppermute | solution.py:158
  16.4 7.2 %collective-permute-done.2.refs_2_ = bf16[256,256]{1,0:T(8,128)(2,1)S(1)} collective-permute-done((bf16[256,256]{1,0:T(8,128)(2,1)S(1)}, bf16[256,256]{1,0:T(8,128)(2,1)S(1)}, u32[]{:S(2)}, u32[]{:S(2)}) %collective-permute-start.2) | collective-permute-done | bytes 131104 | tf_op jit(solution)/shard_map/ppermute | solution.py:158
  23.6 2.7 %collective-permute-start.1 = (bf16[256,256]{1,0:T(8,128)(2,1)S(1)}, bf16[256,256]{1,0:T(8,128)(2,1)S(1)}, u32[]{:S(2)}, u32[]{:S(2)}) collective-permute-start(bf16[256,256]{1,0:T(8,128)(2,1)S(1)} %pad_maximum_fusion.2.refs_2_), channel_id=1, source_target_pairs={{0,28},{4,0},{8,4},{12,8},{16,12},{20,16},{24,20},{28,24},{1,29},{... | collective-permute-start | bytes 393224 | tf_op jit(solution)/shard_map/ppermute | solution.py:158
  26.2 2.6 %collective-permute-done.4.refs_2_ = bf16[256,256]{1,0:T(8,128)(2,1)S(1)} collective-permute-done((bf16[256,256]{1,0:T(8,128)(2,1)S(1)}, bf16[256,256]{1,0:T(8,128)(2,1)S(1)}, u32[]{:S(2)}, u32[]{:S(2)}) %collective-permute-start.4) | collective-permute-done | bytes 131104 | tf_op jit(solution)/shard_map/ppermute | solution.py:158
  28.9 2.7 %collective-permute-start.3 = (bf16[256,256]{1,0:T(8,128)(2,1)S(1)}, bf16[256,256]{1,0:T(8,128)(2,1)S(1)}, u32[]{:S(2)}, u32[]{:S(2)}) collective-permute-start(bf16[256,256]{1,0:T(8,128)(2,1)S(1)} %collective-permute-done.1.refs_1_), channel_id=1, source_target_pairs={{0,28},{4,0},{8,4},{12,8},{16,12},{20,16},{24,20},{28,24},{1,29},{... | collective-permute-start | bytes 393224 | tf_op jit(solution)/shard_map/ppermute | solution.py:158
  31.6 2.3 %collective-permute-done.6.refs_2_ = bf16[256,256]{1,0:T(8,128)(2,1)S(1)} collective-permute-done((bf16[256,256]{1,0:T(8,128)(2,1)S(1)}, bf16[256,256]{1,0:T(8,128)(2,1)S(1)}, u32[]{:S(2)}, u32[]{:S(2)}) %collective-permute-start.6) | collective-permute-done | bytes 131104 | tf_op jit(solution)/shard_map/ppermute | solution.py:158
  33.9 3.0 %collective-permute-start.5 = (bf16[256,256]{1,0:T(8,128)(2,1)S(1)}, bf16[256,256]{1,0:T(8,128)(2,1)S(1)}, u32[]{:S(2)}, u32[]{:S(2)}) collective-permute-start(bf16[256,256]{1,0:T(8,128)(2,1)S(1)} %collective-permute-done.3.refs_1_), channel_id=1, source_target_pairs={{0,28},{4,0},{8,4},{12,8},{16,12},{20,16},{24,20},{28,24},{1,29},{... | collective-permute-start | bytes 393224 | tf_op jit(solution)/shard_map/ppermute | solution.py:158
  36.9 2.3 %collective-permute-done.7.refs_1_ = bf16[256,256]{1,0:T(8,128)(2,1)S(1)} collective-permute-done((bf16[256,256]{1,0:T(8,128)(2,1)S(1)}, bf16[256,256]{1,0:T(8,128)(2,1)S(1)}, u32[]{:S(2)}, u32[]{:S(2)}) %collective-permute-start.7) | collective-permute-done | bytes 131104 | tf_op jit(solution)/shard_map/ppermute | solution.py:158
  39.9 10.8 %all-to-all-done.refs_0_ = bf16[16,288,256]{2,1,0:T(8,128)(2,1)S(1)} async-done(((bf16[16,288,256]{2,1,0:T(8,128)(2,1)}), bf16[16,288,256]{2,1,0:T(8,128)(2,1)S(1)}, u32[]{:S(2)}, u32[]{:S(2)}) %all-to-all-start) | async-done | bytes 2359328 | tf_op jit(solution)/shard_map/all_to_all | solution.py:173
  51.6 6.0 %tile.4 = (f32[16,128,256]{2,1,0:T(8,128)S(1)}, f32[256,256]{1,0:T(8,128)S(1)}, f32[256,256]{1,0:T(8,128)S(1)}) custom-call(bf16[16,288,256]{2,1,0:T(8,128)(2,1)S(1)} %all-to-all-done.refs_0_, bf16[256,256]{1,0:T(8,128)(2,1)S(1)} %copy-done.1, bf16[256,256]{1,0:T(8,128)(2,1)S(1)} %pad_maximum_fusion.2.refs_2_), custom_call_target="tpu_custom_call" | custom-call | flops 5368709120 | bytes 8388608 | tf_op jit(solution)/shard_map/tile/pallas_call | solution.py:132
  57.6 1.7 %collective-permute-start.8 = (bf16[256,256]{1,0:T(8,128)(2,1)S(1)}, bf16[256,256]{1,0:T(8,128)(2,1)S(1)}, u32[]{:S(2)}, u32[]{:S(2)}) collective-permute-start(bf16[256,256]{1,0:T(8,128)(2,1)S(1)} %convert_element_type.46.refs_4_), channel_id=1, source_target_pairs={{0,4},{4,8},{8,12},{12,16},{16,20},{20,24},{24,28},{28,0},{1,5},{5... | collective-permute-start | bytes 393224 | tf_op jit(solution)/shard_map/ppermute | solution.py:158
  59.3 6.0 %tile.5 = (f32[16,128,256]{2,1,0:T(8,128)S(1)}, f32[256,256]{1,0:T(8,128)S(1)}, f32[256,256]{1,0:T(8,128)S(1)}) custom-call(bf16[16,288,256]{2,1,0:T(8,128)(2,1)S(1)} %all-to-all-done.refs_0_, bf16[256,256]{1,0:T(8,128)(2,1)S(1)} %collective-permute-done.5.refs_1_, bf16[256,256]{1,0:T(8,128)(2,1)S(1)} %collective-permute-done.6.refs_2_, ...), custom_call_target="tpu_custom_call" | custom-call | flops 5368709120 | bytes 8388608 | tf_op jit(solution)/shard_map/tile/pallas_call | solution.py:132
  65.4 4.1 %collective-permute-start.12 = (bf16[256,256]{1,0:T(8,128)(2,1)S(1)}, bf16[256,256]{1,0:T(8,128)(2,1)S(1)}, u32[]{:S(2)}, u32[]{:S(2)}) collective-permute-start(bf16[256,256]{1,0:T(8,128)(2,1)S(1)} %convert_element_type.55), channel_id=1, source_target_pairs={{0,28},{4,0},{8,4},{12,8},{16,12},{20,16},{24,20},{28,24},{1,29},{... | collective-permute-start | bytes 393224 | tf_op jit(solution)/shard_map/ppermute | solution.py:158
  69.7 6.0 %tile.6 = (f32[16,128,256]{2,1,0:T(8,128)S(1)}, f32[256,256]{1,0:T(8,128)S(1)}, f32[256,256]{1,0:T(8,128)S(1)}) custom-call(bf16[16,288,256]{2,1,0:T(8,128)(2,1)S(1)} %all-to-all-done.refs_0_, bf16[256,256]{1,0:T(8,128)(2,1)S(1)} %collective-permute-done.3.refs_1_, bf16[256,256]{1,0:T(8,128)(2,1)S(1)} %collective-permute-done.4.refs_2_, ...), custom_call_target="tpu_custom_call" | custom-call | flops 5368709120 | bytes 8388608 | tf_op jit(solution)/shard_map/tile/pallas_call | solution.py:132
  76.5 2.6 %collective-permute-start.13 = (bf16[256,256]{1,0:T(8,128)(2,1)}, bf16[256,256]{1,0:T(8,128)(2,1)}, u32[]{:S(2)}, u32[]{:S(2)}) collective-permute-start(bf16[256,256]{1,0:T(8,128)(2,1)} %add_convert_fusion.2), channel_id=1, source_target_pairs={{0,28},{4,0},{8,4},{12,8},{16,12},{20,16},{24,20},{28,24},{1,29},{... | collective-permute-start | bytes 393224 | tf_op jit(solution)/shard_map/ppermute | solution.py:158
  79.3 6.8 %tile.7 = (bf16[16,128,256]{2,1,0:T(8,128)(2,1)}, f32[256,256]{1,0:T(8,128)S(1)}, f32[256,256]{1,0:T(8,128)S(1)}) custom-call(bf16[16,288,256]{2,1,0:T(8,128)(2,1)S(1)} %all-to-all-done.refs_0_, bf16[256,256]{1,0:T(8,128)(2,1)S(1)} %collective-permute-done.1.refs_1_, bf16[256,256]{1,0:T(8,128)(2,1)S(1)} %collective-permute-done.2.refs_2_, ...), custom_call_target="tpu_custom_call" | custom-call | flops 5368709120 | bytes 8388608 | tf_op jit(solution)/shard_map/tile/pallas_call | solution.py:132
  86.1 3.7 %all-to-all-start.1 = ((bf16[16,128,256]{2,1,0:T(8,128)(2,1)}), bf16[16,128,256]{2,1,0:T(8,128)(2,1)S(1)}, u32[]{:S(2)}, u32[]{:S(2)}) async-start(bf16[16,128,256]{2,1,0:T(8,128)(2,1)} %get-tuple-element.27), calls=%async_computation.1 | async-start | bytes 2097152 | tf_op jit(solution)/shard_map/all_to_all | solution.py:194
  90.7 2.7 %collective-permute-start.14 = (bf16[256,256]{1,0:T(8,128)(2,1)S(1)}, bf16[256,256]{1,0:T(8,128)(2,1)S(1)}, u32[]{:S(2)}, u32[]{:S(2)}) collective-permute-start(bf16[256,256]{1,0:T(8,128)(2,1)S(1)} %add_convert_fusion.1), channel_id=1, source_target_pairs={{0,28},{4,0},{8,4},{12,8},{16,12},{20,16},{24,20},{28,24},{1,29},{... | collective-permute-start | bytes 393224 | tf_op jit(solution)/shard_map/ppermute | solution.py:158
  95.3 4.4 %collective-permute-done.11 = bf16[256,256]{1,0:T(8,128)(2,1)S(1)} collective-permute-done((bf16[256,256]{1,0:T(8,128)(2,1)S(1)}, bf16[256,256]{1,0:T(8,128)(2,1)S(1)}, u32[]{:S(2)}, u32[]{:S(2)}) %collective-permute-start.11) | collective-permute-done | bytes 131104 | tf_op jit(solution)/shard_map/ppermute | solution.py:158
  99.8 4.9 %all-to-all-done.1 = bf16[16,128,256]{2,1,0:T(8,128)(2,1)S(1)} async-done(((bf16[16,128,256]{2,1,0:T(8,128)(2,1)}), bf16[16,128,256]{2,1,0:T(8,128)(2,1)S(1)}, u32[]{:S(2)}, u32[]{:S(2)}) %all-to-all-start.1) | async-done | bytes 1048608 | tf_op jit(solution)/shard_map/all_to_all | solution.py:194
  105.0 3.6 %collective-permute-start.15 = (bf16[3,128,128]{2,1,0:T(8,128)(2,1)S(1)}, bf16[3,128,128]{2,1,0:T(8,128)(2,1)S(1)}, u32[]{:S(2)}, u32[]{:S(2)}) collective-permute-start(bf16[3,128,128]{2,1,0:T(8,128)(2,1)S(1)} %slice.43), channel_id=1, source_target_pairs={{0,1},{1,0},{2,3},{3,2},{4,5},{5,4},{6,7},{7,6},{8,9},{9,8},{10,11... | collective-permute-start | bytes 294920 | tf_op jit(solution)/shard_map/ppermute | solution.py:158
  (43 shorter events, 11.3 us)
Async XLA Ops:
  2.4 4.4 %collective-permute-start = (bf16[272,256]{1,0:T(8,128)(2,1)}, bf16[272,256]{1,0:T(8,128)(2,1)S(1)}, u32[]{:S(2)}, u32[]{:S(2)}) collective-permute-start(bf16[272,256]{1,0:T(8,128)(2,1)} %get-tuple-element.19), channel_id=1, source_target_pairs={{0,1},{1,0},{2,3},{3,2},{4,5},{5,4},{6,7},{7,6},{8,9},{9,8},{10,11... | collective-permute-start | bytes 417800 | tf_op jit(solution)/shard_map/ppermute | solution.py:158
  9.5 5.2 %copy-start.2 = (bf16[128,256]{1,0:T(8,128)(2,1)S(1)}, bf16[128,256]{1,0:T(8,128)(2,1)}, u32[]{:S(2)}) copy-start(bf16[128,256]{1,0:T(8,128)(2,1)} %get-tuple-element.20) | copy-start | bytes 196612
  9.5 41.2 %all-to-all-start = ((bf16[16,288,256]{2,1,0:T(8,128)(2,1)}), bf16[16,288,256]{2,1,0:T(8,128)(2,1)S(1)}, u32[]{:S(2)}, u32[]{:S(2)}) async-start(bf16[16,288,256]{2,1,0:T(8,128)(2,1)} %broadcast_in_dim.2), calls=%async_computation | async-start | bytes 4718592 | tf_op jit(solution)/shard_map/all_to_all | solution.py:173
  14.7 8.9 %collective-permute-start.2 = (bf16[256,256]{1,0:T(8,128)(2,1)S(1)}, bf16[256,256]{1,0:T(8,128)(2,1)S(1)}, u32[]{:S(2)}, u32[]{:S(2)}) collective-permute-start(bf16[256,256]{1,0:T(8,128)(2,1)S(1)} %pad_maximum_fusion.2.refs_2_), channel_id=1, source_target_pairs={{0,4},{4,8},{8,12},{12,16},{16,20},{20,24},{24,28},{28,0},{1,5},{5... | collective-permute-start | bytes 393224 | tf_op jit(solution)/shard_map/ppermute | solution.py:158
  23.6 5.3 %collective-permute-start.4 = (bf16[256,256]{1,0:T(8,128)(2,1)S(1)}, bf16[256,256]{1,0:T(8,128)(2,1)S(1)}, u32[]{:S(2)}, u32[]{:S(2)}) collective-permute-start(bf16[256,256]{1,0:T(8,128)(2,1)S(1)} %collective-permute-done.2.refs_2_), channel_id=1, source_target_pairs={{0,4},{4,8},{8,12},{12,16},{16,20},{20,24},{24,28},{28,0},{1,5},{5... | collective-permute-start | bytes 393224 | tf_op jit(solution)/shard_map/ppermute | solution.py:158
  23.6 5.3 %collective-permute-start.1 = (bf16[256,256]{1,0:T(8,128)(2,1)S(1)}, bf16[256,256]{1,0:T(8,128)(2,1)S(1)}, u32[]{:S(2)}, u32[]{:S(2)}) collective-permute-start(bf16[256,256]{1,0:T(8,128)(2,1)S(1)} %pad_maximum_fusion.2.refs_2_), channel_id=1, source_target_pairs={{0,28},{4,0},{8,4},{12,8},{16,12},{20,16},{24,20},{28,24},{1,29},{... | collective-permute-start | bytes 393224 | tf_op jit(solution)/shard_map/ppermute | solution.py:158
  28.9 5.0 %collective-permute-start.6 = (bf16[256,256]{1,0:T(8,128)(2,1)S(1)}, bf16[256,256]{1,0:T(8,128)(2,1)S(1)}, u32[]{:S(2)}, u32[]{:S(2)}) collective-permute-start(bf16[256,256]{1,0:T(8,128)(2,1)S(1)} %collective-permute-done.4.refs_2_), channel_id=1, source_target_pairs={{0,4},{4,8},{8,12},{12,16},{16,20},{20,24},{24,28},{28,0},{1,5},{5... | collective-permute-start | bytes 393224 | tf_op jit(solution)/shard_map/ppermute | solution.py:158
  28.9 5.0 %collective-permute-start.3 = (bf16[256,256]{1,0:T(8,128)(2,1)S(1)}, bf16[256,256]{1,0:T(8,128)(2,1)S(1)}, u32[]{:S(2)}, u32[]{:S(2)}) collective-permute-start(bf16[256,256]{1,0:T(8,128)(2,1)S(1)} %collective-permute-done.1.refs_1_), channel_id=1, source_target_pairs={{0,28},{4,0},{8,4},{12,8},{16,12},{20,16},{24,20},{28,24},{1,29},{... | collective-permute-start | bytes 393224 | tf_op jit(solution)/shard_map/ppermute | solution.py:158
  33.9 5.3 %collective-permute-start.7 = (bf16[256,256]{1,0:T(8,128)(2,1)S(1)}, bf16[256,256]{1,0:T(8,128)(2,1)S(1)}, u32[]{:S(2)}, u32[]{:S(2)}) collective-permute-start(bf16[256,256]{1,0:T(8,128)(2,1)S(1)} %collective-permute-done.6.refs_2_), channel_id=1, source_target_pairs={{0,4},{4,8},{8,12},{12,16},{16,20},{20,24},{24,28},{28,0},{1,5},{5... | collective-permute-start | bytes 393224 | tf_op jit(solution)/shard_map/ppermute | solution.py:158
  33.9 25.4 %collective-permute-start.5 = (bf16[256,256]{1,0:T(8,128)(2,1)S(1)}, bf16[256,256]{1,0:T(8,128)(2,1)S(1)}, u32[]{:S(2)}, u32[]{:S(2)}) collective-permute-start(bf16[256,256]{1,0:T(8,128)(2,1)S(1)} %collective-permute-done.3.refs_1_), channel_id=1, source_target_pairs={{0,28},{4,0},{8,4},{12,8},{16,12},{20,16},{24,20},{28,24},{1,29},{... | collective-permute-start | bytes 393224 | tf_op jit(solution)/shard_map/ppermute | solution.py:158
  39.2 0.6 copy-start
  50.7 0.9 copy-start.1
  57.6 11.8 %collective-permute-start.8 = (bf16[256,256]{1,0:T(8,128)(2,1)S(1)}, bf16[256,256]{1,0:T(8,128)(2,1)S(1)}, u32[]{:S(2)}, u32[]{:S(2)}) collective-permute-start(bf16[256,256]{1,0:T(8,128)(2,1)S(1)} %convert_element_type.46.refs_4_), channel_id=1, source_target_pairs={{0,4},{4,8},{8,12},{12,16},{16,20},{20,24},{24,28},{28,0},{1,5},{5... | collective-permute-start | bytes 393224 | tf_op jit(solution)/shard_map/ppermute | solution.py:158
  65.4 10.4 %collective-permute-start.12 = (bf16[256,256]{1,0:T(8,128)(2,1)S(1)}, bf16[256,256]{1,0:T(8,128)(2,1)S(1)}, u32[]{:S(2)}, u32[]{:S(2)}) collective-permute-start(bf16[256,256]{1,0:T(8,128)(2,1)S(1)} %convert_element_type.55), channel_id=1, source_target_pairs={{0,28},{4,0},{8,4},{12,8},{16,12},{20,16},{24,20},{28,24},{1,29},{... | collective-permute-start | bytes 393224 | tf_op jit(solution)/shard_map/ppermute | solution.py:158
  69.5 9.7 %collective-permute-start.9 = (bf16[256,256]{1,0:T(8,128)(2,1)S(1)}, bf16[256,256]{1,0:T(8,128)(2,1)S(1)}, u32[]{:S(2)}, u32[]{:S(2)}) collective-permute-start(bf16[256,256]{1,0:T(8,128)(2,1)S(1)} %add_convert_fusion.5.refs_4_), channel_id=1, source_target_pairs={{0,4},{4,8},{8,12},{12,16},{16,20},{20,24},{24,28},{28,0},{1,5},{5... | collective-permute-start | bytes 393224 | tf_op jit(solution)/shard_map/ppermute | solution.py:158
  76.5 13.2 %collective-permute-start.13 = (bf16[256,256]{1,0:T(8,128)(2,1)}, bf16[256,256]{1,0:T(8,128)(2,1)}, u32[]{:S(2)}, u32[]{:S(2)}) collective-permute-start(bf16[256,256]{1,0:T(8,128)(2,1)} %add_convert_fusion.2), channel_id=1, source_target_pairs={{0,28},{4,0},{8,4},{12,8},{16,12},{20,16},{24,20},{28,24},{1,29},{... | collective-permute-start | bytes 393224 | tf_op jit(solution)/shard_map/ppermute | solution.py:158
  79.2 14.2 %collective-permute-start.10 = (bf16[256,256]{1,0:T(8,128)(2,1)S(1)}, bf16[256,256]{1,0:T(8,128)(2,1)}, u32[]{:S(2)}, u32[]{:S(2)}) collective-permute-start(bf16[256,256]{1,0:T(8,128)(2,1)S(1)} %add_convert_fusion.4.refs_4_), channel_id=1, source_target_pairs={{0,4},{4,8},{8,12},{12,16},{16,20},{20,24},{24,28},{28,0},{1,5},{5... | collective-permute-start | bytes 393224 | tf_op jit(solution)/shard_map/ppermute | solution.py:158
  86.1 18.6 %all-to-all-start.1 = ((bf16[16,128,256]{2,1,0:T(8,128)(2,1)}), bf16[16,128,256]{2,1,0:T(8,128)(2,1)S(1)}, u32[]{:S(2)}, u32[]{:S(2)}) async-start(bf16[16,128,256]{2,1,0:T(8,128)(2,1)} %get-tuple-element.27), calls=%async_computation.1 | async-start | bytes 2097152 | tf_op jit(solution)/shard_map/all_to_all | solution.py:194
  90.7 4.7 %collective-permute-start.14 = (bf16[256,256]{1,0:T(8,128)(2,1)S(1)}, bf16[256,256]{1,0:T(8,128)(2,1)S(1)}, u32[]{:S(2)}, u32[]{:S(2)}) collective-permute-start(bf16[256,256]{1,0:T(8,128)(2,1)S(1)} %add_convert_fusion.1), channel_id=1, source_target_pairs={{0,28},{4,0},{8,4},{12,8},{16,12},{20,16},{24,20},{28,24},{1,29},{... | collective-permute-start | bytes 393224 | tf_op jit(solution)/shard_map/ppermute | solution.py:158
  94.3 5.4 %collective-permute-start.11 = (bf16[256,256]{1,0:T(8,128)(2,1)S(1)}, bf16[256,256]{1,0:T(8,128)(2,1)S(1)}, u32[]{:S(2)}, u32[]{:S(2)}) collective-permute-start(bf16[256,256]{1,0:T(8,128)(2,1)S(1)} %add_convert_fusion.3), channel_id=1, source_target_pairs={{0,4},{4,8},{8,12},{12,16},{16,20},{20,24},{24,28},{28,0},{1,5},{5... | collective-permute-start | bytes 393224 | tf_op jit(solution)/shard_map/ppermute | solution.py:158
  105.0 4.5 %collective-permute-start.15 = (bf16[3,128,128]{2,1,0:T(8,128)(2,1)S(1)}, bf16[3,128,128]{2,1,0:T(8,128)(2,1)S(1)}, u32[]{:S(2)}, u32[]{:S(2)}) collective-permute-start(bf16[3,128,128]{2,1,0:T(8,128)(2,1)S(1)} %slice.43), channel_id=1, source_target_pairs={{0,1},{1,0},{2,3},{3,2},{4,5},{5,4},{6,7},{7,6},{8,9},{9,8},{10,11... | collective-permute-start | bytes 294920 | tf_op jit(solution)/shard_map/ppermute | solution.py:158

commit v3 on v2

--- a/solution.py
+++ b/solution.py
@@ -12,7 +12,7 @@
 SCALE = HEAD**-0.5
 LOG2E = math.log2(math.e)
 AXES = ("y", "xh", "z", "xl", "core")
-PLANE = ("y", "xh", "xl")
+GROUP = ("y", "xl")
 ROWS = 256
 STATS = 16
 HALF = 128
@@ -69,24 +69,43 @@
     )(core.reshape(1), *args)
 
 
+def spread_kernel(mine_ref, kv_ref, other_ref, out_ref, keys_ref):
+    rows = HALF + STATS
+    for n in range(out_ref.shape[0]):
+        out_ref[n, :rows, :] = mine_ref[...]
+        out_ref[n, rows:, :] = other_ref[:rows, :]
+    keys_ref[:HALF, :] = kv_ref[...]
+    keys_ref[HALF:, :] = other_ref[rows:, :]
+
+
+def spread_call(n, *args):
+    return pl.pallas_call(
+        spread_kernel,
+        in_specs=[pl.BlockSpec(memory_space=pltpu.VMEM)] * 3,
+        out_specs=[pl.BlockSpec(memory_space=pltpu.VMEM)] * 2,
+        out_shape=[
+            jax.ShapeDtypeStruct((n, 2 * (HALF + STATS), 2 * HEAD), BF16),
+            jax.ShapeDtypeStruct((ROWS, 2 * HEAD), BF16),
+        ],
+        name="spread",
+    )(*args)
+
+
 def tile_kernel(first, chips, *refs):
     if first:
         qg_ref, kv1_ref, kv2_ref, dq_ref, d1_ref, d2_ref, acc_k, acc_v, kt_ref = refs
     else:
         qg_ref, kv1_ref, kv2_ref, old_ref, _, dq_ref, d1_ref, d2_ref, acc_k, acc_v, kt_ref = refs
     step = pl.program_id(0)
-    k = jnp.concatenate([kv1_ref[:, :HEAD], kv2_ref[:, :HEAD]], axis=0)
-    v = jnp.concatenate([kv1_ref[:, HEAD:], kv2_ref[:, HEAD:]], axis=0)
+    blocks = (kv1_ref, kv2_ref)
 
     @pl.when(step == 0)
     def _():
         acc_k[...] = jnp.zeros_like(acc_k)
         acc_v[...] = jnp.zeros_like(acc_v)
-        kt_ref[...] = k.astype(F32).T.astype(BF16)
-
-    kt = kt_ref[...]
-    dk = acc_k[...]
-    dv = acc_v[...]
+        for n, kv_ref in enumerate(blocks):
+            kt_ref[n] = kv_ref[:, :HEAD].astype(F32).T.astype(BF16)
+
     for chip in range(chips):
         qs, gs, lses, deltas = [], [], [], []
         for base in (0, HALF + STATS):
@@ -100,25 +119,23 @@
         g = jnp.concatenate(gs, axis=0)
         lse = jnp.concatenate(lses, axis=1)
         delta = jnp.concatenate(deltas, axis=1)
-        s = lax.dot_general(k, q, NT, preferred_element_type=F32)
-        p = jnp.exp2(s * (SCALE * LOG2E) - lse)
-        dp = lax.dot_general(v, g, NT, preferred_element_type=F32)
-        ds = (SCALE * p * (dp - delta)).astype(BF16)
-        dv = dv + jnp.dot(p.astype(BF16), g, preferred_element_type=F32)
-        dk = dk + jnp.dot(ds, q, preferred_element_type=F32)
-        dq = jnp.dot(kt, ds, preferred_element_type=F32)
-        if not first:
-            dq = dq + old_ref[chip]
-        dq_ref[chip] = dq.astype(dq_ref.dtype)
-    acc_k[...] = dk
-    acc_v[...] = dv
+        total = None if first else old_ref[chip]
+        for n, kv_ref in enumerate(blocks):
+            s = lax.dot_general(kv_ref[:, :HEAD], q, NT, preferred_element_type=F32)
+            p = jnp.exp2(s * (SCALE * LOG2E) - lse)
+            dp = lax.dot_general(kv_ref[:, HEAD:], g, NT, preferred_element_type=F32)
+            ds = (SCALE * p * (dp - delta)).astype(BF16)
+            acc_v[n] += jnp.dot(p.astype(BF16), g, preferred_element_type=F32)
+            acc_k[n] += jnp.dot(ds, q, preferred_element_type=F32)
+            dq = jnp.dot(kt_ref[n], ds, preferred_element_type=F32)
+            total = dq if total is None else total + dq
+        dq_ref[chip] = total.astype(dq_ref.dtype)
 
     @pl.when(step == pl.num_programs(0) - 1)
     def _():
-        d1_ref[:, :HEAD] = dk[:ROWS]
-        d1_ref[:, HEAD:] = dv[:ROWS]
-        d2_ref[:, :HEAD] = dk[ROWS:]
-        d2_ref[:, HEAD:] = dv[ROWS:]
+        for n, d_ref in enumerate((d1_ref, d2_ref)):
+            d_ref[:, :HEAD] = acc_k[n]
+            d_ref[:, HEAD:] = acc_v[n]
 
 
 def tile_call(qg, kv1, kv2, old, after, last):
@@ -126,9 +143,10 @@
     groups, rows, width = qg.shape
     chips = 4
     q_spec = pl.BlockSpec((chips, rows, width), lambda i: (i, 0, 0))
-    kv_spec = pl.BlockSpec((ROWS, width), lambda i: (0, 0))
+    keys = kv1.shape[0]
+    kv_spec = pl.BlockSpec((keys, width), lambda i: (0, 0))
     dq_spec = pl.BlockSpec((chips, HEAD, ROWS), lambda i: (i, 0, 0))
-    pairs = groups * ROWS * 2 * ROWS
+    pairs = groups * ROWS * 2 * keys
     return pl.pallas_call(
         functools.partial(tile_kernel, first, chips),
         grid=(groups // chips,),
@@ -137,13 +155,13 @@
         out_specs=[dq_spec, kv_spec, kv_spec],
         out_shape=[
             jax.ShapeDtypeStruct((groups, HEAD, ROWS), BF16 if last else F32),
-            jax.ShapeDtypeStruct((ROWS, width), F32),
-            jax.ShapeDtypeStruct((ROWS, width), F32),
+            jax.ShapeDtypeStruct((keys, width), F32),
+            jax.ShapeDtypeStruct((keys, width), F32),
         ],
         scratch_shapes=[
-            pltpu.VMEM((2 * ROWS, HEAD), F32),
-            pltpu.VMEM((2 * ROWS, HEAD), F32),
-            pltpu.VMEM((HEAD, 2 * ROWS), BF16),
+            pltpu.VMEM((2, keys, HEAD), F32),
+            pltpu.VMEM((2, keys, HEAD), F32),
+            pltpu.VMEM((2, HEAD, keys), BF16),
         ],
         compiler_params=pltpu.CompilerParams(vmem_limit_bytes=40 * 2**20),
         cost_estimate=pl.CostEstimate(
@@ -165,17 +183,17 @@
         core, queries, key_rows, value_rows, attn_output, grad_output, row_lse
     )
     other = shift(send, "core", 1)
-    query_pack = jnp.concatenate([mine_q, other[: HALF + STATS]], axis=0)
-    key_pack = jnp.concatenate([mine_kv, other[HALF + STATS :]], axis=0)
-
-    plane = math.prod(lax.axis_size(a) for a in PLANE)
-    spread = jnp.broadcast_to(query_pack[None], (plane,) + query_pack.shape)
-    gathered = lax.all_to_all(spread, PLANE, 0, 0, tiled=True)
-    keys = {0: key_pack}
+    peers = math.prod(lax.axis_size(a) for a in GROUP)
+    spread, key_pack = spread_call(peers, mine_q, mine_kv, other)
+    key_pair = jnp.concatenate([key_pack, shift(key_pack, "xh", 1)], axis=0)
+    gathered = lax.all_to_all(spread, GROUP, 0, 0, tiled=True)
+    keys = {0: key_pair}
     for by in (1, 2, 3):
         keys[by] = shift(keys[by - 1], "z", 1)
         keys[-by] = shift(keys[1 - by], "z", -1)
-    keys[4] = shift(keys[3], "z", 1)
+    keys[4] = jnp.concatenate(
+        [shift(keys[3][:ROWS], "z", 1), shift(keys[-3][ROWS:], "z", -1)], axis=0
+    )
 
     def low(x):
         return x.astype(BF16)
@@ -191,8 +209,11 @@
         up = low(du + up_in.astype(F32))
         down = low(dd if down_in is None else dd + down_in.astype(F32))
         after = up
-    returned = lax.all_to_all(total_q, PLANE, 0, 0, tiled=True)
-    grad_kv = own + shift(up, "z", 1).astype(F32) + shift(down, "z", -1).astype(F32)
+    up_in = shift(up, "z", 1)
+    down_in = shift(down, "z", -1)
+    returned = lax.all_to_all(total_q, GROUP, 0, 0, tiled=True)
+    grad_pair = own + up_in.astype(F32) + down_in.astype(F32)
+    grad_kv = grad_pair[:ROWS] + shift(low(grad_pair[ROWS:]), "xh", 1).astype(F32)
 
     grad_q = jnp.sum(returned.astype(F32), axis=0).T
     grads = jnp.stack([grad_q, grad_kv[:, :HEAD], grad_kv[:, HEAD:]]).astype(BF16)

time: 111 us -> 101 us (0.910)
  waiting for transfers between devices: 37.7 us -> 22.4 us
  starting transfers between devices: 37.2 us -> 46.3 us
  other arithmetic: 4.44 us -> 1.25 us
  Pallas kernels: 26.7 us -> 28.3 us
  local copies, waits for them, and re-layouts: 3.36 us -> 1.79 us
    all_to_all x2, waiting for transfers between devices: 15.7 us -> 3.15 us  [the longest x1 3.15 us: local(): returned = lax.all_to_all(total_q, GROUP, 0, 0, tiled=True)]
    ppermute x16 -> x19, starting transfers between devices: 28.4 us -> 36.2 us  [shift(): return lax.ppermute(x, axis, [(i, (i + by) % n) for i in range(n)])]
    ppermute x16 -> x19, waiting for transfers between devices: 22 us -> 19.3 us  [shift(): return lax.ppermute(x, axis, [(i, (i + by) % n) for i in range(n)])]
    convert_element_type x7, other arithmetic: 2.62 us -> 0.33 us  [low(): return x.astype(BF16)]
    pallas_call x0 -> x1, Pallas kernels: none -> 2.13 us  [spread_call(): pl.pallas_call(spread_kernel, in_specs=[pl.BlockSpec(memory_space=pltpu.V...]
    broadcast_in_dim x1 -> x0, local copies, waits for them, and re-layouts: 1.66 us -> none  [local(): spread = jnp.broadcast_to(query_pack[None], (plane,) + query_pack.shape)]
    all_to_all x2, starting transfers between devices: 8.8 us -> 10.1 us  [the longest x1 5.12 us: local(): gathered = lax.all_to_all(spread, GROUP, 0, 0, tiled=True)]
  transfers between devices with their start and end apart: 18 -> 21, of which waited for: 10 -> 10; matrix products, arithmetic and copies ran while one was open for 2% -> 2% of each run, Pallas kernels for 23% -> 18%
where the time goes in v3:
time: 101 us
  starting transfers between devices  46.3 us (46%)
  Pallas kernels  28.3 us (28%)
  waiting for transfers between devices  22.4 us (22%)
  local copies, waits for them, and re-layouts  1.79 us (2%)
  other arithmetic  1.25 us (1%)
    ppermute x19, starting transfers between devices, shift(): return lax.ppermute(x, axis, [(i, (i + by) % n) for i in range(n)])  36.2 us
    pallas_call x4, Pallas kernels, tile_call(): pl.pallas_call(functools.partial(tile_kernel, first, chips), grid=(groups...  24.4 us
    ppermute x19, waiting for transfers between devices, shift(): return lax.ppermute(x, axis, [(i, (i + by) % n) for i in range(n)])  19.3 us
    all_to_all x1, starting transfers between devices, local(): gathered = lax.all_to_all(spread, GROUP, 0, 0, tiled=True)  5.12 us
    all_to_all x1, starting transfers between devices, local(): returned = lax.all_to_all(total_q, GROUP, 0, 0, tiled=True)  4.95 us
    all_to_all x1, waiting for transfers between devices, local(): returned = lax.all_to_all(total_q, GROUP, 0, 0, tiled=True)  3.15 us
    pallas_call x1, Pallas kernels, spread_call(): pl.pallas_call(spread_kernel, in_specs=[pl.BlockSpec(memory_space=pltpu.V...  2.13 us
  transfers between devices with their start and end apart: 21, of which 10 were waited for; matrix products, arithmetic and copies ran while one was open for 2% of the time, Pallas kernels for 18%

profile of v3, /device:TPU:1, one launch (start us, length us, event | category | flops | bytes accessed | tf_op | source)
XLA Modules:
  0.0 101.0 jit_solution(11692686348608449415)
XLA Ops:
  0.6 1.8 %pack.1 = (bf16[144,256]{1,0:T(8,128)(2,1)}, bf16[128,256]{1,0:T(8,128)(2,1)}, bf16[272,256]{1,0:T(8,128)(2,1)}) custom-call(s32[1]{0:T(128)} %bitcast.core_ref, bf16[128,256]{1,0:T(8,128)(2,1)} %q_ref.1, bf16[128,256]{1,0:T(8,128)(2,1)} %k_ref.1, bf16[128,256]{1,0:T(8,128)(2,1)} %v_ref.1, bf16[128,256]{1,0:T(8,128)(2,1)} %o_ref.1, bf16[128,256]{1,0:T(8,128)(2,1)} %g_ref.1, ...), custom_call_target="tpu_custom_call" | custom-call | tf_op jit(solution)/shard_map/pack/pallas_call | solution.py:58
  2.4 3.2 %collective-permute-start = (bf16[272,256]{1,0:T(8,128)(2,1)}, bf16[272,256]{1,0:T(8,128)(2,1)S(1)}, u32[]{:S(2)}, u32[]{:S(2)}) collective-permute-start(bf16[272,256]{1,0:T(8,128)(2,1)} %get-tuple-element.22), channel_id=1, source_target_pairs={{0,1},{1,0},{2,3},{3,2},{4,5},{5,4},{6,7},{7,6},{8,9},{9,8},{10,11... | collective-permute-start | bytes 417800 | tf_op jit(solution)/shard_map/ppermute | solution.py:176
  7.5 2.1 %spread.1 = (bf16[8,288,256]{2,1,0:T(8,128)(2,1)}, bf16[256,256]{1,0:T(8,128)(2,1)}) custom-call(bf16[144,256]{1,0:T(8,128)(2,1)} %get-tuple-element.20.mine_ref, bf16[128,256]{1,0:T(8,128)(2,1)} %get-tuple-element.21.kv_ref, bf16[272,256]{1,0:T(8,128)(2,1)} %copy-done.2), custom_call_target="tpu_custom_call" | custom-call | tf_op jit(solution)/shard_map/spread/pallas_call | solution.py:82
  11.6 4.5 %collective-permute-done.1 = bf16[256,256]{1,0:T(8,128)(2,1)S(1)} collective-permute-done((bf16[256,256]{1,0:T(8,128)(2,1)}, bf16[256,256]{1,0:T(8,128)(2,1)S(1)}, u32[]{:S(2)}, u32[]{:S(2)}) %collective-permute-start.1) | collective-permute-done | bytes 131104 | tf_op jit(solution)/shard_map/ppermute | solution.py:176
  16.2 3.9 %collective-permute-start.2 = (bf16[512,256]{1,0:T(8,128)(2,1)S(1)}, bf16[512,256]{1,0:T(8,128)(2,1)S(1)}, u32[]{:S(2)}, u32[]{:S(2)}) collective-permute-start(bf16[512,256]{1,0:T(8,128)(2,1)S(1)} %constant_dynamic-update-slice_fusion.refs_2_), channel_id=1, source_target_pairs={{0,28},{4,0},{8,4},{12,8},{16,12},{20,16},{24,20},{28,24},{1,29},{... | collective-permute-start | bytes 786440 | tf_op jit(solution)/shard_map/ppermute | solution.py:176
  20.1 5.1 %all-to-all-start = ((bf16[8,288,256]{2,1,0:T(8,128)(2,1)}), bf16[8,288,256]{2,1,0:T(8,128)(2,1)S(1)}, u32[]{:S(2)}, u32[]{:S(2)}) async-start(bf16[8,288,256]{2,1,0:T(8,128)(2,1)} %get-tuple-element.23), calls=%async_computation | async-start | bytes 2359296 | tf_op jit(solution)/shard_map/all_to_all | solution.py:189
  25.5 2.7 %collective-permute-start.4 = (bf16[512,256]{1,0:T(8,128)(2,1)S(1)}, bf16[512,256]{1,0:T(8,128)(2,1)S(1)}, u32[]{:S(2)}, u32[]{:S(2)}) collective-permute-start(bf16[512,256]{1,0:T(8,128)(2,1)S(1)} %collective-permute-done.2.refs_1_), channel_id=1, source_target_pairs={{0,28},{4,0},{8,4},{12,8},{16,12},{20,16},{24,20},{28,24},{1,29},{... | collective-permute-start | bytes 786440 | tf_op jit(solution)/shard_map/ppermute | solution.py:176
  28.1 4.5 %collective-permute-done.5.refs_2_ = bf16[512,256]{1,0:T(8,128)(2,1)S(1)} collective-permute-done((bf16[512,256]{1,0:T(8,128)(2,1)S(1)}, bf16[512,256]{1,0:T(8,128)(2,1)S(1)}, u32[]{:S(2)}, u32[]{:S(2)}) %collective-permute-start.5) | collective-permute-done | bytes 262176 | tf_op jit(solution)/shard_map/ppermute | solution.py:176
  32.7 2.7 %collective-permute-start.6 = (bf16[512,256]{1,0:T(8,128)(2,1)S(1)}, bf16[512,256]{1,0:T(8,128)(2,1)S(1)}, u32[]{:S(2)}, u32[]{:S(2)}) collective-permute-start(bf16[512,256]{1,0:T(8,128)(2,1)S(1)} %collective-permute-done.4.refs_1_), channel_id=1, source_target_pairs={{0,28},{4,0},{8,4},{12,8},{16,12},{20,16},{24,20},{28,24},{1,29},{... | collective-permute-start | bytes 786440 | tf_op jit(solution)/shard_map/ppermute | solution.py:176
  35.3 4.0 %collective-permute-done.7.refs_2_ = bf16[512,256]{1,0:T(8,128)(2,1)S(1)} collective-permute-done((bf16[512,256]{1,0:T(8,128)(2,1)S(1)}, bf16[512,256]{1,0:T(8,128)(2,1)S(1)}, u32[]{:S(2)}, u32[]{:S(2)}) %collective-permute-start.7) | collective-permute-done | bytes 262176 | tf_op jit(solution)/shard_map/ppermute | solution.py:176
  39.5 2.7 %collective-permute-start.9 = (bf16[256,256]{1,0:T(8,128)(2,1)S(1)}, bf16[256,256]{1,0:T(8,128)(2,1)S(1)}, u32[]{:S(2)}, u32[]{:S(2)}) collective-permute-start(bf16[256,256]{1,0:T(8,128)(2,1)S(1)} %slice.48), channel_id=1, source_target_pairs={{0,28},{4,0},{8,4},{12,8},{16,12},{20,16},{24,20},{28,24},{1,29},{... | collective-permute-start | bytes 393224 | tf_op jit(solution)/shard_map/ppermute | solution.py:176
  42.2 2.3 %collective-permute-done.8 = bf16[256,256]{1,0:T(8,128)(2,1)S(1)} collective-permute-done((bf16[256,256]{1,0:T(8,128)(2,1)S(1)}, bf16[256,256]{1,0:T(8,128)(2,1)S(1)}, u32[]{:S(2)}, u32[]{:S(2)}) %collective-permute-start.8) | collective-permute-done | bytes 131104 | tf_op jit(solution)/shard_map/ppermute | solution.py:176
  44.5 5.9 %tile.4 = (f32[8,128,256]{2,1,0:T(8,128)S(1)}, f32[512,256]{1,0:T(8,128)S(1)}, f32[512,256]{1,0:T(8,128)S(1)}) custom-call(bf16[8,288,256]{2,1,0:T(8,128)(2,1)S(1)} %all-to-all-done.refs_0_, bf16[512,256]{1,0:T(8,128)(2,1)S(1)} %pad_maximum_fusion.refs_1_, bf16[512,256]{1,0:T(8,128)(2,1)S(1)} %constant_dynamic-update-slice_fusion.refs_2_), custom_call_target="tpu_custom_call" | custom-call | flops 5368709120 | bytes 8388608 | tf_op jit(solution)/shard_map/tile/pallas_call | solution.py:150
  50.7 5.9 %tile.5 = (f32[8,128,256]{2,1,0:T(8,128)S(1)}, f32[512,256]{1,0:T(8,128)S(1)}, f32[512,256]{1,0:T(8,128)S(1)}) custom-call(bf16[8,288,256]{2,1,0:T(8,128)(2,1)S(1)} %all-to-all-done.refs_0_, bf16[512,256]{1,0:T(8,128)(2,1)S(1)} %collective-permute-done.6.refs_1_, bf16[512,256]{1,0:T(8,128)(2,1)S(1)} %collective-permute-done.7.refs_2_, ...), custom_call_target="tpu_custom_call" | custom-call | flops 5368709120 | bytes 8388608 | tf_op jit(solution)/shard_map/tile/pallas_call | solution.py:150
  56.7 2.8 %collective-permute-start.14 = (bf16[512,256]{1,0:T(8,128)(2,1)S(1)}, bf16[512,256]{1,0:T(8,128)(2,1)S(1)}, u32[]{:S(2)}, u32[]{:S(2)}) collective-permute-start(bf16[512,256]{1,0:T(8,128)(2,1)S(1)} %convert_element_type.59), channel_id=1, source_target_pairs={{0,28},{4,0},{8,4},{12,8},{16,12},{20,16},{24,20},{28,24},{1,29},{... | collective-permute-start | bytes 786440 | tf_op jit(solution)/shard_map/ppermute | solution.py:176
  59.7 5.9 %tile.6 = (f32[8,128,256]{2,1,0:T(8,128)S(1)}, f32[512,256]{1,0:T(8,128)S(1)}, f32[512,256]{1,0:T(8,128)S(1)}) custom-call(bf16[8,288,256]{2,1,0:T(8,128)(2,1)S(1)} %all-to-all-done.refs_0_, bf16[512,256]{1,0:T(8,128)(2,1)S(1)} %copy-done.1, bf16[512,256]{1,0:T(8,128)(2,1)S(1)} %collective-permute-done.5.refs_2_, ...), custom_call_target="tpu_custom_call" | custom-call | flops 5368709120 | bytes 8388608 | tf_op jit(solution)/shard_map/tile/pallas_call | solution.py:150
  65.7 2.7 %collective-permute-start.15 = (bf16[512,256]{1,0:T(8,128)(2,1)S(1)}, bf16[512,256]{1,0:T(8,128)(2,1)S(1)}, u32[]{:S(2)}, u32[]{:S(2)}) collective-permute-start(bf16[512,256]{1,0:T(8,128)(2,1)S(1)} %add_convert_fusion.1), channel_id=1, source_target_pairs={{0,28},{4,0},{8,4},{12,8},{16,12},{20,16},{24,20},{28,24},{1,29},{... | collective-permute-start | bytes 786440 | tf_op jit(solution)/shard_map/ppermute | solution.py:176
  68.6 6.6 %tile.7 = (bf16[8,128,256]{2,1,0:T(8,128)(2,1)}, f32[512,256]{1,0:T(8,128)S(1)}, f32[512,256]{1,0:T(8,128)S(1)}) custom-call(bf16[8,288,256]{2,1,0:T(8,128)(2,1)S(1)} %all-to-all-done.refs_0_, bf16[512,256]{1,0:T(8,128)(2,1)S(1)} %collective-permute-done.2.refs_1_, bf16[512,256]{1,0:T(8,128)(2,1)S(1)} %collective-permute-done.3.refs_2_, ...), custom_call_target="tpu_custom_call" | custom-call | flops 5368709120 | bytes 8388608 | tf_op jit(solution)/shard_map/tile/pallas_call | solution.py:150
  75.3 2.9 %collective-permute-start.16 = (bf16[512,256]{1,0:T(8,128)(2,1)S(1)}, bf16[512,256]{1,0:T(8,128)(2,1)S(1)}, u32[]{:S(2)}, u32[]{:S(2)}) collective-permute-start(bf16[512,256]{1,0:T(8,128)(2,1)S(1)} %add_convert_fusion), channel_id=1, source_target_pairs={{0,28},{4,0},{8,4},{12,8},{16,12},{20,16},{24,20},{28,24},{1,29},{... | collective-permute-start | bytes 786440 | tf_op jit(solution)/shard_map/ppermute | solution.py:176
  78.4 5.0 %all-to-all-start.1 = ((bf16[8,128,256]{2,1,0:T(8,128)(2,1)}), bf16[8,128,256]{2,1,0:T(8,128)(2,1)S(1)}, u32[]{:S(2)}, u32[]{:S(2)}) async-start(bf16[8,128,256]{2,1,0:T(8,128)(2,1)} %get-tuple-element.31), calls=%async_computation.1 | async-start | bytes 1048576 | tf_op jit(solution)/shard_map/all_to_all | solution.py:214
  83.3 1.5 %collective-permute-done.13 = bf16[512,256]{1,0:T(8,128)(2,1)S(1)} collective-permute-done((bf16[512,256]{1,0:T(8,128)(2,1)S(1)}, bf16[512,256]{1,0:T(8,128)(2,1)S(1)}, u32[]{:S(2)}, u32[]{:S(2)}) %collective-permute-start.13) | collective-permute-done | bytes 262176 | tf_op jit(solution)/shard_map/ppermute | solution.py:176
  84.9 2.8 %collective-permute-start.17 = (bf16[256,256]{1,0:T(8,128)(2,1)S(1)}, bf16[256,256]{1,0:T(8,128)(2,1)S(1)}, u32[]{:S(2)}, u32[]{:S(2)}) collective-permute-start(bf16[256,256]{1,0:T(8,128)(2,1)S(1)} %slice.83), channel_id=1, source_target_pairs={{0,32},{32,0},{1,33},{33,1},{2,34},{34,2},{3,35},{35,3},{4,36},{36... | collective-permute-start | bytes 393224 | tf_op jit(solution)/shard_map/ppermute | solution.py:176
  87.7 3.1 %all-to-all-done.1 = bf16[8,128,256]{2,1,0:T(8,128)(2,1)S(1)} async-done(((bf16[8,128,256]{2,1,0:T(8,128)(2,1)}), bf16[8,128,256]{2,1,0:T(8,128)(2,1)S(1)}, u32[]{:S(2)}, u32[]{:S(2)}) %all-to-all-start.1) | async-done | bytes 524320 | tf_op jit(solution)/shard_map/all_to_all | solution.py:214
  91.3 8.0 %collective-permute-start.18 = (bf16[3,128,128]{2,1,0:T(8,128)(2,1)S(1)}, bf16[3,128,128]{2,1,0:T(8,128)(2,1)S(1)}, u32[]{:S(2)}, u32[]{:S(2)}) collective-permute-start(bf16[3,128,128]{2,1,0:T(8,128)(2,1)S(1)} %slice.54), channel_id=1, source_target_pairs={{0,1},{1,0},{2,3},{3,2},{4,5},{5,4},{6,7},{7,6},{8,9},{9,8},{10,11... | collective-permute-start | bytes 294920 | tf_op jit(solution)/shard_map/ppermute | solution.py:176
  (52 shorter events, 7.3 us)
Async XLA Ops:
  2.4 4.4 %collective-permute-start = (bf16[272,256]{1,0:T(8,128)(2,1)}, bf16[272,256]{1,0:T(8,128)(2,1)S(1)}, u32[]{:S(2)}, u32[]{:S(2)}) collective-permute-start(bf16[272,256]{1,0:T(8,128)(2,1)} %get-tuple-element.22), channel_id=1, source_target_pairs={{0,1},{1,0},{2,3},{3,2},{4,5},{5,4},{6,7},{7,6},{8,9},{9,8},{10,11... | collective-permute-start | bytes 417800 | tf_op jit(solution)/shard_map/ppermute | solution.py:176
  6.9 0.7 copy-start.2
  9.7 6.4 %collective-permute-start.1 = (bf16[256,256]{1,0:T(8,128)(2,1)}, bf16[256,256]{1,0:T(8,128)(2,1)S(1)}, u32[]{:S(2)}, u32[]{:S(2)}) collective-permute-start(bf16[256,256]{1,0:T(8,128)(2,1)} %get-tuple-element.24), channel_id=1, source_target_pairs={{0,32},{32,0},{1,33},{33,1},{2,34},{34,2},{3,35},{35,3},{4,36},{36... | collective-permute-start | bytes 393224 | tf_op jit(solution)/shard_map/ppermute | solution.py:176
  16.1 9.4 %collective-permute-start.3 = (bf16[512,256]{1,0:T(8,128)(2,1)S(1)}, bf16[512,256]{1,0:T(8,128)(2,1)S(1)}, u32[]{:S(2)}, u32[]{:S(2)}) collective-permute-start(bf16[512,256]{1,0:T(8,128)(2,1)S(1)} %constant_dynamic-update-slice_fusion.refs_2_), channel_id=1, source_target_pairs={{0,4},{4,8},{8,12},{12,16},{16,20},{20,24},{24,28},{28,0},{1,5},{5... | collective-permute-start | bytes 786440 | tf_op jit(solution)/shard_map/ppermute | solution.py:176
  16.2 9.3 %collective-permute-start.2 = (bf16[512,256]{1,0:T(8,128)(2,1)S(1)}, bf16[512,256]{1,0:T(8,128)(2,1)S(1)}, u32[]{:S(2)}, u32[]{:S(2)}) collective-permute-start(bf16[512,256]{1,0:T(8,128)(2,1)S(1)} %constant_dynamic-update-slice_fusion.refs_2_), channel_id=1, source_target_pairs={{0,28},{4,0},{8,4},{12,8},{16,12},{20,16},{24,20},{28,24},{1,29},{... | collective-permute-start | bytes 786440 | tf_op jit(solution)/shard_map/ppermute | solution.py:176
  20.1 24.4 %all-to-all-start = ((bf16[8,288,256]{2,1,0:T(8,128)(2,1)}), bf16[8,288,256]{2,1,0:T(8,128)(2,1)S(1)}, u32[]{:S(2)}, u32[]{:S(2)}) async-start(bf16[8,288,256]{2,1,0:T(8,128)(2,1)} %get-tuple-element.23), calls=%async_computation | async-start | bytes 2359296 | tf_op jit(solution)/shard_map/all_to_all | solution.py:189
  25.5 7.2 %collective-permute-start.5 = (bf16[512,256]{1,0:T(8,128)(2,1)S(1)}, bf16[512,256]{1,0:T(8,128)(2,1)S(1)}, u32[]{:S(2)}, u32[]{:S(2)}) collective-permute-start(bf16[512,256]{1,0:T(8,128)(2,1)S(1)} %collective-permute-done.3.refs_2_), channel_id=1, source_target_pairs={{0,4},{4,8},{8,12},{12,16},{16,20},{20,24},{24,28},{28,0},{1,5},{5... | collective-permute-start | bytes 786440 | tf_op jit(solution)/shard_map/ppermute | solution.py:176
  25.5 7.2 %collective-permute-start.4 = (bf16[512,256]{1,0:T(8,128)(2,1)S(1)}, bf16[512,256]{1,0:T(8,128)(2,1)S(1)}, u32[]{:S(2)}, u32[]{:S(2)}) collective-permute-start(bf16[512,256]{1,0:T(8,128)(2,1)S(1)} %collective-permute-done.2.refs_1_), channel_id=1, source_target_pairs={{0,28},{4,0},{8,4},{12,8},{16,12},{20,16},{24,20},{28,24},{1,29},{... | collective-permute-start | bytes 786440 | tf_op jit(solution)/shard_map/ppermute | solution.py:176
  32.7 6.7 %collective-permute-start.7 = (bf16[512,256]{1,0:T(8,128)(2,1)S(1)}, bf16[512,256]{1,0:T(8,128)(2,1)S(1)}, u32[]{:S(2)}, u32[]{:S(2)}) collective-permute-start(bf16[512,256]{1,0:T(8,128)(2,1)S(1)} %collective-permute-done.5.refs_2_), channel_id=1, source_target_pairs={{0,4},{4,8},{8,12},{12,16},{16,20},{20,24},{24,28},{28,0},{1,5},{5... | collective-permute-start | bytes 786440 | tf_op jit(solution)/shard_map/ppermute | solution.py:176
  32.7 11.9 %copy-start = (bf16[512,256]{1,0:T(8,128)(2,1)}, bf16[512,256]{1,0:T(8,128)(2,1)S(1)}, u32[]{:S(2)}) copy-start(bf16[512,256]{1,0:T(8,128)(2,1)S(1)} %collective-permute-done.4.refs_1_) | copy-start | bytes 786436
  32.7 6.8 %collective-permute-start.6 = (bf16[512,256]{1,0:T(8,128)(2,1)S(1)}, bf16[512,256]{1,0:T(8,128)(2,1)S(1)}, u32[]{:S(2)}, u32[]{:S(2)}) collective-permute-start(bf16[512,256]{1,0:T(8,128)(2,1)S(1)} %collective-permute-done.4.refs_1_), channel_id=1, source_target_pairs={{0,28},{4,0},{8,4},{12,8},{16,12},{20,16},{24,20},{28,24},{1,29},{... | collective-permute-start | bytes 786440 | tf_op jit(solution)/shard_map/ppermute | solution.py:176
  39.4 5.1 %collective-permute-start.8 = (bf16[256,256]{1,0:T(8,128)(2,1)S(1)}, bf16[256,256]{1,0:T(8,128)(2,1)S(1)}, u32[]{:S(2)}, u32[]{:S(2)}) collective-permute-start(bf16[256,256]{1,0:T(8,128)(2,1)S(1)} %slice.47), channel_id=1, source_target_pairs={{0,4},{4,8},{8,12},{12,16},{16,20},{20,24},{24,28},{28,0},{1,5},{5... | collective-permute-start | bytes 393224 | tf_op jit(solution)/shard_map/ppermute | solution.py:176
  39.5 5.0 %collective-permute-start.9 = (bf16[256,256]{1,0:T(8,128)(2,1)S(1)}, bf16[256,256]{1,0:T(8,128)(2,1)S(1)}, u32[]{:S(2)}, u32[]{:S(2)}) collective-permute-start(bf16[256,256]{1,0:T(8,128)(2,1)S(1)} %slice.48), channel_id=1, source_target_pairs={{0,28},{4,0},{8,4},{12,8},{16,12},{20,16},{24,20},{28,24},{1,29},{... | collective-permute-start | bytes 393224 | tf_op jit(solution)/shard_map/ppermute | solution.py:176
  50.4 9.1 %collective-permute-start.10 = (bf16[512,256]{1,0:T(8,128)(2,1)S(1)}, bf16[512,256]{1,0:T(8,128)(2,1)S(1)}, u32[]{:S(2)}, u32[]{:S(2)}) collective-permute-start(bf16[512,256]{1,0:T(8,128)(2,1)S(1)} %convert_element_type.50.refs_4_), channel_id=1, source_target_pairs={{0,4},{4,8},{8,12},{12,16},{16,20},{20,24},{24,28},{28,0},{1,5},{5... | collective-permute-start | bytes 786440 | tf_op jit(solution)/shard_map/ppermute | solution.py:176
  56.7 3.0 %copy-start.1 = (bf16[512,256]{1,0:T(8,128)(2,1)S(1)}, bf16[512,256]{1,0:T(8,128)(2,1)}, u32[]{:S(2)}) copy-start(bf16[512,256]{1,0:T(8,128)(2,1)} %copy-done) | copy-start | bytes 786436
  56.7 8.9 %collective-permute-start.14 = (bf16[512,256]{1,0:T(8,128)(2,1)S(1)}, bf16[512,256]{1,0:T(8,128)(2,1)S(1)}, u32[]{:S(2)}, u32[]{:S(2)}) collective-permute-start(bf16[512,256]{1,0:T(8,128)(2,1)S(1)} %convert_element_type.59), channel_id=1, source_target_pairs={{0,28},{4,0},{8,4},{12,8},{16,12},{20,16},{24,20},{28,24},{1,29},{... | collective-permute-start | bytes 786440 | tf_op jit(solution)/shard_map/ppermute | solution.py:176
  59.6 8.8 %collective-permute-start.11 = (bf16[512,256]{1,0:T(8,128)(2,1)S(1)}, bf16[512,256]{1,0:T(8,128)(2,1)S(1)}, u32[]{:S(2)}, u32[]{:S(2)}) collective-permute-start(bf16[512,256]{1,0:T(8,128)(2,1)S(1)} %add_convert_fusion.4.refs_4_), channel_id=1, source_target_pairs={{0,4},{4,8},{8,12},{12,16},{16,20},{20,24},{24,28},{28,0},{1,5},{5... | collective-permute-start | bytes 786440 | tf_op jit(solution)/shard_map/ppermute | solution.py:176
  65.7 9.5 %collective-permute-start.15 = (bf16[512,256]{1,0:T(8,128)(2,1)S(1)}, bf16[512,256]{1,0:T(8,128)(2,1)S(1)}, u32[]{:S(2)}, u32[]{:S(2)}) collective-permute-start(bf16[512,256]{1,0:T(8,128)(2,1)S(1)} %add_convert_fusion.1), channel_id=1, source_target_pairs={{0,28},{4,0},{8,4},{12,8},{16,12},{20,16},{24,20},{28,24},{1,29},{... | collective-permute-start | bytes 786440 | tf_op jit(solution)/shard_map/ppermute | solution.py:176
  68.5 9.7 %collective-permute-start.12 = (bf16[512,256]{1,0:T(8,128)(2,1)S(1)}, bf16[512,256]{1,0:T(8,128)(2,1)S(1)}, u32[]{:S(2)}, u32[]{:S(2)}) collective-permute-start(bf16[512,256]{1,0:T(8,128)(2,1)S(1)} %add_convert_fusion.3.refs_4_), channel_id=1, source_target_pairs={{0,4},{4,8},{8,12},{12,16},{16,20},{20,24},{24,28},{28,0},{1,5},{5... | collective-permute-start | bytes 786440 | tf_op jit(solution)/shard_map/ppermute | solution.py:176
  75.3 8.0 %collective-permute-start.16 = (bf16[512,256]{1,0:T(8,128)(2,1)S(1)}, bf16[512,256]{1,0:T(8,128)(2,1)S(1)}, u32[]{:S(2)}, u32[]{:S(2)}) collective-permute-start(bf16[512,256]{1,0:T(8,128)(2,1)S(1)} %add_convert_fusion), channel_id=1, source_target_pairs={{0,28},{4,0},{8,4},{12,8},{16,12},{20,16},{24,20},{28,24},{1,29},{... | collective-permute-start | bytes 786440 | tf_op jit(solution)/shard_map/ppermute | solution.py:176
  78.3 6.5 %collective-permute-start.13 = (bf16[512,256]{1,0:T(8,128)(2,1)S(1)}, bf16[512,256]{1,0:T(8,128)(2,1)S(1)}, u32[]{:S(2)}, u32[]{:S(2)}) collective-permute-start(bf16[512,256]{1,0:T(8,128)(2,1)S(1)} %add_convert_fusion.2), channel_id=1, source_target_pairs={{0,4},{4,8},{8,12},{12,16},{16,20},{20,24},{24,28},{28,0},{1,5},{5... | collective-permute-start | bytes 786440 | tf_op jit(solution)/shard_map/ppermute | solution.py:176
  78.4 12.5 %all-to-all-start.1 = ((bf16[8,128,256]{2,1,0:T(8,128)(2,1)}), bf16[8,128,256]{2,1,0:T(8,128)(2,1)S(1)}, u32[]{:S(2)}, u32[]{:S(2)}) async-start(bf16[8,128,256]{2,1,0:T(8,128)(2,1)} %get-tuple-element.31), calls=%async_computation.1 | async-start | bytes 1048576 | tf_op jit(solution)/shard_map/all_to_all | solution.py:214
  84.9 6.3 %collective-permute-start.17 = (bf16[256,256]{1,0:T(8,128)(2,1)S(1)}, bf16[256,256]{1,0:T(8,128)(2,1)S(1)}, u32[]{:S(2)}, u32[]{:S(2)}) collective-permute-start(bf16[256,256]{1,0:T(8,128)(2,1)S(1)} %slice.83), channel_id=1, source_target_pairs={{0,32},{32,0},{1,33},{33,1},{2,34},{34,2},{3,35},{35,3},{4,36},{36... | collective-permute-start | bytes 393224 | tf_op jit(solution)/shard_map/ppermute | solution.py:176
  91.3 8.9 %collective-permute-start.18 = (bf16[3,128,128]{2,1,0:T(8,128)(2,1)S(1)}, bf16[3,128,128]{2,1,0:T(8,128)(2,1)S(1)}, u32[]{:S(2)}, u32[]{:S(2)}) collective-permute-start(bf16[3,128,128]{2,1,0:T(8,128)(2,1)S(1)} %slice.54), channel_id=1, source_target_pairs={{0,1},{1,0},{2,3},{3,2},{4,5},{5,4},{6,7},{7,6},{8,9},{9,8},{10,11... | collective-permute-start | bytes 294920 | tf_op jit(solution)/shard_map/ppermute | solution.py:176

commit v4 on v3

--- a/solution.py
+++ b/solution.py
@@ -13,6 +13,7 @@
 LOG2E = math.log2(math.e)
 AXES = ("y", "xh", "z", "xl", "core")
 GROUP = ("y", "xl")
+OWNERS = ("y", "xl", "core")
 ROWS = 256
 STATS = 16
 HALF = 128
@@ -28,7 +29,7 @@
     return jnp.concatenate([hi.astype(F32), mid.astype(F32), low.astype(F32)], axis=0)
 
 
-def pack_kernel(core_ref, q_ref, k_ref, v_ref, o_ref, g_ref, lse_ref, qg_ref, kv_ref, send_ref):
+def pack_kernel(core_ref, q_ref, k_ref, v_ref, o_ref, g_ref, lse_ref, qg_ref, kv_ref, send_ref, far_ref):
     def fill(head, qg, kv):
         cols = slice(head * HEAD, (head + 1) * HEAD)
         g = g_ref[:, cols]
@@ -51,6 +52,7 @@
         def _():
             fill(core, qg_ref, kv_ref)
             fill(1 - core, send_qg, send_kv)
+            far_ref[...] = send_kv[...]
 
 
 def pack_call(core, *args):
@@ -59,45 +61,46 @@
         pack_kernel,
         in_specs=[pl.BlockSpec(memory_space=pltpu.SMEM)]
         + [pl.BlockSpec(memory_space=pltpu.VMEM)] * 6,
-        out_specs=[pl.BlockSpec(memory_space=pltpu.VMEM)] * 3,
+        out_specs=[pl.BlockSpec(memory_space=pltpu.VMEM)] * 4,
         out_shape=[
             jax.ShapeDtypeStruct((HALF + STATS, width), BF16),
             jax.ShapeDtypeStruct((HALF, width), BF16),
             jax.ShapeDtypeStruct((2 * HALF + STATS, width), BF16),
+            jax.ShapeDtypeStruct((HALF, width), BF16),
         ],
         name="pack",
     )(core.reshape(1), *args)
 
 
-def spread_kernel(mine_ref, kv_ref, other_ref, out_ref, keys_ref):
+def spread_kernel(mine_ref, other_ref, out_ref):
     rows = HALF + STATS
     for n in range(out_ref.shape[0]):
         out_ref[n, :rows, :] = mine_ref[...]
         out_ref[n, rows:, :] = other_ref[:rows, :]
-    keys_ref[:HALF, :] = kv_ref[...]
-    keys_ref[HALF:, :] = other_ref[rows:, :]
 
 
 def spread_call(n, *args):
     return pl.pallas_call(
         spread_kernel,
-        in_specs=[pl.BlockSpec(memory_space=pltpu.VMEM)] * 3,
-        out_specs=[pl.BlockSpec(memory_space=pltpu.VMEM)] * 2,
-        out_shape=[
-            jax.ShapeDtypeStruct((n, 2 * (HALF + STATS), 2 * HEAD), BF16),
-            jax.ShapeDtypeStruct((ROWS, 2 * HEAD), BF16),
-        ],
+        in_specs=[pl.BlockSpec(memory_space=pltpu.VMEM)] * 2,
+        out_specs=pl.BlockSpec(memory_space=pltpu.VMEM),
+        out_shape=jax.ShapeDtypeStruct((n, 2 * (HALF + STATS), 2 * HEAD), BF16),
         name="spread",
     )(*args)
 
 
-def tile_kernel(first, chips, *refs):
-    if first:
-        qg_ref, kv1_ref, kv2_ref, dq_ref, d1_ref, d2_ref, acc_k, acc_v, kt_ref = refs
-    else:
-        qg_ref, kv1_ref, kv2_ref, old_ref, _, dq_ref, d1_ref, d2_ref, acc_k, acc_v, kt_ref = refs
+def tile_kernel(count, first, last, chips, *refs):
+    refs = list(refs)
+    core_ref = refs.pop(0) if last else None
+    qg_ref = refs.pop(0)
+    blocks = [refs.pop(0) for _ in range(count)]
+    if not first:
+        old_ref = refs.pop(0)
+        refs.pop(0)
+    dq_ref = refs.pop(0)
+    sums = [refs.pop(0) for _ in range(count)]
+    acc_k, acc_v, kt_ref = refs
     step = pl.program_id(0)
-    blocks = (kv1_ref, kv2_ref)
 
     @pl.when(step == 0)
     def _():
@@ -129,46 +132,57 @@
             acc_k[n] += jnp.dot(ds, q, preferred_element_type=F32)
             dq = jnp.dot(kt_ref[n], ds, preferred_element_type=F32)
             total = dq if total is None else total + dq
-        dq_ref[chip] = total.astype(dq_ref.dtype)
+        if last:
+            core = core_ref[0]
+            dq_ref[2 * chip + core] = total[:, :HALF].astype(BF16)
+            dq_ref[2 * chip + 1 - core] = total[:, HALF:].astype(BF16)
+        else:
+            dq_ref[chip] = total
 
     @pl.when(step == pl.num_programs(0) - 1)
     def _():
-        for n, d_ref in enumerate((d1_ref, d2_ref)):
+        for n, d_ref in enumerate(sums):
             d_ref[:, :HEAD] = acc_k[n]
             d_ref[:, HEAD:] = acc_v[n]
 
 
-def tile_call(qg, kv1, kv2, old, after, last):
-    first = old is None
+def tile_call(qg, blocks, old=None, after=None, core=None):
+    first, last = old is None, core is not None
     groups, rows, width = qg.shape
+    count, keys = len(blocks), blocks[0].shape[0]
     chips = 4
     q_spec = pl.BlockSpec((chips, rows, width), lambda i: (i, 0, 0))
-    keys = kv1.shape[0]
     kv_spec = pl.BlockSpec((keys, width), lambda i: (0, 0))
     dq_spec = pl.BlockSpec((chips, HEAD, ROWS), lambda i: (i, 0, 0))
-    pairs = groups * ROWS * 2 * keys
+    dq_shape = jax.ShapeDtypeStruct((groups, HEAD, ROWS), F32)
+    out_spec = dq_spec
+    if last:
+        out_spec = pl.BlockSpec((2 * chips, HEAD, HALF), lambda i: (i, 0, 0))
+        dq_shape = jax.ShapeDtypeStruct((2 * groups, HEAD, HALF), BF16)
+    args, specs = [qg, *blocks], [q_spec] + [kv_spec] * count
+    if last:
+        args, specs = [core.reshape(1)] + args, [pl.BlockSpec(memory_space=pltpu.SMEM)] + specs
+    if not first:
+        args += [old, after]
+        specs += [dq_spec, pl.BlockSpec(memory_space=pl.ANY)]
+    pairs = groups * ROWS * count * keys
     return pl.pallas_call(
-        functools.partial(tile_kernel, first, chips),
+        functools.partial(tile_kernel, count, first, last, chips),
         grid=(groups // chips,),
-        in_specs=[q_spec, kv_spec, kv_spec]
-        + ([] if first else [dq_spec, pl.BlockSpec(memory_space=pl.ANY)]),
-        out_specs=[dq_spec, kv_spec, kv_spec],
-        out_shape=[
-            jax.ShapeDtypeStruct((groups, HEAD, ROWS), BF16 if last else F32),
-            jax.ShapeDtypeStruct((keys, width), F32),
-            jax.ShapeDtypeStruct((keys, width), F32),
-        ],
+        in_specs=specs,
+        out_specs=[out_spec] + [kv_spec] * count,
+        out_shape=[dq_shape] + [jax.ShapeDtypeStruct((keys, width), F32)] * count,
         scratch_shapes=[
-            pltpu.VMEM((2, keys, HEAD), F32),
-            pltpu.VMEM((2, keys, HEAD), F32),
-            pltpu.VMEM((2, HEAD, keys), BF16),
+            pltpu.VMEM((count, keys, HEAD), F32),
+            pltpu.VMEM((count, keys, HEAD), F32),
+            pltpu.VMEM((count, HEAD, keys), BF16),
         ],
         compiler_params=pltpu.CompilerParams(vmem_limit_bytes=40 * 2**20),
         cost_estimate=pl.CostEstimate(
             flops=pairs * HEAD * 20, bytes_accessed=8 * 2**20, transcendentals=pairs
         ),
         name="tile",
-    )(*((qg, kv1, kv2) if first else (qg, kv1, kv2, old, after)))
+    )(*args)
 
 
 def shift(x, axis, by):
@@ -179,13 +193,19 @@
 def local(queries, key_rows, value_rows, attn_output, grad_output, row_lse):
     core = lax.axis_index("core")
     even = core == 0
-    mine_q, mine_kv, send = pack_call(
+    mine_q, mine_kv, send, far_kv = pack_call(
         core, queries, key_rows, value_rows, attn_output, grad_output, row_lse
     )
+    corners = lax.axis_size("xh") * lax.axis_size("core")
+    across = shift(mine_kv, "xh", 1)
+    diagonal = lax.ppermute(
+        far_kv, ("xh", "core"), [(i, corners - 1 - i) for i in range(corners)]
+    )
     other = shift(send, "core", 1)
+    key_pair = jnp.concatenate([mine_kv, other[HALF + STATS :], across, diagonal], axis=0)
+
     peers = math.prod(lax.axis_size(a) for a in GROUP)
-    spread, key_pack = spread_call(peers, mine_q, mine_kv, other)
-    key_pair = jnp.concatenate([key_pack, shift(key_pack, "xh", 1)], axis=0)
+    spread = spread_call(peers, mine_q, other)
     gathered = lax.all_to_all(spread, GROUP, 0, 0, tiled=True)
     keys = {0: key_pair}
     for by in (1, 2, 3):
@@ -198,31 +218,35 @@
     def low(x):
         return x.astype(BF16)
 
-    total_q, far, own = tile_call(gathered, keys[4], keys[0], None, None, False)
+    total_q, own = tile_call(gathered, [keys[0]])
+    total_q, far = tile_call(gathered, [keys[4]], total_q, keys[4])
     up = low(far)
     down = None
     after = up
     for by in (3, 2, 1):
         up_in = shift(up, "z", 1)
         down_in = None if down is None else shift(down, "z", -1)
-        total_q, du, dd = tile_call(gathered, keys[-by], keys[by], total_q, after, by == 1)
+        total_q, du, dd = tile_call(
+            gathered, [keys[-by], keys[by]], total_q, after, core if by == 1 else None
+        )
         up = low(du + up_in.astype(F32))
         down = low(dd if down_in is None else dd + down_in.astype(F32))
         after = up
     up_in = shift(up, "z", 1)
     down_in = shift(down, "z", -1)
-    returned = lax.all_to_all(total_q, GROUP, 0, 0, tiled=True)
+    returned = lax.all_to_all(total_q, OWNERS, 0, 0, tiled=True)
     grad_pair = own + up_in.astype(F32) + down_in.astype(F32)
     grad_kv = grad_pair[:ROWS] + shift(low(grad_pair[ROWS:]), "xh", 1).astype(F32)
-
-    grad_q = jnp.sum(returned.astype(F32), axis=0).T
-    grads = jnp.stack([grad_q, grad_kv[:, :HEAD], grad_kv[:, HEAD:]]).astype(BF16)
-    kept = grads[:, :HALF]
-    moved = shift(grads[:, HALF:], "core", 1)
-    out = jnp.concatenate(
-        [jnp.where(even, kept, moved), jnp.where(even, moved, kept)], axis=2
-    )
-    return out[0], out[1], out[2]
+    grad_kv = low(grad_kv)
+    kept = grad_kv[:HALF]
+    moved = shift(grad_kv[HALF:], "core", 1)
+    lower, upper = jnp.where(even, kept, moved), jnp.where(even, moved, kept)
+    grad_k = jnp.concatenate([lower[:, :HEAD], upper[:, :HEAD]], axis=1)
+    grad_v = jnp.concatenate([lower[:, HEAD:], upper[:, HEAD:]], axis=1)
+
+    heads = returned.reshape(peers, 2 * HEAD, HALF).astype(F32)
+    grad_q = low(jnp.sum(heads, axis=0).T)
+    return grad_q, grad_k, grad_v
 
 
 def solution(mesh):

time: 101 us -> 108 us (1.069)
  waiting for transfers between devices: 22.4 us -> 26.1 us
  starting transfers between devices: 46.3 us -> 48.7 us
  other arithmetic: 1.25 us -> 2.67 us
    all_to_all x1, starting transfers between devices: 4.95 us -> 11.4 us  [local(): returned = lax.all_to_all(total_q, OWNERS, 0, 0, tiled=True)]
    ppermute x19, starting transfers between devices: 36.2 us -> 30.9 us  [shift(): return lax.ppermute(x, axis, [(i, (i + by) % n) for i in range(n)])]
    ppermute x19, waiting for transfers between devices: 19.3 us -> 24.5 us  [shift(): return lax.ppermute(x, axis, [(i, (i + by) % n) for i in range(n)])]
    all_to_all x1, waiting for transfers between devices: 3.15 us -> 0.01 us  [local(): returned = lax.all_to_all(total_q, OWNERS, 0, 0, tiled=True)]
    ppermute x0 -> x1, starting transfers between devices: none -> 2.18 us  [local(): lax.ppermute(far_kv, ('xh', 'core'), [(i, corners - 1 - i) for i in range...]
    concatenate x0 -> x3, other arithmetic: none -> 2.13 us  [the longest x1 0.86 us: local(): jnp.concatenate([mine_kv, other[HALF + STATS:], across, diagonal], axis=0)]
    ppermute x0 -> x1, waiting for transfers between devices: none -> 1.63 us  [local(): lax.ppermute(far_kv, ('xh', 'core'), [(i, corners - 1 - i) for i in range...]
    pallas_call x4 -> x5, Pallas kernels: 24.4 us -> 24.6 us  [tile_call(): pl.pallas_call(functools.partial(tile_kernel, count, first, last, chips),...]
  transfers between devices with their start and end apart: 21 -> 22, of which waited for: 10 -> 8; matrix products, arithmetic and copies ran while one was open for 2% -> 1% of each run, Pallas kernels for 18% -> 19%
where the time goes in v4:
time: 108 us
  starting transfers between devices  48.7 us (45%)
  Pallas kernels  28.5 us (26%)
  waiting for transfers between devices  26.1 us (24%)
  other arithmetic  2.67 us (2%)
    ppermute x19, starting transfers between devices, shift(): return lax.ppermute(x, axis, [(i, (i + by) % n) for i in range(n)])  30.9 us
    pallas_call x5, Pallas kernels, tile_call(): pl.pallas_call(functools.partial(tile_kernel, count, first, last, chips),...  24.6 us
    ppermute x19, waiting for transfers between devices, shift(): return lax.ppermute(x, axis, [(i, (i + by) % n) for i in range(n)])  24.5 us
    all_to_all x1, starting transfers between devices, local(): returned = lax.all_to_all(total_q, OWNERS, 0, 0, tiled=True)  11.4 us
    all_to_all x1, starting transfers between devices, local(): gathered = lax.all_to_all(spread, GROUP, 0, 0, tiled=True)  4.22 us
    ppermute x1, starting transfers between devices, local(): lax.ppermute(far_kv, ('xh', 'core'), [(i, corners - 1 - i) for i in range...  2.18 us
  transfers between devices with their start and end apart: 22, of which 8 were waited for; matrix products, arithmetic and copies ran while one was open for 1% of the time, Pallas kernels for 19%

profile of v4, /device:TPU:1, one launch (start us, length us, event | category | flops | bytes accessed | tf_op | source)
XLA Modules:
  0.0 107.7 jit_solution(7327746634520799648)
XLA Ops:
  2.4 3.2 %collective-permute-start = (bf16[272,256]{1,0:T(8,128)(2,1)}, bf16[272,256]{1,0:T(8,128)(2,1)S(1)}, u32[]{:S(2)}, u32[]{:S(2)}) collective-permute-start(bf16[272,256]{1,0:T(8,128)(2,1)} %get-tuple-element.21), channel_id=1, source_target_pairs={{0,1},{1,0},{2,3},{3,2},{4,5},{5,4},{6,7},{7,6},{8,9},{9,8},{10,11... | collective-permute-start | bytes 417800 | tf_op jit(solution)/shard_map/ppermute | solution.py:190
  6.7 2.2 %collective-permute-start.2 = (bf16[128,256]{1,0:T(8,128)(2,1)}, bf16[128,256]{1,0:T(8,128)(2,1)S(1)}, u32[]{:S(2)}, u32[]{:S(2)}) collective-permute-start(bf16[128,256]{1,0:T(8,128)(2,1)} %get-tuple-element.23), channel_id=1, source_target_pairs={{0,33},{1,32},{32,1},{33,0},{2,35},{3,34},{34,3},{35,2},{4,37},{5,... | collective-permute-start | bytes 196616 | tf_op jit(solution)/shard_map/ppermute | solution.py:201
  8.9 2.2 %collective-permute-done.1 = bf16[128,256]{1,0:T(8,128)(2,1)S(1)} collective-permute-done((bf16[128,256]{1,0:T(8,128)(2,1)}, bf16[128,256]{1,0:T(8,128)(2,1)S(1)}, u32[]{:S(2)}, u32[]{:S(2)}) %collective-permute-start.1) | collective-permute-done | bytes 65568 | tf_op jit(solution)/shard_map/ppermute | solution.py:190
  13.6 5.4 %collective-permute-start.3 = (bf16[512,256]{1,0:T(8,128)(2,1)S(1)}, bf16[512,256]{1,0:T(8,128)(2,1)S(1)}, u32[]{:S(2)}, u32[]{:S(2)}) collective-permute-start(bf16[512,256]{1,0:T(8,128)(2,1)S(1)} %pad_maximum_fusion.refs_1_), channel_id=1, source_target_pairs={{0,28},{4,0},{8,4},{12,8},{16,12},{20,16},{24,20},{28,24},{1,29},{... | collective-permute-start | bytes 786440 | tf_op jit(solution)/shard_map/ppermute | solution.py:190
  19.0 2.0 %spread.1 = bf16[8,288,256]{2,1,0:T(8,128)(2,1)} custom-call(bf16[144,256]{1,0:T(8,128)(2,1)} %get-tuple-element.20.mine_ref, bf16[272,256]{1,0:T(8,128)(2,1)} %copy-done.2), custom_call_target="tpu_custom_call" | custom-call | tf_op jit(solution)/shard_map/spread/pallas_call | solution.py:83
  21.0 4.2 %all-to-all-start = ((bf16[8,288,256]{2,1,0:T(8,128)(2,1)}), bf16[8,288,256]{2,1,0:T(8,128)(2,1)S(1)}, u32[]{:S(2)}, u32[]{:S(2)}) async-start(bf16[8,288,256]{2,1,0:T(8,128)(2,1)} %spread.1), calls=%async_computation | async-start | bytes 2359296 | tf_op jit(solution)/shard_map/all_to_all | solution.py:209
  25.3 2.7 %collective-permute-start.5 = (bf16[512,256]{1,0:T(8,128)(2,1)S(1)}, bf16[512,256]{1,0:T(8,128)(2,1)S(1)}, u32[]{:S(2)}, u32[]{:S(2)}) collective-permute-start(bf16[512,256]{1,0:T(8,128)(2,1)S(1)} %collective-permute-done.3.refs_2_), channel_id=1, source_target_pairs={{0,28},{4,0},{8,4},{12,8},{16,12},{20,16},{24,20},{28,24},{1,29},{... | collective-permute-start | bytes 786440 | tf_op jit(solution)/shard_map/ppermute | solution.py:190
  28.0 4.4 %collective-permute-done.5.refs_1_ = bf16[512,256]{1,0:T(8,128)(2,1)S(1)} collective-permute-done((bf16[512,256]{1,0:T(8,128)(2,1)S(1)}, bf16[512,256]{1,0:T(8,128)(2,1)S(1)}, u32[]{:S(2)}, u32[]{:S(2)}) %collective-permute-start.5) | collective-permute-done | bytes 262176 | tf_op jit(solution)/shard_map/ppermute | solution.py:190
  32.4 3.4 %collective-permute-start.7 = (bf16[512,256]{1,0:T(8,128)(2,1)S(1)}, bf16[512,256]{1,0:T(8,128)(2,1)S(1)}, u32[]{:S(2)}, u32[]{:S(2)}) collective-permute-start(bf16[512,256]{1,0:T(8,128)(2,1)S(1)} %collective-permute-done.5.refs_1_), channel_id=1, source_target_pairs={{0,28},{4,0},{8,4},{12,8},{16,12},{20,16},{24,20},{28,24},{1,29},{... | collective-permute-start | bytes 786440 | tf_op jit(solution)/shard_map/ppermute | solution.py:190
  35.8 3.3 %collective-permute-done.7.refs_1_ = bf16[512,256]{1,0:T(8,128)(2,1)S(1)} collective-permute-done((bf16[512,256]{1,0:T(8,128)(2,1)S(1)}, bf16[512,256]{1,0:T(8,128)(2,1)S(1)}, u32[]{:S(2)}, u32[]{:S(2)}) %collective-permute-start.7) | collective-permute-done | bytes 262176 | tf_op jit(solution)/shard_map/ppermute | solution.py:190
  39.1 3.6 %collective-permute-start.10 = (bf16[256,256]{1,0:T(8,128)(2,1)S(1)}, bf16[256,256]{1,0:T(8,128)(2,1)S(1)}, u32[]{:S(2)}, u32[]{:S(2)}) collective-permute-start(bf16[256,256]{1,0:T(8,128)(2,1)S(1)} %slice.47), channel_id=1, source_target_pairs={{0,28},{4,0},{8,4},{12,8},{16,12},{20,16},{24,20},{28,24},{1,29},{... | collective-permute-start | bytes 393224 | tf_op jit(solution)/shard_map/ppermute | solution.py:190
  42.8 1.8 %collective-permute-done.10 = bf16[256,256]{1,0:T(8,128)(2,1)S(1)} collective-permute-done((bf16[256,256]{1,0:T(8,128)(2,1)S(1)}, bf16[256,256]{1,0:T(8,128)(2,1)S(1)}, u32[]{:S(2)}, u32[]{:S(2)}) %collective-permute-start.10) | collective-permute-done | bytes 131104 | tf_op jit(solution)/shard_map/ppermute | solution.py:190
  44.7 3.2 %collective-permute-done.9 = bf16[256,256]{1,0:T(8,128)(2,1)S(1)} collective-permute-done((bf16[256,256]{1,0:T(8,128)(2,1)S(1)}, bf16[256,256]{1,0:T(8,128)(2,1)S(1)}, u32[]{:S(2)}, u32[]{:S(2)}) %collective-permute-start.9) | collective-permute-done | bytes 131104 | tf_op jit(solution)/shard_map/ppermute | solution.py:190
  47.9 3.0 %tile.5 = (f32[8,128,256]{2,1,0:T(8,128)S(1)}, f32[512,256]{1,0:T(8,128)S(1)}) custom-call(bf16[8,288,256]{2,1,0:T(8,128)(2,1)S(1)} %all-to-all-done.refs_0_.refs_1_, bf16[512,256]{1,0:T(8,128)(2,1)S(1)} %pad_maximum_fusion.refs_1_), custom_call_target="tpu_custom_call" | custom-call | flops 2684354560 | bytes 8388608 | tf_op jit(solution)/shard_map/tile/pallas_call | solution.py:169
  50.9 3.1 %tile.6 = (f32[8,128,256]{2,1,0:T(8,128)S(1)}, f32[512,256]{1,0:T(8,128)S(1)}) custom-call(bf16[8,288,256]{2,1,0:T(8,128)(2,1)S(1)} %all-to-all-done.refs_0_.refs_1_, bf16[512,256]{1,0:T(8,128)(2,1)S(1)} %pad_maximum_fusion.1.refs_1_.refs_3_, f32[8,128,256]{2,1,0:T(8,128)S(1)} %get-tuple-element.24.refs_2_, ...), custom_call_target="tpu_custom_call" | custom-call | flops 2684354560 | bytes 8388608 | tf_op jit(solution)/shard_map/tile/pallas_call | solution.py:169
  54.3 5.9 %tile.7 = (f32[8,128,256]{2,1,0:T(8,128)S(1)}, f32[512,256]{1,0:T(8,128)S(1)}, f32[512,256]{1,0:T(8,128)S(1)}) custom-call(bf16[8,288,256]{2,1,0:T(8,128)(2,1)S(1)} %all-to-all-done.refs_0_.refs_1_, bf16[512,256]{1,0:T(8,128)(2,1)S(1)} %collective-permute-done.7.refs_1_, bf16[512,256]{1,0:T(8,128)(2,1)S(1)} %collective-permute-done.8.refs_2_, ...), custom_call_target="tpu_custom_call" | custom-call | flops 5368709120 | bytes 8388608 | tf_op jit(solution)/shard_map/tile/pallas_call | solution.py:169
  60.3 2.7 %collective-permute-start.15 = (bf16[512,256]{1,0:T(8,128)(2,1)S(1)}, bf16[512,256]{1,0:T(8,128)(2,1)S(1)}, u32[]{:S(2)}, u32[]{:S(2)}) collective-permute-start(bf16[512,256]{1,0:T(8,128)(2,1)S(1)} %convert_element_type.73), channel_id=1, source_target_pairs={{0,28},{4,0},{8,4},{12,8},{16,12},{20,16},{24,20},{28,24},{1,29},{... | collective-permute-start | bytes 786440 | tf_op jit(solution)/shard_map/ppermute | solution.py:190
  63.2 5.9 %tile.8 = (f32[8,128,256]{2,1,0:T(8,128)S(1)}, f32[512,256]{1,0:T(8,128)S(1)}, f32[512,256]{1,0:T(8,128)S(1)}) custom-call(bf16[8,288,256]{2,1,0:T(8,128)(2,1)S(1)} %all-to-all-done.refs_0_.refs_1_, bf16[512,256]{1,0:T(8,128)(2,1)S(1)} %collective-permute-done.5.refs_1_, bf16[512,256]{1,0:T(8,128)(2,1)S(1)} %copy-done.1, ...), custom_call_target="tpu_custom_call" | custom-call | flops 5368709120 | bytes 8388608 | tf_op jit(solution)/shard_map/tile/pallas_call | solution.py:169
  69.2 2.7 %collective-permute-start.16 = (bf16[512,256]{1,0:T(8,128)(2,1)S(1)}, bf16[512,256]{1,0:T(8,128)(2,1)S(1)}, u32[]{:S(2)}, u32[]{:S(2)}) collective-permute-start(bf16[512,256]{1,0:T(8,128)(2,1)S(1)} %add_convert_fusion.1), channel_id=1, source_target_pairs={{0,28},{4,0},{8,4},{12,8},{16,12},{20,16},{24,20},{28,24},{1,29},{... | collective-permute-start | bytes 786440 | tf_op jit(solution)/shard_map/ppermute | solution.py:190
  72.1 6.6 %tile.9 = (bf16[16,128,128]{2,1,0:T(8,128)(2,1)}, f32[512,256]{1,0:T(8,128)S(1)}, f32[512,256]{1,0:T(8,128)S(1)}) custom-call(s32[1]{0:T(128)} %bitcast.core_ref.refs_0_, bf16[8,288,256]{2,1,0:T(8,128)(2,1)S(1)} %all-to-all-done.refs_0_.refs_1_, bf16[512,256]{1,0:T(8,128)(2,1)S(1)} %collective-permute-done.3.refs_2_, ...), custom_call_target="tpu_custom_call" | custom-call | flops 5368709120 | bytes 8388608 | tf_op jit(solution)/shard_map/tile/pallas_call | solution.py:169
  78.8 2.9 %collective-permute-start.17 = (bf16[512,256]{1,0:T(8,128)(2,1)S(1)}, bf16[512,256]{1,0:T(8,128)(2,1)S(1)}, u32[]{:S(2)}, u32[]{:S(2)}) collective-permute-start(bf16[512,256]{1,0:T(8,128)(2,1)S(1)} %add_convert_fusion), channel_id=1, source_target_pairs={{0,28},{4,0},{8,4},{12,8},{16,12},{20,16},{24,20},{28,24},{1,29},{... | collective-permute-start | bytes 786440 | tf_op jit(solution)/shard_map/ppermute | solution.py:190
  81.9 11.4 %all-to-all-start.1 = ((bf16[16,128,128]{2,1,0:T(8,128)(2,1)}), bf16[16,128,128]{2,1,0:T(8,128)(2,1)S(1)}, u32[]{:S(2)}, u32[]{:S(2)}) async-start(bf16[16,128,128]{2,1,0:T(8,128)(2,1)} %get-tuple-element.31), calls=%async_computation.1 | async-start | bytes 1048576 | tf_op jit(solution)/shard_map/all_to_all | solution.py:237
  93.3 1.8 %collective-permute-start.18 = (bf16[256,256]{1,0:T(8,128)(2,1)S(1)}, bf16[256,256]{1,0:T(8,128)(2,1)S(1)}, u32[]{:S(2)}, u32[]{:S(2)}) collective-permute-start(bf16[256,256]{1,0:T(8,128)(2,1)S(1)} %slice.62), channel_id=1, source_target_pairs={{0,32},{32,0},{1,33},{33,1},{2,34},{34,2},{3,35},{35,3},{4,36},{36... | collective-permute-start | bytes 393224 | tf_op jit(solution)/shard_map/ppermute | solution.py:190
  95.2 9.5 %collective-permute-done.18 = bf16[256,256]{1,0:T(8,128)(2,1)S(1)} collective-permute-done((bf16[256,256]{1,0:T(8,128)(2,1)S(1)}, bf16[256,256]{1,0:T(8,128)(2,1)S(1)}, u32[]{:S(2)}, u32[]{:S(2)}) %collective-permute-start.18) | collective-permute-done | bytes 131104 | tf_op jit(solution)/shard_map/ppermute | solution.py:190
  (55 shorter events, 9.3 us)
Async XLA Ops:
  2.4 6.4 %collective-permute-start = (bf16[272,256]{1,0:T(8,128)(2,1)}, bf16[272,256]{1,0:T(8,128)(2,1)S(1)}, u32[]{:S(2)}, u32[]{:S(2)}) collective-permute-start(bf16[272,256]{1,0:T(8,128)(2,1)} %get-tuple-element.21), channel_id=1, source_target_pairs={{0,1},{1,0},{2,3},{3,2},{4,5},{5,4},{6,7},{7,6},{8,9},{9,8},{10,11... | collective-permute-start | bytes 417800 | tf_op jit(solution)/shard_map/ppermute | solution.py:190
  5.7 5.4 %collective-permute-start.1 = (bf16[128,256]{1,0:T(8,128)(2,1)}, bf16[128,256]{1,0:T(8,128)(2,1)S(1)}, u32[]{:S(2)}, u32[]{:S(2)}) collective-permute-start(bf16[128,256]{1,0:T(8,128)(2,1)} %get-tuple-element.22), channel_id=1, source_target_pairs={{0,32},{32,0},{1,33},{33,1},{2,34},{34,2},{3,35},{35,3},{4,36},{36... | collective-permute-start | bytes 196616 | tf_op jit(solution)/shard_map/ppermute | solution.py:190
  6.7 6.0 %collective-permute-start.2 = (bf16[128,256]{1,0:T(8,128)(2,1)}, bf16[128,256]{1,0:T(8,128)(2,1)S(1)}, u32[]{:S(2)}, u32[]{:S(2)}) collective-permute-start(bf16[128,256]{1,0:T(8,128)(2,1)} %get-tuple-element.23), channel_id=1, source_target_pairs={{0,33},{1,32},{32,1},{33,0},{2,35},{3,34},{34,3},{35,2},{4,37},{5,... | collective-permute-start | bytes 196616 | tf_op jit(solution)/shard_map/ppermute | solution.py:201
  8.9 10.1 %copy-start.2 = (bf16[272,256]{1,0:T(8,128)(2,1)}, bf16[272,256]{1,0:T(8,128)(2,1)S(1)}, u32[]{:S(2)}) copy-start(bf16[272,256]{1,0:T(8,128)(2,1)S(1)} %collective-permute-done.other_ref) | copy-start | bytes 417796
  13.6 11.7 %collective-permute-start.3 = (bf16[512,256]{1,0:T(8,128)(2,1)S(1)}, bf16[512,256]{1,0:T(8,128)(2,1)S(1)}, u32[]{:S(2)}, u32[]{:S(2)}) collective-permute-start(bf16[512,256]{1,0:T(8,128)(2,1)S(1)} %pad_maximum_fusion.refs_1_), channel_id=1, source_target_pairs={{0,28},{4,0},{8,4},{12,8},{16,12},{20,16},{24,20},{28,24},{1,29},{... | collective-permute-start | bytes 786440 | tf_op jit(solution)/shard_map/ppermute | solution.py:190
  19.0 9.0 %collective-permute-start.4 = (bf16[512,256]{1,0:T(8,128)(2,1)S(1)}, bf16[512,256]{1,0:T(8,128)(2,1)S(1)}, u32[]{:S(2)}, u32[]{:S(2)}) collective-permute-start(bf16[512,256]{1,0:T(8,128)(2,1)S(1)} %pad_maximum_fusion.refs_1_), channel_id=1, source_target_pairs={{0,4},{4,8},{8,12},{12,16},{16,20},{20,24},{24,28},{28,0},{1,5},{5... | collective-permute-start | bytes 786440 | tf_op jit(solution)/shard_map/ppermute | solution.py:190
  21.0 26.8 %all-to-all-start = ((bf16[8,288,256]{2,1,0:T(8,128)(2,1)}), bf16[8,288,256]{2,1,0:T(8,128)(2,1)S(1)}, u32[]{:S(2)}, u32[]{:S(2)}) async-start(bf16[8,288,256]{2,1,0:T(8,128)(2,1)} %spread.1), calls=%async_computation | async-start | bytes 2359296 | tf_op jit(solution)/shard_map/all_to_all | solution.py:209
  25.3 7.1 %collective-permute-start.5 = (bf16[512,256]{1,0:T(8,128)(2,1)S(1)}, bf16[512,256]{1,0:T(8,128)(2,1)S(1)}, u32[]{:S(2)}, u32[]{:S(2)}) collective-permute-start(bf16[512,256]{1,0:T(8,128)(2,1)S(1)} %collective-permute-done.3.refs_2_), channel_id=1, source_target_pairs={{0,28},{4,0},{8,4},{12,8},{16,12},{20,16},{24,20},{28,24},{1,29},{... | collective-permute-start | bytes 786440 | tf_op jit(solution)/shard_map/ppermute | solution.py:190
  28.0 7.8 %collective-permute-start.6 = (bf16[512,256]{1,0:T(8,128)(2,1)S(1)}, bf16[512,256]{1,0:T(8,128)(2,1)S(1)}, u32[]{:S(2)}, u32[]{:S(2)}) collective-permute-start(bf16[512,256]{1,0:T(8,128)(2,1)S(1)} %collective-permute-done.4.refs_3_), channel_id=1, source_target_pairs={{0,4},{4,8},{8,12},{12,16},{16,20},{20,24},{24,28},{28,0},{1,5},{5... | collective-permute-start | bytes 786440 | tf_op jit(solution)/shard_map/ppermute | solution.py:190
  32.4 6.7 %collective-permute-start.7 = (bf16[512,256]{1,0:T(8,128)(2,1)S(1)}, bf16[512,256]{1,0:T(8,128)(2,1)S(1)}, u32[]{:S(2)}, u32[]{:S(2)}) collective-permute-start(bf16[512,256]{1,0:T(8,128)(2,1)S(1)} %collective-permute-done.5.refs_1_), channel_id=1, source_target_pairs={{0,28},{4,0},{8,4},{12,8},{16,12},{20,16},{24,20},{28,24},{1,29},{... | collective-permute-start | bytes 786440 | tf_op jit(solution)/shard_map/ppermute | solution.py:190
  35.8 8.9 %copy-start = (bf16[512,256]{1,0:T(8,128)(2,1)}, bf16[512,256]{1,0:T(8,128)(2,1)S(1)}, u32[]{:S(2)}) copy-start(bf16[512,256]{1,0:T(8,128)(2,1)S(1)} %collective-permute-done.6.refs_2_) | copy-start | bytes 786436
  35.8 6.9 %collective-permute-start.8 = (bf16[512,256]{1,0:T(8,128)(2,1)S(1)}, bf16[512,256]{1,0:T(8,128)(2,1)S(1)}, u32[]{:S(2)}, u32[]{:S(2)}) collective-permute-start(bf16[512,256]{1,0:T(8,128)(2,1)S(1)} %collective-permute-done.6.refs_2_), channel_id=1, source_target_pairs={{0,4},{4,8},{8,12},{12,16},{16,20},{20,24},{24,28},{28,0},{1,5},{5... | collective-permute-start | bytes 786440 | tf_op jit(solution)/shard_map/ppermute | solution.py:190
  39.1 5.6 %collective-permute-start.10 = (bf16[256,256]{1,0:T(8,128)(2,1)S(1)}, bf16[256,256]{1,0:T(8,128)(2,1)S(1)}, u32[]{:S(2)}, u32[]{:S(2)}) collective-permute-start(bf16[256,256]{1,0:T(8,128)(2,1)S(1)} %slice.47), channel_id=1, source_target_pairs={{0,28},{4,0},{8,4},{12,8},{16,12},{20,16},{24,20},{28,24},{1,29},{... | collective-permute-start | bytes 393224 | tf_op jit(solution)/shard_map/ppermute | solution.py:190
  42.7 5.1 %collective-permute-start.9 = (bf16[256,256]{1,0:T(8,128)(2,1)S(1)}, bf16[256,256]{1,0:T(8,128)(2,1)S(1)}, u32[]{:S(2)}, u32[]{:S(2)}) collective-permute-start(bf16[256,256]{1,0:T(8,128)(2,1)S(1)} %slice.46), channel_id=1, source_target_pairs={{0,4},{4,8},{8,12},{12,16},{16,20},{20,24},{24,28},{28,0},{1,5},{5... | collective-permute-start | bytes 393224 | tf_op jit(solution)/shard_map/ppermute | solution.py:190
  54.0 9.0 %collective-permute-start.11 = (bf16[512,256]{1,0:T(8,128)(2,1)S(1)}, bf16[512,256]{1,0:T(8,128)(2,1)S(1)}, u32[]{:S(2)}, u32[]{:S(2)}) collective-permute-start(bf16[512,256]{1,0:T(8,128)(2,1)S(1)} %convert_element_type.61.refs_4_), channel_id=1, source_target_pairs={{0,4},{4,8},{8,12},{12,16},{16,20},{20,24},{24,28},{28,0},{1,5},{5... | collective-permute-start | bytes 786440 | tf_op jit(solution)/shard_map/ppermute | solution.py:190
  60.3 8.8 %collective-permute-start.15 = (bf16[512,256]{1,0:T(8,128)(2,1)S(1)}, bf16[512,256]{1,0:T(8,128)(2,1)S(1)}, u32[]{:S(2)}, u32[]{:S(2)}) collective-permute-start(bf16[512,256]{1,0:T(8,128)(2,1)S(1)} %convert_element_type.73), channel_id=1, source_target_pairs={{0,28},{4,0},{8,4},{12,8},{16,12},{20,16},{24,20},{28,24},{1,29},{... | collective-permute-start | bytes 786440 | tf_op jit(solution)/shard_map/ppermute | solution.py:190
  63.1 8.8 %collective-permute-start.12 = (bf16[512,256]{1,0:T(8,128)(2,1)S(1)}, bf16[512,256]{1,0:T(8,128)(2,1)S(1)}, u32[]{:S(2)}, u32[]{:S(2)}) collective-permute-start(bf16[512,256]{1,0:T(8,128)(2,1)S(1)} %add_convert_fusion.4.refs_4_), channel_id=1, source_target_pairs={{0,4},{4,8},{8,12},{12,16},{16,20},{20,24},{24,28},{28,0},{1,5},{5... | collective-permute-start | bytes 786440 | tf_op jit(solution)/shard_map/ppermute | solution.py:190
  69.2 9.5 %collective-permute-start.16 = (bf16[512,256]{1,0:T(8,128)(2,1)S(1)}, bf16[512,256]{1,0:T(8,128)(2,1)S(1)}, u32[]{:S(2)}, u32[]{:S(2)}) collective-permute-start(bf16[512,256]{1,0:T(8,128)(2,1)S(1)} %add_convert_fusion.1), channel_id=1, source_target_pairs={{0,28},{4,0},{8,4},{12,8},{16,12},{20,16},{24,20},{28,24},{1,29},{... | collective-permute-start | bytes 786440 | tf_op jit(solution)/shard_map/ppermute | solution.py:190
  72.0 9.7 %collective-permute-start.13 = (bf16[512,256]{1,0:T(8,128)(2,1)S(1)}, bf16[512,256]{1,0:T(8,128)(2,1)S(1)}, u32[]{:S(2)}, u32[]{:S(2)}) collective-permute-start(bf16[512,256]{1,0:T(8,128)(2,1)S(1)} %add_convert_fusion.3.refs_5_), channel_id=1, source_target_pairs={{0,4},{4,8},{8,12},{12,16},{16,20},{20,24},{24,28},{28,0},{1,5},{5... | collective-permute-start | bytes 786440 | tf_op jit(solution)/shard_map/ppermute | solution.py:190
  78.8 14.4 %collective-permute-start.17 = (bf16[512,256]{1,0:T(8,128)(2,1)S(1)}, bf16[512,256]{1,0:T(8,128)(2,1)S(1)}, u32[]{:S(2)}, u32[]{:S(2)}) collective-permute-start(bf16[512,256]{1,0:T(8,128)(2,1)S(1)} %add_convert_fusion), channel_id=1, source_target_pairs={{0,28},{4,0},{8,4},{12,8},{16,12},{20,16},{24,20},{28,24},{1,29},{... | collective-permute-start | bytes 786440 | tf_op jit(solution)/shard_map/ppermute | solution.py:190
  81.8 11.5 %collective-permute-start.14 = (bf16[512,256]{1,0:T(8,128)(2,1)S(1)}, bf16[512,256]{1,0:T(8,128)(2,1)S(1)}, u32[]{:S(2)}, u32[]{:S(2)}) collective-permute-start(bf16[512,256]{1,0:T(8,128)(2,1)S(1)} %add_convert_fusion.2), channel_id=1, source_target_pairs={{0,4},{4,8},{8,12},{12,16},{16,20},{20,24},{24,28},{28,0},{1,5},{5... | collective-permute-start | bytes 786440 | tf_op jit(solution)/shard_map/ppermute | solution.py:190
  81.9 23.6 %all-to-all-start.1 = ((bf16[16,128,128]{2,1,0:T(8,128)(2,1)}), bf16[16,128,128]{2,1,0:T(8,128)(2,1)S(1)}, u32[]{:S(2)}, u32[]{:S(2)}) async-start(bf16[16,128,128]{2,1,0:T(8,128)(2,1)} %get-tuple-element.31), calls=%async_computation.1 | async-start | bytes 1048576 | tf_op jit(solution)/shard_map/all_to_all | solution.py:237
  93.3 11.4 %collective-permute-start.18 = (bf16[256,256]{1,0:T(8,128)(2,1)S(1)}, bf16[256,256]{1,0:T(8,128)(2,1)S(1)}, u32[]{:S(2)}, u32[]{:S(2)}) collective-permute-start(bf16[256,256]{1,0:T(8,128)(2,1)S(1)} %slice.62), channel_id=1, source_target_pairs={{0,32},{32,0},{1,33},{33,1},{2,34},{34,2},{3,35},{35,3},{4,36},{36... | collective-permute-start | bytes 393224 | tf_op jit(solution)/shard_map/ppermute | solution.py:190
  104.8 1.6 %collective-permute-start.19 = (bf16[128,256]{1,0:T(8,128)(2,1)S(1)}, bf16[128,256]{1,0:T(8,128)(2,1)S(1)}, u32[]{:S(2)}, u32[]{:S(2)}) collective-permute-start(bf16[128,256]{1,0:T(8,128)(2,1)S(1)} %slice.51), channel_id=1, source_target_pairs={{0,1},{1,0},{2,3},{3,2},{4,5},{5,4},{6,7},{7,6},{8,9},{9,8},{10,11... | collective-permute-start | bytes 196616 | tf_op jit(solution)/shard_map/ppermute | solution.py:190
  (1 other events, 2.9 us)

commit v5 on v4

--- a/solution.py
+++ b/solution.py
@@ -13,7 +13,6 @@
 LOG2E = math.log2(math.e)
 AXES = ("y", "xh", "z", "xl", "core")
 GROUP = ("y", "xl")
-OWNERS = ("y", "xl", "core")
 ROWS = 256
 STATS = 16
 HALF = 128
@@ -89,9 +88,42 @@
     )(*args)
 
 
-def tile_kernel(count, first, last, chips, *refs):
+def join_kernel(mine_ref, other_ref, across_ref, diagonal_ref, _, out_ref):
+    out_ref[:HALF, :] = mine_ref[...]
+    out_ref[HALF:ROWS, :] = other_ref[HALF + STATS :, :]
+    out_ref[ROWS : ROWS + HALF, :] = across_ref[...]
+    out_ref[ROWS + HALF :, :] = diagonal_ref[...]
+
+
+def join_call(*args):
+    vmem = pl.BlockSpec(memory_space=pltpu.VMEM)
+    return pl.pallas_call(
+        join_kernel,
+        in_specs=[vmem] * 4 + [pl.BlockSpec(memory_space=pl.ANY)],
+        out_specs=vmem,
+        out_shape=jax.ShapeDtypeStruct((2 * ROWS, 2 * HEAD), BF16),
+        name="join",
+    )(*args)
+
+
+def cut_kernel(low_ref, high_ref, _, first_ref, second_ref):
+    first_ref[...] = low_ref[:ROWS, :]
+    second_ref[...] = high_ref[ROWS:, :]
+
+
+def cut_call(*args):
+    vmem = pl.BlockSpec(memory_space=pltpu.VMEM)
+    return pl.pallas_call(
+        cut_kernel,
+        in_specs=[vmem] * 2 + [pl.BlockSpec(memory_space=pl.ANY)],
+        out_specs=[vmem] * 2,
+        out_shape=[jax.ShapeDtypeStruct((ROWS, 2 * HEAD), BF16)] * 2,
+        name="cut",
+    )(*args)
+
+
+def tile_kernel(count, first, chips, *refs):
     refs = list(refs)
-    core_ref = refs.pop(0) if last else None
     qg_ref = refs.pop(0)
     blocks = [refs.pop(0) for _ in range(count)]
     if not first:
@@ -132,12 +164,7 @@
             acc_k[n] += jnp.dot(ds, q, preferred_element_type=F32)
             dq = jnp.dot(kt_ref[n], ds, preferred_element_type=F32)
             total = dq if total is None else total + dq
-        if last:
-            core = core_ref[0]
-            dq_ref[2 * chip + core] = total[:, :HALF].astype(BF16)
-            dq_ref[2 * chip + 1 - core] = total[:, HALF:].astype(BF16)
-        else:
-            dq_ref[chip] = total
+        dq_ref[chip] = total.astype(dq_ref.dtype)
 
     @pl.when(step == pl.num_programs(0) - 1)
     def _():
@@ -146,31 +173,25 @@
             d_ref[:, HEAD:] = acc_v[n]
 
 
-def tile_call(qg, blocks, old=None, after=None, core=None):
-    first, last = old is None, core is not None
+def tile_call(qg, blocks, old=None, after=None, last=False):
+    first = old is None
     groups, rows, width = qg.shape
     count, keys = len(blocks), blocks[0].shape[0]
     chips = 4
     q_spec = pl.BlockSpec((chips, rows, width), lambda i: (i, 0, 0))
     kv_spec = pl.BlockSpec((keys, width), lambda i: (0, 0))
     dq_spec = pl.BlockSpec((chips, HEAD, ROWS), lambda i: (i, 0, 0))
-    dq_shape = jax.ShapeDtypeStruct((groups, HEAD, ROWS), F32)
-    out_spec = dq_spec
-    if last:
-        out_spec = pl.BlockSpec((2 * chips, HEAD, HALF), lambda i: (i, 0, 0))
-        dq_shape = jax.ShapeDtypeStruct((2 * groups, HEAD, HALF), BF16)
+    dq_shape = jax.ShapeDtypeStruct((groups, HEAD, ROWS), BF16 if last else F32)
     args, specs = [qg, *blocks], [q_spec] + [kv_spec] * count
-    if last:
-        args, specs = [core.reshape(1)] + args, [pl.BlockSpec(memory_space=pltpu.SMEM)] + specs
     if not first:
         args += [old, after]
         specs += [dq_spec, pl.BlockSpec(memory_space=pl.ANY)]
     pairs = groups * ROWS * count * keys
     return pl.pallas_call(
-        functools.partial(tile_kernel, count, first, last, chips),
+        functools.partial(tile_kernel, count, first, chips),
         grid=(groups // chips,),
         in_specs=specs,
-        out_specs=[out_spec] + [kv_spec] * count,
+        out_specs=[dq_spec] + [kv_spec] * count,
         out_shape=[dq_shape] + [jax.ShapeDtypeStruct((keys, width), F32)] * count,
         scratch_shapes=[
             pltpu.VMEM((count, keys, HEAD), F32),
@@ -202,23 +223,22 @@
         far_kv, ("xh", "core"), [(i, corners - 1 - i) for i in range(corners)]
     )
     other = shift(send, "core", 1)
-    key_pair = jnp.concatenate([mine_kv, other[HALF + STATS :], across, diagonal], axis=0)
-
     peers = math.prod(lax.axis_size(a) for a in GROUP)
     spread = spread_call(peers, mine_q, other)
     gathered = lax.all_to_all(spread, GROUP, 0, 0, tiled=True)
-    keys = {0: key_pair}
+    keys = {0: join_call(mine_kv, other, across, diagonal, spread)}
     for by in (1, 2, 3):
         keys[by] = shift(keys[by - 1], "z", 1)
         keys[-by] = shift(keys[1 - by], "z", -1)
+    total_q, own = tile_call(gathered, [keys[0]])
+    first_half, second_half = cut_call(keys[3], keys[-3], own)
     keys[4] = jnp.concatenate(
-        [shift(keys[3][:ROWS], "z", 1), shift(keys[-3][ROWS:], "z", -1)], axis=0
+        [shift(first_half, "z", 1), shift(second_half, "z", -1)], axis=0
     )
 
     def low(x):
         return x.astype(BF16)
 
-    total_q, own = tile_call(gathered, [keys[0]])
     total_q, far = tile_call(gathered, [keys[4]], total_q, keys[4])
     up = low(far)
     down = None
@@ -227,26 +247,25 @@
         up_in = shift(up, "z", 1)
         down_in = None if down is None else shift(down, "z", -1)
         total_q, du, dd = tile_call(
-            gathered, [keys[-by], keys[by]], total_q, after, core if by == 1 else None
+            gathered, [keys[-by], keys[by]], total_q, after, by == 1
         )
         up = low(du + up_in.astype(F32))
         down = low(dd if down_in is None else dd + down_in.astype(F32))
         after = up
     up_in = shift(up, "z", 1)
     down_in = shift(down, "z", -1)
-    returned = lax.all_to_all(total_q, OWNERS, 0, 0, tiled=True)
+    returned = lax.all_to_all(total_q, GROUP, 0, 0, tiled=True)
     grad_pair = own + up_in.astype(F32) + down_in.astype(F32)
     grad_kv = grad_pair[:ROWS] + shift(low(grad_pair[ROWS:]), "xh", 1).astype(F32)
-    grad_kv = low(grad_kv)
-    kept = grad_kv[:HALF]
-    moved = shift(grad_kv[HALF:], "core", 1)
-    lower, upper = jnp.where(even, kept, moved), jnp.where(even, moved, kept)
-    grad_k = jnp.concatenate([lower[:, :HEAD], upper[:, :HEAD]], axis=1)
-    grad_v = jnp.concatenate([lower[:, HEAD:], upper[:, HEAD:]], axis=1)
-
-    heads = returned.reshape(peers, 2 * HEAD, HALF).astype(F32)
-    grad_q = low(jnp.sum(heads, axis=0).T)
-    return grad_q, grad_k, grad_v
+
+    grad_q = jnp.sum(returned.astype(F32), axis=0).T
+    grads = jnp.stack([grad_q, grad_kv[:, :HEAD], grad_kv[:, HEAD:]]).astype(BF16)
+    kept = grads[:, :HALF]
+    moved = shift(grads[:, HALF:], "core", 1)
+    out = jnp.concatenate(
+        [jnp.where(even, kept, moved), jnp.where(even, moved, kept)], axis=2
+    )
+    return out[0], out[1], out[2]
 
 
 def solution(mesh):

time: 108 us -> 127 us (1.18)
  waiting for transfers between devices: 26.1 us -> 38.6 us
  local copies, waits for them, and re-layouts: 0.83 us -> 6.1 us
  Pallas kernels: 28.5 us -> 31.9 us
  other arithmetic: 2.67 us -> 1.25 us
    ppermute x19, waiting for transfers between devices: 24.5 us -> 32.5 us  [shift(): return lax.ppermute(x, axis, [(i, (i + by) % n) for i in range(n)])]
    ppermute x19, starting transfers between devices: 30.9 us -> 38.4 us  [shift(): return lax.ppermute(x, axis, [(i, (i + by) % n) for i in range(n)])]
    all_to_all x1, starting transfers between devices: 11.4 us -> 4.75 us  [local(): returned = lax.all_to_all(total_q, GROUP, 0, 0, tiled=True)]
    unnamed x7 -> x28, local copies, waits for them, and re-layouts: 0.75 us -> 5.95 us
    all_to_all x1, waiting for transfers between devices: 0.01 us -> 4.19 us  [local(): returned = lax.all_to_all(total_q, GROUP, 0, 0, tiled=True)]
    pallas_call x5 -> x7, Pallas kernels: 24.6 us -> 28 us  [the longest x5 24.6 us: tile_call(): pl.pallas_call(functools.partial(tile_kernel, count, first, chips), grid=...]
    concatenate x4 -> x1, other arithmetic: 2.15 us -> 0.02 us  [local(): jnp.concatenate([shift(first_half, 'z', 1), shift(second_half, 'z', -1)],...]
  transfers between devices with their start and end apart: 22 -> 22, of which waited for: 8 -> 11; matrix products, arithmetic and copies ran while one was open for 1% -> 0% of each run, Pallas kernels for 19% -> 18%
where the time goes in v5:
time: 127 us
  starting transfers between devices  48.1 us (38%)
  waiting for transfers between devices  38.6 us (30%)
  Pallas kernels  31.9 us (25%)
  local copies, waits for them, and re-layouts  6.1 us (5%)
    ppermute x19, starting transfers between devices, shift(): return lax.ppermute(x, axis, [(i, (i + by) % n) for i in range(n)])  38.4 us
    ppermute x19, waiting for transfers between devices, shift(): return lax.ppermute(x, axis, [(i, (i + by) % n) for i in range(n)])  32.5 us
    pallas_call x5, Pallas kernels, tile_call(): pl.pallas_call(functools.partial(tile_kernel, count, first, chips), grid=...  24.6 us
    unnamed x28, local copies, waits for them, and re-layouts  5.95 us
    all_to_all x1, starting transfers between devices, local(): returned = lax.all_to_all(total_q, GROUP, 0, 0, tiled=True)  4.75 us
    all_to_all x1, waiting for transfers between devices, local(): returned = lax.all_to_all(total_q, GROUP, 0, 0, tiled=True)  4.19 us
    all_to_all x1, starting transfers between devices, local(): gathered = lax.all_to_all(spread, GROUP, 0, 0, tiled=True)  3.69 us
  transfers between devices with their start and end apart: 22, of which 11 were waited for; matrix products, arithmetic and copies ran while one was open for 0% of the time, Pallas kernels for 18%

profile of v5, /device:TPU:1, one launch (start us, length us, event | category | flops | bytes accessed | tf_op | source)
XLA Modules:
  0.0 126.9 jit_solution(16168295487492637042)
XLA Ops:
  2.4 3.2 %collective-permute-start = (bf16[272,256]{1,0:T(8,128)(2,1)}, bf16[272,256]{1,0:T(8,128)(2,1)S(1)}, u32[]{:S(2)}, u32[]{:S(2)}) collective-permute-start(bf16[272,256]{1,0:T(8,128)(2,1)} %get-tuple-element.23), channel_id=1, source_target_pairs={{0,1},{1,0},{2,3},{3,2},{4,5},{5,4},{6,7},{7,6},{8,9},{9,8},{10,11... | collective-permute-start | bytes 417800 | tf_op jit(solution)/shard_map/ppermute | solution.py:211
  7.5 2.1 %spread.1._ = bf16[8,288,256]{2,1,0:T(8,128)(2,1)} custom-call(bf16[144,256]{1,0:T(8,128)(2,1)} %get-tuple-element.22.mine_ref, bf16[272,256]{1,0:T(8,128)(2,1)} %copy-done.9), custom_call_target="tpu_custom_call" | custom-call | tf_op jit(solution)/shard_map/spread/pallas_call | solution.py:82
  9.6 3.7 %all-to-all-start = ((bf16[8,288,256]{2,1,0:T(8,128)(2,1)}), bf16[8,288,256]{2,1,0:T(8,128)(2,1)S(1)}, u32[]{:S(2)}, u32[]{:S(2)}) async-start(bf16[8,288,256]{2,1,0:T(8,128)(2,1)} %spread.1._), calls=%async_computation | async-start | bytes 2359296 | tf_op jit(solution)/shard_map/all_to_all | solution.py:228
  13.3 2.3 %collective-permute-start.1 = (bf16[128,256]{1,0:T(8,128)(2,1)S(1)}, bf16[128,256]{1,0:T(8,128)(2,1)S(1)}, u32[]{:S(2)}, u32[]{:S(2)}) collective-permute-start(bf16[128,256]{1,0:T(8,128)(2,1)S(1)} %copy-done.10), channel_id=1, source_target_pairs={{0,32},{32,0},{1,33},{33,1},{2,34},{34,2},{3,35},{35,3},{4,36},{36... | collective-permute-start | bytes 196616 | tf_op jit(solution)/shard_map/ppermute | solution.py:211
  17.0 13.4 %collective-permute-done.1.across_ref = bf16[128,256]{1,0:T(8,128)(2,1)S(1)} collective-permute-done((bf16[128,256]{1,0:T(8,128)(2,1)S(1)}, bf16[128,256]{1,0:T(8,128)(2,1)S(1)}, u32[]{:S(2)}, u32[]{:S(2)}) %collective-permute-start.1) | collective-permute-done | bytes 65568 | tf_op jit(solution)/shard_map/ppermute | solution.py:211
  34.6 5.6 %collective-permute-start.3 = (bf16[512,256]{1,0:T(8,128)(2,1)}, bf16[512,256]{1,0:T(8,128)(2,1)S(1)}, u32[]{:S(2)}, u32[]{:S(2)}) collective-permute-start(bf16[512,256]{1,0:T(8,128)(2,1)} %join.1.refs_1_), channel_id=1, source_target_pairs={{0,28},{4,0},{8,4},{12,8},{16,12},{20,16},{24,20},{28,24},{1,29},{... | collective-permute-start | bytes 786440 | tf_op jit(solution)/shard_map/ppermute | solution.py:211
  40.2 5.4 %collective-permute-done.3.refs_1_ = bf16[512,256]{1,0:T(8,128)(2,1)S(1)} collective-permute-done((bf16[512,256]{1,0:T(8,128)(2,1)}, bf16[512,256]{1,0:T(8,128)(2,1)S(1)}, u32[]{:S(2)}, u32[]{:S(2)}) %collective-permute-start.3) | collective-permute-done | bytes 262176 | tf_op jit(solution)/shard_map/ppermute | solution.py:211
  45.5 3.3 %collective-permute-start.5 = (bf16[512,256]{1,0:T(8,128)(2,1)S(1)}, bf16[512,256]{1,0:T(8,128)(2,1)S(1)}, u32[]{:S(2)}, u32[]{:S(2)}) collective-permute-start(bf16[512,256]{1,0:T(8,128)(2,1)S(1)} %collective-permute-done.3.refs_1_), channel_id=1, source_target_pairs={{0,28},{4,0},{8,4},{12,8},{16,12},{20,16},{24,20},{28,24},{1,29},{... | collective-permute-start | bytes 786440 | tf_op jit(solution)/shard_map/ppermute | solution.py:211
  48.8 4.1 %collective-permute-done.5.refs_1_ = bf16[512,256]{1,0:T(8,128)(2,1)S(1)} collective-permute-done((bf16[512,256]{1,0:T(8,128)(2,1)S(1)}, bf16[512,256]{1,0:T(8,128)(2,1)S(1)}, u32[]{:S(2)}, u32[]{:S(2)}) %collective-permute-start.5) | collective-permute-done | bytes 262176 | tf_op jit(solution)/shard_map/ppermute | solution.py:211
  52.9 3.4 %collective-permute-start.7 = (bf16[512,256]{1,0:T(8,128)(2,1)S(1)}, bf16[512,256]{1,0:T(8,128)(2,1)S(1)}, u32[]{:S(2)}, u32[]{:S(2)}) collective-permute-start(bf16[512,256]{1,0:T(8,128)(2,1)S(1)} %collective-permute-done.5.refs_1_), channel_id=1, source_target_pairs={{0,28},{4,0},{8,4},{12,8},{16,12},{20,16},{24,20},{28,24},{1,29},{... | collective-permute-start | bytes 786440 | tf_op jit(solution)/shard_map/ppermute | solution.py:211
  57.3 3.0 %tile.5 = (f32[8,128,256]{2,1,0:T(8,128)S(1)}, f32[512,256]{1,0:T(8,128)S(1)}) custom-call(bf16[8,288,256]{2,1,0:T(8,128)(2,1)S(1)} %all-to-all-done.refs_0_, bf16[512,256]{1,0:T(8,128)(2,1)S(1)} %copy-done.2), custom_call_target="tpu_custom_call" | custom-call | flops 2684354560 | bytes 8388608 | tf_op jit(solution)/shard_map/tile/pallas_call | solution.py:190
  65.2 2.1 %collective-permute-start.10 = (bf16[256,256]{1,0:T(8,128)(2,1)}, bf16[256,256]{1,0:T(8,128)(2,1)S(1)}, u32[]{:S(2)}, u32[]{:S(2)}) collective-permute-start(bf16[256,256]{1,0:T(8,128)(2,1)} %get-tuple-element.28), channel_id=1, source_target_pairs={{0,28},{4,0},{8,4},{12,8},{16,12},{20,16},{24,20},{28,24},{1,29},{... | collective-permute-start | bytes 393224 | tf_op jit(solution)/shard_map/ppermute | solution.py:211
  67.4 2.3 %collective-permute-done.10 = bf16[256,256]{1,0:T(8,128)(2,1)S(1)} collective-permute-done((bf16[256,256]{1,0:T(8,128)(2,1)}, bf16[256,256]{1,0:T(8,128)(2,1)S(1)}, u32[]{:S(2)}, u32[]{:S(2)}) %collective-permute-start.10) | collective-permute-done | bytes 131104 | tf_op jit(solution)/shard_map/ppermute | solution.py:211
  69.6 3.0 %collective-permute-done.9 = bf16[256,256]{1,0:T(8,128)(2,1)S(1)} collective-permute-done((bf16[256,256]{1,0:T(8,128)(2,1)}, bf16[256,256]{1,0:T(8,128)(2,1)S(1)}, u32[]{:S(2)}, u32[]{:S(2)}) %collective-permute-start.9) | collective-permute-done | bytes 131104 | tf_op jit(solution)/shard_map/ppermute | solution.py:211
  73.9 3.0 %tile.6 = (f32[8,128,256]{2,1,0:T(8,128)S(1)}, f32[512,256]{1,0:T(8,128)S(1)}) custom-call(bf16[8,288,256]{2,1,0:T(8,128)(2,1)S(1)} %all-to-all-done.refs_0_, bf16[512,256]{1,0:T(8,128)(2,1)S(1)} %pad_maximum_fusion.refs_1_.refs_3_, f32[8,128,256]{2,1,0:T(8,128)S(1)} %copy-done.8, bf16[512,256]{1,0:T(8,128)(2,1)S(1)} %pad_maximum_fusion.refs_1_.refs_3_), custom_call_target="tpu_custom_call" | custom-call | flops 2684354560 | bytes 8388608 | tf_op jit(solution)/shard_map/tile/pallas_call | solution.py:190
  77.3 5.9 %tile.7 = (f32[8,128,256]{2,1,0:T(8,128)S(1)}, f32[512,256]{1,0:T(8,128)S(1)}, f32[512,256]{1,0:T(8,128)S(1)}) custom-call(bf16[8,288,256]{2,1,0:T(8,128)(2,1)S(1)} %all-to-all-done.refs_0_, bf16[512,256]{1,0:T(8,128)(2,1)S(1)} %copy-done.4, bf16[512,256]{1,0:T(8,128)(2,1)S(1)} %copy-done.6, f32[8,128,256]{2,1,0:T(8,128)S(1)} %get-tuple-element.30.refs_3_, ...), custom_call_target="tpu_custom_call" | custom-call | flops 5368709120 | bytes 8388608 | tf_op jit(solution)/shard_map/tile/pallas_call | solution.py:190
  83.2 2.7 %collective-permute-start.15 = (bf16[512,256]{1,0:T(8,128)(2,1)S(1)}, bf16[512,256]{1,0:T(8,128)(2,1)S(1)}, u32[]{:S(2)}, u32[]{:S(2)}) collective-permute-start(bf16[512,256]{1,0:T(8,128)(2,1)S(1)} %convert_element_type.59), channel_id=1, source_target_pairs={{0,28},{4,0},{8,4},{12,8},{16,12},{20,16},{24,20},{28,24},{1,29},{... | collective-permute-start | bytes 786440 | tf_op jit(solution)/shard_map/ppermute | solution.py:211
  86.1 5.9 %tile.8 = (f32[8,128,256]{2,1,0:T(8,128)S(1)}, f32[512,256]{1,0:T(8,128)S(1)}, f32[512,256]{1,0:T(8,128)S(1)}) custom-call(bf16[8,288,256]{2,1,0:T(8,128)(2,1)S(1)} %all-to-all-done.refs_0_, bf16[512,256]{1,0:T(8,128)(2,1)S(1)} %collective-permute-done.5.refs_1_, bf16[512,256]{1,0:T(8,128)(2,1)S(1)} %collective-permute-done.6.refs_2_, ...), custom_call_target="tpu_custom_call" | custom-call | flops 5368709120 | bytes 8388608 | tf_op jit(solution)/shard_map/tile/pallas_call | solution.py:190
  92.1 2.7 %collective-permute-start.16 = (bf16[512,256]{1,0:T(8,128)(2,1)S(1)}, bf16[512,256]{1,0:T(8,128)(2,1)S(1)}, u32[]{:S(2)}, u32[]{:S(2)}) collective-permute-start(bf16[512,256]{1,0:T(8,128)(2,1)S(1)} %add_convert_fusion.1), channel_id=1, source_target_pairs={{0,28},{4,0},{8,4},{12,8},{16,12},{20,16},{24,20},{28,24},{1,29},{... | collective-permute-start | bytes 786440 | tf_op jit(solution)/shard_map/ppermute | solution.py:211
  95.0 6.7 %tile.9 = (bf16[8,128,256]{2,1,0:T(8,128)(2,1)}, f32[512,256]{1,0:T(8,128)S(1)}, f32[512,256]{1,0:T(8,128)S(1)}) custom-call(bf16[8,288,256]{2,1,0:T(8,128)(2,1)S(1)} %all-to-all-done.refs_0_, bf16[512,256]{1,0:T(8,128)(2,1)S(1)} %collective-permute-done.3.refs_1_, bf16[512,256]{1,0:T(8,128)(2,1)S(1)} %collective-permute-done.4.refs_2_, ...), custom_call_target="tpu_custom_call" | custom-call | flops 5368709120 | bytes 8388608 | tf_op jit(solution)/shard_map/tile/pallas_call | solution.py:190
  101.7 2.9 %collective-permute-start.17 = (bf16[512,256]{1,0:T(8,128)(2,1)S(1)}, bf16[512,256]{1,0:T(8,128)(2,1)S(1)}, u32[]{:S(2)}, u32[]{:S(2)}) collective-permute-start(bf16[512,256]{1,0:T(8,128)(2,1)S(1)} %add_convert_fusion), channel_id=1, source_target_pairs={{0,28},{4,0},{8,4},{12,8},{16,12},{20,16},{24,20},{28,24},{1,29},{... | collective-permute-start | bytes 786440 | tf_op jit(solution)/shard_map/ppermute | solution.py:211
  104.8 4.8 %all-to-all-start.1 = ((bf16[8,128,256]{2,1,0:T(8,128)(2,1)}), bf16[8,128,256]{2,1,0:T(8,128)(2,1)S(1)}, u32[]{:S(2)}, u32[]{:S(2)}) async-start(bf16[8,128,256]{2,1,0:T(8,128)(2,1)} %get-tuple-element.36), calls=%async_computation.1 | async-start | bytes 1048576 | tf_op jit(solution)/shard_map/all_to_all | solution.py:257
  112.9 4.2 %all-to-all-done.1 = bf16[8,128,256]{2,1,0:T(8,128)(2,1)S(1)} async-done(((bf16[8,128,256]{2,1,0:T(8,128)(2,1)}), bf16[8,128,256]{2,1,0:T(8,128)(2,1)S(1)}, u32[]{:S(2)}, u32[]{:S(2)}) %all-to-all-start.1) | async-done | bytes 524320 | tf_op jit(solution)/shard_map/all_to_all | solution.py:257
  117.4 7.9 %collective-permute-start.19 = (bf16[3,128,128]{2,1,0:T(8,128)(2,1)S(1)}, bf16[3,128,128]{2,1,0:T(8,128)(2,1)S(1)}, u32[]{:S(2)}, u32[]{:S(2)}) collective-permute-start(bf16[3,128,128]{2,1,0:T(8,128)(2,1)S(1)} %slice.44), channel_id=1, source_target_pairs={{0,1},{1,0},{2,3},{3,2},{4,5},{5,4},{6,7},{7,6},{8,9},{9,8},{10,11... | collective-permute-start | bytes 294920 | tf_op jit(solution)/shard_map/ppermute | solution.py:211
  (75 shorter events, 22.4 us)
Async XLA Ops:
  2.4 4.4 %collective-permute-start = (bf16[272,256]{1,0:T(8,128)(2,1)}, bf16[272,256]{1,0:T(8,128)(2,1)S(1)}, u32[]{:S(2)}, u32[]{:S(2)}) collective-permute-start(bf16[272,256]{1,0:T(8,128)(2,1)} %get-tuple-element.23), channel_id=1, source_target_pairs={{0,1},{1,0},{2,3},{3,2},{4,5},{5,4},{6,7},{7,6},{8,9},{9,8},{10,11... | collective-permute-start | bytes 417800 | tf_op jit(solution)/shard_map/ppermute | solution.py:211
  9.6 6.1 %copy-start.13 = (bf16[128,256]{1,0:T(8,128)(2,1)S(1)}, bf16[128,256]{1,0:T(8,128)(2,1)}, u32[]{:S(2)}) copy-start(bf16[128,256]{1,0:T(8,128)(2,1)} %get-tuple-element.25) | copy-start | bytes 196612
  9.6 46.8 %all-to-all-start = ((bf16[8,288,256]{2,1,0:T(8,128)(2,1)}), bf16[8,288,256]{2,1,0:T(8,128)(2,1)S(1)}, u32[]{:S(2)}, u32[]{:S(2)}) async-start(bf16[8,288,256]{2,1,0:T(8,128)(2,1)} %spread.1._), calls=%async_computation | async-start | bytes 2359296 | tf_op jit(solution)/shard_map/all_to_all | solution.py:228
  13.3 17.0 %collective-permute-start.1 = (bf16[128,256]{1,0:T(8,128)(2,1)S(1)}, bf16[128,256]{1,0:T(8,128)(2,1)S(1)}, u32[]{:S(2)}, u32[]{:S(2)}) collective-permute-start(bf16[128,256]{1,0:T(8,128)(2,1)S(1)} %copy-done.10), channel_id=1, source_target_pairs={{0,32},{32,0},{1,33},{33,1},{2,34},{34,2},{3,35},{35,3},{4,36},{36... | collective-permute-start | bytes 196616 | tf_op jit(solution)/shard_map/ppermute | solution.py:211
  15.7 16.6 %collective-permute-start.2 = (bf16[128,256]{1,0:T(8,128)(2,1)S(1)}, bf16[128,256]{1,0:T(8,128)(2,1)S(1)}, u32[]{:S(2)}, u32[]{:S(2)}) collective-permute-start(bf16[128,256]{1,0:T(8,128)(2,1)S(1)} %copy-done.13), channel_id=1, source_target_pairs={{0,33},{1,32},{32,1},{33,0},{2,35},{3,34},{34,3},{35,2},{4,37},{5,... | collective-permute-start | bytes 196616 | tf_op jit(solution)/shard_map/ppermute | solution.py:222
  34.6 10.9 %collective-permute-start.3 = (bf16[512,256]{1,0:T(8,128)(2,1)}, bf16[512,256]{1,0:T(8,128)(2,1)S(1)}, u32[]{:S(2)}, u32[]{:S(2)}) collective-permute-start(bf16[512,256]{1,0:T(8,128)(2,1)} %join.1.refs_1_), channel_id=1, source_target_pairs={{0,28},{4,0},{8,4},{12,8},{16,12},{20,16},{24,20},{28,24},{1,29},{... | collective-permute-start | bytes 786440 | tf_op jit(solution)/shard_map/ppermute | solution.py:211
  40.2 8.7 %collective-permute-start.4 = (bf16[512,256]{1,0:T(8,128)(2,1)}, bf16[512,256]{1,0:T(8,128)(2,1)S(1)}, u32[]{:S(2)}, u32[]{:S(2)}) collective-permute-start(bf16[512,256]{1,0:T(8,128)(2,1)} %join.1.refs_1_), channel_id=1, source_target_pairs={{0,4},{4,8},{8,12},{12,16},{16,20},{20,24},{24,28},{28,0},{1,5},{5... | collective-permute-start | bytes 786440 | tf_op jit(solution)/shard_map/ppermute | solution.py:211
  45.5 7.4 %collective-permute-start.5 = (bf16[512,256]{1,0:T(8,128)(2,1)S(1)}, bf16[512,256]{1,0:T(8,128)(2,1)S(1)}, u32[]{:S(2)}, u32[]{:S(2)}) collective-permute-start(bf16[512,256]{1,0:T(8,128)(2,1)S(1)} %collective-permute-done.3.refs_1_), channel_id=1, source_target_pairs={{0,28},{4,0},{8,4},{12,8},{16,12},{20,16},{24,20},{28,24},{1,29},{... | collective-permute-start | bytes 786440 | tf_op jit(solution)/shard_map/ppermute | solution.py:211
  48.8 7.5 %collective-permute-start.6 = (bf16[512,256]{1,0:T(8,128)(2,1)S(1)}, bf16[512,256]{1,0:T(8,128)(2,1)S(1)}, u32[]{:S(2)}, u32[]{:S(2)}) collective-permute-start(bf16[512,256]{1,0:T(8,128)(2,1)S(1)} %collective-permute-done.4.refs_2_), channel_id=1, source_target_pairs={{0,4},{4,8},{8,12},{12,16},{16,20},{20,24},{24,28},{28,0},{1,5},{5... | collective-permute-start | bytes 786440 | tf_op jit(solution)/shard_map/ppermute | solution.py:211
  52.9 9.2 %collective-permute-start.7 = (bf16[512,256]{1,0:T(8,128)(2,1)S(1)}, bf16[512,256]{1,0:T(8,128)(2,1)S(1)}, u32[]{:S(2)}, u32[]{:S(2)}) collective-permute-start(bf16[512,256]{1,0:T(8,128)(2,1)S(1)} %collective-permute-done.5.refs_1_), channel_id=1, source_target_pairs={{0,28},{4,0},{8,4},{12,8},{16,12},{20,16},{24,20},{28,24},{1,29},{... | collective-permute-start | bytes 786440 | tf_op jit(solution)/shard_map/ppermute | solution.py:211
  56.4 6.4 %collective-permute-start.8 = (bf16[512,256]{1,0:T(8,128)(2,1)S(1)}, bf16[512,256]{1,0:T(8,128)(2,1)S(1)}, u32[]{:S(2)}, u32[]{:S(2)}) collective-permute-start(bf16[512,256]{1,0:T(8,128)(2,1)S(1)} %collective-permute-done.6.refs_2_), channel_id=1, source_target_pairs={{0,4},{4,8},{8,12},{12,16},{16,20},{20,24},{24,28},{28,0},{1,5},{5... | collective-permute-start | bytes 786440 | tf_op jit(solution)/shard_map/ppermute | solution.py:211
  65.2 4.4 %collective-permute-start.10 = (bf16[256,256]{1,0:T(8,128)(2,1)}, bf16[256,256]{1,0:T(8,128)(2,1)S(1)}, u32[]{:S(2)}, u32[]{:S(2)}) collective-permute-start(bf16[256,256]{1,0:T(8,128)(2,1)} %get-tuple-element.28), channel_id=1, source_target_pairs={{0,28},{4,0},{8,4},{12,8},{16,12},{20,16},{24,20},{28,24},{1,29},{... | collective-permute-start | bytes 393224 | tf_op jit(solution)/shard_map/ppermute | solution.py:211
  67.4 5.2 %collective-permute-start.9 = (bf16[256,256]{1,0:T(8,128)(2,1)}, bf16[256,256]{1,0:T(8,128)(2,1)S(1)}, u32[]{:S(2)}, u32[]{:S(2)}) collective-permute-start(bf16[256,256]{1,0:T(8,128)(2,1)} %get-tuple-element.27), channel_id=1, source_target_pairs={{0,4},{4,8},{8,12},{12,16},{16,20},{20,24},{24,28},{28,0},{1,5},{5... | collective-permute-start | bytes 393224 | tf_op jit(solution)/shard_map/ppermute | solution.py:211
  77.0 9.0 %collective-permute-start.11 = (bf16[512,256]{1,0:T(8,128)(2,1)S(1)}, bf16[512,256]{1,0:T(8,128)(2,1)S(1)}, u32[]{:S(2)}, u32[]{:S(2)}) collective-permute-start(bf16[512,256]{1,0:T(8,128)(2,1)S(1)} %convert_element_type.50.refs_4_), channel_id=1, source_target_pairs={{0,4},{4,8},{8,12},{12,16},{16,20},{20,24},{24,28},{28,0},{1,5},{5... | collective-permute-start | bytes 786440 | tf_op jit(solution)/shard_map/ppermute | solution.py:211
  83.2 8.8 %collective-permute-start.15 = (bf16[512,256]{1,0:T(8,128)(2,1)S(1)}, bf16[512,256]{1,0:T(8,128)(2,1)S(1)}, u32[]{:S(2)}, u32[]{:S(2)}) collective-permute-start(bf16[512,256]{1,0:T(8,128)(2,1)S(1)} %convert_element_type.59), channel_id=1, source_target_pairs={{0,28},{4,0},{8,4},{12,8},{16,12},{20,16},{24,20},{28,24},{1,29},{... | collective-permute-start | bytes 786440 | tf_op jit(solution)/shard_map/ppermute | solution.py:211
  86.0 8.8 %collective-permute-start.12 = (bf16[512,256]{1,0:T(8,128)(2,1)S(1)}, bf16[512,256]{1,0:T(8,128)(2,1)S(1)}, u32[]{:S(2)}, u32[]{:S(2)}) collective-permute-start(bf16[512,256]{1,0:T(8,128)(2,1)S(1)} %add_convert_fusion.4.refs_4_), channel_id=1, source_target_pairs={{0,4},{4,8},{8,12},{12,16},{16,20},{20,24},{24,28},{28,0},{1,5},{5... | collective-permute-start | bytes 786440 | tf_op jit(solution)/shard_map/ppermute | solution.py:211
  92.1 9.5 %collective-permute-start.16 = (bf16[512,256]{1,0:T(8,128)(2,1)S(1)}, bf16[512,256]{1,0:T(8,128)(2,1)S(1)}, u32[]{:S(2)}, u32[]{:S(2)}) collective-permute-start(bf16[512,256]{1,0:T(8,128)(2,1)S(1)} %add_convert_fusion.1), channel_id=1, source_target_pairs={{0,28},{4,0},{8,4},{12,8},{16,12},{20,16},{24,20},{28,24},{1,29},{... | collective-permute-start | bytes 786440 | tf_op jit(solution)/shard_map/ppermute | solution.py:211
  94.9 9.8 %collective-permute-start.13 = (bf16[512,256]{1,0:T(8,128)(2,1)S(1)}, bf16[512,256]{1,0:T(8,128)(2,1)S(1)}, u32[]{:S(2)}, u32[]{:S(2)}) collective-permute-start(bf16[512,256]{1,0:T(8,128)(2,1)S(1)} %add_convert_fusion.3.refs_4_), channel_id=1, source_target_pairs={{0,4},{4,8},{8,12},{12,16},{16,20},{20,24},{24,28},{28,0},{1,5},{5... | collective-permute-start | bytes 786440 | tf_op jit(solution)/shard_map/ppermute | solution.py:211
  101.7 9.5 %copy-start.1 = (f32[512,256]{1,0:T(8,128)S(1)}, f32[512,256]{1,0:T(8,128)}, u32[]{:S(2)}) copy-start(f32[512,256]{1,0:T(8,128)} %copy-done) | copy-start | bytes 1572868
  101.7 7.8 %collective-permute-start.17 = (bf16[512,256]{1,0:T(8,128)(2,1)S(1)}, bf16[512,256]{1,0:T(8,128)(2,1)S(1)}, u32[]{:S(2)}, u32[]{:S(2)}) collective-permute-start(bf16[512,256]{1,0:T(8,128)(2,1)S(1)} %add_convert_fusion), channel_id=1, source_target_pairs={{0,28},{4,0},{8,4},{12,8},{16,12},{20,16},{24,20},{28,24},{1,29},{... | collective-permute-start | bytes 786440 | tf_op jit(solution)/shard_map/ppermute | solution.py:211
  104.7 6.5 %collective-permute-start.14 = (bf16[512,256]{1,0:T(8,128)(2,1)S(1)}, bf16[512,256]{1,0:T(8,128)(2,1)S(1)}, u32[]{:S(2)}, u32[]{:S(2)}) collective-permute-start(bf16[512,256]{1,0:T(8,128)(2,1)S(1)} %add_convert_fusion.2), channel_id=1, source_target_pairs={{0,4},{4,8},{8,12},{12,16},{16,20},{20,24},{24,28},{28,0},{1,5},{5... | collective-permute-start | bytes 786440 | tf_op jit(solution)/shard_map/ppermute | solution.py:211
  104.8 12.3 %all-to-all-start.1 = ((bf16[8,128,256]{2,1,0:T(8,128)(2,1)}), bf16[8,128,256]{2,1,0:T(8,128)(2,1)S(1)}, u32[]{:S(2)}, u32[]{:S(2)}) async-start(bf16[8,128,256]{2,1,0:T(8,128)(2,1)} %get-tuple-element.36), calls=%async_computation.1 | async-start | bytes 1048576 | tf_op jit(solution)/shard_map/all_to_all | solution.py:257
  111.3 6.0 %collective-permute-start.18 = (bf16[256,256]{1,0:T(8,128)(2,1)S(1)}, bf16[256,256]{1,0:T(8,128)(2,1)S(1)}, u32[]{:S(2)}, u32[]{:S(2)}) collective-permute-start(bf16[256,256]{1,0:T(8,128)(2,1)S(1)} %slice.73), channel_id=1, source_target_pairs={{0,32},{32,0},{1,33},{33,1},{2,34},{34,2},{3,35},{35,3},{4,36},{36... | collective-permute-start | bytes 393224 | tf_op jit(solution)/shard_map/ppermute | solution.py:211
  117.4 8.8 %collective-permute-start.19 = (bf16[3,128,128]{2,1,0:T(8,128)(2,1)S(1)}, bf16[3,128,128]{2,1,0:T(8,128)(2,1)S(1)}, u32[]{:S(2)}, u32[]{:S(2)}) collective-permute-start(bf16[3,128,128]{2,1,0:T(8,128)(2,1)S(1)} %slice.44), channel_id=1, source_target_pairs={{0,1},{1,0},{2,3},{3,2},{4,5},{5,4},{6,7},{7,6},{8,9},{9,8},{10,11... | collective-permute-start | bytes 294920 | tf_op jit(solution)/shard_map/ppermute | solution.py:211
  (12 other events, 19.0 us)

commit v6 on v3

--- a/solution.py
+++ b/solution.py
@@ -28,7 +28,7 @@
     return jnp.concatenate([hi.astype(F32), mid.astype(F32), low.astype(F32)], axis=0)
 
 
-def pack_kernel(core_ref, q_ref, k_ref, v_ref, o_ref, g_ref, lse_ref, qg_ref, kv_ref, send_ref):
+def pack_kernel(core_ref, q_ref, k_ref, v_ref, o_ref, g_ref, lse_ref, qg_ref, kv_ref, send_ref, far_ref):
     def fill(head, qg, kv):
         cols = slice(head * HEAD, (head + 1) * HEAD)
         g = g_ref[:, cols]
@@ -51,6 +51,7 @@
         def _():
             fill(core, qg_ref, kv_ref)
             fill(1 - core, send_qg, send_kv)
+            far_ref[...] = send_kv[...]
 
 
 def pack_call(core, *args):
@@ -59,29 +60,30 @@
         pack_kernel,
         in_specs=[pl.BlockSpec(memory_space=pltpu.SMEM)]
         + [pl.BlockSpec(memory_space=pltpu.VMEM)] * 6,
-        out_specs=[pl.BlockSpec(memory_space=pltpu.VMEM)] * 3,
+        out_specs=[pl.BlockSpec(memory_space=pltpu.VMEM)] * 4,
         out_shape=[
             jax.ShapeDtypeStruct((HALF + STATS, width), BF16),
             jax.ShapeDtypeStruct((HALF, width), BF16),
             jax.ShapeDtypeStruct((2 * HALF + STATS, width), BF16),
+            jax.ShapeDtypeStruct((HALF, width), BF16),
         ],
         name="pack",
     )(core.reshape(1), *args)
 
 
-def spread_kernel(mine_ref, kv_ref, other_ref, out_ref, keys_ref):
+def spread_kernel(mine_ref, other_ref, across_ref, diagonal_ref, out_ref, keys_ref):
     rows = HALF + STATS
     for n in range(out_ref.shape[0]):
         out_ref[n, :rows, :] = mine_ref[...]
         out_ref[n, rows:, :] = other_ref[:rows, :]
-    keys_ref[:HALF, :] = kv_ref[...]
-    keys_ref[HALF:, :] = other_ref[rows:, :]
+    keys_ref[:HALF, :] = across_ref[...]
+    keys_ref[HALF:, :] = diagonal_ref[...]
 
 
 def spread_call(n, *args):
     return pl.pallas_call(
         spread_kernel,
-        in_specs=[pl.BlockSpec(memory_space=pltpu.VMEM)] * 3,
+        in_specs=[pl.BlockSpec(memory_space=pltpu.VMEM)] * 4,
         out_specs=[pl.BlockSpec(memory_space=pltpu.VMEM)] * 2,
         out_shape=[
             jax.ShapeDtypeStruct((n, 2 * (HALF + STATS), 2 * HEAD), BF16),
@@ -92,19 +94,24 @@
 
 
 def tile_kernel(first, chips, *refs):
-    if first:
-        qg_ref, kv1_ref, kv2_ref, dq_ref, d1_ref, d2_ref, acc_k, acc_v, kt_ref = refs
-    else:
-        qg_ref, kv1_ref, kv2_ref, old_ref, _, dq_ref, d1_ref, d2_ref, acc_k, acc_v, kt_ref = refs
+    refs = list(refs)
+    qg_ref = refs.pop(0)
+    blocks = [(refs.pop(0), refs.pop(0)) for _ in range(2)]
+    if not first:
+        old_ref = refs.pop(0)
+        refs.pop(0)
+    dq_ref, d1_ref, d2_ref, acc_k, acc_v, kt_ref = refs
     step = pl.program_id(0)
-    blocks = (kv1_ref, kv2_ref)
+
+    def part(block, cols):
+        return jnp.concatenate([ref[:, cols] for ref in block], axis=0)
 
     @pl.when(step == 0)
     def _():
         acc_k[...] = jnp.zeros_like(acc_k)
         acc_v[...] = jnp.zeros_like(acc_v)
-        for n, kv_ref in enumerate(blocks):
-            kt_ref[n] = kv_ref[:, :HEAD].astype(F32).T.astype(BF16)
+        for n, block in enumerate(blocks):
+            kt_ref[n] = part(block, slice(0, HEAD)).astype(F32).T.astype(BF16)
 
     for chip in range(chips):
         qs, gs, lses, deltas = [], [], [], []
@@ -120,10 +127,11 @@
         lse = jnp.concatenate(lses, axis=1)
         delta = jnp.concatenate(deltas, axis=1)
         total = None if first else old_ref[chip]
-        for n, kv_ref in enumerate(blocks):
-            s = lax.dot_general(kv_ref[:, :HEAD], q, NT, preferred_element_type=F32)
+        for n, block in enumerate(blocks):
+            k, v = part(block, slice(0, HEAD)), part(block, slice(HEAD, 2 * HEAD))
+            s = lax.dot_general(k, q, NT, preferred_element_type=F32)
             p = jnp.exp2(s * (SCALE * LOG2E) - lse)
-            dp = lax.dot_general(kv_ref[:, HEAD:], g, NT, preferred_element_type=F32)
+            dp = lax.dot_general(v, g, NT, preferred_element_type=F32)
             ds = (SCALE * p * (dp - delta)).astype(BF16)
             acc_v[n] += jnp.dot(p.astype(BF16), g, preferred_element_type=F32)
             acc_k[n] += jnp.dot(ds, q, preferred_element_type=F32)
@@ -138,21 +146,22 @@
             d_ref[:, HEAD:] = acc_v[n]
 
 
-def tile_call(qg, kv1, kv2, old, after, last):
+def tile_call(qg, pair1, pair2, old, after, last):
     first = old is None
     groups, rows, width = qg.shape
     chips = 4
     q_spec = pl.BlockSpec((chips, rows, width), lambda i: (i, 0, 0))
-    keys = kv1.shape[0]
-    kv_spec = pl.BlockSpec((keys, width), lambda i: (0, 0))
+    keys = 2 * ROWS
+    kv_spec = pl.BlockSpec((ROWS, width), lambda i: (0, 0))
+    sum_spec = pl.BlockSpec((keys, width), lambda i: (0, 0))
     dq_spec = pl.BlockSpec((chips, HEAD, ROWS), lambda i: (i, 0, 0))
     pairs = groups * ROWS * 2 * keys
     return pl.pallas_call(
         functools.partial(tile_kernel, first, chips),
         grid=(groups // chips,),
-        in_specs=[q_spec, kv_spec, kv_spec]
+        in_specs=[q_spec] + [kv_spec] * 4
         + ([] if first else [dq_spec, pl.BlockSpec(memory_space=pl.ANY)]),
-        out_specs=[dq_spec, kv_spec, kv_spec],
+        out_specs=[dq_spec, sum_spec, sum_spec],
         out_shape=[
             jax.ShapeDtypeStruct((groups, HEAD, ROWS), BF16 if last else F32),
             jax.ShapeDtypeStruct((keys, width), F32),
@@ -168,7 +177,7 @@
             flops=pairs * HEAD * 20, bytes_accessed=8 * 2**20, transcendentals=pairs
         ),
         name="tile",
-    )(*((qg, kv1, kv2) if first else (qg, kv1, kv2, old, after)))
+    )(*((qg, *pair1, *pair2) if first else (qg, *pair1, *pair2, old, after)))
 
 
 def shift(x, axis, by):
@@ -179,21 +188,24 @@
 def local(queries, key_rows, value_rows, attn_output, grad_output, row_lse):
     core = lax.axis_index("core")
     even = core == 0
-    mine_q, mine_kv, send = pack_call(
+    mine_q, mine_kv, send, far_kv = pack_call(
         core, queries, key_rows, value_rows, attn_output, grad_output, row_lse
     )
     other = shift(send, "core", 1)
+    corners = lax.axis_size("xh") * lax.axis_size("core")
+    across = shift(mine_kv, "xh", 1)
+    diagonal = lax.ppermute(
+        far_kv, ("xh", "core"), [(i, corners - 1 - i) for i in range(corners)]
+    )
+    near = jnp.concatenate([mine_kv, other[HALF + STATS :]], axis=0)
     peers = math.prod(lax.axis_size(a) for a in GROUP)
-    spread, key_pack = spread_call(peers, mine_q, mine_kv, other)
-    key_pair = jnp.concatenate([key_pack, shift(key_pack, "xh", 1)], axis=0)
+    spread, partner = spread_call(peers, mine_q, other, across, diagonal)
     gathered = lax.all_to_all(spread, GROUP, 0, 0, tiled=True)
-    keys = {0: key_pair}
+    keys = {0: [near, partner]}
     for by in (1, 2, 3):
-        keys[by] = shift(keys[by - 1], "z", 1)
-        keys[-by] = shift(keys[1 - by], "z", -1)
-    keys[4] = jnp.concatenate(
-        [shift(keys[3][:ROWS], "z", 1), shift(keys[-3][ROWS:], "z", -1)], axis=0
-    )
+        keys[by] = [shift(x, "z", 1) for x in keys[by - 1]]
+        keys[-by] = [shift(x, "z", -1) for x in keys[1 - by]]
+    keys[4] = [shift(keys[3][0], "z", 1), shift(keys[-3][1], "z", -1)]
 
     def low(x):
         return x.astype(BF16)

time: 101 us -> 107 us (1.059)
  starting transfers between devices: 46.3 us -> 57.1 us
  waiting for transfers between devices: 22.4 us -> 16.2 us
    ppermute x19 -> x25, starting transfers between devices: 36.2 us -> 45.5 us  [shift(): return lax.ppermute(x, axis, [(i, (i + by) % n) for i in range(n)])]
    ppermute x19 -> x25, waiting for transfers between devices: 19.3 us -> 10.1 us  [shift(): return lax.ppermute(x, axis, [(i, (i + by) % n) for i in range(n)])]
    ppermute x0 -> x1, starting transfers between devices: none -> 2.18 us  [local(): lax.ppermute(far_kv, ('xh', 'core'), [(i, corners - 1 - i) for i in range...]
    ppermute x0 -> x1, waiting for transfers between devices: none -> 1.63 us  [local(): lax.ppermute(far_kv, ('xh', 'core'), [(i, corners - 1 - i) for i in range...]
    all_to_all x1, waiting for transfers between devices: 3.15 us -> 4.44 us  [local(): returned = lax.all_to_all(total_q, GROUP, 0, 0, tiled=True)]
    unnamed x7 -> x14, local copies, waits for them, and re-layouts: 1.61 us -> 2.24 us
  transfers between devices with their start and end apart: 21 -> 28, of which waited for: 10 -> 9; matrix products, arithmetic and copies ran while one was open for 2% -> 1% of each run, Pallas kernels for 18% -> 24%
where the time goes in v6:
time: 107 us
  starting transfers between devices  57.1 us (53%)
  Pallas kernels  29.1 us (27%)
  waiting for transfers between devices  16.2 us (15%)
  local copies, waits for them, and re-layouts  2.39 us (2%)
  other arithmetic  1.25 us (1%)
    ppermute x25, starting transfers between devices, shift(): return lax.ppermute(x, axis, [(i, (i + by) % n) for i in range(n)])  45.5 us
    pallas_call x4, Pallas kernels, tile_call(): pl.pallas_call(functools.partial(tile_kernel, first, chips), grid=(groups...  25.2 us
    ppermute x25, waiting for transfers between devices, shift(): return lax.ppermute(x, axis, [(i, (i + by) % n) for i in range(n)])  10.1 us
    all_to_all x1, starting transfers between devices, local(): returned = lax.all_to_all(total_q, GROUP, 0, 0, tiled=True)  5.27 us
    all_to_all x1, waiting for transfers between devices, local(): returned = lax.all_to_all(total_q, GROUP, 0, 0, tiled=True)  4.44 us
    all_to_all x1, starting transfers between devices, local(): gathered = lax.all_to_all(spread, GROUP, 0, 0, tiled=True)  4.14 us
    unnamed x14, local copies, waits for them, and re-layouts  2.24 us
    ppermute x1, starting transfers between devices, local(): lax.ppermute(far_kv, ('xh', 'core'), [(i, corners - 1 - i) for i in range...  2.18 us
  transfers between devices with their start and end apart: 28, of which 9 were waited for; matrix products, arithmetic and copies ran while one was open for 1% of the time, Pallas kernels for 24%

profile of v6, /device:TPU:1, one launch (start us, length us, event | category | flops | bytes accessed | tf_op | source)
XLA Modules:
  0.0 107.0 jit_solution(16334209023996970784)
XLA Ops:
  2.4 3.2 %collective-permute-start = (bf16[272,256]{1,0:T(8,128)(2,1)}, bf16[272,256]{1,0:T(8,128)(2,1)S(1)}, u32[]{:S(2)}, u32[]{:S(2)}) collective-permute-start(bf16[272,256]{1,0:T(8,128)(2,1)} %get-tuple-element.22), channel_id=1, source_target_pairs={{0,1},{1,0},{2,3},{3,2},{4,5},{5,4},{6,7},{7,6},{8,9},{9,8},{10,11... | collective-permute-start | bytes 417800 | tf_op jit(solution)/shard_map/ppermute | solution.py:185
  6.7 2.2 %collective-permute-start.2 = (bf16[128,256]{1,0:T(8,128)(2,1)}, bf16[128,256]{1,0:T(8,128)(2,1)S(1)}, u32[]{:S(2)}, u32[]{:S(2)}) collective-permute-start(bf16[128,256]{1,0:T(8,128)(2,1)} %get-tuple-element.24), channel_id=1, source_target_pairs={{0,33},{1,32},{32,1},{33,0},{2,35},{3,34},{34,3},{35,2},{4,37},{5,... | collective-permute-start | bytes 196616 | tf_op jit(solution)/shard_map/ppermute | solution.py:197
  8.9 2.2 %collective-permute-done.1.across_ref = bf16[128,256]{1,0:T(8,128)(2,1)S(1)} collective-permute-done((bf16[128,256]{1,0:T(8,128)(2,1)}, bf16[128,256]{1,0:T(8,128)(2,1)S(1)}, u32[]{:S(2)}, u32[]{:S(2)}) %collective-permute-start.1) | collective-permute-done | bytes 65568 | tf_op jit(solution)/shard_map/ppermute | solution.py:185
  13.4 2.1 %spread.1 = (bf16[8,288,256]{2,1,0:T(8,128)(2,1)}, bf16[256,256]{1,0:T(8,128)(2,1)}) custom-call(bf16[144,256]{1,0:T(8,128)(2,1)} %get-tuple-element.21.mine_ref, bf16[272,256]{1,0:T(8,128)(2,1)} %copy-done.3, bf16[128,256]{1,0:T(8,128)(2,1)} %copy-done.5, bf16[128,256]{1,0:T(8,128)(2,1)} %copy-done.6), custom_call_target="tpu_custom_call" | custom-call | tf_op jit(solution)/shard_map/spread/pallas_call | solution.py:84
  15.5 4.1 %all-to-all-start = ((bf16[8,288,256]{2,1,0:T(8,128)(2,1)}), bf16[8,288,256]{2,1,0:T(8,128)(2,1)S(1)}, u32[]{:S(2)}, u32[]{:S(2)}) async-start(bf16[8,288,256]{2,1,0:T(8,128)(2,1)} %get-tuple-element.25), calls=%async_computation | async-start | bytes 2359296 | tf_op jit(solution)/shard_map/all_to_all | solution.py:203
  19.7 5.7 %collective-permute-start.4 = (bf16[256,256]{1,0:T(8,128)(2,1)S(1)}, bf16[256,256]{1,0:T(8,128)(2,1)S(1)}, u32[]{:S(2)}, u32[]{:S(2)}) collective-permute-start(bf16[256,256]{1,0:T(8,128)(2,1)S(1)} %copy-done), channel_id=1, source_target_pairs={{0,28},{4,0},{8,4},{12,8},{16,12},{20,16},{24,20},{28,24},{1,29},{... | collective-permute-start | bytes 393224 | tf_op jit(solution)/shard_map/ppermute | solution.py:185
  25.4 2.1 %collective-permute-done.4.refs_2_ = bf16[256,256]{1,0:T(8,128)(2,1)S(1)} collective-permute-done((bf16[256,256]{1,0:T(8,128)(2,1)S(1)}, bf16[256,256]{1,0:T(8,128)(2,1)S(1)}, u32[]{:S(2)}, u32[]{:S(2)}) %collective-permute-start.4) | collective-permute-done | bytes 131104 | tf_op jit(solution)/shard_map/ppermute | solution.py:185
  27.5 3.4 %collective-permute-start.8 = (bf16[256,256]{1,0:T(8,128)(2,1)S(1)}, bf16[256,256]{1,0:T(8,128)(2,1)S(1)}, u32[]{:S(2)}, u32[]{:S(2)}) collective-permute-start(bf16[256,256]{1,0:T(8,128)(2,1)S(1)} %collective-permute-done.4.refs_2_), channel_id=1, source_target_pairs={{0,28},{4,0},{8,4},{12,8},{16,12},{20,16},{24,20},{28,24},{1,29},{... | collective-permute-start | bytes 393224 | tf_op jit(solution)/shard_map/ppermute | solution.py:185
  30.9 2.7 %collective-permute-start.3 = (bf16[256,256]{1,0:T(8,128)(2,1)S(1)}, bf16[256,256]{1,0:T(8,128)(2,1)S(1)}, u32[]{:S(2)}, u32[]{:S(2)}) collective-permute-start(bf16[256,256]{1,0:T(8,128)(2,1)S(1)} %pad_maximum_fusion.1.refs_3_), channel_id=1, source_target_pairs={{0,28},{4,0},{8,4},{12,8},{16,12},{20,16},{24,20},{28,24},{1,29},{... | collective-permute-start | bytes 393224 | tf_op jit(solution)/shard_map/ppermute | solution.py:185
  33.6 2.6 %collective-permute-start.12 = (bf16[256,256]{1,0:T(8,128)(2,1)S(1)}, bf16[256,256]{1,0:T(8,128)(2,1)S(1)}, u32[]{:S(2)}, u32[]{:S(2)}) collective-permute-start(bf16[256,256]{1,0:T(8,128)(2,1)S(1)} %collective-permute-done.8.refs_2_), channel_id=1, source_target_pairs={{0,28},{4,0},{8,4},{12,8},{16,12},{20,16},{24,20},{28,24},{1,29},{... | collective-permute-start | bytes 393224 | tf_op jit(solution)/shard_map/ppermute | solution.py:185
  36.2 1.9 %collective-permute-done.6.refs_4_ = bf16[256,256]{1,0:T(8,128)(2,1)S(1)} collective-permute-done((bf16[256,256]{1,0:T(8,128)(2,1)S(1)}, bf16[256,256]{1,0:T(8,128)(2,1)S(1)}, u32[]{:S(2)}, u32[]{:S(2)}) %collective-permute-start.6) | collective-permute-done | bytes 131104 | tf_op jit(solution)/shard_map/ppermute | solution.py:185
  38.1 2.7 %collective-permute-start.7 = (bf16[256,256]{1,0:T(8,128)(2,1)S(1)}, bf16[256,256]{1,0:T(8,128)(2,1)S(1)}, u32[]{:S(2)}, u32[]{:S(2)}) collective-permute-start(bf16[256,256]{1,0:T(8,128)(2,1)S(1)} %collective-permute-done.3.refs_1_), channel_id=1, source_target_pairs={{0,28},{4,0},{8,4},{12,8},{16,12},{20,16},{24,20},{28,24},{1,29},{... | collective-permute-start | bytes 393224 | tf_op jit(solution)/shard_map/ppermute | solution.py:185
  40.8 2.1 %collective-permute-start.16 = (bf16[256,256]{1,0:T(8,128)(2,1)S(1)}, bf16[256,256]{1,0:T(8,128)(2,1)S(1)}, u32[]{:S(2)}, u32[]{:S(2)}) collective-permute-start(bf16[256,256]{1,0:T(8,128)(2,1)S(1)} %collective-permute-done.12.refs_2_), channel_id=1, source_target_pairs={{0,28},{4,0},{8,4},{12,8},{16,12},{20,16},{24,20},{28,24},{1,29},{... | collective-permute-start | bytes 393224 | tf_op jit(solution)/shard_map/ppermute | solution.py:185
  43.1 3.1 %collective-permute-start.11 = (bf16[256,256]{1,0:T(8,128)(2,1)S(1)}, bf16[256,256]{1,0:T(8,128)(2,1)}, u32[]{:S(2)}, u32[]{:S(2)}) collective-permute-start(bf16[256,256]{1,0:T(8,128)(2,1)S(1)} %collective-permute-done.7.refs_1_), channel_id=1, source_target_pairs={{0,28},{4,0},{8,4},{12,8},{16,12},{20,16},{24,20},{28,24},{1,29},{... | collective-permute-start | bytes 393224 | tf_op jit(solution)/shard_map/ppermute | solution.py:185
  49.5 5.8 %tile.4 = (f32[8,128,256]{2,1,0:T(8,128)S(1)}, f32[512,256]{1,0:T(8,128)S(1)}, f32[512,256]{1,0:T(8,128)S(1)}) custom-call(bf16[8,288,256]{2,1,0:T(8,128)(2,1)S(1)} %all-to-all-done.refs_0_, bf16[256,256]{1,0:T(8,128)(2,1)S(1)} %copy-done.2, bf16[256,256]{1,0:T(8,128)(2,1)S(1)} %collective-permute-done.16.refs_2_, ...), custom_call_target="tpu_custom_call" | custom-call | flops 5368709120 | bytes 8388608 | tf_op jit(solution)/shard_map/tile/pallas_call | solution.py:159
  55.5 6.8 %tile.5 = (f32[8,128,256]{2,1,0:T(8,128)S(1)}, f32[512,256]{1,0:T(8,128)S(1)}, f32[512,256]{1,0:T(8,128)S(1)}) custom-call(bf16[8,288,256]{2,1,0:T(8,128)(2,1)S(1)} %all-to-all-done.refs_0_, bf16[256,256]{1,0:T(8,128)(2,1)} %collective-permute-done.11.refs_1_, bf16[256,256]{1,0:T(8,128)(2,1)S(1)} %collective-permute-done.12.refs_2_, ...), custom_call_target="tpu_custom_call" | custom-call | flops 5368709120 | bytes 8388608 | tf_op jit(solution)/shard_map/tile/pallas_call | solution.py:159
  62.4 2.7 %collective-permute-start.21 = (bf16[512,256]{1,0:T(8,128)(2,1)S(1)}, bf16[512,256]{1,0:T(8,128)(2,1)S(1)}, u32[]{:S(2)}, u32[]{:S(2)}) collective-permute-start(bf16[512,256]{1,0:T(8,128)(2,1)S(1)} %convert_element_type.59), channel_id=1, source_target_pairs={{0,28},{4,0},{8,4},{12,8},{16,12},{20,16},{24,20},{28,24},{1,29},{... | collective-permute-start | bytes 786440 | tf_op jit(solution)/shard_map/ppermute | solution.py:185
  65.2 5.9 %tile.6 = (f32[8,128,256]{2,1,0:T(8,128)S(1)}, f32[512,256]{1,0:T(8,128)S(1)}, f32[512,256]{1,0:T(8,128)S(1)}) custom-call(bf16[8,288,256]{2,1,0:T(8,128)(2,1)S(1)} %all-to-all-done.refs_0_, bf16[256,256]{1,0:T(8,128)(2,1)S(1)} %collective-permute-done.7.refs_1_, bf16[256,256]{1,0:T(8,128)(2,1)S(1)} %collective-permute-done.8.refs_2_, ...), custom_call_target="tpu_custom_call" | custom-call | flops 5368709120 | bytes 8388608 | tf_op jit(solution)/shard_map/tile/pallas_call | solution.py:159
  71.2 2.9 %collective-permute-start.22 = (bf16[512,256]{1,0:T(8,128)(2,1)S(1)}, bf16[512,256]{1,0:T(8,128)(2,1)S(1)}, u32[]{:S(2)}, u32[]{:S(2)}) collective-permute-start(bf16[512,256]{1,0:T(8,128)(2,1)S(1)} %add_convert_fusion.1), channel_id=1, source_target_pairs={{0,28},{4,0},{8,4},{12,8},{16,12},{20,16},{24,20},{28,24},{1,29},{... | collective-permute-start | bytes 786440 | tf_op jit(solution)/shard_map/ppermute | solution.py:185
  74.3 6.6 %tile.7 = (bf16[8,128,256]{2,1,0:T(8,128)(2,1)}, f32[512,256]{1,0:T(8,128)S(1)}, f32[512,256]{1,0:T(8,128)S(1)}) custom-call(bf16[8,288,256]{2,1,0:T(8,128)(2,1)S(1)} %all-to-all-done.refs_0_, bf16[256,256]{1,0:T(8,128)(2,1)S(1)} %collective-permute-done.3.refs_1_, bf16[256,256]{1,0:T(8,128)(2,1)S(1)} %collective-permute-done.4.refs_2_, ...), custom_call_target="tpu_custom_call" | custom-call | flops 5368709120 | bytes 8388608 | tf_op jit(solution)/shard_map/tile/pallas_call | solution.py:159
  81.0 2.7 %collective-permute-start.23 = (bf16[512,256]{1,0:T(8,128)(2,1)S(1)}, bf16[512,256]{1,0:T(8,128)(2,1)S(1)}, u32[]{:S(2)}, u32[]{:S(2)}) collective-permute-start(bf16[512,256]{1,0:T(8,128)(2,1)S(1)} %add_convert_fusion), channel_id=1, source_target_pairs={{0,28},{4,0},{8,4},{12,8},{16,12},{20,16},{24,20},{28,24},{1,29},{... | collective-permute-start | bytes 786440 | tf_op jit(solution)/shard_map/ppermute | solution.py:185
  83.9 5.3 %all-to-all-start.1 = ((bf16[8,128,256]{2,1,0:T(8,128)(2,1)}), bf16[8,128,256]{2,1,0:T(8,128)(2,1)S(1)}, u32[]{:S(2)}, u32[]{:S(2)}) async-start(bf16[8,128,256]{2,1,0:T(8,128)(2,1)} %get-tuple-element.33), calls=%async_computation.1 | async-start | bytes 1048576 | tf_op jit(solution)/shard_map/all_to_all | solution.py:226
  92.2 4.4 %all-to-all-done.1 = bf16[8,128,256]{2,1,0:T(8,128)(2,1)S(1)} async-done(((bf16[8,128,256]{2,1,0:T(8,128)(2,1)}), bf16[8,128,256]{2,1,0:T(8,128)(2,1)S(1)}, u32[]{:S(2)}, u32[]{:S(2)}) %all-to-all-start.1) | async-done | bytes 524320 | tf_op jit(solution)/shard_map/all_to_all | solution.py:226
  97.0 8.3 %collective-permute-start.25 = (bf16[3,128,128]{2,1,0:T(8,128)(2,1)S(1)}, bf16[3,128,128]{2,1,0:T(8,128)(2,1)S(1)}, u32[]{:S(2)}, u32[]{:S(2)}) collective-permute-start(bf16[3,128,128]{2,1,0:T(8,128)(2,1)S(1)} %slice.49), channel_id=1, source_target_pairs={{0,1},{1,0},{2,3},{3,2},{4,5},{5,4},{6,7},{7,6},{8,9},{9,8},{10,11... | collective-permute-start | bytes 294920 | tf_op jit(solution)/shard_map/ppermute | solution.py:185
  (72 shorter events, 14.4 us)
Async XLA Ops:
  2.4 10.3 %collective-permute-start = (bf16[272,256]{1,0:T(8,128)(2,1)}, bf16[272,256]{1,0:T(8,128)(2,1)S(1)}, u32[]{:S(2)}, u32[]{:S(2)}) collective-permute-start(bf16[272,256]{1,0:T(8,128)(2,1)} %get-tuple-element.22), channel_id=1, source_target_pairs={{0,1},{1,0},{2,3},{3,2},{4,5},{5,4},{6,7},{7,6},{8,9},{9,8},{10,11... | collective-permute-start | bytes 417800 | tf_op jit(solution)/shard_map/ppermute | solution.py:185
  5.7 5.4 %collective-permute-start.1 = (bf16[128,256]{1,0:T(8,128)(2,1)}, bf16[128,256]{1,0:T(8,128)(2,1)S(1)}, u32[]{:S(2)}, u32[]{:S(2)}) collective-permute-start(bf16[128,256]{1,0:T(8,128)(2,1)} %get-tuple-element.23), channel_id=1, source_target_pairs={{0,32},{32,0},{1,33},{33,1},{2,34},{34,2},{3,35},{35,3},{4,36},{36... | collective-permute-start | bytes 196616 | tf_op jit(solution)/shard_map/ppermute | solution.py:185
  6.7 6.0 %collective-permute-start.2 = (bf16[128,256]{1,0:T(8,128)(2,1)}, bf16[128,256]{1,0:T(8,128)(2,1)S(1)}, u32[]{:S(2)}, u32[]{:S(2)}) collective-permute-start(bf16[128,256]{1,0:T(8,128)(2,1)} %get-tuple-element.24), channel_id=1, source_target_pairs={{0,33},{1,32},{32,1},{33,0},{2,35},{3,34},{34,3},{35,2},{4,37},{5,... | collective-permute-start | bytes 196616 | tf_op jit(solution)/shard_map/ppermute | solution.py:197
  15.5 33.1 %all-to-all-start = ((bf16[8,288,256]{2,1,0:T(8,128)(2,1)}), bf16[8,288,256]{2,1,0:T(8,128)(2,1)S(1)}, u32[]{:S(2)}, u32[]{:S(2)}) async-start(bf16[8,288,256]{2,1,0:T(8,128)(2,1)} %get-tuple-element.25), calls=%async_computation | async-start | bytes 2359296 | tf_op jit(solution)/shard_map/all_to_all | solution.py:203
  19.7 7.8 %collective-permute-start.4 = (bf16[256,256]{1,0:T(8,128)(2,1)S(1)}, bf16[256,256]{1,0:T(8,128)(2,1)S(1)}, u32[]{:S(2)}, u32[]{:S(2)}) collective-permute-start(bf16[256,256]{1,0:T(8,128)(2,1)S(1)} %copy-done), channel_id=1, source_target_pairs={{0,28},{4,0},{8,4},{12,8},{16,12},{20,16},{24,20},{28,24},{1,29},{... | collective-permute-start | bytes 393224 | tf_op jit(solution)/shard_map/ppermute | solution.py:185
  25.3 5.6 %collective-permute-start.5 = (bf16[256,256]{1,0:T(8,128)(2,1)S(1)}, bf16[256,256]{1,0:T(8,128)(2,1)S(1)}, u32[]{:S(2)}, u32[]{:S(2)}) collective-permute-start(bf16[256,256]{1,0:T(8,128)(2,1)S(1)} %pad_maximum_fusion.1.refs_3_), channel_id=1, source_target_pairs={{0,4},{4,8},{8,12},{12,16},{16,20},{20,24},{24,28},{28,0},{1,5},{5... | collective-permute-start | bytes 393224 | tf_op jit(solution)/shard_map/ppermute | solution.py:185
  27.5 6.1 %collective-permute-start.8 = (bf16[256,256]{1,0:T(8,128)(2,1)S(1)}, bf16[256,256]{1,0:T(8,128)(2,1)S(1)}, u32[]{:S(2)}, u32[]{:S(2)}) collective-permute-start(bf16[256,256]{1,0:T(8,128)(2,1)S(1)} %collective-permute-done.4.refs_2_), channel_id=1, source_target_pairs={{0,28},{4,0},{8,4},{12,8},{16,12},{20,16},{24,20},{28,24},{1,29},{... | collective-permute-start | bytes 393224 | tf_op jit(solution)/shard_map/ppermute | solution.py:185
  30.9 7.2 %collective-permute-start.6 = (bf16[256,256]{1,0:T(8,128)(2,1)S(1)}, bf16[256,256]{1,0:T(8,128)(2,1)S(1)}, u32[]{:S(2)}, u32[]{:S(2)}) collective-permute-start(bf16[256,256]{1,0:T(8,128)(2,1)S(1)} %copy-done), channel_id=1, source_target_pairs={{0,4},{4,8},{8,12},{12,16},{16,20},{20,24},{24,28},{28,0},{1,5},{5... | collective-permute-start | bytes 393224 | tf_op jit(solution)/shard_map/ppermute | solution.py:185
  30.9 7.2 %collective-permute-start.3 = (bf16[256,256]{1,0:T(8,128)(2,1)S(1)}, bf16[256,256]{1,0:T(8,128)(2,1)S(1)}, u32[]{:S(2)}, u32[]{:S(2)}) collective-permute-start(bf16[256,256]{1,0:T(8,128)(2,1)S(1)} %pad_maximum_fusion.1.refs_3_), channel_id=1, source_target_pairs={{0,28},{4,0},{8,4},{12,8},{16,12},{20,16},{24,20},{28,24},{1,29},{... | collective-permute-start | bytes 393224 | tf_op jit(solution)/shard_map/ppermute | solution.py:185
  33.6 7.2 %collective-permute-start.12 = (bf16[256,256]{1,0:T(8,128)(2,1)S(1)}, bf16[256,256]{1,0:T(8,128)(2,1)S(1)}, u32[]{:S(2)}, u32[]{:S(2)}) collective-permute-start(bf16[256,256]{1,0:T(8,128)(2,1)S(1)} %collective-permute-done.8.refs_2_), channel_id=1, source_target_pairs={{0,28},{4,0},{8,4},{12,8},{16,12},{20,16},{24,20},{28,24},{1,29},{... | collective-permute-start | bytes 393224 | tf_op jit(solution)/shard_map/ppermute | solution.py:185
  36.2 6.7 %collective-permute-start.13 = (bf16[256,256]{1,0:T(8,128)(2,1)S(1)}, bf16[256,256]{1,0:T(8,128)(2,1)S(1)}, u32[]{:S(2)}, u32[]{:S(2)}) collective-permute-start(bf16[256,256]{1,0:T(8,128)(2,1)S(1)} %collective-permute-done.9.refs_3_), channel_id=1, source_target_pairs={{0,4},{4,8},{8,12},{12,16},{16,20},{20,24},{24,28},{28,0},{1,5},{5... | collective-permute-start | bytes 393224 | tf_op jit(solution)/shard_map/ppermute | solution.py:185
  40.8 5.5 %collective-permute-start.16 = (bf16[256,256]{1,0:T(8,128)(2,1)S(1)}, bf16[256,256]{1,0:T(8,128)(2,1)S(1)}, u32[]{:S(2)}, u32[]{:S(2)}) collective-permute-start(bf16[256,256]{1,0:T(8,128)(2,1)S(1)} %collective-permute-done.12.refs_2_), channel_id=1, source_target_pairs={{0,28},{4,0},{8,4},{12,8},{16,12},{20,16},{24,20},{28,24},{1,29},{... | collective-permute-start | bytes 393224 | tf_op jit(solution)/shard_map/ppermute | solution.py:185
  43.1 12.4 %collective-permute-start.14 = (bf16[256,256]{1,0:T(8,128)(2,1)S(1)}, bf16[256,256]{1,0:T(8,128)(2,1)S(1)}, u32[]{:S(2)}, u32[]{:S(2)}) collective-permute-start(bf16[256,256]{1,0:T(8,128)(2,1)S(1)} %collective-permute-done.10.refs_4_), channel_id=1, source_target_pairs={{0,4},{4,8},{8,12},{12,16},{16,20},{20,24},{24,28},{28,0},{1,5},{5... | collective-permute-start | bytes 393224 | tf_op jit(solution)/shard_map/ppermute | solution.py:185
  43.1 12.3 %collective-permute-start.11 = (bf16[256,256]{1,0:T(8,128)(2,1)S(1)}, bf16[256,256]{1,0:T(8,128)(2,1)}, u32[]{:S(2)}, u32[]{:S(2)}) collective-permute-start(bf16[256,256]{1,0:T(8,128)(2,1)S(1)} %collective-permute-done.7.refs_1_), channel_id=1, source_target_pairs={{0,28},{4,0},{8,4},{12,8},{16,12},{20,16},{24,20},{28,24},{1,29},{... | collective-permute-start | bytes 393224 | tf_op jit(solution)/shard_map/ppermute | solution.py:185
  55.4 9.7 %collective-permute-start.17 = (bf16[512,256]{1,0:T(8,128)(2,1)S(1)}, bf16[512,256]{1,0:T(8,128)(2,1)S(1)}, u32[]{:S(2)}, u32[]{:S(2)}) collective-permute-start(bf16[512,256]{1,0:T(8,128)(2,1)S(1)} %convert_element_type.50.refs_6_), channel_id=1, source_target_pairs={{0,4},{4,8},{8,12},{12,16},{16,20},{20,24},{24,28},{28,0},{1,5},{5... | collective-permute-start | bytes 786440 | tf_op jit(solution)/shard_map/ppermute | solution.py:185
  62.4 8.8 %collective-permute-start.21 = (bf16[512,256]{1,0:T(8,128)(2,1)S(1)}, bf16[512,256]{1,0:T(8,128)(2,1)S(1)}, u32[]{:S(2)}, u32[]{:S(2)}) collective-permute-start(bf16[512,256]{1,0:T(8,128)(2,1)S(1)} %convert_element_type.59), channel_id=1, source_target_pairs={{0,28},{4,0},{8,4},{12,8},{16,12},{20,16},{24,20},{28,24},{1,29},{... | collective-permute-start | bytes 786440 | tf_op jit(solution)/shard_map/ppermute | solution.py:185
  65.1 9.0 %collective-permute-start.18 = (bf16[512,256]{1,0:T(8,128)(2,1)S(1)}, bf16[512,256]{1,0:T(8,128)(2,1)S(1)}, u32[]{:S(2)}, u32[]{:S(2)}) collective-permute-start(bf16[512,256]{1,0:T(8,128)(2,1)S(1)} %add_convert_fusion.4.refs_6_), channel_id=1, source_target_pairs={{0,4},{4,8},{8,12},{12,16},{16,20},{20,24},{24,28},{28,0},{1,5},{5... | collective-permute-start | bytes 786440 | tf_op jit(solution)/shard_map/ppermute | solution.py:185
  71.2 9.7 %collective-permute-start.22 = (bf16[512,256]{1,0:T(8,128)(2,1)S(1)}, bf16[512,256]{1,0:T(8,128)(2,1)S(1)}, u32[]{:S(2)}, u32[]{:S(2)}) collective-permute-start(bf16[512,256]{1,0:T(8,128)(2,1)S(1)} %add_convert_fusion.1), channel_id=1, source_target_pairs={{0,28},{4,0},{8,4},{12,8},{16,12},{20,16},{24,20},{28,24},{1,29},{... | collective-permute-start | bytes 786440 | tf_op jit(solution)/shard_map/ppermute | solution.py:185
  74.2 9.5 %collective-permute-start.19 = (bf16[512,256]{1,0:T(8,128)(2,1)S(1)}, bf16[512,256]{1,0:T(8,128)(2,1)S(1)}, u32[]{:S(2)}, u32[]{:S(2)}) collective-permute-start(bf16[512,256]{1,0:T(8,128)(2,1)S(1)} %add_convert_fusion.3.refs_6_), channel_id=1, source_target_pairs={{0,4},{4,8},{8,12},{12,16},{16,20},{20,24},{24,28},{28,0},{1,5},{5... | collective-permute-start | bytes 786440 | tf_op jit(solution)/shard_map/ppermute | solution.py:185
  81.0 8.1 %collective-permute-start.23 = (bf16[512,256]{1,0:T(8,128)(2,1)S(1)}, bf16[512,256]{1,0:T(8,128)(2,1)S(1)}, u32[]{:S(2)}, u32[]{:S(2)}) collective-permute-start(bf16[512,256]{1,0:T(8,128)(2,1)S(1)} %add_convert_fusion), channel_id=1, source_target_pairs={{0,28},{4,0},{8,4},{12,8},{16,12},{20,16},{24,20},{28,24},{1,29},{... | collective-permute-start | bytes 786440 | tf_op jit(solution)/shard_map/ppermute | solution.py:185
  83.8 6.5 %collective-permute-start.20 = (bf16[512,256]{1,0:T(8,128)(2,1)S(1)}, bf16[512,256]{1,0:T(8,128)(2,1)S(1)}, u32[]{:S(2)}, u32[]{:S(2)}) collective-permute-start(bf16[512,256]{1,0:T(8,128)(2,1)S(1)} %add_convert_fusion.2), channel_id=1, source_target_pairs={{0,4},{4,8},{8,12},{12,16},{16,20},{20,24},{24,28},{28,0},{1,5},{5... | collective-permute-start | bytes 786440 | tf_op jit(solution)/shard_map/ppermute | solution.py:185
  83.9 12.8 %all-to-all-start.1 = ((bf16[8,128,256]{2,1,0:T(8,128)(2,1)}), bf16[8,128,256]{2,1,0:T(8,128)(2,1)S(1)}, u32[]{:S(2)}, u32[]{:S(2)}) async-start(bf16[8,128,256]{2,1,0:T(8,128)(2,1)} %get-tuple-element.33), calls=%async_computation.1 | async-start | bytes 1048576 | tf_op jit(solution)/shard_map/all_to_all | solution.py:226
  90.4 6.5 %collective-permute-start.24 = (bf16[256,256]{1,0:T(8,128)(2,1)S(1)}, bf16[256,256]{1,0:T(8,128)(2,1)S(1)}, u32[]{:S(2)}, u32[]{:S(2)}) collective-permute-start(bf16[256,256]{1,0:T(8,128)(2,1)S(1)} %slice.78), channel_id=1, source_target_pairs={{0,32},{32,0},{1,33},{33,1},{2,34},{34,2},{3,35},{35,3},{4,36},{36... | collective-permute-start | bytes 393224 | tf_op jit(solution)/shard_map/ppermute | solution.py:185
  97.0 9.3 %collective-permute-start.25 = (bf16[3,128,128]{2,1,0:T(8,128)(2,1)S(1)}, bf16[3,128,128]{2,1,0:T(8,128)(2,1)S(1)}, u32[]{:S(2)}, u32[]{:S(2)}) collective-permute-start(bf16[3,128,128]{2,1,0:T(8,128)(2,1)S(1)} %slice.49), channel_id=1, source_target_pairs={{0,1},{1,0},{2,3},{3,2},{4,5},{5,4},{6,7},{7,6},{8,9},{9,8},{10,11... | collective-permute-start | bytes 294920 | tf_op jit(solution)/shard_map/ppermute | solution.py:185
  (12 other events, 48.7 us)

commit v7 on v6

--- a/solution.py
+++ b/solution.py
@@ -71,24 +71,19 @@
     )(core.reshape(1), *args)
 
 
-def spread_kernel(mine_ref, other_ref, across_ref, diagonal_ref, out_ref, keys_ref):
+def spread_kernel(mine_ref, other_ref, _, out_ref):
     rows = HALF + STATS
     for n in range(out_ref.shape[0]):
         out_ref[n, :rows, :] = mine_ref[...]
         out_ref[n, rows:, :] = other_ref[:rows, :]
-    keys_ref[:HALF, :] = across_ref[...]
-    keys_ref[HALF:, :] = diagonal_ref[...]
 
 
 def spread_call(n, *args):
     return pl.pallas_call(
         spread_kernel,
-        in_specs=[pl.BlockSpec(memory_space=pltpu.VMEM)] * 4,
-        out_specs=[pl.BlockSpec(memory_space=pltpu.VMEM)] * 2,
-        out_shape=[
-            jax.ShapeDtypeStruct((n, 2 * (HALF + STATS), 2 * HEAD), BF16),
-            jax.ShapeDtypeStruct((ROWS, 2 * HEAD), BF16),
-        ],
+        in_specs=[pl.BlockSpec(memory_space=pltpu.VMEM)] * 3,
+        out_specs=pl.BlockSpec(memory_space=pltpu.VMEM),
+        out_shape=jax.ShapeDtypeStruct((n, 2 * (HALF + STATS), 2 * HEAD), BF16),
         name="spread",
     )(*args)
 
@@ -172,7 +167,7 @@
             pltpu.VMEM((2, keys, HEAD), F32),
             pltpu.VMEM((2, HEAD, keys), BF16),
         ],
-        compiler_params=pltpu.CompilerParams(vmem_limit_bytes=40 * 2**20),
+        compiler_params=pltpu.CompilerParams(vmem_limit_bytes=24 * 2**20),
         cost_estimate=pl.CostEstimate(
             flops=pairs * HEAD * 20, bytes_accessed=8 * 2**20, transcendentals=pairs
         ),
@@ -198,14 +193,15 @@
         far_kv, ("xh", "core"), [(i, corners - 1 - i) for i in range(corners)]
     )
     near = jnp.concatenate([mine_kv, other[HALF + STATS :]], axis=0)
-    peers = math.prod(lax.axis_size(a) for a in GROUP)
-    spread, partner = spread_call(peers, mine_q, other, across, diagonal)
-    gathered = lax.all_to_all(spread, GROUP, 0, 0, tiled=True)
+    partner = jnp.concatenate([across, diagonal], axis=0)
     keys = {0: [near, partner]}
     for by in (1, 2, 3):
         keys[by] = [shift(x, "z", 1) for x in keys[by - 1]]
         keys[-by] = [shift(x, "z", -1) for x in keys[1 - by]]
     keys[4] = [shift(keys[3][0], "z", 1), shift(keys[-3][1], "z", -1)]
+    peers = math.prod(lax.axis_size(a) for a in GROUP)
+    spread = spread_call(peers, mine_q, other, keys[1][0])
+    gathered = lax.all_to_all(spread, GROUP, 0, 0, tiled=True)
 
     def low(x):
         return x.astype(BF16)

time: 107 us -> 125 us (1.17)
  waiting for transfers between devices: 16.2 us -> 39 us
  starting transfers between devices: 57.1 us -> 51.2 us
    ppermute x25, waiting for transfers between devices: 10.1 us -> 32.5 us  [shift(): return lax.ppermute(x, axis, [(i, (i + by) % n) for i in range(n)])]
    ppermute x25, starting transfers between devices: 45.5 us -> 39.5 us  [shift(): return lax.ppermute(x, axis, [(i, (i + by) % n) for i in range(n)])]
  transfers between devices with their start and end apart: 28 -> 28, of which waited for: 9 -> 11; matrix products, arithmetic and copies ran while one was open for 1% -> 0% of each run, Pallas kernels for 24% -> 20%
where the time goes in v7:
time: 125 us
  starting transfers between devices  51.2 us (41%)
  waiting for transfers between devices  39 us (31%)
  Pallas kernels  29.1 us (23%)
  local copies, waits for them, and re-layouts  2.37 us (2%)
  other arithmetic  2.13 us (2%)
    ppermute x25, starting transfers between devices, shift(): return lax.ppermute(x, axis, [(i, (i + by) % n) for i in range(n)])  39.5 us
    ppermute x25, waiting for transfers between devices, shift(): return lax.ppermute(x, axis, [(i, (i + by) % n) for i in range(n)])  32.5 us
    pallas_call x4, Pallas kernels, tile_call(): pl.pallas_call(functools.partial(tile_kernel, first, chips), grid=(groups...  25.2 us
    all_to_all x1, starting transfers between devices, local(): gathered = lax.all_to_all(spread, GROUP, 0, 0, tiled=True)  5.25 us
    all_to_all x1, starting transfers between devices, local(): returned = lax.all_to_all(total_q, GROUP, 0, 0, tiled=True)  4.55 us
    all_to_all x1, waiting for transfers between devices, local(): returned = lax.all_to_all(total_q, GROUP, 0, 0, tiled=True)  3.97 us
  transfers between devices with their start and end apart: 28, of which 11 were waited for; matrix products, arithmetic and copies ran while one was open for 0% of the time, Pallas kernels for 20%

profile of v7, /device:TPU:1, one launch (start us, length us, event | category | flops | bytes accessed | tf_op | source)
XLA Modules:
  0.0 124.6 jit_solution(3217622548946495575)
XLA Ops:
  2.4 3.2 %collective-permute-start = (bf16[272,256]{1,0:T(8,128)(2,1)}, bf16[272,256]{1,0:T(8,128)(2,1)S(1)}, u32[]{:S(2)}, u32[]{:S(2)}) collective-permute-start(bf16[272,256]{1,0:T(8,128)(2,1)} %get-tuple-element.20), channel_id=1, source_target_pairs={{0,1},{1,0},{2,3},{3,2},{4,5},{5,4},{6,7},{7,6},{8,9},{9,8},{10,11... | collective-permute-start | bytes 417800 | tf_op jit(solution)/shard_map/ppermute | solution.py:180
  7.9 7.4 %collective-permute-done.1._.refs_3_ = bf16[256,256]{1,0:T(8,128)(2,1)S(1)} collective-permute-done((bf16[256,256]{1,0:T(8,128)(2,1)S(1)}, bf16[256,256]{1,0:T(8,128)(2,1)S(1)}, u32[]{:S(2)}, u32[]{:S(2)}) %collective-permute-start.1) | collective-permute-done | bytes 131104 | tf_op jit(solution)/shard_map/ppermute | solution.py:180
  15.9 2.1 %spread.1 = bf16[8,288,256]{2,1,0:T(8,128)(2,1)} custom-call(bf16[144,256]{1,0:T(8,128)(2,1)} %get-tuple-element.19.mine_ref, bf16[272,256]{1,0:T(8,128)(2,1)} %copy-done.4, bf16[256,256]{1,0:T(8,128)(2,1)} %copy-done), custom_call_target="tpu_custom_call" | custom-call | tf_op jit(solution)/shard_map/spread/pallas_call | solution.py:82
  18.1 5.2 %all-to-all-start = ((bf16[8,288,256]{2,1,0:T(8,128)(2,1)}), bf16[8,288,256]{2,1,0:T(8,128)(2,1)S(1)}, u32[]{:S(2)}, u32[]{:S(2)}) async-start(bf16[8,288,256]{2,1,0:T(8,128)(2,1)} %spread.1), calls=%async_computation | async-start | bytes 2359296 | tf_op jit(solution)/shard_map/all_to_all | solution.py:204
  23.3 2.5 %collective-permute-start.3 = (bf16[128,256]{1,0:T(8,128)(2,1)S(1)}, bf16[128,256]{1,0:T(8,128)(2,1)S(1)}, u32[]{:S(2)}, u32[]{:S(2)}) collective-permute-start(bf16[128,256]{1,0:T(8,128)(2,1)S(1)} %copy-done.5), channel_id=1, source_target_pairs={{0,32},{32,0},{1,33},{33,1},{2,34},{34,2},{3,35},{35,3},{4,36},{36... | collective-permute-start | bytes 196616 | tf_op jit(solution)/shard_map/ppermute | solution.py:180
  27.7 12.2 %collective-permute-done.3 = bf16[128,256]{1,0:T(8,128)(2,1)S(1)} collective-permute-done((bf16[128,256]{1,0:T(8,128)(2,1)S(1)}, bf16[128,256]{1,0:T(8,128)(2,1)S(1)}, u32[]{:S(2)}, u32[]{:S(2)}) %collective-permute-start.3) | collective-permute-done | bytes 65568 | tf_op jit(solution)/shard_map/ppermute | solution.py:180
  39.9 2.5 %collective-permute-done.4 = bf16[128,256]{1,0:T(8,128)(2,1)S(1)} collective-permute-done((bf16[128,256]{1,0:T(8,128)(2,1)S(1)}, bf16[128,256]{1,0:T(8,128)(2,1)S(1)}, u32[]{:S(2)}, u32[]{:S(2)}) %collective-permute-start.4) | collective-permute-done | bytes 65568 | tf_op jit(solution)/shard_map/ppermute | solution.py:192
  43.5 4.0 %collective-permute-done.5.refs_2_ = bf16[256,256]{1,0:T(8,128)(2,1)S(1)} collective-permute-done((bf16[256,256]{1,0:T(8,128)(2,1)S(1)}, bf16[256,256]{1,0:T(8,128)(2,1)S(1)}, u32[]{:S(2)}, u32[]{:S(2)}) %collective-permute-start.5) | collective-permute-done | bytes 131104 | tf_op jit(solution)/shard_map/ppermute | solution.py:180
  47.5 2.3 %collective-permute-start.8 = (bf16[256,256]{1,0:T(8,128)(2,1)S(1)}, bf16[256,256]{1,0:T(8,128)(2,1)S(1)}, u32[]{:S(2)}, u32[]{:S(2)}) collective-permute-start(bf16[256,256]{1,0:T(8,128)(2,1)S(1)} %collective-permute-done.5.refs_2_), channel_id=1, source_target_pairs={{0,28},{4,0},{8,4},{12,8},{16,12},{20,16},{24,20},{28,24},{1,29},{... | collective-permute-start | bytes 393224 | tf_op jit(solution)/shard_map/ppermute | solution.py:180
  49.8 2.7 %collective-permute-start.2 = (bf16[256,256]{1,0:T(8,128)(2,1)S(1)}, bf16[256,256]{1,0:T(8,128)(2,1)S(1)}, u32[]{:S(2)}, u32[]{:S(2)}) collective-permute-start(bf16[256,256]{1,0:T(8,128)(2,1)S(1)} %pad_maximum_fusion.1.refs_3_), channel_id=1, source_target_pairs={{0,28},{4,0},{8,4},{12,8},{16,12},{20,16},{24,20},{28,24},{1,29},{... | collective-permute-start | bytes 393224 | tf_op jit(solution)/shard_map/ppermute | solution.py:180
  52.5 2.6 %collective-permute-start.12 = (bf16[256,256]{1,0:T(8,128)(2,1)S(1)}, bf16[256,256]{1,0:T(8,128)(2,1)S(1)}, u32[]{:S(2)}, u32[]{:S(2)}) collective-permute-start(bf16[256,256]{1,0:T(8,128)(2,1)S(1)} %collective-permute-done.8.refs_2_), channel_id=1, source_target_pairs={{0,28},{4,0},{8,4},{12,8},{16,12},{20,16},{24,20},{28,24},{1,29},{... | collective-permute-start | bytes 393224 | tf_op jit(solution)/shard_map/ppermute | solution.py:180
  55.2 2.5 %collective-permute-done.6.refs_4_ = bf16[256,256]{1,0:T(8,128)(2,1)S(1)} collective-permute-done((bf16[256,256]{1,0:T(8,128)(2,1)S(1)}, bf16[256,256]{1,0:T(8,128)(2,1)S(1)}, u32[]{:S(2)}, u32[]{:S(2)}) %collective-permute-start.6) | collective-permute-done | bytes 131104 | tf_op jit(solution)/shard_map/ppermute | solution.py:180
  57.7 2.7 %collective-permute-start.7 = (bf16[256,256]{1,0:T(8,128)(2,1)S(1)}, bf16[256,256]{1,0:T(8,128)(2,1)S(1)}, u32[]{:S(2)}, u32[]{:S(2)}) collective-permute-start(bf16[256,256]{1,0:T(8,128)(2,1)S(1)} %collective-permute-done.2.refs_1_), channel_id=1, source_target_pairs={{0,28},{4,0},{8,4},{12,8},{16,12},{20,16},{24,20},{28,24},{1,29},{... | collective-permute-start | bytes 393224 | tf_op jit(solution)/shard_map/ppermute | solution.py:180
  63.3 2.7 %collective-permute-start.11 = (bf16[256,256]{1,0:T(8,128)(2,1)S(1)}, bf16[256,256]{1,0:T(8,128)(2,1)}, u32[]{:S(2)}, u32[]{:S(2)}) collective-permute-start(bf16[256,256]{1,0:T(8,128)(2,1)S(1)} %collective-permute-done.7.refs_1_), channel_id=1, source_target_pairs={{0,28},{4,0},{8,4},{12,8},{16,12},{20,16},{24,20},{28,24},{1,29},{... | collective-permute-start | bytes 393224 | tf_op jit(solution)/shard_map/ppermute | solution.py:180
  68.5 5.8 %tile.4 = (f32[8,128,256]{2,1,0:T(8,128)S(1)}, f32[512,256]{1,0:T(8,128)S(1)}, f32[512,256]{1,0:T(8,128)S(1)}) custom-call(bf16[8,288,256]{2,1,0:T(8,128)(2,1)S(1)} %all-to-all-done.refs_0_, bf16[256,256]{1,0:T(8,128)(2,1)S(1)} %copy-done.3, bf16[256,256]{1,0:T(8,128)(2,1)S(1)} %collective-permute-done.16.refs_2_, ...), custom_call_target="tpu_custom_call" | custom-call | flops 5368709120 | bytes 8388608 | tf_op jit(solution)/shard_map/tile/pallas_call | solution.py:154
  74.4 6.8 %tile.5 = (f32[8,128,256]{2,1,0:T(8,128)S(1)}, f32[512,256]{1,0:T(8,128)S(1)}, f32[512,256]{1,0:T(8,128)S(1)}) custom-call(bf16[8,288,256]{2,1,0:T(8,128)(2,1)S(1)} %all-to-all-done.refs_0_, bf16[256,256]{1,0:T(8,128)(2,1)} %collective-permute-done.11.refs_1_, bf16[256,256]{1,0:T(8,128)(2,1)S(1)} %collective-permute-done.12.refs_2_, ...), custom_call_target="tpu_custom_call" | custom-call | flops 5368709120 | bytes 8388608 | tf_op jit(solution)/shard_map/tile/pallas_call | solution.py:154
  81.3 2.7 %collective-permute-start.21 = (bf16[512,256]{1,0:T(8,128)(2,1)S(1)}, bf16[512,256]{1,0:T(8,128)(2,1)S(1)}, u32[]{:S(2)}, u32[]{:S(2)}) collective-permute-start(bf16[512,256]{1,0:T(8,128)(2,1)S(1)} %convert_element_type.59), channel_id=1, source_target_pairs={{0,28},{4,0},{8,4},{12,8},{16,12},{20,16},{24,20},{28,24},{1,29},{... | collective-permute-start | bytes 786440 | tf_op jit(solution)/shard_map/ppermute | solution.py:180
  84.2 5.9 %tile.6 = (f32[8,128,256]{2,1,0:T(8,128)S(1)}, f32[512,256]{1,0:T(8,128)S(1)}, f32[512,256]{1,0:T(8,128)S(1)}) custom-call(bf16[8,288,256]{2,1,0:T(8,128)(2,1)S(1)} %all-to-all-done.refs_0_, bf16[256,256]{1,0:T(8,128)(2,1)S(1)} %collective-permute-done.7.refs_1_, bf16[256,256]{1,0:T(8,128)(2,1)S(1)} %collective-permute-done.8.refs_2_, ...), custom_call_target="tpu_custom_call" | custom-call | flops 5368709120 | bytes 8388608 | tf_op jit(solution)/shard_map/tile/pallas_call | solution.py:154
  90.2 2.9 %collective-permute-start.22 = (bf16[512,256]{1,0:T(8,128)(2,1)S(1)}, bf16[512,256]{1,0:T(8,128)(2,1)S(1)}, u32[]{:S(2)}, u32[]{:S(2)}) collective-permute-start(bf16[512,256]{1,0:T(8,128)(2,1)S(1)} %add_convert_fusion.1), channel_id=1, source_target_pairs={{0,28},{4,0},{8,4},{12,8},{16,12},{20,16},{24,20},{28,24},{1,29},{... | collective-permute-start | bytes 786440 | tf_op jit(solution)/shard_map/ppermute | solution.py:180
  93.3 6.6 %tile.7 = (bf16[8,128,256]{2,1,0:T(8,128)(2,1)}, f32[512,256]{1,0:T(8,128)S(1)}, f32[512,256]{1,0:T(8,128)S(1)}) custom-call(bf16[8,288,256]{2,1,0:T(8,128)(2,1)S(1)} %all-to-all-done.refs_0_, bf16[256,256]{1,0:T(8,128)(2,1)S(1)} %collective-permute-done.2.refs_1_, bf16[256,256]{1,0:T(8,128)(2,1)S(1)} %collective-permute-done.5.refs_2_, ...), custom_call_target="tpu_custom_call" | custom-call | flops 5368709120 | bytes 8388608 | tf_op jit(solution)/shard_map/tile/pallas_call | solution.py:154
  99.9 2.7 %collective-permute-start.23 = (bf16[512,256]{1,0:T(8,128)(2,1)S(1)}, bf16[512,256]{1,0:T(8,128)(2,1)S(1)}, u32[]{:S(2)}, u32[]{:S(2)}) collective-permute-start(bf16[512,256]{1,0:T(8,128)(2,1)S(1)} %add_convert_fusion), channel_id=1, source_target_pairs={{0,28},{4,0},{8,4},{12,8},{16,12},{20,16},{24,20},{28,24},{1,29},{... | collective-permute-start | bytes 786440 | tf_op jit(solution)/shard_map/ppermute | solution.py:180
  102.8 4.5 %all-to-all-start.1 = ((bf16[8,128,256]{2,1,0:T(8,128)(2,1)}), bf16[8,128,256]{2,1,0:T(8,128)(2,1)S(1)}, u32[]{:S(2)}, u32[]{:S(2)}) async-start(bf16[8,128,256]{2,1,0:T(8,128)(2,1)} %get-tuple-element.29), calls=%async_computation.1 | async-start | bytes 1048576 | tf_op jit(solution)/shard_map/all_to_all | solution.py:222
  110.9 4.0 %all-to-all-done.1 = bf16[8,128,256]{2,1,0:T(8,128)(2,1)S(1)} async-done(((bf16[8,128,256]{2,1,0:T(8,128)(2,1)}), bf16[8,128,256]{2,1,0:T(8,128)(2,1)S(1)}, u32[]{:S(2)}, u32[]{:S(2)}) %all-to-all-start.1) | async-done | bytes 524320 | tf_op jit(solution)/shard_map/all_to_all | solution.py:222
  115.2 7.8 %collective-permute-start.25 = (bf16[3,128,128]{2,1,0:T(8,128)(2,1)S(1)}, bf16[3,128,128]{2,1,0:T(8,128)(2,1)S(1)}, u32[]{:S(2)}, u32[]{:S(2)}) collective-permute-start(bf16[3,128,128]{2,1,0:T(8,128)(2,1)S(1)} %slice.49), channel_id=1, source_target_pairs={{0,1},{1,0},{2,3},{3,2},{4,5},{5,4},{6,7},{7,6},{8,9},{9,8},{10,11... | collective-permute-start | bytes 294920 | tf_op jit(solution)/shard_map/ppermute | solution.py:180
  (73 shorter events, 19.2 us)
Async XLA Ops:
  7.8 7.5 %collective-permute-start.1 = (bf16[256,256]{1,0:T(8,128)(2,1)S(1)}, bf16[256,256]{1,0:T(8,128)(2,1)S(1)}, u32[]{:S(2)}, u32[]{:S(2)}) collective-permute-start(bf16[256,256]{1,0:T(8,128)(2,1)S(1)} %pad_maximum_fusion.1.refs_3_), channel_id=1, source_target_pairs={{0,4},{4,8},{8,12},{12,16},{16,20},{20,24},{24,28},{28,0},{1,5},{5... | collective-permute-start | bytes 393224 | tf_op jit(solution)/shard_map/ppermute | solution.py:180
  18.1 49.5 %all-to-all-start = ((bf16[8,288,256]{2,1,0:T(8,128)(2,1)}), bf16[8,288,256]{2,1,0:T(8,128)(2,1)S(1)}, u32[]{:S(2)}, u32[]{:S(2)}) async-start(bf16[8,288,256]{2,1,0:T(8,128)(2,1)} %spread.1), calls=%async_computation | async-start | bytes 2359296 | tf_op jit(solution)/shard_map/all_to_all | solution.py:204
  23.3 16.6 %collective-permute-start.3 = (bf16[128,256]{1,0:T(8,128)(2,1)S(1)}, bf16[128,256]{1,0:T(8,128)(2,1)S(1)}, u32[]{:S(2)}, u32[]{:S(2)}) collective-permute-start(bf16[128,256]{1,0:T(8,128)(2,1)S(1)} %copy-done.5), channel_id=1, source_target_pairs={{0,32},{32,0},{1,33},{33,1},{2,34},{34,2},{3,35},{35,3},{4,36},{36... | collective-permute-start | bytes 196616 | tf_op jit(solution)/shard_map/ppermute | solution.py:180
  25.9 16.6 %collective-permute-start.4 = (bf16[128,256]{1,0:T(8,128)(2,1)S(1)}, bf16[128,256]{1,0:T(8,128)(2,1)S(1)}, u32[]{:S(2)}, u32[]{:S(2)}) collective-permute-start(bf16[128,256]{1,0:T(8,128)(2,1)S(1)} %copy-done.6), channel_id=1, source_target_pairs={{0,33},{1,32},{32,1},{33,0},{2,35},{3,34},{34,3},{35,2},{4,37},{5,... | collective-permute-start | bytes 196616 | tf_op jit(solution)/shard_map/ppermute | solution.py:192
  49.8 7.9 %collective-permute-start.6 = (bf16[256,256]{1,0:T(8,128)(2,1)S(1)}, bf16[256,256]{1,0:T(8,128)(2,1)S(1)}, u32[]{:S(2)}, u32[]{:S(2)}) collective-permute-start(bf16[256,256]{1,0:T(8,128)(2,1)S(1)} %constant_dynamic-update-slice_fusion.refs_4_), channel_id=1, source_target_pairs={{0,4},{4,8},{8,12},{12,16},{16,20},{20,24},{24,28},{28,0},{1,5},{5... | collective-permute-start | bytes 393224 | tf_op jit(solution)/shard_map/ppermute | solution.py:180
  49.8 7.9 %collective-permute-start.2 = (bf16[256,256]{1,0:T(8,128)(2,1)S(1)}, bf16[256,256]{1,0:T(8,128)(2,1)S(1)}, u32[]{:S(2)}, u32[]{:S(2)}) collective-permute-start(bf16[256,256]{1,0:T(8,128)(2,1)S(1)} %pad_maximum_fusion.1.refs_3_), channel_id=1, source_target_pairs={{0,28},{4,0},{8,4},{12,8},{16,12},{20,16},{24,20},{28,24},{1,29},{... | collective-permute-start | bytes 393224 | tf_op jit(solution)/shard_map/ppermute | solution.py:180
  52.5 7.8 %collective-permute-start.12 = (bf16[256,256]{1,0:T(8,128)(2,1)S(1)}, bf16[256,256]{1,0:T(8,128)(2,1)S(1)}, u32[]{:S(2)}, u32[]{:S(2)}) collective-permute-start(bf16[256,256]{1,0:T(8,128)(2,1)S(1)} %collective-permute-done.8.refs_2_), channel_id=1, source_target_pairs={{0,28},{4,0},{8,4},{12,8},{16,12},{20,16},{24,20},{28,24},{1,29},{... | collective-permute-start | bytes 393224 | tf_op jit(solution)/shard_map/ppermute | solution.py:180
  55.2 5.7 %collective-permute-start.13 = (bf16[256,256]{1,0:T(8,128)(2,1)S(1)}, bf16[256,256]{1,0:T(8,128)(2,1)S(1)}, u32[]{:S(2)}, u32[]{:S(2)}) collective-permute-start(bf16[256,256]{1,0:T(8,128)(2,1)S(1)} %collective-permute-done.9.refs_3_), channel_id=1, source_target_pairs={{0,4},{4,8},{8,12},{12,16},{16,20},{20,24},{24,28},{28,0},{1,5},{5... | collective-permute-start | bytes 393224 | tf_op jit(solution)/shard_map/ppermute | solution.py:180
  57.7 5.6 %collective-permute-start.10 = (bf16[256,256]{1,0:T(8,128)(2,1)S(1)}, bf16[256,256]{1,0:T(8,128)(2,1)S(1)}, u32[]{:S(2)}, u32[]{:S(2)}) collective-permute-start(bf16[256,256]{1,0:T(8,128)(2,1)S(1)} %collective-permute-done.6.refs_4_), channel_id=1, source_target_pairs={{0,4},{4,8},{8,12},{12,16},{16,20},{20,24},{24,28},{28,0},{1,5},{5... | collective-permute-start | bytes 393224 | tf_op jit(solution)/shard_map/ppermute | solution.py:180
  57.7 5.6 %collective-permute-start.7 = (bf16[256,256]{1,0:T(8,128)(2,1)S(1)}, bf16[256,256]{1,0:T(8,128)(2,1)S(1)}, u32[]{:S(2)}, u32[]{:S(2)}) collective-permute-start(bf16[256,256]{1,0:T(8,128)(2,1)S(1)} %collective-permute-done.2.refs_1_), channel_id=1, source_target_pairs={{0,28},{4,0},{8,4},{12,8},{16,12},{20,16},{24,20},{28,24},{1,29},{... | collective-permute-start | bytes 393224 | tf_op jit(solution)/shard_map/ppermute | solution.py:180
  60.4 5.6 %collective-permute-start.16 = (bf16[256,256]{1,0:T(8,128)(2,1)S(1)}, bf16[256,256]{1,0:T(8,128)(2,1)S(1)}, u32[]{:S(2)}, u32[]{:S(2)}) collective-permute-start(bf16[256,256]{1,0:T(8,128)(2,1)S(1)} %collective-permute-done.12.refs_2_), channel_id=1, source_target_pairs={{0,28},{4,0},{8,4},{12,8},{16,12},{20,16},{24,20},{28,24},{1,29},{... | collective-permute-start | bytes 393224 | tf_op jit(solution)/shard_map/ppermute | solution.py:180
  60.8 6.1 %collective-permute-start.15 = (bf16[256,256]{1,0:T(8,128)(2,1)S(1)}, bf16[256,256]{1,0:T(8,128)(2,1)S(1)}, u32[]{:S(2)}, u32[]{:S(2)}) collective-permute-start(bf16[256,256]{1,0:T(8,128)(2,1)S(1)} %collective-permute-done.13.refs_3_), channel_id=1, source_target_pairs={{0,4},{4,8},{8,12},{12,16},{16,20},{20,24},{24,28},{28,0},{1,5},{5... | collective-permute-start | bytes 393224 | tf_op jit(solution)/shard_map/ppermute | solution.py:180
  63.3 11.2 %collective-permute-start.14 = (bf16[256,256]{1,0:T(8,128)(2,1)S(1)}, bf16[256,256]{1,0:T(8,128)(2,1)S(1)}, u32[]{:S(2)}, u32[]{:S(2)}) collective-permute-start(bf16[256,256]{1,0:T(8,128)(2,1)S(1)} %collective-permute-done.10.refs_4_), channel_id=1, source_target_pairs={{0,4},{4,8},{8,12},{12,16},{16,20},{20,24},{24,28},{28,0},{1,5},{5... | collective-permute-start | bytes 393224 | tf_op jit(solution)/shard_map/ppermute | solution.py:180
  63.3 11.2 %collective-permute-start.11 = (bf16[256,256]{1,0:T(8,128)(2,1)S(1)}, bf16[256,256]{1,0:T(8,128)(2,1)}, u32[]{:S(2)}, u32[]{:S(2)}) collective-permute-start(bf16[256,256]{1,0:T(8,128)(2,1)S(1)} %collective-permute-done.7.refs_1_), channel_id=1, source_target_pairs={{0,28},{4,0},{8,4},{12,8},{16,12},{20,16},{24,20},{28,24},{1,29},{... | collective-permute-start | bytes 393224 | tf_op jit(solution)/shard_map/ppermute | solution.py:180
  74.3 9.7 %collective-permute-start.17 = (bf16[512,256]{1,0:T(8,128)(2,1)S(1)}, bf16[512,256]{1,0:T(8,128)(2,1)S(1)}, u32[]{:S(2)}, u32[]{:S(2)}) collective-permute-start(bf16[512,256]{1,0:T(8,128)(2,1)S(1)} %convert_element_type.50.refs_6_), channel_id=1, source_target_pairs={{0,4},{4,8},{8,12},{12,16},{16,20},{20,24},{24,28},{28,0},{1,5},{5... | collective-permute-start | bytes 786440 | tf_op jit(solution)/shard_map/ppermute | solution.py:180
  81.3 8.8 %collective-permute-start.21 = (bf16[512,256]{1,0:T(8,128)(2,1)S(1)}, bf16[512,256]{1,0:T(8,128)(2,1)S(1)}, u32[]{:S(2)}, u32[]{:S(2)}) collective-permute-start(bf16[512,256]{1,0:T(8,128)(2,1)S(1)} %convert_element_type.59), channel_id=1, source_target_pairs={{0,28},{4,0},{8,4},{12,8},{16,12},{20,16},{24,20},{28,24},{1,29},{... | collective-permute-start | bytes 786440 | tf_op jit(solution)/shard_map/ppermute | solution.py:180
  84.1 9.0 %collective-permute-start.18 = (bf16[512,256]{1,0:T(8,128)(2,1)S(1)}, bf16[512,256]{1,0:T(8,128)(2,1)S(1)}, u32[]{:S(2)}, u32[]{:S(2)}) collective-permute-start(bf16[512,256]{1,0:T(8,128)(2,1)S(1)} %add_convert_fusion.4.refs_6_), channel_id=1, source_target_pairs={{0,4},{4,8},{8,12},{12,16},{16,20},{20,24},{24,28},{28,0},{1,5},{5... | collective-permute-start | bytes 786440 | tf_op jit(solution)/shard_map/ppermute | solution.py:180
  90.2 9.7 %collective-permute-start.22 = (bf16[512,256]{1,0:T(8,128)(2,1)S(1)}, bf16[512,256]{1,0:T(8,128)(2,1)S(1)}, u32[]{:S(2)}, u32[]{:S(2)}) collective-permute-start(bf16[512,256]{1,0:T(8,128)(2,1)S(1)} %add_convert_fusion.1), channel_id=1, source_target_pairs={{0,28},{4,0},{8,4},{12,8},{16,12},{20,16},{24,20},{28,24},{1,29},{... | collective-permute-start | bytes 786440 | tf_op jit(solution)/shard_map/ppermute | solution.py:180
  93.2 9.5 %collective-permute-start.19 = (bf16[512,256]{1,0:T(8,128)(2,1)S(1)}, bf16[512,256]{1,0:T(8,128)(2,1)S(1)}, u32[]{:S(2)}, u32[]{:S(2)}) collective-permute-start(bf16[512,256]{1,0:T(8,128)(2,1)S(1)} %add_convert_fusion.3.refs_6_), channel_id=1, source_target_pairs={{0,4},{4,8},{8,12},{12,16},{16,20},{20,24},{24,28},{28,0},{1,5},{5... | collective-permute-start | bytes 786440 | tf_op jit(solution)/shard_map/ppermute | solution.py:180
  99.9 7.4 %collective-permute-start.23 = (bf16[512,256]{1,0:T(8,128)(2,1)S(1)}, bf16[512,256]{1,0:T(8,128)(2,1)S(1)}, u32[]{:S(2)}, u32[]{:S(2)}) collective-permute-start(bf16[512,256]{1,0:T(8,128)(2,1)S(1)} %add_convert_fusion), channel_id=1, source_target_pairs={{0,28},{4,0},{8,4},{12,8},{16,12},{20,16},{24,20},{28,24},{1,29},{... | collective-permute-start | bytes 786440 | tf_op jit(solution)/shard_map/ppermute | solution.py:180
  102.7 6.5 %collective-permute-start.20 = (bf16[512,256]{1,0:T(8,128)(2,1)S(1)}, bf16[512,256]{1,0:T(8,128)(2,1)S(1)}, u32[]{:S(2)}, u32[]{:S(2)}) collective-permute-start(bf16[512,256]{1,0:T(8,128)(2,1)S(1)} %add_convert_fusion.2), channel_id=1, source_target_pairs={{0,4},{4,8},{8,12},{12,16},{16,20},{20,24},{24,28},{28,0},{1,5},{5... | collective-permute-start | bytes 786440 | tf_op jit(solution)/shard_map/ppermute | solution.py:180
  102.8 12.1 %all-to-all-start.1 = ((bf16[8,128,256]{2,1,0:T(8,128)(2,1)}), bf16[8,128,256]{2,1,0:T(8,128)(2,1)S(1)}, u32[]{:S(2)}, u32[]{:S(2)}) async-start(bf16[8,128,256]{2,1,0:T(8,128)(2,1)} %get-tuple-element.29), calls=%async_computation.1 | async-start | bytes 1048576 | tf_op jit(solution)/shard_map/all_to_all | solution.py:222
  109.3 5.8 %collective-permute-start.24 = (bf16[256,256]{1,0:T(8,128)(2,1)S(1)}, bf16[256,256]{1,0:T(8,128)(2,1)S(1)}, u32[]{:S(2)}, u32[]{:S(2)}) collective-permute-start(bf16[256,256]{1,0:T(8,128)(2,1)S(1)} %slice.78), channel_id=1, source_target_pairs={{0,32},{32,0},{1,33},{33,1},{2,34},{34,2},{3,35},{35,3},{4,36},{36... | collective-permute-start | bytes 393224 | tf_op jit(solution)/shard_map/ppermute | solution.py:180
  115.2 8.7 %collective-permute-start.25 = (bf16[3,128,128]{2,1,0:T(8,128)(2,1)S(1)}, bf16[3,128,128]{2,1,0:T(8,128)(2,1)S(1)}, u32[]{:S(2)}, u32[]{:S(2)}) collective-permute-start(bf16[3,128,128]{2,1,0:T(8,128)(2,1)S(1)} %slice.49), channel_id=1, source_target_pairs={{0,1},{1,0},{2,3},{3,2},{4,5},{5,4},{6,7},{7,6},{8,9},{9,8},{10,11... | collective-permute-start | bytes 294920 | tf_op jit(solution)/shard_map/ppermute | solution.py:180
  (11 other events, 75.3 us)

commit v8 on v7

--- a/solution.py
+++ b/solution.py
@@ -71,7 +71,7 @@
     )(core.reshape(1), *args)
 
 
-def spread_kernel(mine_ref, other_ref, _, out_ref):
+def spread_kernel(mine_ref, other_ref, _a, _b, out_ref):
     rows = HALF + STATS
     for n in range(out_ref.shape[0]):
         out_ref[n, :rows, :] = mine_ref[...]
@@ -81,7 +81,7 @@
 def spread_call(n, *args):
     return pl.pallas_call(
         spread_kernel,
-        in_specs=[pl.BlockSpec(memory_space=pltpu.VMEM)] * 3,
+        in_specs=[pl.BlockSpec(memory_space=pltpu.VMEM)] * 4,
         out_specs=pl.BlockSpec(memory_space=pltpu.VMEM),
         out_shape=jax.ShapeDtypeStruct((n, 2 * (HALF + STATS), 2 * HEAD), BF16),
         name="spread",
@@ -200,7 +200,7 @@
         keys[-by] = [shift(x, "z", -1) for x in keys[1 - by]]
     keys[4] = [shift(keys[3][0], "z", 1), shift(keys[-3][1], "z", -1)]
     peers = math.prod(lax.axis_size(a) for a in GROUP)
-    spread = spread_call(peers, mine_q, other, keys[1][0])
+    spread = spread_call(peers, mine_q, other, keys[1][1], keys[-1][1])
     gathered = lax.all_to_all(spread, GROUP, 0, 0, tiled=True)
 
     def low(x):

time: 125 us -> 109 us (0.87)
  waiting for transfers between devices: 39 us -> 22.9 us
    ppermute x25, waiting for transfers between devices: 32.5 us -> 15.2 us  [shift(): return lax.ppermute(x, axis, [(i, (i + by) % n) for i in range(n)])]
    ppermute x1, waiting for transfers between devices: 2.49 us -> 3.81 us  [local(): lax.ppermute(far_kv, ('xh', 'core'), [(i, corners - 1 - i) for i in range...]
  transfers between devices with their start and end apart: 28 -> 28, of which waited for: 11 -> 10; matrix products, arithmetic and copies ran while one was open for 0% -> 1% of each run, Pallas kernels for 20% -> 23%
where the time goes in v8:
time: 109 us
  starting transfers between devices  52.4 us (48%)
  Pallas kernels  29.2 us (27%)
  waiting for transfers between devices  22.9 us (21%)
  local copies, waits for them, and re-layouts  2.44 us (2%)
  other arithmetic  1.25 us (1%)
    ppermute x25, starting transfers between devices, shift(): return lax.ppermute(x, axis, [(i, (i + by) % n) for i in range(n)])  40 us
    pallas_call x4, Pallas kernels, tile_call(): pl.pallas_call(functools.partial(tile_kernel, first, chips), grid=(groups...  25.2 us
    ppermute x25, waiting for transfers between devices, shift(): return lax.ppermute(x, axis, [(i, (i + by) % n) for i in range(n)])  15.2 us
    all_to_all x1, starting transfers between devices, local(): returned = lax.all_to_all(total_q, GROUP, 0, 0, tiled=True)  5.27 us
    all_to_all x1, starting transfers between devices, local(): gathered = lax.all_to_all(spread, GROUP, 0, 0, tiled=True)  4.36 us
    all_to_all x1, waiting for transfers between devices, local(): returned = lax.all_to_all(total_q, GROUP, 0, 0, tiled=True)  3.94 us
    ppermute x1, waiting for transfers between devices, local(): lax.ppermute(far_kv, ('xh', 'core'), [(i, corners - 1 - i) for i in range...  3.81 us
    ppermute x1, starting transfers between devices, local(): lax.ppermute(far_kv, ('xh', 'core'), [(i, corners - 1 - i) for i in range...  2.8 us
  transfers between devices with their start and end apart: 28, of which 10 were waited for; matrix products, arithmetic and copies ran while one was open for 1% of the time, Pallas kernels for 23%

profile of v8, /device:TPU:1, one launch (start us, length us, event | category | flops | bytes accessed | tf_op | source)
XLA Modules:
  0.0 109.1 jit_solution(1611009715632695760)
XLA Ops:
  2.4 3.6 %collective-permute-start.1 = (bf16[128,256]{1,0:T(8,128)(2,1)}, bf16[128,256]{1,0:T(8,128)(2,1)S(1)}, u32[]{:S(2)}, u32[]{:S(2)}) collective-permute-start(bf16[128,256]{1,0:T(8,128)(2,1)} %get-tuple-element.21), channel_id=1, source_target_pairs={{0,32},{32,0},{1,33},{33,1},{2,34},{34,2},{3,35},{35,3},{4,36},{36... | collective-permute-start | bytes 196616 | tf_op jit(solution)/shard_map/ppermute | solution.py:180
  6.0 2.8 %collective-permute-start.2 = (bf16[128,256]{1,0:T(8,128)(2,1)}, bf16[128,256]{1,0:T(8,128)(2,1)S(1)}, u32[]{:S(2)}, u32[]{:S(2)}) collective-permute-start(bf16[128,256]{1,0:T(8,128)(2,1)} %get-tuple-element.22), channel_id=1, source_target_pairs={{0,33},{1,32},{32,1},{33,0},{2,35},{3,34},{34,3},{35,2},{4,37},{5,... | collective-permute-start | bytes 196616 | tf_op jit(solution)/shard_map/ppermute | solution.py:192
  8.8 3.8 %collective-permute-done.2 = bf16[128,256]{1,0:T(8,128)(2,1)S(1)} collective-permute-done((bf16[128,256]{1,0:T(8,128)(2,1)}, bf16[128,256]{1,0:T(8,128)(2,1)S(1)}, u32[]{:S(2)}, u32[]{:S(2)}) %collective-permute-start.2) | collective-permute-done | bytes 65568 | tf_op jit(solution)/shard_map/ppermute | solution.py:192
  13.8 4.0 %collective-permute-start.4 = (bf16[256,256]{1,0:T(8,128)(2,1)S(1)}, bf16[256,256]{1,0:T(8,128)(2,1)S(1)}, u32[]{:S(2)}, u32[]{:S(2)}) collective-permute-start(bf16[256,256]{1,0:T(8,128)(2,1)S(1)} %constant_dynamic-update-slice_fusion.refs_4_), channel_id=1, source_target_pairs={{0,28},{4,0},{8,4},{12,8},{16,12},{20,16},{24,20},{28,24},{1,29},{... | collective-permute-start | bytes 393224 | tf_op jit(solution)/shard_map/ppermute | solution.py:180
  17.8 3.1 %collective-permute-done.3._a.refs_4_ = bf16[256,256]{1,0:T(8,128)(2,1)S(1)} collective-permute-done((bf16[256,256]{1,0:T(8,128)(2,1)S(1)}, bf16[256,256]{1,0:T(8,128)(2,1)S(1)}, u32[]{:S(2)}, u32[]{:S(2)}) %collective-permute-start.3) | collective-permute-done | bytes 131104 | tf_op jit(solution)/shard_map/ppermute | solution.py:180
  23.9 4.4 %all-to-all-start = ((bf16[8,288,256]{2,1,0:T(8,128)(2,1)}), bf16[8,288,256]{2,1,0:T(8,128)(2,1)S(1)}, u32[]{:S(2)}, u32[]{:S(2)}) async-start(bf16[8,288,256]{2,1,0:T(8,128)(2,1)} %spread.1), calls=%async_computation | async-start | bytes 2359296 | tf_op jit(solution)/shard_map/all_to_all | solution.py:204
  28.4 2.7 %collective-permute-start.8 = (bf16[256,256]{1,0:T(8,128)(2,1)S(1)}, bf16[256,256]{1,0:T(8,128)(2,1)S(1)}, u32[]{:S(2)}, u32[]{:S(2)}) collective-permute-start(bf16[256,256]{1,0:T(8,128)(2,1)S(1)} %copy-done.3), channel_id=1, source_target_pairs={{0,28},{4,0},{8,4},{12,8},{16,12},{20,16},{24,20},{28,24},{1,29},{... | collective-permute-start | bytes 393224 | tf_op jit(solution)/shard_map/ppermute | solution.py:180
  31.0 2.3 %collective-permute-done.6.refs_3_ = bf16[256,256]{1,0:T(8,128)(2,1)S(1)} collective-permute-done((bf16[256,256]{1,0:T(8,128)(2,1)S(1)}, bf16[256,256]{1,0:T(8,128)(2,1)S(1)}, u32[]{:S(2)}, u32[]{:S(2)}) %collective-permute-start.6) | collective-permute-done | bytes 131104 | tf_op jit(solution)/shard_map/ppermute | solution.py:180
  33.4 2.7 %collective-permute-start.5 = (bf16[256,256]{1,0:T(8,128)(2,1)S(1)}, bf16[256,256]{1,0:T(8,128)(2,1)S(1)}, u32[]{:S(2)}, u32[]{:S(2)}) collective-permute-start(bf16[256,256]{1,0:T(8,128)(2,1)S(1)} %pad_maximum_fusion.1.refs_3_), channel_id=1, source_target_pairs={{0,28},{4,0},{8,4},{12,8},{16,12},{20,16},{24,20},{28,24},{1,29},{... | collective-permute-start | bytes 393224 | tf_op jit(solution)/shard_map/ppermute | solution.py:180
  36.1 2.6 %collective-permute-done.9.refs_3_ = bf16[256,256]{1,0:T(8,128)(2,1)S(1)} collective-permute-done((bf16[256,256]{1,0:T(8,128)(2,1)S(1)}, bf16[256,256]{1,0:T(8,128)(2,1)S(1)}, u32[]{:S(2)}, u32[]{:S(2)}) %collective-permute-start.9) | collective-permute-done | bytes 131104 | tf_op jit(solution)/shard_map/ppermute | solution.py:180
  38.7 2.7 %collective-permute-start.7 = (bf16[256,256]{1,0:T(8,128)(2,1)S(1)}, bf16[256,256]{1,0:T(8,128)(2,1)S(1)}, u32[]{:S(2)}, u32[]{:S(2)}) collective-permute-start(bf16[256,256]{1,0:T(8,128)(2,1)S(1)} %collective-permute-done.5.refs_1_), channel_id=1, source_target_pairs={{0,28},{4,0},{8,4},{12,8},{16,12},{20,16},{24,20},{28,24},{1,29},{... | collective-permute-start | bytes 393224 | tf_op jit(solution)/shard_map/ppermute | solution.py:180
  45.5 2.7 %collective-permute-start.11 = (bf16[256,256]{1,0:T(8,128)(2,1)S(1)}, bf16[256,256]{1,0:T(8,128)(2,1)}, u32[]{:S(2)}, u32[]{:S(2)}) collective-permute-start(bf16[256,256]{1,0:T(8,128)(2,1)S(1)} %collective-permute-done.7.refs_1_), channel_id=1, source_target_pairs={{0,28},{4,0},{8,4},{12,8},{16,12},{20,16},{24,20},{28,24},{1,29},{... | collective-permute-start | bytes 393224 | tf_op jit(solution)/shard_map/ppermute | solution.py:180
  48.1 2.3 %collective-permute-done.15.refs_1_ = bf16[256,256]{1,0:T(8,128)(2,1)S(1)} collective-permute-done((bf16[256,256]{1,0:T(8,128)(2,1)S(1)}, bf16[256,256]{1,0:T(8,128)(2,1)S(1)}, u32[]{:S(2)}, u32[]{:S(2)}) %collective-permute-start.15) | collective-permute-done | bytes 131104 | tf_op jit(solution)/shard_map/ppermute | solution.py:180
  52.0 5.8 %tile.4 = (f32[8,128,256]{2,1,0:T(8,128)S(1)}, f32[512,256]{1,0:T(8,128)S(1)}, f32[512,256]{1,0:T(8,128)S(1)}) custom-call(bf16[8,288,256]{2,1,0:T(8,128)(2,1)S(1)} %all-to-all-done.refs_0_, bf16[256,256]{1,0:T(8,128)(2,1)S(1)} %copy-done.5, bf16[256,256]{1,0:T(8,128)(2,1)S(1)} %collective-permute-done.16.refs_2_, ...), custom_call_target="tpu_custom_call" | custom-call | flops 5368709120 | bytes 8388608 | tf_op jit(solution)/shard_map/tile/pallas_call | solution.py:154
  58.0 6.8 %tile.5 = (f32[8,128,256]{2,1,0:T(8,128)S(1)}, f32[512,256]{1,0:T(8,128)S(1)}, f32[512,256]{1,0:T(8,128)S(1)}) custom-call(bf16[8,288,256]{2,1,0:T(8,128)(2,1)S(1)} %all-to-all-done.refs_0_, bf16[256,256]{1,0:T(8,128)(2,1)} %collective-permute-done.11.refs_1_, bf16[256,256]{1,0:T(8,128)(2,1)S(1)} %collective-permute-done.12.refs_2_, ...), custom_call_target="tpu_custom_call" | custom-call | flops 5368709120 | bytes 8388608 | tf_op jit(solution)/shard_map/tile/pallas_call | solution.py:154
  64.9 2.7 %collective-permute-start.21 = (bf16[512,256]{1,0:T(8,128)(2,1)S(1)}, bf16[512,256]{1,0:T(8,128)(2,1)S(1)}, u32[]{:S(2)}, u32[]{:S(2)}) collective-permute-start(bf16[512,256]{1,0:T(8,128)(2,1)S(1)} %convert_element_type.59), channel_id=1, source_target_pairs={{0,28},{4,0},{8,4},{12,8},{16,12},{20,16},{24,20},{28,24},{1,29},{... | collective-permute-start | bytes 786440 | tf_op jit(solution)/shard_map/ppermute | solution.py:180
  67.7 5.9 %tile.6 = (f32[8,128,256]{2,1,0:T(8,128)S(1)}, f32[512,256]{1,0:T(8,128)S(1)}, f32[512,256]{1,0:T(8,128)S(1)}) custom-call(bf16[8,288,256]{2,1,0:T(8,128)(2,1)S(1)} %all-to-all-done.refs_0_, bf16[256,256]{1,0:T(8,128)(2,1)S(1)} %collective-permute-done.7.refs_1_, bf16[256,256]{1,0:T(8,128)(2,1)S(1)} %collective-permute-done.8.refs_2_, ...), custom_call_target="tpu_custom_call" | custom-call | flops 5368709120 | bytes 8388608 | tf_op jit(solution)/shard_map/tile/pallas_call | solution.py:154
  73.7 2.9 %collective-permute-start.22 = (bf16[512,256]{1,0:T(8,128)(2,1)S(1)}, bf16[512,256]{1,0:T(8,128)(2,1)S(1)}, u32[]{:S(2)}, u32[]{:S(2)}) collective-permute-start(bf16[512,256]{1,0:T(8,128)(2,1)S(1)} %add_convert_fusion.1), channel_id=1, source_target_pairs={{0,28},{4,0},{8,4},{12,8},{16,12},{20,16},{24,20},{28,24},{1,29},{... | collective-permute-start | bytes 786440 | tf_op jit(solution)/shard_map/ppermute | solution.py:180
  76.8 6.6 %tile.7 = (bf16[8,128,256]{2,1,0:T(8,128)(2,1)}, f32[512,256]{1,0:T(8,128)S(1)}, f32[512,256]{1,0:T(8,128)S(1)}) custom-call(bf16[8,288,256]{2,1,0:T(8,128)(2,1)S(1)} %all-to-all-done.refs_0_, bf16[256,256]{1,0:T(8,128)(2,1)S(1)} %collective-permute-done.5.refs_1_, bf16[256,256]{1,0:T(8,128)(2,1)S(1)} %copy-done.3, ...), custom_call_target="tpu_custom_call" | custom-call | flops 5368709120 | bytes 8388608 | tf_op jit(solution)/shard_map/tile/pallas_call | solution.py:154
  83.5 2.7 %collective-permute-start.23 = (bf16[512,256]{1,0:T(8,128)(2,1)S(1)}, bf16[512,256]{1,0:T(8,128)(2,1)S(1)}, u32[]{:S(2)}, u32[]{:S(2)}) collective-permute-start(bf16[512,256]{1,0:T(8,128)(2,1)S(1)} %add_convert_fusion), channel_id=1, source_target_pairs={{0,28},{4,0},{8,4},{12,8},{16,12},{20,16},{24,20},{28,24},{1,29},{... | collective-permute-start | bytes 786440 | tf_op jit(solution)/shard_map/ppermute | solution.py:180
  86.4 5.3 %all-to-all-start.1 = ((bf16[8,128,256]{2,1,0:T(8,128)(2,1)}), bf16[8,128,256]{2,1,0:T(8,128)(2,1)S(1)}, u32[]{:S(2)}, u32[]{:S(2)}) async-start(bf16[8,128,256]{2,1,0:T(8,128)(2,1)} %get-tuple-element.29), calls=%async_computation.1 | async-start | bytes 1048576 | tf_op jit(solution)/shard_map/all_to_all | solution.py:222
  92.9 2.3 %collective-permute-start.24 = (bf16[256,256]{1,0:T(8,128)(2,1)S(1)}, bf16[256,256]{1,0:T(8,128)(2,1)S(1)}, u32[]{:S(2)}, u32[]{:S(2)}) collective-permute-start(bf16[256,256]{1,0:T(8,128)(2,1)S(1)} %slice.78), channel_id=1, source_target_pairs={{0,32},{32,0},{1,33},{33,1},{2,34},{34,2},{3,35},{35,3},{4,36},{36... | collective-permute-start | bytes 393224 | tf_op jit(solution)/shard_map/ppermute | solution.py:180
  95.3 3.9 %all-to-all-done.1 = bf16[8,128,256]{2,1,0:T(8,128)(2,1)S(1)} async-done(((bf16[8,128,256]{2,1,0:T(8,128)(2,1)}), bf16[8,128,256]{2,1,0:T(8,128)(2,1)S(1)}, u32[]{:S(2)}, u32[]{:S(2)}) %all-to-all-start.1) | async-done | bytes 524320 | tf_op jit(solution)/shard_map/all_to_all | solution.py:222
  99.5 7.9 %collective-permute-start.25 = (bf16[3,128,128]{2,1,0:T(8,128)(2,1)S(1)}, bf16[3,128,128]{2,1,0:T(8,128)(2,1)S(1)}, u32[]{:S(2)}, u32[]{:S(2)}) collective-permute-start(bf16[3,128,128]{2,1,0:T(8,128)(2,1)S(1)} %slice.49), channel_id=1, source_target_pairs={{0,1},{1,0},{2,3},{3,2},{4,5},{5,4},{6,7},{7,6},{8,9},{9,8},{10,11... | collective-permute-start | bytes 294920 | tf_op jit(solution)/shard_map/ppermute | solution.py:180
  (76 shorter events, 15.4 us)
Async XLA Ops:
  2.4 6.4 %collective-permute-start.1 = (bf16[128,256]{1,0:T(8,128)(2,1)}, bf16[128,256]{1,0:T(8,128)(2,1)S(1)}, u32[]{:S(2)}, u32[]{:S(2)}) collective-permute-start(bf16[128,256]{1,0:T(8,128)(2,1)} %get-tuple-element.21), channel_id=1, source_target_pairs={{0,32},{32,0},{1,33},{33,1},{2,34},{34,2},{3,35},{35,3},{4,36},{36... | collective-permute-start | bytes 196616 | tf_op jit(solution)/shard_map/ppermute | solution.py:180
  6.0 6.6 %collective-permute-start.2 = (bf16[128,256]{1,0:T(8,128)(2,1)}, bf16[128,256]{1,0:T(8,128)(2,1)S(1)}, u32[]{:S(2)}, u32[]{:S(2)}) collective-permute-start(bf16[128,256]{1,0:T(8,128)(2,1)} %get-tuple-element.22), channel_id=1, source_target_pairs={{0,33},{1,32},{32,1},{33,0},{2,35},{3,34},{34,3},{35,2},{4,37},{5,... | collective-permute-start | bytes 196616 | tf_op jit(solution)/shard_map/ppermute | solution.py:192
  8.8 9.0 %collective-permute-start = (bf16[272,256]{1,0:T(8,128)(2,1)}, bf16[272,256]{1,0:T(8,128)(2,1)S(1)}, u32[]{:S(2)}, u32[]{:S(2)}) collective-permute-start(bf16[272,256]{1,0:T(8,128)(2,1)} %get-tuple-element.20), channel_id=1, source_target_pairs={{0,1},{1,0},{2,3},{3,2},{4,5},{5,4},{6,7},{7,6},{8,9},{9,8},{10,11... | collective-permute-start | bytes 417800 | tf_op jit(solution)/shard_map/ppermute | solution.py:180
  12.7 8.3 %collective-permute-start.3 = (bf16[256,256]{1,0:T(8,128)(2,1)S(1)}, bf16[256,256]{1,0:T(8,128)(2,1)S(1)}, u32[]{:S(2)}, u32[]{:S(2)}) collective-permute-start(bf16[256,256]{1,0:T(8,128)(2,1)S(1)} %constant_dynamic-update-slice_fusion.refs_4_), channel_id=1, source_target_pairs={{0,4},{4,8},{8,12},{12,16},{16,20},{20,24},{24,28},{28,0},{1,5},{5... | collective-permute-start | bytes 393224 | tf_op jit(solution)/shard_map/ppermute | solution.py:180
  13.8 7.2 %collective-permute-start.4 = (bf16[256,256]{1,0:T(8,128)(2,1)S(1)}, bf16[256,256]{1,0:T(8,128)(2,1)S(1)}, u32[]{:S(2)}, u32[]{:S(2)}) collective-permute-start(bf16[256,256]{1,0:T(8,128)(2,1)S(1)} %constant_dynamic-update-slice_fusion.refs_4_), channel_id=1, source_target_pairs={{0,28},{4,0},{8,4},{12,8},{16,12},{20,16},{24,20},{28,24},{1,29},{... | collective-permute-start | bytes 393224 | tf_op jit(solution)/shard_map/ppermute | solution.py:180
  23.9 27.2 %all-to-all-start = ((bf16[8,288,256]{2,1,0:T(8,128)(2,1)}), bf16[8,288,256]{2,1,0:T(8,128)(2,1)S(1)}, u32[]{:S(2)}, u32[]{:S(2)}) async-start(bf16[8,288,256]{2,1,0:T(8,128)(2,1)} %spread.1), calls=%async_computation | async-start | bytes 2359296 | tf_op jit(solution)/shard_map/all_to_all | solution.py:204
  28.4 7.7 %collective-permute-start.8 = (bf16[256,256]{1,0:T(8,128)(2,1)S(1)}, bf16[256,256]{1,0:T(8,128)(2,1)S(1)}, u32[]{:S(2)}, u32[]{:S(2)}) collective-permute-start(bf16[256,256]{1,0:T(8,128)(2,1)S(1)} %copy-done.3), channel_id=1, source_target_pairs={{0,28},{4,0},{8,4},{12,8},{16,12},{20,16},{24,20},{28,24},{1,29},{... | collective-permute-start | bytes 393224 | tf_op jit(solution)/shard_map/ppermute | solution.py:180
  36.1 5.4 %collective-permute-start.12 = (bf16[256,256]{1,0:T(8,128)(2,1)S(1)}, bf16[256,256]{1,0:T(8,128)(2,1)S(1)}, u32[]{:S(2)}, u32[]{:S(2)}) collective-permute-start(bf16[256,256]{1,0:T(8,128)(2,1)S(1)} %collective-permute-done.8.refs_2_), channel_id=1, source_target_pairs={{0,28},{4,0},{8,4},{12,8},{16,12},{20,16},{24,20},{28,24},{1,29},{... | collective-permute-start | bytes 393224 | tf_op jit(solution)/shard_map/ppermute | solution.py:180
  38.7 6.7 %collective-permute-start.10 = (bf16[256,256]{1,0:T(8,128)(2,1)S(1)}, bf16[256,256]{1,0:T(8,128)(2,1)S(1)}, u32[]{:S(2)}, u32[]{:S(2)}) collective-permute-start(bf16[256,256]{1,0:T(8,128)(2,1)S(1)} %copy-done.1), channel_id=1, source_target_pairs={{0,4},{4,8},{8,12},{12,16},{16,20},{20,24},{24,28},{28,0},{1,5},{5... | collective-permute-start | bytes 393224 | tf_op jit(solution)/shard_map/ppermute | solution.py:180
  38.7 6.7 %collective-permute-start.7 = (bf16[256,256]{1,0:T(8,128)(2,1)S(1)}, bf16[256,256]{1,0:T(8,128)(2,1)S(1)}, u32[]{:S(2)}, u32[]{:S(2)}) collective-permute-start(bf16[256,256]{1,0:T(8,128)(2,1)S(1)} %collective-permute-done.5.refs_1_), channel_id=1, source_target_pairs={{0,28},{4,0},{8,4},{12,8},{16,12},{20,16},{24,20},{28,24},{1,29},{... | collective-permute-start | bytes 393224 | tf_op jit(solution)/shard_map/ppermute | solution.py:180
  41.5 6.6 %collective-permute-start.16 = (bf16[256,256]{1,0:T(8,128)(2,1)S(1)}, bf16[256,256]{1,0:T(8,128)(2,1)S(1)}, u32[]{:S(2)}, u32[]{:S(2)}) collective-permute-start(bf16[256,256]{1,0:T(8,128)(2,1)S(1)} %collective-permute-done.12.refs_2_), channel_id=1, source_target_pairs={{0,28},{4,0},{8,4},{12,8},{16,12},{20,16},{24,20},{28,24},{1,29},{... | collective-permute-start | bytes 393224 | tf_op jit(solution)/shard_map/ppermute | solution.py:180
  43.7 6.7 %collective-permute-start.15 = (bf16[256,256]{1,0:T(8,128)(2,1)S(1)}, bf16[256,256]{1,0:T(8,128)(2,1)S(1)}, u32[]{:S(2)}, u32[]{:S(2)}) collective-permute-start(bf16[256,256]{1,0:T(8,128)(2,1)S(1)} %collective-permute-done.13.refs_3_), channel_id=1, source_target_pairs={{0,4},{4,8},{8,12},{12,16},{16,20},{20,24},{24,28},{28,0},{1,5},{5... | collective-permute-start | bytes 393224 | tf_op jit(solution)/shard_map/ppermute | solution.py:180
  45.4 12.6 %collective-permute-start.14 = (bf16[256,256]{1,0:T(8,128)(2,1)S(1)}, bf16[256,256]{1,0:T(8,128)(2,1)S(1)}, u32[]{:S(2)}, u32[]{:S(2)}) collective-permute-start(bf16[256,256]{1,0:T(8,128)(2,1)S(1)} %collective-permute-done.10.refs_4_), channel_id=1, source_target_pairs={{0,4},{4,8},{8,12},{12,16},{16,20},{20,24},{24,28},{28,0},{1,5},{5... | collective-permute-start | bytes 393224 | tf_op jit(solution)/shard_map/ppermute | solution.py:180
  45.5 12.6 %collective-permute-start.11 = (bf16[256,256]{1,0:T(8,128)(2,1)S(1)}, bf16[256,256]{1,0:T(8,128)(2,1)}, u32[]{:S(2)}, u32[]{:S(2)}) collective-permute-start(bf16[256,256]{1,0:T(8,128)(2,1)S(1)} %collective-permute-done.7.refs_1_), channel_id=1, source_target_pairs={{0,28},{4,0},{8,4},{12,8},{16,12},{20,16},{24,20},{28,24},{1,29},{... | collective-permute-start | bytes 393224 | tf_op jit(solution)/shard_map/ppermute | solution.py:180
  57.9 9.7 %collective-permute-start.17 = (bf16[512,256]{1,0:T(8,128)(2,1)S(1)}, bf16[512,256]{1,0:T(8,128)(2,1)S(1)}, u32[]{:S(2)}, u32[]{:S(2)}) collective-permute-start(bf16[512,256]{1,0:T(8,128)(2,1)S(1)} %convert_element_type.50.refs_6_), channel_id=1, source_target_pairs={{0,4},{4,8},{8,12},{12,16},{16,20},{20,24},{24,28},{28,0},{1,5},{5... | collective-permute-start | bytes 786440 | tf_op jit(solution)/shard_map/ppermute | solution.py:180
  64.9 8.8 %collective-permute-start.21 = (bf16[512,256]{1,0:T(8,128)(2,1)S(1)}, bf16[512,256]{1,0:T(8,128)(2,1)S(1)}, u32[]{:S(2)}, u32[]{:S(2)}) collective-permute-start(bf16[512,256]{1,0:T(8,128)(2,1)S(1)} %convert_element_type.59), channel_id=1, source_target_pairs={{0,28},{4,0},{8,4},{12,8},{16,12},{20,16},{24,20},{28,24},{1,29},{... | collective-permute-start | bytes 786440 | tf_op jit(solution)/shard_map/ppermute | solution.py:180
  67.6 9.0 %collective-permute-start.18 = (bf16[512,256]{1,0:T(8,128)(2,1)S(1)}, bf16[512,256]{1,0:T(8,128)(2,1)S(1)}, u32[]{:S(2)}, u32[]{:S(2)}) collective-permute-start(bf16[512,256]{1,0:T(8,128)(2,1)S(1)} %add_convert_fusion.4.refs_6_), channel_id=1, source_target_pairs={{0,4},{4,8},{8,12},{12,16},{16,20},{20,24},{24,28},{28,0},{1,5},{5... | collective-permute-start | bytes 786440 | tf_op jit(solution)/shard_map/ppermute | solution.py:180
  73.7 9.7 %collective-permute-start.22 = (bf16[512,256]{1,0:T(8,128)(2,1)S(1)}, bf16[512,256]{1,0:T(8,128)(2,1)S(1)}, u32[]{:S(2)}, u32[]{:S(2)}) collective-permute-start(bf16[512,256]{1,0:T(8,128)(2,1)S(1)} %add_convert_fusion.1), channel_id=1, source_target_pairs={{0,28},{4,0},{8,4},{12,8},{16,12},{20,16},{24,20},{28,24},{1,29},{... | collective-permute-start | bytes 786440 | tf_op jit(solution)/shard_map/ppermute | solution.py:180
  76.7 9.5 %collective-permute-start.19 = (bf16[512,256]{1,0:T(8,128)(2,1)S(1)}, bf16[512,256]{1,0:T(8,128)(2,1)S(1)}, u32[]{:S(2)}, u32[]{:S(2)}) collective-permute-start(bf16[512,256]{1,0:T(8,128)(2,1)S(1)} %add_convert_fusion.3.refs_6_), channel_id=1, source_target_pairs={{0,4},{4,8},{8,12},{12,16},{16,20},{20,24},{24,28},{28,0},{1,5},{5... | collective-permute-start | bytes 786440 | tf_op jit(solution)/shard_map/ppermute | solution.py:180
  83.5 8.1 %collective-permute-start.23 = (bf16[512,256]{1,0:T(8,128)(2,1)S(1)}, bf16[512,256]{1,0:T(8,128)(2,1)S(1)}, u32[]{:S(2)}, u32[]{:S(2)}) collective-permute-start(bf16[512,256]{1,0:T(8,128)(2,1)S(1)} %add_convert_fusion), channel_id=1, source_target_pairs={{0,28},{4,0},{8,4},{12,8},{16,12},{20,16},{24,20},{28,24},{1,29},{... | collective-permute-start | bytes 786440 | tf_op jit(solution)/shard_map/ppermute | solution.py:180
  86.3 6.5 %collective-permute-start.20 = (bf16[512,256]{1,0:T(8,128)(2,1)S(1)}, bf16[512,256]{1,0:T(8,128)(2,1)S(1)}, u32[]{:S(2)}, u32[]{:S(2)}) collective-permute-start(bf16[512,256]{1,0:T(8,128)(2,1)S(1)} %add_convert_fusion.2), channel_id=1, source_target_pairs={{0,4},{4,8},{8,12},{12,16},{16,20},{20,24},{24,28},{28,0},{1,5},{5... | collective-permute-start | bytes 786440 | tf_op jit(solution)/shard_map/ppermute | solution.py:180
  86.4 12.8 %all-to-all-start.1 = ((bf16[8,128,256]{2,1,0:T(8,128)(2,1)}), bf16[8,128,256]{2,1,0:T(8,128)(2,1)S(1)}, u32[]{:S(2)}, u32[]{:S(2)}) async-start(bf16[8,128,256]{2,1,0:T(8,128)(2,1)} %get-tuple-element.29), calls=%async_computation.1 | async-start | bytes 1048576 | tf_op jit(solution)/shard_map/all_to_all | solution.py:222
  92.9 6.5 %collective-permute-start.24 = (bf16[256,256]{1,0:T(8,128)(2,1)S(1)}, bf16[256,256]{1,0:T(8,128)(2,1)S(1)}, u32[]{:S(2)}, u32[]{:S(2)}) collective-permute-start(bf16[256,256]{1,0:T(8,128)(2,1)S(1)} %slice.78), channel_id=1, source_target_pairs={{0,32},{32,0},{1,33},{33,1},{2,34},{34,2},{3,35},{35,3},{4,36},{36... | collective-permute-start | bytes 393224 | tf_op jit(solution)/shard_map/ppermute | solution.py:180
  99.5 8.9 %collective-permute-start.25 = (bf16[3,128,128]{2,1,0:T(8,128)(2,1)S(1)}, bf16[3,128,128]{2,1,0:T(8,128)(2,1)S(1)}, u32[]{:S(2)}, u32[]{:S(2)}) collective-permute-start(bf16[3,128,128]{2,1,0:T(8,128)(2,1)S(1)} %slice.49), channel_id=1, source_target_pairs={{0,1},{1,0},{2,3},{3,2},{4,5},{5,4},{6,7},{7,6},{8,9},{9,8},{10,11... | collective-permute-start | bytes 294920 | tf_op jit(solution)/shard_map/ppermute | solution.py:180
  (13 other events, 55.0 us)

commit v9 on v3

--- a/solution.py
+++ b/solution.py
@@ -91,13 +91,18 @@
     )(*args)
 
 
-def tile_kernel(first, chips, *refs):
-    if first:
-        qg_ref, kv1_ref, kv2_ref, dq_ref, d1_ref, d2_ref, acc_k, acc_v, kt_ref = refs
-    else:
-        qg_ref, kv1_ref, kv2_ref, old_ref, _, dq_ref, d1_ref, d2_ref, acc_k, acc_v, kt_ref = refs
+def tile_kernel(count, first, waits, chips, *refs):
+    refs = list(refs)
+    qg_ref = refs.pop(0)
+    blocks = [refs.pop(0) for _ in range(count)]
+    if not first:
+        old_ref = refs.pop(0)
+    if waits:
+        refs.pop(0)
+    dq_ref = refs.pop(0)
+    sums = [refs.pop(0) for _ in range(count)]
+    acc_k, acc_v, kt_ref = refs
     step = pl.program_id(0)
-    blocks = (kv1_ref, kv2_ref)
 
     @pl.when(step == 0)
     def _():
@@ -133,42 +138,45 @@
 
     @pl.when(step == pl.num_programs(0) - 1)
     def _():
-        for n, d_ref in enumerate((d1_ref, d2_ref)):
+        for n, d_ref in enumerate(sums):
             d_ref[:, :HEAD] = acc_k[n]
             d_ref[:, HEAD:] = acc_v[n]
 
 
-def tile_call(qg, kv1, kv2, old, after, last):
+def tile_call(qg, blocks, old=None, after=None, last=False):
     first = old is None
     groups, rows, width = qg.shape
+    count, keys = len(blocks), blocks[0].shape[0]
     chips = 4
     q_spec = pl.BlockSpec((chips, rows, width), lambda i: (i, 0, 0))
-    keys = kv1.shape[0]
     kv_spec = pl.BlockSpec((keys, width), lambda i: (0, 0))
     dq_spec = pl.BlockSpec((chips, HEAD, ROWS), lambda i: (i, 0, 0))
-    pairs = groups * ROWS * 2 * keys
+    dq_shape = jax.ShapeDtypeStruct((groups, HEAD, ROWS), BF16 if last else F32)
+    args, specs = [qg, *blocks], [q_spec] + [kv_spec] * count
+    if not first:
+        args.append(old)
+        specs.append(dq_spec)
+    if after is not None:
+        args.append(after)
+        specs.append(pl.BlockSpec(memory_space=pl.ANY))
+    pairs = groups * ROWS * count * keys
     return pl.pallas_call(
-        functools.partial(tile_kernel, first, chips),
+        functools.partial(tile_kernel, count, first, after is not None, chips),
         grid=(groups // chips,),
-        in_specs=[q_spec, kv_spec, kv_spec]
-        + ([] if first else [dq_spec, pl.BlockSpec(memory_space=pl.ANY)]),
-        out_specs=[dq_spec, kv_spec, kv_spec],
-        out_shape=[
-            jax.ShapeDtypeStruct((groups, HEAD, ROWS), BF16 if last else F32),
-            jax.ShapeDtypeStruct((keys, width), F32),
-            jax.ShapeDtypeStruct((keys, width), F32),
-        ],
+        in_specs=specs,
+        out_specs=[dq_spec] + [kv_spec] * count,
+        out_shape=[dq_shape] + [jax.ShapeDtypeStruct((keys, width), F32)] * count,
         scratch_shapes=[
-            pltpu.VMEM((2, keys, HEAD), F32),
-            pltpu.VMEM((2, keys, HEAD), F32),
-            pltpu.VMEM((2, HEAD, keys), BF16),
+            pltpu.VMEM((count, keys, HEAD), F32),
+            pltpu.VMEM((count, keys, HEAD), F32),
+            pltpu.VMEM((count, HEAD, keys), BF16),
         ],
         compiler_params=pltpu.CompilerParams(vmem_limit_bytes=40 * 2**20),
         cost_estimate=pl.CostEstimate(
             flops=pairs * HEAD * 20, bytes_accessed=8 * 2**20, transcendentals=pairs
         ),
         name="tile",
-    )(*((qg, kv1, kv2) if first else (qg, kv1, kv2, old, after)))
+    )(*args)
 
 
 def shift(x, axis, by):
@@ -191,26 +199,35 @@
     for by in (1, 2, 3):
         keys[by] = shift(keys[by - 1], "z", 1)
         keys[-by] = shift(keys[1 - by], "z", -1)
+    total_q, own = tile_call(gathered, [keys[0]])
+    zero = jnp.minimum(jnp.abs(own[0, 0]), 0.0).astype(BF16)
     keys[4] = jnp.concatenate(
-        [shift(keys[3][:ROWS], "z", 1), shift(keys[-3][ROWS:], "z", -1)], axis=0
+        [shift(keys[3][:ROWS] + zero, "z", 1), shift(keys[-3][ROWS:] + zero, "z", -1)],
+        axis=0,
     )
 
     def low(x):
         return x.astype(BF16)
 
-    total_q, far, own = tile_call(gathered, keys[4], keys[0], None, None, False)
+    total_q, far = tile_call(gathered, [keys[4]], total_q)
     up = low(far)
     down = None
     after = up
-    for by in (3, 2, 1):
+    for by in (3, 2):
         up_in = shift(up, "z", 1)
         down_in = None if down is None else shift(down, "z", -1)
-        total_q, du, dd = tile_call(gathered, keys[-by], keys[by], total_q, after, by == 1)
+        total_q, du, dd = tile_call(gathered, [keys[-by], keys[by]], total_q, after)
         up = low(du + up_in.astype(F32))
         down = low(dd if down_in is None else dd + down_in.astype(F32))
         after = up
     up_in = shift(up, "z", 1)
     down_in = shift(down, "z", -1)
+    total_q, dd = tile_call(gathered, [keys[1]], total_q, after)
+    down = low(dd + down_in.astype(F32))
+    down_in = shift(down, "z", -1)
+    total_q, du = tile_call(gathered, [keys[-1]], total_q, down, True)
+    up = low(du + up_in.astype(F32))
+    up_in = shift(up, "z", 1)
     returned = lax.all_to_all(total_q, GROUP, 0, 0, tiled=True)
     grad_pair = own + up_in.astype(F32) + down_in.astype(F32)
     grad_kv = grad_pair[:ROWS] + shift(low(grad_pair[ROWS:]), "xh", 1).astype(F32)

time: 101 us -> 119 us (1.18)
  waiting for transfers between devices: 22.4 us -> 37.7 us
  starting transfers between devices: 46.3 us -> 48.2 us
    ppermute x19, waiting for transfers between devices: 19.3 us -> 33.5 us  [shift(): return lax.ppermute(x, axis, [(i, (i + by) % n) for i in range(n)])]
    ppermute x19, starting transfers between devices: 36.2 us -> 40.7 us  [shift(): return lax.ppermute(x, axis, [(i, (i + by) % n) for i in range(n)])]
    all_to_all x1, starting transfers between devices: 5.12 us -> 3.69 us  [local(): gathered = lax.all_to_all(spread, GROUP, 0, 0, tiled=True)]
    pallas_call x4 -> x6, Pallas kernels: 24.4 us -> 24.8 us  [tile_call(): pl.pallas_call(functools.partial(tile_kernel, count, first, after is not...]
  transfers between devices with their start and end apart: 21 -> 21, of which waited for: 10 -> 10; matrix products, arithmetic and copies ran while one was open for 2% -> 1% of each run, Pallas kernels for 18% -> 18%
where the time goes in v9:
time: 119 us
  starting transfers between devices  48.2 us (41%)
  waiting for transfers between devices  37.7 us (32%)
  Pallas kernels  28.7 us (24%)
  between operations  1.57 us (1%)
  local copies, waits for them, and re-layouts  1.34 us (1%)
  other arithmetic  1.28 us (1%)
    ppermute x19, starting transfers between devices, shift(): return lax.ppermute(x, axis, [(i, (i + by) % n) for i in range(n)])  40.7 us
    ppermute x19, waiting for transfers between devices, shift(): return lax.ppermute(x, axis, [(i, (i + by) % n) for i in range(n)])  33.5 us
    pallas_call x6, Pallas kernels, tile_call(): pl.pallas_call(functools.partial(tile_kernel, count, first, after is not...  24.8 us
    all_to_all x1, waiting for transfers between devices, local(): returned = lax.all_to_all(total_q, GROUP, 0, 0, tiled=True)  4.17 us
    all_to_all x1, starting transfers between devices, local(): returned = lax.all_to_all(total_q, GROUP, 0, 0, tiled=True)  3.77 us
    all_to_all x1, starting transfers between devices, local(): gathered = lax.all_to_all(spread, GROUP, 0, 0, tiled=True)  3.69 us
  transfers between devices with their start and end apart: 21, of which 10 were waited for; matrix products, arithmetic and copies ran while one was open for 1% of the time, Pallas kernels for 18%

profile of v9, /device:TPU:1, one launch (start us, length us, event | category | flops | bytes accessed | tf_op | source)
XLA Modules:
  0.0 118.8 jit_solution(5026322110788379386)
XLA Ops:
  2.4 3.2 %collective-permute-start = (bf16[272,256]{1,0:T(8,128)(2,1)}, bf16[272,256]{1,0:T(8,128)(2,1)S(1)}, u32[]{:S(2)}, u32[]{:S(2)}) collective-permute-start(bf16[272,256]{1,0:T(8,128)(2,1)} %get-tuple-element.24), channel_id=1, source_target_pairs={{0,1},{1,0},{2,3},{3,2},{4,5},{5,4},{6,7},{7,6},{8,9},{9,8},{10,11... | collective-permute-start | bytes 417800 | tf_op jit(solution)/shard_map/ppermute | solution.py:184
  9.7 3.7 %all-to-all-start = ((bf16[8,288,256]{2,1,0:T(8,128)(2,1)}), bf16[8,288,256]{2,1,0:T(8,128)(2,1)S(1)}, u32[]{:S(2)}, u32[]{:S(2)}) async-start(bf16[8,288,256]{2,1,0:T(8,128)(2,1)} %get-tuple-element.25), calls=%async_computation | async-start | bytes 2359296 | tf_op jit(solution)/shard_map/all_to_all | solution.py:197
  13.4 2.3 %collective-permute-start.1 = (bf16[256,256]{1,0:T(8,128)(2,1)S(1)}, bf16[256,256]{1,0:T(8,128)(2,1)S(1)}, u32[]{:S(2)}, u32[]{:S(2)}) collective-permute-start(bf16[256,256]{1,0:T(8,128)(2,1)S(1)} %copy-done.1), channel_id=1, source_target_pairs={{0,32},{32,0},{1,33},{33,1},{2,34},{34,2},{3,35},{35,3},{4,36},{36... | collective-permute-start | bytes 393224 | tf_op jit(solution)/shard_map/ppermute | solution.py:184
  15.8 16.1 %collective-permute-done.1 = bf16[256,256]{1,0:T(8,128)(2,1)S(1)} collective-permute-done((bf16[256,256]{1,0:T(8,128)(2,1)S(1)}, bf16[256,256]{1,0:T(8,128)(2,1)S(1)}, u32[]{:S(2)}, u32[]{:S(2)}) %collective-permute-start.1) | collective-permute-done | bytes 131104 | tf_op jit(solution)/shard_map/ppermute | solution.py:184
  33.6 4.0 %collective-permute-start.2 = (bf16[512,256]{1,0:T(8,128)(2,1)S(1)}, bf16[512,256]{1,0:T(8,128)(2,1)S(1)}, u32[]{:S(2)}, u32[]{:S(2)}) collective-permute-start(bf16[512,256]{1,0:T(8,128)(2,1)S(1)} %constant_dynamic-update-slice_fusion.refs_1_), channel_id=1, source_target_pairs={{0,28},{4,0},{8,4},{12,8},{16,12},{20,16},{24,20},{28,24},{1,29},{... | collective-permute-start | bytes 786440 | tf_op jit(solution)/shard_map/ppermute | solution.py:184
  37.6 5.3 %collective-permute-done.3.refs_1_ = bf16[512,256]{1,0:T(8,128)(2,1)S(1)} collective-permute-done((bf16[512,256]{1,0:T(8,128)(2,1)S(1)}, bf16[512,256]{1,0:T(8,128)(2,1)S(1)}, u32[]{:S(2)}, u32[]{:S(2)}) %collective-permute-start.3) | collective-permute-done | bytes 262176 | tf_op jit(solution)/shard_map/ppermute | solution.py:184
  43.0 2.7 %collective-permute-start.4 = (bf16[512,256]{1,0:T(8,128)(2,1)S(1)}, bf16[512,256]{1,0:T(8,128)(2,1)S(1)}, u32[]{:S(2)}, u32[]{:S(2)}) collective-permute-start(bf16[512,256]{1,0:T(8,128)(2,1)S(1)} %collective-permute-done.2.refs_1_), channel_id=1, source_target_pairs={{0,28},{4,0},{8,4},{12,8},{16,12},{20,16},{24,20},{28,24},{1,29},{... | collective-permute-start | bytes 786440 | tf_op jit(solution)/shard_map/ppermute | solution.py:184
  45.6 4.5 %collective-permute-done.5.refs_2_ = bf16[512,256]{1,0:T(8,128)(2,1)S(1)} collective-permute-done((bf16[512,256]{1,0:T(8,128)(2,1)S(1)}, bf16[512,256]{1,0:T(8,128)(2,1)S(1)}, u32[]{:S(2)}, u32[]{:S(2)}) %collective-permute-start.5) | collective-permute-done | bytes 262176 | tf_op jit(solution)/shard_map/ppermute | solution.py:184
  50.1 2.7 %collective-permute-start.6 = (bf16[512,256]{1,0:T(8,128)(2,1)S(1)}, bf16[512,256]{1,0:T(8,128)(2,1)S(1)}, u32[]{:S(2)}, u32[]{:S(2)}) collective-permute-start(bf16[512,256]{1,0:T(8,128)(2,1)S(1)} %collective-permute-done.4.refs_1_), channel_id=1, source_target_pairs={{0,28},{4,0},{8,4},{12,8},{16,12},{20,16},{24,20},{28,24},{1,29},{... | collective-permute-start | bytes 786440 | tf_op jit(solution)/shard_map/ppermute | solution.py:184
  52.8 3.0 %tile.6 = (f32[8,128,256]{2,1,0:T(8,128)S(1)}, f32[512,256]{1,0:T(8,128)S(1)}) custom-call(bf16[8,288,256]{2,1,0:T(8,128)(2,1)S(1)} %all-to-all-done.refs_0_, bf16[512,256]{1,0:T(8,128)(2,1)S(1)} %constant_dynamic-update-slice_fusion.refs_1_), custom_call_target="tpu_custom_call" | custom-call | flops 2684354560 | bytes 8388608 | tf_op jit(solution)/shard_map/tile/pallas_call | solution.py:163
  57.2 2.7 %collective-permute-start.9 = (bf16[256,256]{1,0:T(8,128)(2,1)S(1)}, bf16[256,256]{1,0:T(8,128)(2,1)S(1)}, u32[]{:S(2)}, u32[]{:S(2)}) collective-permute-start(bf16[256,256]{1,0:T(8,128)(2,1)S(1)} %slice_add_fusion.1), channel_id=1, source_target_pairs={{0,28},{4,0},{8,4},{12,8},{16,12},{20,16},{24,20},{28,24},{1,29},{... | collective-permute-start | bytes 393224 | tf_op jit(solution)/shard_map/ppermute | solution.py:184
  59.9 2.3 %collective-permute-done.8 = bf16[256,256]{1,0:T(8,128)(2,1)S(1)} collective-permute-done((bf16[256,256]{1,0:T(8,128)(2,1)S(1)}, bf16[256,256]{1,0:T(8,128)(2,1)S(1)}, u32[]{:S(2)}, u32[]{:S(2)}) %collective-permute-start.8) | collective-permute-done | bytes 131104 | tf_op jit(solution)/shard_map/ppermute | solution.py:184
  62.2 3.1 %tile.7 = (f32[8,128,256]{2,1,0:T(8,128)S(1)}, f32[512,256]{1,0:T(8,128)S(1)}) custom-call(bf16[8,288,256]{2,1,0:T(8,128)(2,1)S(1)} %all-to-all-done.refs_0_, bf16[512,256]{1,0:T(8,128)(2,1)S(1)} %pad_maximum_fusion.refs_1_, f32[8,128,256]{2,1,0:T(8,128)S(1)} %get-tuple-element.28.refs_2_), custom_call_target="tpu_custom_call" | custom-call | flops 2684354560 | bytes 8388608 | tf_op jit(solution)/shard_map/tile/pallas_call | solution.py:163
  65.6 5.9 %tile.8 = (f32[8,128,256]{2,1,0:T(8,128)S(1)}, f32[512,256]{1,0:T(8,128)S(1)}, f32[512,256]{1,0:T(8,128)S(1)}) custom-call(bf16[8,288,256]{2,1,0:T(8,128)(2,1)S(1)} %all-to-all-done.refs_0_, bf16[512,256]{1,0:T(8,128)(2,1)S(1)} %collective-permute-done.6.refs_1_, bf16[512,256]{1,0:T(8,128)(2,1)S(1)} %collective-permute-done.7.refs_2_, ...), custom_call_target="tpu_custom_call" | custom-call | flops 5368709120 | bytes 8388608 | tf_op jit(solution)/shard_map/tile/pallas_call | solution.py:163
  71.6 2.8 %collective-permute-start.12 = (bf16[512,256]{1,0:T(8,128)(2,1)S(1)}, bf16[512,256]{1,0:T(8,128)(2,1)S(1)}, u32[]{:S(2)}, u32[]{:S(2)}) collective-permute-start(bf16[512,256]{1,0:T(8,128)(2,1)S(1)} %convert_element_type.63), channel_id=1, source_target_pairs={{0,28},{4,0},{8,4},{12,8},{16,12},{20,16},{24,20},{28,24},{1,29},{... | collective-permute-start | bytes 786440 | tf_op jit(solution)/shard_map/ppermute | solution.py:184
  74.6 5.9 %tile.9 = (f32[8,128,256]{2,1,0:T(8,128)S(1)}, f32[512,256]{1,0:T(8,128)S(1)}, f32[512,256]{1,0:T(8,128)S(1)}) custom-call(bf16[8,288,256]{2,1,0:T(8,128)(2,1)S(1)} %all-to-all-done.refs_0_, bf16[512,256]{1,0:T(8,128)(2,1)S(1)} %collective-permute-done.4.refs_1_, bf16[512,256]{1,0:T(8,128)(2,1)S(1)} %collective-permute-done.5.refs_2_, ...), custom_call_target="tpu_custom_call" | custom-call | flops 5368709120 | bytes 8388608 | tf_op jit(solution)/shard_map/tile/pallas_call | solution.py:163
  80.6 2.7 %collective-permute-start.13 = (bf16[512,256]{1,0:T(8,128)(2,1)S(1)}, bf16[512,256]{1,0:T(8,128)(2,1)S(1)}, u32[]{:S(2)}, u32[]{:S(2)}) collective-permute-start(bf16[512,256]{1,0:T(8,128)(2,1)S(1)} %add_convert_fusion.2), channel_id=1, source_target_pairs={{0,28},{4,0},{8,4},{12,8},{16,12},{20,16},{24,20},{28,24},{1,29},{... | collective-permute-start | bytes 786440 | tf_op jit(solution)/shard_map/ppermute | solution.py:184
  83.4 3.1 %tile.10 = (f32[8,128,256]{2,1,0:T(8,128)S(1)}, f32[512,256]{1,0:T(8,128)S(1)}) custom-call(bf16[8,288,256]{2,1,0:T(8,128)(2,1)S(1)} %all-to-all-done.refs_0_, bf16[512,256]{1,0:T(8,128)(2,1)S(1)} %collective-permute-done.3.refs_1_, f32[8,128,256]{2,1,0:T(8,128)S(1)} %get-tuple-element.33.refs_2_, bf16[512,256]{1,0:T(8,128)(2,1)S(1)} %add_convert_fusion.3.refs_3_), custom_call_target="tpu_custom_call" | custom-call | flops 2684354560 | bytes 8388608 | tf_op jit(solution)/shard_map/tile/pallas_call | solution.py:163
  86.7 3.4 %collective-permute-start.16 = (bf16[512,256]{1,0:T(8,128)(2,1)S(1)}, bf16[512,256]{1,0:T(8,128)(2,1)S(1)}, u32[]{:S(2)}, u32[]{:S(2)}) collective-permute-start(bf16[512,256]{1,0:T(8,128)(2,1)S(1)} %add_convert_fusion.1.refs_3_), channel_id=1, source_target_pairs={{0,28},{4,0},{8,4},{12,8},{16,12},{20,16},{24,20},{28,24},{1,29},{... | collective-permute-start | bytes 786440 | tf_op jit(solution)/shard_map/ppermute | solution.py:184
  90.1 3.7 %tile.11 = (bf16[8,128,256]{2,1,0:T(8,128)(2,1)}, f32[512,256]{1,0:T(8,128)S(1)}) custom-call(bf16[8,288,256]{2,1,0:T(8,128)(2,1)S(1)} %all-to-all-done.refs_0_, bf16[512,256]{1,0:T(8,128)(2,1)S(1)} %collective-permute-done.2.refs_1_, f32[8,128,256]{2,1,0:T(8,128)S(1)} %get-tuple-element.35.refs_2_, bf16[512,256]{1,0:T(8,128)(2,1)S(1)} %add_convert_fusion.1.refs_3_), custom_call_target="tpu_custom_call" | custom-call | flops 2684354560 | bytes 8388608 | tf_op jit(solution)/shard_map/tile/pallas_call | solution.py:163
  94.0 3.8 %all-to-all-start.1 = ((bf16[8,128,256]{2,1,0:T(8,128)(2,1)}), bf16[8,128,256]{2,1,0:T(8,128)(2,1)S(1)}, u32[]{:S(2)}, u32[]{:S(2)}) async-start(bf16[8,128,256]{2,1,0:T(8,128)(2,1)} %get-tuple-element.39), calls=%async_computation.1 | async-start | bytes 1048576 | tf_op jit(solution)/shard_map/all_to_all | solution.py:231
  97.8 2.6 %collective-permute-done.15 = bf16[512,256]{1,0:T(8,128)(2,1)S(1)} collective-permute-done((bf16[512,256]{1,0:T(8,128)(2,1)S(1)}, bf16[512,256]{1,0:T(8,128)(2,1)S(1)}, u32[]{:S(2)}, u32[]{:S(2)}) %collective-permute-start.15) | collective-permute-done | bytes 262176 | tf_op jit(solution)/shard_map/ppermute | solution.py:184
  101.1 4.2 %all-to-all-done.1 = bf16[8,128,256]{2,1,0:T(8,128)(2,1)S(1)} async-done(((bf16[8,128,256]{2,1,0:T(8,128)(2,1)}), bf16[8,128,256]{2,1,0:T(8,128)(2,1)S(1)}, u32[]{:S(2)}, u32[]{:S(2)}) %all-to-all-start.1) | async-done | bytes 524320 | tf_op jit(solution)/shard_map/all_to_all | solution.py:231
  106.0 11.1 %collective-permute-start.18 = (bf16[3,128,128]{2,1,0:T(8,128)(2,1)S(1)}, bf16[3,128,128]{2,1,0:T(8,128)(2,1)S(1)}, u32[]{:S(2)}, u32[]{:S(2)}) collective-permute-start(bf16[3,128,128]{2,1,0:T(8,128)(2,1)S(1)} %slice.58), channel_id=1, source_target_pairs={{0,1},{1,0},{2,3},{3,2},{4,5},{5,4},{6,7},{7,6},{8,9},{9,8},{10,11... | collective-permute-start | bytes 294920 | tf_op jit(solution)/shard_map/ppermute | solution.py:184
  (53 shorter events, 12.2 us)
Async XLA Ops:
  2.4 4.4 %collective-permute-start = (bf16[272,256]{1,0:T(8,128)(2,1)}, bf16[272,256]{1,0:T(8,128)(2,1)S(1)}, u32[]{:S(2)}, u32[]{:S(2)}) collective-permute-start(bf16[272,256]{1,0:T(8,128)(2,1)} %get-tuple-element.24), channel_id=1, source_target_pairs={{0,1},{1,0},{2,3},{3,2},{4,5},{5,4},{6,7},{7,6},{8,9},{9,8},{10,11... | collective-permute-start | bytes 417800 | tf_op jit(solution)/shard_map/ppermute | solution.py:184
  6.9 0.7 copy-start
  9.7 3.7 %copy-start.1 = (bf16[256,256]{1,0:T(8,128)(2,1)S(1)}, bf16[256,256]{1,0:T(8,128)(2,1)}, u32[]{:S(2)}) copy-start(bf16[256,256]{1,0:T(8,128)(2,1)} %get-tuple-element.26) | copy-start | bytes 393220
  9.7 43.1 %all-to-all-start = ((bf16[8,288,256]{2,1,0:T(8,128)(2,1)}), bf16[8,288,256]{2,1,0:T(8,128)(2,1)S(1)}, u32[]{:S(2)}, u32[]{:S(2)}) async-start(bf16[8,288,256]{2,1,0:T(8,128)(2,1)} %get-tuple-element.25), calls=%async_computation | async-start | bytes 2359296 | tf_op jit(solution)/shard_map/all_to_all | solution.py:197
  13.4 18.4 %collective-permute-start.1 = (bf16[256,256]{1,0:T(8,128)(2,1)S(1)}, bf16[256,256]{1,0:T(8,128)(2,1)S(1)}, u32[]{:S(2)}, u32[]{:S(2)}) collective-permute-start(bf16[256,256]{1,0:T(8,128)(2,1)S(1)} %copy-done.1), channel_id=1, source_target_pairs={{0,32},{32,0},{1,33},{33,1},{2,34},{34,2},{3,35},{35,3},{4,36},{36... | collective-permute-start | bytes 393224 | tf_op jit(solution)/shard_map/ppermute | solution.py:184
  31.9 11.1 %collective-permute-start.3 = (bf16[512,256]{1,0:T(8,128)(2,1)S(1)}, bf16[512,256]{1,0:T(8,128)(2,1)S(1)}, u32[]{:S(2)}, u32[]{:S(2)}) collective-permute-start(bf16[512,256]{1,0:T(8,128)(2,1)S(1)} %constant_dynamic-update-slice_fusion.refs_1_), channel_id=1, source_target_pairs={{0,4},{4,8},{8,12},{12,16},{16,20},{20,24},{24,28},{28,0},{1,5},{5... | collective-permute-start | bytes 786440 | tf_op jit(solution)/shard_map/ppermute | solution.py:184
  33.6 9.4 %collective-permute-start.2 = (bf16[512,256]{1,0:T(8,128)(2,1)S(1)}, bf16[512,256]{1,0:T(8,128)(2,1)S(1)}, u32[]{:S(2)}, u32[]{:S(2)}) collective-permute-start(bf16[512,256]{1,0:T(8,128)(2,1)S(1)} %constant_dynamic-update-slice_fusion.refs_1_), channel_id=1, source_target_pairs={{0,28},{4,0},{8,4},{12,8},{16,12},{20,16},{24,20},{28,24},{1,29},{... | collective-permute-start | bytes 786440 | tf_op jit(solution)/shard_map/ppermute | solution.py:184
  42.9 7.2 %collective-permute-start.5 = (bf16[512,256]{1,0:T(8,128)(2,1)S(1)}, bf16[512,256]{1,0:T(8,128)(2,1)S(1)}, u32[]{:S(2)}, u32[]{:S(2)}) collective-permute-start(bf16[512,256]{1,0:T(8,128)(2,1)S(1)} %collective-permute-done.3.refs_1_), channel_id=1, source_target_pairs={{0,4},{4,8},{8,12},{12,16},{16,20},{20,24},{24,28},{28,0},{1,5},{5... | collective-permute-start | bytes 786440 | tf_op jit(solution)/shard_map/ppermute | solution.py:184
  43.0 7.2 %collective-permute-start.4 = (bf16[512,256]{1,0:T(8,128)(2,1)S(1)}, bf16[512,256]{1,0:T(8,128)(2,1)S(1)}, u32[]{:S(2)}, u32[]{:S(2)}) collective-permute-start(bf16[512,256]{1,0:T(8,128)(2,1)S(1)} %collective-permute-done.2.refs_1_), channel_id=1, source_target_pairs={{0,28},{4,0},{8,4},{12,8},{16,12},{20,16},{24,20},{28,24},{1,29},{... | collective-permute-start | bytes 786440 | tf_op jit(solution)/shard_map/ppermute | solution.py:184
  50.1 6.9 %collective-permute-start.7 = (bf16[512,256]{1,0:T(8,128)(2,1)S(1)}, bf16[512,256]{1,0:T(8,128)(2,1)S(1)}, u32[]{:S(2)}, u32[]{:S(2)}) collective-permute-start(bf16[512,256]{1,0:T(8,128)(2,1)S(1)} %collective-permute-done.5.refs_2_), channel_id=1, source_target_pairs={{0,4},{4,8},{8,12},{12,16},{16,20},{20,24},{24,28},{28,0},{1,5},{5... | collective-permute-start | bytes 786440 | tf_op jit(solution)/shard_map/ppermute | solution.py:184
  50.1 7.0 %collective-permute-start.6 = (bf16[512,256]{1,0:T(8,128)(2,1)S(1)}, bf16[512,256]{1,0:T(8,128)(2,1)S(1)}, u32[]{:S(2)}, u32[]{:S(2)}) collective-permute-start(bf16[512,256]{1,0:T(8,128)(2,1)S(1)} %collective-permute-done.4.refs_1_), channel_id=1, source_target_pairs={{0,28},{4,0},{8,4},{12,8},{16,12},{20,16},{24,20},{28,24},{1,29},{... | collective-permute-start | bytes 786440 | tf_op jit(solution)/shard_map/ppermute | solution.py:184
  57.1 5.1 %collective-permute-start.8 = (bf16[256,256]{1,0:T(8,128)(2,1)S(1)}, bf16[256,256]{1,0:T(8,128)(2,1)S(1)}, u32[]{:S(2)}, u32[]{:S(2)}) collective-permute-start(bf16[256,256]{1,0:T(8,128)(2,1)S(1)} %slice_add_fusion.2), channel_id=1, source_target_pairs={{0,4},{4,8},{8,12},{12,16},{16,20},{20,24},{24,28},{28,0},{1,5},{5... | collective-permute-start | bytes 393224 | tf_op jit(solution)/shard_map/ppermute | solution.py:184
  57.2 5.0 %collective-permute-start.9 = (bf16[256,256]{1,0:T(8,128)(2,1)S(1)}, bf16[256,256]{1,0:T(8,128)(2,1)S(1)}, u32[]{:S(2)}, u32[]{:S(2)}) collective-permute-start(bf16[256,256]{1,0:T(8,128)(2,1)S(1)} %slice_add_fusion.1), channel_id=1, source_target_pairs={{0,28},{4,0},{8,4},{12,8},{16,12},{20,16},{24,20},{28,24},{1,29},{... | collective-permute-start | bytes 393224 | tf_op jit(solution)/shard_map/ppermute | solution.py:184
  65.3 9.1 %collective-permute-start.10 = (bf16[512,256]{1,0:T(8,128)(2,1)S(1)}, bf16[512,256]{1,0:T(8,128)(2,1)S(1)}, u32[]{:S(2)}, u32[]{:S(2)}) collective-permute-start(bf16[512,256]{1,0:T(8,128)(2,1)S(1)} %convert_element_type.58.refs_4_), channel_id=1, source_target_pairs={{0,4},{4,8},{8,12},{12,16},{16,20},{20,24},{24,28},{28,0},{1,5},{5... | collective-permute-start | bytes 786440 | tf_op jit(solution)/shard_map/ppermute | solution.py:184
  71.6 8.9 %collective-permute-start.12 = (bf16[512,256]{1,0:T(8,128)(2,1)S(1)}, bf16[512,256]{1,0:T(8,128)(2,1)S(1)}, u32[]{:S(2)}, u32[]{:S(2)}) collective-permute-start(bf16[512,256]{1,0:T(8,128)(2,1)S(1)} %convert_element_type.63), channel_id=1, source_target_pairs={{0,28},{4,0},{8,4},{12,8},{16,12},{20,16},{24,20},{28,24},{1,29},{... | collective-permute-start | bytes 786440 | tf_op jit(solution)/shard_map/ppermute | solution.py:184
  74.5 8.8 %collective-permute-start.11 = (bf16[512,256]{1,0:T(8,128)(2,1)S(1)}, bf16[512,256]{1,0:T(8,128)(2,1)S(1)}, u32[]{:S(2)}, u32[]{:S(2)}) collective-permute-start(bf16[512,256]{1,0:T(8,128)(2,1)S(1)} %add_convert_fusion.4.refs_4_), channel_id=1, source_target_pairs={{0,4},{4,8},{8,12},{12,16},{16,20},{20,24},{24,28},{28,0},{1,5},{5... | collective-permute-start | bytes 786440 | tf_op jit(solution)/shard_map/ppermute | solution.py:184
  80.6 6.0 %collective-permute-start.13 = (bf16[512,256]{1,0:T(8,128)(2,1)S(1)}, bf16[512,256]{1,0:T(8,128)(2,1)S(1)}, u32[]{:S(2)}, u32[]{:S(2)}) collective-permute-start(bf16[512,256]{1,0:T(8,128)(2,1)S(1)} %add_convert_fusion.2), channel_id=1, source_target_pairs={{0,28},{4,0},{8,4},{12,8},{16,12},{20,16},{24,20},{28,24},{1,29},{... | collective-permute-start | bytes 786440 | tf_op jit(solution)/shard_map/ppermute | solution.py:184
  83.3 10.5 %collective-permute-start.14 = (bf16[512,256]{1,0:T(8,128)(2,1)S(1)}, bf16[512,256]{1,0:T(8,128)(2,1)S(1)}, u32[]{:S(2)}, u32[]{:S(2)}) collective-permute-start(bf16[512,256]{1,0:T(8,128)(2,1)S(1)} %add_convert_fusion.3.refs_3_), channel_id=1, source_target_pairs={{0,4},{4,8},{8,12},{12,16},{16,20},{20,24},{24,28},{28,0},{1,5},{5... | collective-permute-start | bytes 786440 | tf_op jit(solution)/shard_map/ppermute | solution.py:184
  86.7 11.1 %collective-permute-start.16 = (bf16[512,256]{1,0:T(8,128)(2,1)S(1)}, bf16[512,256]{1,0:T(8,128)(2,1)S(1)}, u32[]{:S(2)}, u32[]{:S(2)}) collective-permute-start(bf16[512,256]{1,0:T(8,128)(2,1)S(1)} %add_convert_fusion.1.refs_3_), channel_id=1, source_target_pairs={{0,28},{4,0},{8,4},{12,8},{16,12},{20,16},{24,20},{28,24},{1,29},{... | collective-permute-start | bytes 786440 | tf_op jit(solution)/shard_map/ppermute | solution.py:184
  93.9 6.5 %collective-permute-start.15 = (bf16[512,256]{1,0:T(8,128)(2,1)S(1)}, bf16[512,256]{1,0:T(8,128)(2,1)S(1)}, u32[]{:S(2)}, u32[]{:S(2)}) collective-permute-start(bf16[512,256]{1,0:T(8,128)(2,1)S(1)} %add_convert_fusion), channel_id=1, source_target_pairs={{0,4},{4,8},{8,12},{12,16},{16,20},{20,24},{24,28},{28,0},{1,5},{5... | collective-permute-start | bytes 786440 | tf_op jit(solution)/shard_map/ppermute | solution.py:184
  94.0 11.3 %all-to-all-start.1 = ((bf16[8,128,256]{2,1,0:T(8,128)(2,1)}), bf16[8,128,256]{2,1,0:T(8,128)(2,1)S(1)}, u32[]{:S(2)}, u32[]{:S(2)}) async-start(bf16[8,128,256]{2,1,0:T(8,128)(2,1)} %get-tuple-element.39), calls=%async_computation.1 | async-start | bytes 1048576 | tf_op jit(solution)/shard_map/all_to_all | solution.py:231
  100.5 5.4 %collective-permute-start.17 = (bf16[256,256]{1,0:T(8,128)(2,1)S(1)}, bf16[256,256]{1,0:T(8,128)(2,1)S(1)}, u32[]{:S(2)}, u32[]{:S(2)}) collective-permute-start(bf16[256,256]{1,0:T(8,128)(2,1)S(1)} %slice.89), channel_id=1, source_target_pairs={{0,32},{32,0},{1,33},{33,1},{2,34},{34,2},{3,35},{35,3},{4,36},{36... | collective-permute-start | bytes 393224 | tf_op jit(solution)/shard_map/ppermute | solution.py:184
  106.0 12.1 %collective-permute-start.18 = (bf16[3,128,128]{2,1,0:T(8,128)(2,1)S(1)}, bf16[3,128,128]{2,1,0:T(8,128)(2,1)S(1)}, u32[]{:S(2)}, u32[]{:S(2)}) collective-permute-start(bf16[3,128,128]{2,1,0:T(8,128)(2,1)S(1)} %slice.58), channel_id=1, source_target_pairs={{0,1},{1,0},{2,3},{3,2},{4,5},{5,4},{6,7},{7,6},{8,9},{9,8},{10,11... | collective-permute-start | bytes 294920 | tf_op jit(solution)/shard_map/ppermute | solution.py:184

commit v10 on v3

--- a/solution.py
+++ b/solution.py
@@ -198,21 +198,20 @@
     def low(x):
         return x.astype(BF16)
 
-    total_q, far, own = tile_call(gathered, keys[4], keys[0], None, None, False)
-    up = low(far)
-    down = None
-    after = up
-    for by in (3, 2, 1):
-        up_in = shift(up, "z", 1)
-        down_in = None if down is None else shift(down, "z", -1)
+    total_q, du, dd = tile_call(gathered, keys[-3], keys[3], None, None, False)
+    up, down = low(du), low(dd)
+    up_in, down_in = shift(up, "z", 1), shift(down, "z", -1)
+    total_q, far, own = tile_call(gathered, keys[4], keys[0], total_q, up, False)
+    far = low(far)
+    after = far
+    for by in (2, 1):
         total_q, du, dd = tile_call(gathered, keys[-by], keys[by], total_q, after, by == 1)
-        up = low(du + up_in.astype(F32))
-        down = low(dd if down_in is None else dd + down_in.astype(F32))
+        up, down = low(du + up_in.astype(F32)), low(dd + down_in.astype(F32))
+        up_in, down_in = shift(up, "z", 1), shift(down, "z", -1)
         after = up
-    up_in = shift(up, "z", 1)
-    down_in = shift(down, "z", -1)
+    far_in = shift(far, "z", 4)
     returned = lax.all_to_all(total_q, GROUP, 0, 0, tiled=True)
-    grad_pair = own + up_in.astype(F32) + down_in.astype(F32)
+    grad_pair = own + far_in.astype(F32) + up_in.astype(F32) + down_in.astype(F32)
     grad_kv = grad_pair[:ROWS] + shift(low(grad_pair[ROWS:]), "xh", 1).astype(F32)
 
     grad_q = jnp.sum(returned.astype(F32), axis=0).T

time: 101 us -> 101 us (level)
  waiting for transfers between devices: 22.4 us -> 25.9 us
  starting transfers between devices: 46.3 us -> 43.8 us
    all_to_all x1, waiting for transfers between devices: 3.15 us -> 5.55 us  [local(): returned = lax.all_to_all(total_q, GROUP, 0, 0, tiled=True)]
    ppermute x19, starting transfers between devices: 36.2 us -> 34.7 us  [shift(): return lax.ppermute(x, axis, [(i, (i + by) % n) for i in range(n)])]
    ppermute x19, waiting for transfers between devices: 19.3 us -> 20.3 us  [shift(): return lax.ppermute(x, axis, [(i, (i + by) % n) for i in range(n)])]
  transfers between devices with their start and end apart: 21 -> 21, of which waited for: 10 -> 8; matrix products, arithmetic and copies ran while one was open for 2% -> 1% of each run, Pallas kernels for 18% -> 24%
where the time goes in v10:
time: 101 us
  starting transfers between devices  43.8 us (43%)
  Pallas kernels  28.2 us (28%)
  waiting for transfers between devices  25.9 us (26%)
  other arithmetic  1.27 us (1%)
    ppermute x19, starting transfers between devices, shift(): return lax.ppermute(x, axis, [(i, (i + by) % n) for i in range(n)])  34.7 us
    pallas_call x4, Pallas kernels, tile_call(): pl.pallas_call(functools.partial(tile_kernel, first, chips), grid=(groups...  24.3 us
    ppermute x19, waiting for transfers between devices, shift(): return lax.ppermute(x, axis, [(i, (i + by) % n) for i in range(n)])  20.3 us
    all_to_all x1, waiting for transfers between devices, local(): returned = lax.all_to_all(total_q, GROUP, 0, 0, tiled=True)  5.55 us
    all_to_all x1, starting transfers between devices, local(): returned = lax.all_to_all(total_q, GROUP, 0, 0, tiled=True)  4.76 us
    all_to_all x1, starting transfers between devices, local(): gathered = lax.all_to_all(spread, GROUP, 0, 0, tiled=True)  4.35 us
    pallas_call x1, Pallas kernels, spread_call(): pl.pallas_call(spread_kernel, in_specs=[pl.BlockSpec(memory_space=pltpu.V...  2.11 us
  transfers between devices with their start and end apart: 21, of which 8 were waited for; matrix products, arithmetic and copies ran while one was open for 1% of the time, Pallas kernels for 24%

profile of v10, /device:TPU:1, one launch (start us, length us, event | category | flops | bytes accessed | tf_op | source)
XLA Modules:
  0.0 100.9 jit_solution(7309140090326638199)
XLA Ops:
  0.6 1.8 %pack.1 = (bf16[144,256]{1,0:T(8,128)(2,1)}, bf16[128,256]{1,0:T(8,128)(2,1)}, bf16[272,256]{1,0:T(8,128)(2,1)}) custom-call(s32[1]{0:T(128)} %bitcast.core_ref, bf16[128,256]{1,0:T(8,128)(2,1)} %q_ref.1, bf16[128,256]{1,0:T(8,128)(2,1)} %k_ref.1, bf16[128,256]{1,0:T(8,128)(2,1)} %v_ref.1, bf16[128,256]{1,0:T(8,128)(2,1)} %o_ref.1, bf16[128,256]{1,0:T(8,128)(2,1)} %g_ref.1, ...), custom_call_target="tpu_custom_call" | custom-call | tf_op jit(solution)/shard_map/pack/pallas_call | solution.py:58
  2.4 3.2 %collective-permute-start = (bf16[272,256]{1,0:T(8,128)(2,1)}, bf16[272,256]{1,0:T(8,128)(2,1)S(1)}, u32[]{:S(2)}, u32[]{:S(2)}) collective-permute-start(bf16[272,256]{1,0:T(8,128)(2,1)} %get-tuple-element.22), channel_id=1, source_target_pairs={{0,1},{1,0},{2,3},{3,2},{4,5},{5,4},{6,7},{7,6},{8,9},{9,8},{10,11... | collective-permute-start | bytes 417800 | tf_op jit(solution)/shard_map/ppermute | solution.py:176
  7.5 2.1 %spread.1 = (bf16[8,288,256]{2,1,0:T(8,128)(2,1)}, bf16[256,256]{1,0:T(8,128)(2,1)}) custom-call(bf16[144,256]{1,0:T(8,128)(2,1)} %get-tuple-element.20.mine_ref, bf16[128,256]{1,0:T(8,128)(2,1)} %get-tuple-element.21.kv_ref, bf16[272,256]{1,0:T(8,128)(2,1)} %copy-done), custom_call_target="tpu_custom_call" | custom-call | tf_op jit(solution)/shard_map/spread/pallas_call | solution.py:82
  10.7 4.4 %all-to-all-start = ((bf16[8,288,256]{2,1,0:T(8,128)(2,1)}), bf16[8,288,256]{2,1,0:T(8,128)(2,1)S(1)}, u32[]{:S(2)}, u32[]{:S(2)}) async-start(bf16[8,288,256]{2,1,0:T(8,128)(2,1)} %get-tuple-element.23), calls=%async_computation | async-start | bytes 2359296 | tf_op jit(solution)/shard_map/all_to_all | solution.py:189
  16.8 4.0 %collective-permute-start.2 = (bf16[512,256]{1,0:T(8,128)(2,1)S(1)}, bf16[512,256]{1,0:T(8,128)(2,1)S(1)}, u32[]{:S(2)}, u32[]{:S(2)}) collective-permute-start(bf16[512,256]{1,0:T(8,128)(2,1)S(1)} %constant_dynamic-update-slice_fusion.refs_2_), channel_id=1, source_target_pairs={{0,28},{4,0},{8,4},{12,8},{16,12},{20,16},{24,20},{28,24},{1,29},{... | collective-permute-start | bytes 786440 | tf_op jit(solution)/shard_map/ppermute | solution.py:176
  20.8 5.7 %collective-permute-done.3.refs_2_ = bf16[512,256]{1,0:T(8,128)(2,1)S(1)} collective-permute-done((bf16[512,256]{1,0:T(8,128)(2,1)S(1)}, bf16[512,256]{1,0:T(8,128)(2,1)S(1)}, u32[]{:S(2)}, u32[]{:S(2)}) %collective-permute-start.3) | collective-permute-done | bytes 262176 | tf_op jit(solution)/shard_map/ppermute | solution.py:176
  26.5 2.7 %collective-permute-start.4 = (bf16[512,256]{1,0:T(8,128)(2,1)S(1)}, bf16[512,256]{1,0:T(8,128)(2,1)S(1)}, u32[]{:S(2)}, u32[]{:S(2)}) collective-permute-start(bf16[512,256]{1,0:T(8,128)(2,1)S(1)} %collective-permute-done.2.refs_1_), channel_id=1, source_target_pairs={{0,28},{4,0},{8,4},{12,8},{16,12},{20,16},{24,20},{28,24},{1,29},{... | collective-permute-start | bytes 786440 | tf_op jit(solution)/shard_map/ppermute | solution.py:176
  29.2 4.8 %collective-permute-done.5.refs_2_ = bf16[512,256]{1,0:T(8,128)(2,1)S(1)} collective-permute-done((bf16[512,256]{1,0:T(8,128)(2,1)S(1)}, bf16[512,256]{1,0:T(8,128)(2,1)S(1)}, u32[]{:S(2)}, u32[]{:S(2)}) %collective-permute-start.5) | collective-permute-done | bytes 262176 | tf_op jit(solution)/shard_map/ppermute | solution.py:176
  34.0 2.7 %collective-permute-start.8 = (bf16[512,256]{1,0:T(8,128)(2,1)S(1)}, bf16[512,256]{1,0:T(8,128)(2,1)S(1)}, u32[]{:S(2)}, u32[]{:S(2)}) collective-permute-start(bf16[512,256]{1,0:T(8,128)(2,1)S(1)} %collective-permute-done.4.refs_1_), channel_id=1, source_target_pairs={{0,28},{4,0},{8,4},{12,8},{16,12},{20,16},{24,20},{28,24},{1,29},{... | collective-permute-start | bytes 786440 | tf_op jit(solution)/shard_map/ppermute | solution.py:176
  36.6 3.8 %collective-permute-done.6.refs_2_ = bf16[512,256]{1,0:T(8,128)(2,1)S(1)} collective-permute-done((bf16[512,256]{1,0:T(8,128)(2,1)S(1)}, bf16[512,256]{1,0:T(8,128)(2,1)S(1)}, u32[]{:S(2)}, u32[]{:S(2)}) %collective-permute-start.6) | collective-permute-done | bytes 262176 | tf_op jit(solution)/shard_map/ppermute | solution.py:176
  40.5 2.7 %collective-permute-start.9 = (bf16[256,256]{1,0:T(8,128)(2,1)S(1)}, bf16[256,256]{1,0:T(8,128)(2,1)S(1)}, u32[]{:S(2)}, u32[]{:S(2)}) collective-permute-start(bf16[256,256]{1,0:T(8,128)(2,1)S(1)} %slice.48), channel_id=1, source_target_pairs={{0,28},{4,0},{8,4},{12,8},{16,12},{20,16},{24,20},{28,24},{1,29},{... | collective-permute-start | bytes 393224 | tf_op jit(solution)/shard_map/ppermute | solution.py:176
  43.3 5.8 %tile.4 = (f32[8,128,256]{2,1,0:T(8,128)S(1)}, f32[512,256]{1,0:T(8,128)S(1)}, f32[512,256]{1,0:T(8,128)S(1)}) custom-call(bf16[8,288,256]{2,1,0:T(8,128)(2,1)S(1)} %all-to-all-done.refs_0_, bf16[512,256]{1,0:T(8,128)(2,1)S(1)} %collective-permute-done.8.refs_1_, bf16[512,256]{1,0:T(8,128)(2,1)S(1)} %collective-permute-done.6.refs_2_), custom_call_target="tpu_custom_call" | custom-call | flops 5368709120 | bytes 8388608 | tf_op jit(solution)/shard_map/tile/pallas_call | solution.py:150
  49.3 1.4 %collective-permute-start.10 = (bf16[512,256]{1,0:T(8,128)(2,1)S(1)}, bf16[512,256]{1,0:T(8,128)(2,1)S(1)}, u32[]{:S(2)}, u32[]{:S(2)}) collective-permute-start(bf16[512,256]{1,0:T(8,128)(2,1)S(1)} %convert_element_type.50.refs_4_), channel_id=1, source_target_pairs={{0,4},{4,8},{8,12},{12,16},{16,20},{20,24},{24,28},{28,0},{1,5},{5... | collective-permute-start | bytes 786440 | tf_op jit(solution)/shard_map/ppermute | solution.py:176
  50.8 5.9 %tile.5 = (f32[8,128,256]{2,1,0:T(8,128)S(1)}, f32[512,256]{1,0:T(8,128)S(1)}, f32[512,256]{1,0:T(8,128)S(1)}) custom-call(bf16[8,288,256]{2,1,0:T(8,128)(2,1)S(1)} %all-to-all-done.refs_0_, bf16[512,256]{1,0:T(8,128)(2,1)S(1)} %pad_maximum_fusion.refs_1_, bf16[512,256]{1,0:T(8,128)(2,1)S(1)} %constant_dynamic-update-slice_fusion.refs_2_, ...), custom_call_target="tpu_custom_call" | custom-call | flops 5368709120 | bytes 8388608 | tf_op jit(solution)/shard_map/tile/pallas_call | solution.py:150
  56.7 3.5 %collective-permute-start.11 = (bf16[512,256]{1,0:T(8,128)(2,1)S(1)}, bf16[512,256]{1,0:T(8,128)(2,1)S(1)}, u32[]{:S(2)}, u32[]{:S(2)}) collective-permute-start(bf16[512,256]{1,0:T(8,128)(2,1)S(1)} %convert_element_type.51.refs_4_), channel_id=1, source_target_pairs={{0,16},{4,20},{8,24},{12,28},{16,0},{20,4},{24,8},{28,12},{1,17},{... | collective-permute-start | bytes 786440 | tf_op jit(solution)/shard_map/ppermute | solution.py:176
  60.2 5.9 %tile.6 = (f32[8,128,256]{2,1,0:T(8,128)S(1)}, f32[512,256]{1,0:T(8,128)S(1)}, f32[512,256]{1,0:T(8,128)S(1)}) custom-call(bf16[8,288,256]{2,1,0:T(8,128)(2,1)S(1)} %all-to-all-done.refs_0_, bf16[512,256]{1,0:T(8,128)(2,1)S(1)} %collective-permute-done.4.refs_1_, bf16[512,256]{1,0:T(8,128)(2,1)S(1)} %collective-permute-done.5.refs_2_, ...), custom_call_target="tpu_custom_call" | custom-call | flops 5368709120 | bytes 8388608 | tf_op jit(solution)/shard_map/tile/pallas_call | solution.py:150
  66.3 2.7 %collective-permute-start.15 = (bf16[512,256]{1,0:T(8,128)(2,1)S(1)}, bf16[512,256]{1,0:T(8,128)(2,1)S(1)}, u32[]{:S(2)}, u32[]{:S(2)}) collective-permute-start(bf16[512,256]{1,0:T(8,128)(2,1)S(1)} %add_convert_fusion.1), channel_id=1, source_target_pairs={{0,28},{4,0},{8,4},{12,8},{16,12},{20,16},{24,20},{28,24},{1,29},{... | collective-permute-start | bytes 786440 | tf_op jit(solution)/shard_map/ppermute | solution.py:176
  69.1 6.6 %tile.7 = (bf16[8,128,256]{2,1,0:T(8,128)(2,1)}, f32[512,256]{1,0:T(8,128)S(1)}, f32[512,256]{1,0:T(8,128)S(1)}) custom-call(bf16[8,288,256]{2,1,0:T(8,128)(2,1)S(1)} %all-to-all-done.refs_0_, bf16[512,256]{1,0:T(8,128)(2,1)S(1)} %collective-permute-done.2.refs_1_, bf16[512,256]{1,0:T(8,128)(2,1)S(1)} %collective-permute-done.3.refs_2_, ...), custom_call_target="tpu_custom_call" | custom-call | flops 5368709120 | bytes 8388608 | tf_op jit(solution)/shard_map/tile/pallas_call | solution.py:150
  75.7 2.9 %collective-permute-done.12 = bf16[512,256]{1,0:T(8,128)(2,1)S(1)} collective-permute-done((bf16[512,256]{1,0:T(8,128)(2,1)S(1)}, bf16[512,256]{1,0:T(8,128)(2,1)S(1)}, u32[]{:S(2)}, u32[]{:S(2)}) %collective-permute-start.12) | collective-permute-done | bytes 262176 | tf_op jit(solution)/shard_map/ppermute | solution.py:176
  78.8 2.7 %collective-permute-start.16 = (bf16[512,256]{1,0:T(8,128)(2,1)S(1)}, bf16[512,256]{1,0:T(8,128)(2,1)S(1)}, u32[]{:S(2)}, u32[]{:S(2)}) collective-permute-start(bf16[512,256]{1,0:T(8,128)(2,1)S(1)} %add_convert_fusion), channel_id=1, source_target_pairs={{0,28},{4,0},{8,4},{12,8},{16,12},{20,16},{24,20},{28,24},{1,29},{... | collective-permute-start | bytes 786440 | tf_op jit(solution)/shard_map/ppermute | solution.py:176
  81.5 4.8 %all-to-all-start.1 = ((bf16[8,128,256]{2,1,0:T(8,128)(2,1)}), bf16[8,128,256]{2,1,0:T(8,128)(2,1)S(1)}, u32[]{:S(2)}, u32[]{:S(2)}) async-start(bf16[8,128,256]{2,1,0:T(8,128)(2,1)} %get-tuple-element.31), calls=%async_computation.1 | async-start | bytes 1048576 | tf_op jit(solution)/shard_map/all_to_all | solution.py:213
  86.4 1.8 %collective-permute-start.17 = (bf16[256,256]{1,0:T(8,128)(2,1)S(1)}, bf16[256,256]{1,0:T(8,128)(2,1)S(1)}, u32[]{:S(2)}, u32[]{:S(2)}) collective-permute-start(bf16[256,256]{1,0:T(8,128)(2,1)S(1)} %slice.83), channel_id=1, source_target_pairs={{0,32},{32,0},{1,33},{33,1},{2,34},{34,2},{3,35},{35,3},{4,36},{36... | collective-permute-start | bytes 393224 | tf_op jit(solution)/shard_map/ppermute | solution.py:176
  88.3 5.6 %all-to-all-done.1 = bf16[8,128,256]{2,1,0:T(8,128)(2,1)S(1)} async-done(((bf16[8,128,256]{2,1,0:T(8,128)(2,1)}), bf16[8,128,256]{2,1,0:T(8,128)(2,1)S(1)}, u32[]{:S(2)}, u32[]{:S(2)}) %all-to-all-start.1) | async-done | bytes 524320 | tf_op jit(solution)/shard_map/all_to_all | solution.py:213
  94.1 5.2 %collective-permute-start.18 = (bf16[3,128,128]{2,1,0:T(8,128)(2,1)S(1)}, bf16[3,128,128]{2,1,0:T(8,128)(2,1)S(1)}, u32[]{:S(2)}, u32[]{:S(2)}) collective-permute-start(bf16[3,128,128]{2,1,0:T(8,128)(2,1)S(1)} %slice.54), channel_id=1, source_target_pairs={{0,1},{1,0},{2,3},{3,2},{4,5},{5,4},{6,7},{7,6},{8,9},{9,8},{10,11... | collective-permute-start | bytes 294920 | tf_op jit(solution)/shard_map/ppermute | solution.py:176
  (50 shorter events, 7.4 us)
Async XLA Ops:
  2.4 4.4 %collective-permute-start = (bf16[272,256]{1,0:T(8,128)(2,1)}, bf16[272,256]{1,0:T(8,128)(2,1)S(1)}, u32[]{:S(2)}, u32[]{:S(2)}) collective-permute-start(bf16[272,256]{1,0:T(8,128)(2,1)} %get-tuple-element.22), channel_id=1, source_target_pairs={{0,1},{1,0},{2,3},{3,2},{4,5},{5,4},{6,7},{7,6},{8,9},{9,8},{10,11... | collective-permute-start | bytes 417800 | tf_op jit(solution)/shard_map/ppermute | solution.py:176
  6.9 0.7 copy-start
  9.7 6.4 %collective-permute-start.1 = (bf16[256,256]{1,0:T(8,128)(2,1)}, bf16[256,256]{1,0:T(8,128)(2,1)S(1)}, u32[]{:S(2)}, u32[]{:S(2)}) collective-permute-start(bf16[256,256]{1,0:T(8,128)(2,1)} %get-tuple-element.24), channel_id=1, source_target_pairs={{0,32},{32,0},{1,33},{33,1},{2,34},{34,2},{3,35},{35,3},{4,36},{36... | collective-permute-start | bytes 393224 | tf_op jit(solution)/shard_map/ppermute | solution.py:176
  10.7 4.4 %copy-start.1 = (bf16[256,256]{1,0:T(8,128)(2,1)S(1)}, bf16[256,256]{1,0:T(8,128)(2,1)}, u32[]{:S(2)}) copy-start(bf16[256,256]{1,0:T(8,128)(2,1)} %get-tuple-element.24) | copy-start | bytes 393220
  10.7 32.6 %all-to-all-start = ((bf16[8,288,256]{2,1,0:T(8,128)(2,1)}), bf16[8,288,256]{2,1,0:T(8,128)(2,1)S(1)}, u32[]{:S(2)}, u32[]{:S(2)}) async-start(bf16[8,288,256]{2,1,0:T(8,128)(2,1)} %get-tuple-element.23), calls=%async_computation | async-start | bytes 2359296 | tf_op jit(solution)/shard_map/all_to_all | solution.py:189
  16.1 10.4 %collective-permute-start.3 = (bf16[512,256]{1,0:T(8,128)(2,1)S(1)}, bf16[512,256]{1,0:T(8,128)(2,1)S(1)}, u32[]{:S(2)}, u32[]{:S(2)}) collective-permute-start(bf16[512,256]{1,0:T(8,128)(2,1)S(1)} %constant_dynamic-update-slice_fusion.refs_2_), channel_id=1, source_target_pairs={{0,4},{4,8},{8,12},{12,16},{16,20},{20,24},{24,28},{28,0},{1,5},{5... | collective-permute-start | bytes 786440 | tf_op jit(solution)/shard_map/ppermute | solution.py:176
  16.8 9.7 %collective-permute-start.2 = (bf16[512,256]{1,0:T(8,128)(2,1)S(1)}, bf16[512,256]{1,0:T(8,128)(2,1)S(1)}, u32[]{:S(2)}, u32[]{:S(2)}) collective-permute-start(bf16[512,256]{1,0:T(8,128)(2,1)S(1)} %constant_dynamic-update-slice_fusion.refs_2_), channel_id=1, source_target_pairs={{0,28},{4,0},{8,4},{12,8},{16,12},{20,16},{24,20},{28,24},{1,29},{... | collective-permute-start | bytes 786440 | tf_op jit(solution)/shard_map/ppermute | solution.py:176
  26.5 7.5 %collective-permute-start.5 = (bf16[512,256]{1,0:T(8,128)(2,1)S(1)}, bf16[512,256]{1,0:T(8,128)(2,1)S(1)}, u32[]{:S(2)}, u32[]{:S(2)}) collective-permute-start(bf16[512,256]{1,0:T(8,128)(2,1)S(1)} %collective-permute-done.3.refs_2_), channel_id=1, source_target_pairs={{0,4},{4,8},{8,12},{12,16},{16,20},{20,24},{24,28},{28,0},{1,5},{5... | collective-permute-start | bytes 786440 | tf_op jit(solution)/shard_map/ppermute | solution.py:176
  26.5 7.5 %collective-permute-start.4 = (bf16[512,256]{1,0:T(8,128)(2,1)S(1)}, bf16[512,256]{1,0:T(8,128)(2,1)S(1)}, u32[]{:S(2)}, u32[]{:S(2)}) collective-permute-start(bf16[512,256]{1,0:T(8,128)(2,1)S(1)} %collective-permute-done.2.refs_1_), channel_id=1, source_target_pairs={{0,28},{4,0},{8,4},{12,8},{16,12},{20,16},{24,20},{28,24},{1,29},{... | collective-permute-start | bytes 786440 | tf_op jit(solution)/shard_map/ppermute | solution.py:176
  34.0 6.4 %collective-permute-start.6 = (bf16[512,256]{1,0:T(8,128)(2,1)S(1)}, bf16[512,256]{1,0:T(8,128)(2,1)S(1)}, u32[]{:S(2)}, u32[]{:S(2)}) collective-permute-start(bf16[512,256]{1,0:T(8,128)(2,1)S(1)} %collective-permute-done.5.refs_2_), channel_id=1, source_target_pairs={{0,4},{4,8},{8,12},{12,16},{16,20},{20,24},{24,28},{28,0},{1,5},{5... | collective-permute-start | bytes 786440 | tf_op jit(solution)/shard_map/ppermute | solution.py:176
  34.0 6.5 %collective-permute-start.8 = (bf16[512,256]{1,0:T(8,128)(2,1)S(1)}, bf16[512,256]{1,0:T(8,128)(2,1)S(1)}, u32[]{:S(2)}, u32[]{:S(2)}) collective-permute-start(bf16[512,256]{1,0:T(8,128)(2,1)S(1)} %collective-permute-done.4.refs_1_), channel_id=1, source_target_pairs={{0,28},{4,0},{8,4},{12,8},{16,12},{20,16},{24,20},{28,24},{1,29},{... | collective-permute-start | bytes 786440 | tf_op jit(solution)/shard_map/ppermute | solution.py:176
  40.4 10.3 %collective-permute-start.7 = (bf16[256,256]{1,0:T(8,128)(2,1)S(1)}, bf16[256,256]{1,0:T(8,128)(2,1)S(1)}, u32[]{:S(2)}, u32[]{:S(2)}) collective-permute-start(bf16[256,256]{1,0:T(8,128)(2,1)S(1)} %slice.47), channel_id=1, source_target_pairs={{0,4},{4,8},{8,12},{12,16},{16,20},{20,24},{24,28},{28,0},{1,5},{5... | collective-permute-start | bytes 393224 | tf_op jit(solution)/shard_map/ppermute | solution.py:176
  40.5 10.2 %collective-permute-start.9 = (bf16[256,256]{1,0:T(8,128)(2,1)S(1)}, bf16[256,256]{1,0:T(8,128)(2,1)S(1)}, u32[]{:S(2)}, u32[]{:S(2)}) collective-permute-start(bf16[256,256]{1,0:T(8,128)(2,1)S(1)} %slice.48), channel_id=1, source_target_pairs={{0,28},{4,0},{8,4},{12,8},{16,12},{20,16},{24,20},{28,24},{1,29},{... | collective-permute-start | bytes 393224 | tf_op jit(solution)/shard_map/ppermute | solution.py:176
  49.2 17.1 %collective-permute-start.14 = (bf16[512,256]{1,0:T(8,128)(2,1)S(1)}, bf16[512,256]{1,0:T(8,128)(2,1)S(1)}, u32[]{:S(2)}, u32[]{:S(2)}) collective-permute-start(bf16[512,256]{1,0:T(8,128)(2,1)S(1)} %convert_element_type.59), channel_id=1, source_target_pairs={{0,28},{4,0},{8,4},{12,8},{16,12},{20,16},{24,20},{28,24},{1,29},{... | collective-permute-start | bytes 786440 | tf_op jit(solution)/shard_map/ppermute | solution.py:176
  49.3 16.8 %collective-permute-start.10 = (bf16[512,256]{1,0:T(8,128)(2,1)S(1)}, bf16[512,256]{1,0:T(8,128)(2,1)S(1)}, u32[]{:S(2)}, u32[]{:S(2)}) collective-permute-start(bf16[512,256]{1,0:T(8,128)(2,1)S(1)} %convert_element_type.50.refs_4_), channel_id=1, source_target_pairs={{0,4},{4,8},{8,12},{12,16},{16,20},{20,24},{24,28},{28,0},{1,5},{5... | collective-permute-start | bytes 786440 | tf_op jit(solution)/shard_map/ppermute | solution.py:176
  56.7 29.5 %collective-permute-start.11 = (bf16[512,256]{1,0:T(8,128)(2,1)S(1)}, bf16[512,256]{1,0:T(8,128)(2,1)S(1)}, u32[]{:S(2)}, u32[]{:S(2)}) collective-permute-start(bf16[512,256]{1,0:T(8,128)(2,1)S(1)} %convert_element_type.51.refs_4_), channel_id=1, source_target_pairs={{0,16},{4,20},{8,24},{12,28},{16,0},{20,4},{24,8},{28,12},{1,17},{... | collective-permute-start | bytes 786440 | tf_op jit(solution)/shard_map/ppermute | solution.py:176
  66.2 12.4 %collective-permute-start.12 = (bf16[512,256]{1,0:T(8,128)(2,1)S(1)}, bf16[512,256]{1,0:T(8,128)(2,1)S(1)}, u32[]{:S(2)}, u32[]{:S(2)}) collective-permute-start(bf16[512,256]{1,0:T(8,128)(2,1)S(1)} %add_convert_fusion.3.refs_4_), channel_id=1, source_target_pairs={{0,4},{4,8},{8,12},{12,16},{16,20},{20,24},{24,28},{28,0},{1,5},{5... | collective-permute-start | bytes 786440 | tf_op jit(solution)/shard_map/ppermute | solution.py:176
  66.3 12.4 %collective-permute-start.15 = (bf16[512,256]{1,0:T(8,128)(2,1)S(1)}, bf16[512,256]{1,0:T(8,128)(2,1)S(1)}, u32[]{:S(2)}, u32[]{:S(2)}) collective-permute-start(bf16[512,256]{1,0:T(8,128)(2,1)S(1)} %add_convert_fusion.1), channel_id=1, source_target_pairs={{0,28},{4,0},{8,4},{12,8},{16,12},{20,16},{24,20},{28,24},{1,29},{... | collective-permute-start | bytes 786440 | tf_op jit(solution)/shard_map/ppermute | solution.py:176
  78.6 7.7 %collective-permute-start.13 = (bf16[512,256]{1,0:T(8,128)(2,1)S(1)}, bf16[512,256]{1,0:T(8,128)(2,1)S(1)}, u32[]{:S(2)}, u32[]{:S(2)}) collective-permute-start(bf16[512,256]{1,0:T(8,128)(2,1)S(1)} %add_convert_fusion.2), channel_id=1, source_target_pairs={{0,4},{4,8},{8,12},{12,16},{16,20},{20,24},{24,28},{28,0},{1,5},{5... | collective-permute-start | bytes 786440 | tf_op jit(solution)/shard_map/ppermute | solution.py:176
  78.8 7.5 %collective-permute-start.16 = (bf16[512,256]{1,0:T(8,128)(2,1)S(1)}, bf16[512,256]{1,0:T(8,128)(2,1)S(1)}, u32[]{:S(2)}, u32[]{:S(2)}) collective-permute-start(bf16[512,256]{1,0:T(8,128)(2,1)S(1)} %add_convert_fusion), channel_id=1, source_target_pairs={{0,28},{4,0},{8,4},{12,8},{16,12},{20,16},{24,20},{28,24},{1,29},{... | collective-permute-start | bytes 786440 | tf_op jit(solution)/shard_map/ppermute | solution.py:176
  81.5 12.3 %all-to-all-start.1 = ((bf16[8,128,256]{2,1,0:T(8,128)(2,1)}), bf16[8,128,256]{2,1,0:T(8,128)(2,1)S(1)}, u32[]{:S(2)}, u32[]{:S(2)}) async-start(bf16[8,128,256]{2,1,0:T(8,128)(2,1)} %get-tuple-element.31), calls=%async_computation.1 | async-start | bytes 1048576 | tf_op jit(solution)/shard_map/all_to_all | solution.py:213
  86.4 7.6 %collective-permute-start.17 = (bf16[256,256]{1,0:T(8,128)(2,1)S(1)}, bf16[256,256]{1,0:T(8,128)(2,1)S(1)}, u32[]{:S(2)}, u32[]{:S(2)}) collective-permute-start(bf16[256,256]{1,0:T(8,128)(2,1)S(1)} %slice.83), channel_id=1, source_target_pairs={{0,32},{32,0},{1,33},{33,1},{2,34},{34,2},{3,35},{35,3},{4,36},{36... | collective-permute-start | bytes 393224 | tf_op jit(solution)/shard_map/ppermute | solution.py:176
  94.1 6.1 %collective-permute-start.18 = (bf16[3,128,128]{2,1,0:T(8,128)(2,1)S(1)}, bf16[3,128,128]{2,1,0:T(8,128)(2,1)S(1)}, u32[]{:S(2)}, u32[]{:S(2)}) collective-permute-start(bf16[3,128,128]{2,1,0:T(8,128)(2,1)S(1)} %slice.54), channel_id=1, source_target_pairs={{0,1},{1,0},{2,3},{3,2},{4,5},{5,4},{6,7},{7,6},{8,9},{9,8},{10,11... | collective-permute-start | bytes 294920 | tf_op jit(solution)/shard_map/ppermute | solution.py:176

commit v11 on v9

--- a/solution.py
+++ b/solution.py
@@ -28,7 +28,7 @@
     return jnp.concatenate([hi.astype(F32), mid.astype(F32), low.astype(F32)], axis=0)
 
 
-def pack_kernel(core_ref, q_ref, k_ref, v_ref, o_ref, g_ref, lse_ref, qg_ref, kv_ref, send_ref):
+def pack_kernel(core_ref, q_ref, k_ref, v_ref, o_ref, g_ref, lse_ref, mine_ref, send_ref):
     def fill(head, qg, kv):
         cols = slice(head * HEAD, (head + 1) * HEAD)
         g = g_ref[:, cols]
@@ -43,14 +43,15 @@
         kv[:, :HEAD] = k_ref[:, cols]
         kv[:, HEAD:] = v_ref[:, cols]
 
-    send_qg = send_ref.at[: HALF + STATS]
-    send_kv = send_ref.at[HALF + STATS :]
+    def halves(ref):
+        return ref.at[: HALF + STATS], ref.at[HALF + STATS :]
+
     for core in range(2):
 
         @pl.when(core_ref[0] == core)
         def _():
-            fill(core, qg_ref, kv_ref)
-            fill(1 - core, send_qg, send_kv)
+            fill(core, *halves(mine_ref))
+            fill(1 - core, *halves(send_ref))
 
 
 def pack_call(core, *args):
@@ -59,29 +60,25 @@
         pack_kernel,
         in_specs=[pl.BlockSpec(memory_space=pltpu.SMEM)]
         + [pl.BlockSpec(memory_space=pltpu.VMEM)] * 6,
-        out_specs=[pl.BlockSpec(memory_space=pltpu.VMEM)] * 3,
-        out_shape=[
-            jax.ShapeDtypeStruct((HALF + STATS, width), BF16),
-            jax.ShapeDtypeStruct((HALF, width), BF16),
-            jax.ShapeDtypeStruct((2 * HALF + STATS, width), BF16),
-        ],
+        out_specs=[pl.BlockSpec(memory_space=pltpu.VMEM)] * 2,
+        out_shape=[jax.ShapeDtypeStruct((2 * HALF + STATS, width), BF16)] * 2,
         name="pack",
     )(core.reshape(1), *args)
 
 
-def spread_kernel(mine_ref, kv_ref, other_ref, out_ref, keys_ref):
+def spread_kernel(mine_ref, other_ref, out_ref, keys_ref):
     rows = HALF + STATS
     for n in range(out_ref.shape[0]):
-        out_ref[n, :rows, :] = mine_ref[...]
+        out_ref[n, :rows, :] = mine_ref[:rows, :]
         out_ref[n, rows:, :] = other_ref[:rows, :]
-    keys_ref[:HALF, :] = kv_ref[...]
+    keys_ref[:HALF, :] = mine_ref[rows:, :]
     keys_ref[HALF:, :] = other_ref[rows:, :]
 
 
 def spread_call(n, *args):
     return pl.pallas_call(
         spread_kernel,
-        in_specs=[pl.BlockSpec(memory_space=pltpu.VMEM)] * 3,
+        in_specs=[pl.BlockSpec(memory_space=pltpu.VMEM)] * 2,
         out_specs=[pl.BlockSpec(memory_space=pltpu.VMEM)] * 2,
         out_shape=[
             jax.ShapeDtypeStruct((n, 2 * (HALF + STATS), 2 * HEAD), BF16),
@@ -187,49 +184,42 @@
 def local(queries, key_rows, value_rows, attn_output, grad_output, row_lse):
     core = lax.axis_index("core")
     even = core == 0
-    mine_q, mine_kv, send = pack_call(
+    mine, send = pack_call(
         core, queries, key_rows, value_rows, attn_output, grad_output, row_lse
     )
     other = shift(send, "core", 1)
     peers = math.prod(lax.axis_size(a) for a in GROUP)
-    spread, key_pack = spread_call(peers, mine_q, mine_kv, other)
+    spread, key_pack = spread_call(peers, mine, other)
     key_pair = jnp.concatenate([key_pack, shift(key_pack, "xh", 1)], axis=0)
     gathered = lax.all_to_all(spread, GROUP, 0, 0, tiled=True)
     keys = {0: key_pair}
     for by in (1, 2, 3):
         keys[by] = shift(keys[by - 1], "z", 1)
         keys[-by] = shift(keys[1 - by], "z", -1)
-    total_q, own = tile_call(gathered, [keys[0]])
-    zero = jnp.minimum(jnp.abs(own[0, 0]), 0.0).astype(BF16)
     keys[4] = jnp.concatenate(
-        [shift(keys[3][:ROWS] + zero, "z", 1), shift(keys[-3][ROWS:] + zero, "z", -1)],
-        axis=0,
+        [shift(keys[3][:ROWS], "z", 1), shift(keys[-3][ROWS:], "z", -1)], axis=0
     )
 
     def low(x):
         return x.astype(BF16)
 
-    total_q, far = tile_call(gathered, [keys[4]], total_q)
-    up = low(far)
-    down = None
-    after = up
-    for by in (3, 2):
-        up_in = shift(up, "z", 1)
-        down_in = None if down is None else shift(down, "z", -1)
-        total_q, du, dd = tile_call(gathered, [keys[-by], keys[by]], total_q, after)
-        up = low(du + up_in.astype(F32))
-        down = low(dd if down_in is None else dd + down_in.astype(F32))
+    total_q, own = tile_call(gathered, [keys[0]])
+    total_q, du, dd = tile_call(gathered, [keys[-3], keys[3]], total_q)
+    up, down = low(du), low(dd)
+    up_in, down_in = shift(up, "z", 1), shift(down, "z", -1)
+    total_q, far = tile_call(gathered, [keys[4]], total_q, up)
+    far = low(far)
+    after = far
+    for by in (2, 1):
+        total_q, du, dd = tile_call(
+            gathered, [keys[-by], keys[by]], total_q, after, by == 1
+        )
+        up, down = low(du + up_in.astype(F32)), low(dd + down_in.astype(F32))
+        up_in, down_in = shift(up, "z", 1), shift(down, "z", -1)
         after = up
-    up_in = shift(up, "z", 1)
-    down_in = shift(down, "z", -1)
-    total_q, dd = tile_call(gathered, [keys[1]], total_q, after)
-    down = low(dd + down_in.astype(F32))
-    down_in = shift(down, "z", -1)
-    total_q, du = tile_call(gathered, [keys[-1]], total_q, down, True)
-    up = low(du + up_in.astype(F32))
-    up_in = shift(up, "z", 1)
+    far_in = shift(far, "z", 4)
     returned = lax.all_to_all(total_q, GROUP, 0, 0, tiled=True)
-    grad_pair = own + up_in.astype(F32) + down_in.astype(F32)
+    grad_pair = own + far_in.astype(F32) + up_in.astype(F32) + down_in.astype(F32)
     grad_kv = grad_pair[:ROWS] + shift(low(grad_pair[ROWS:]), "xh", 1).astype(F32)
 
     grad_q = jnp.sum(returned.astype(F32), axis=0).T

time: 119 us -> 104 us (0.87)
  waiting for transfers between devices: 37.7 us -> 24 us
  starting transfers between devices: 48.2 us -> 45.8 us
    ppermute x19, waiting for transfers between devices: 33.5 us -> 19.8 us  [shift(): return lax.ppermute(x, axis, [(i, (i + by) % n) for i in range(n)])]
    ppermute x19, starting transfers between devices: 40.7 us -> 37.1 us  [shift(): return lax.ppermute(x, axis, [(i, (i + by) % n) for i in range(n)])]
    pallas_call x6 -> x5, Pallas kernels: 24.8 us -> 24.5 us  [tile_call(): pl.pallas_call(functools.partial(tile_kernel, count, first, after is not...]
  transfers between devices with their start and end apart: 21 -> 21, of which waited for: 10 -> 9; matrix products, arithmetic and copies ran while one was open for 1% -> 3% of each run, Pallas kernels for 18% -> 24%
where the time goes in v11:
time: 104 us
  starting transfers between devices  45.8 us (44%)
  Pallas kernels  28.5 us (27%)
  waiting for transfers between devices  24 us (23%)
  other arithmetic  2.23 us (2%)
  local copies, waits for them, and re-layouts  2.17 us (2%)
    ppermute x19, starting transfers between devices, shift(): return lax.ppermute(x, axis, [(i, (i + by) % n) for i in range(n)])  37.1 us
    pallas_call x5, Pallas kernels, tile_call(): pl.pallas_call(functools.partial(tile_kernel, count, first, after is not...  24.5 us
    ppermute x19, waiting for transfers between devices, shift(): return lax.ppermute(x, axis, [(i, (i + by) % n) for i in range(n)])  19.8 us
    all_to_all x1, starting transfers between devices, local(): gathered = lax.all_to_all(spread, GROUP, 0, 0, tiled=True)  4.35 us
    all_to_all x1, starting transfers between devices, local(): returned = lax.all_to_all(total_q, GROUP, 0, 0, tiled=True)  4.34 us
    all_to_all x1, waiting for transfers between devices, local(): returned = lax.all_to_all(total_q, GROUP, 0, 0, tiled=True)  4.21 us
    pallas_call x1, Pallas kernels, spread_call(): pl.pallas_call(spread_kernel, in_specs=[pl.BlockSpec(memory_space=pltpu.V...  2.1 us
  transfers between devices with their start and end apart: 21, of which 9 were waited for; matrix products, arithmetic and copies ran while one was open for 3% of the time, Pallas kernels for 24%

profile of v11, /device:TPU:1, one launch (start us, length us, event | category | flops | bytes accessed | tf_op | source)
XLA Modules:
  0.0 103.5 jit_solution(8873178074720144461)
XLA Ops:
  0.6 1.8 %pack.1 = (bf16[272,256]{1,0:T(8,128)(2,1)}, bf16[272,256]{1,0:T(8,128)(2,1)}) custom-call(s32[1]{0:T(128)} %bitcast.core_ref, bf16[128,256]{1,0:T(8,128)(2,1)} %q_ref.1, bf16[128,256]{1,0:T(8,128)(2,1)} %k_ref.1, bf16[128,256]{1,0:T(8,128)(2,1)} %v_ref.1, bf16[128,256]{1,0:T(8,128)(2,1)} %o_ref.1, bf16[128,256]{1,0:T(8,128)(2,1)} %g_ref.1, f32[2,128]{1,0:T(2,128)} %lse_ref.1), custom_call_target="tpu_custom_call" | custom-call | tf_op jit(solution)/shard_map/pack/pallas_call | solution.py:59
  2.5 3.2 %collective-permute-start = (bf16[272,256]{1,0:T(8,128)(2,1)}, bf16[272,256]{1,0:T(8,128)(2,1)S(1)}, u32[]{:S(2)}, u32[]{:S(2)}) collective-permute-start(bf16[272,256]{1,0:T(8,128)(2,1)} %get-tuple-element.21), channel_id=1, source_target_pairs={{0,1},{1,0},{2,3},{3,2},{4,5},{5,4},{6,7},{7,6},{8,9},{9,8},{10,11... | collective-permute-start | bytes 417800 | tf_op jit(solution)/shard_map/ppermute | solution.py:181
  7.6 2.1 %spread.1 = (bf16[8,288,256]{2,1,0:T(8,128)(2,1)}, bf16[256,256]{1,0:T(8,128)(2,1)}) custom-call(bf16[272,256]{1,0:T(8,128)(2,1)} %get-tuple-element.20.mine_ref, bf16[272,256]{1,0:T(8,128)(2,1)} %copy-done), custom_call_target="tpu_custom_call" | custom-call | tf_op jit(solution)/shard_map/spread/pallas_call | solution.py:79
  10.7 4.4 %all-to-all-start = ((bf16[8,288,256]{2,1,0:T(8,128)(2,1)}), bf16[8,288,256]{2,1,0:T(8,128)(2,1)S(1)}, u32[]{:S(2)}, u32[]{:S(2)}) async-start(bf16[8,288,256]{2,1,0:T(8,128)(2,1)} %get-tuple-element.22), calls=%async_computation | async-start | bytes 2359296 | tf_op jit(solution)/shard_map/all_to_all | solution.py:194
  16.8 4.0 %collective-permute-start.2 = (bf16[512,256]{1,0:T(8,128)(2,1)S(1)}, bf16[512,256]{1,0:T(8,128)(2,1)S(1)}, u32[]{:S(2)}, u32[]{:S(2)}) collective-permute-start(bf16[512,256]{1,0:T(8,128)(2,1)S(1)} %constant_dynamic-update-slice_fusion.refs_1_), channel_id=1, source_target_pairs={{0,28},{4,0},{8,4},{12,8},{16,12},{20,16},{24,20},{28,24},{1,29},{... | collective-permute-start | bytes 786440 | tf_op jit(solution)/shard_map/ppermute | solution.py:181
  20.8 5.7 %collective-permute-done.3.refs_2_ = bf16[512,256]{1,0:T(8,128)(2,1)S(1)} collective-permute-done((bf16[512,256]{1,0:T(8,128)(2,1)S(1)}, bf16[512,256]{1,0:T(8,128)(2,1)S(1)}, u32[]{:S(2)}, u32[]{:S(2)}) %collective-permute-start.3) | collective-permute-done | bytes 262176 | tf_op jit(solution)/shard_map/ppermute | solution.py:181
  26.5 2.7 %collective-permute-start.4 = (bf16[512,256]{1,0:T(8,128)(2,1)S(1)}, bf16[512,256]{1,0:T(8,128)(2,1)S(1)}, u32[]{:S(2)}, u32[]{:S(2)}) collective-permute-start(bf16[512,256]{1,0:T(8,128)(2,1)S(1)} %collective-permute-done.2.refs_1_), channel_id=1, source_target_pairs={{0,28},{4,0},{8,4},{12,8},{16,12},{20,16},{24,20},{28,24},{1,29},{... | collective-permute-start | bytes 786440 | tf_op jit(solution)/shard_map/ppermute | solution.py:181
  29.2 4.8 %collective-permute-done.5.refs_2_ = bf16[512,256]{1,0:T(8,128)(2,1)S(1)} collective-permute-done((bf16[512,256]{1,0:T(8,128)(2,1)S(1)}, bf16[512,256]{1,0:T(8,128)(2,1)S(1)}, u32[]{:S(2)}, u32[]{:S(2)}) %collective-permute-start.5) | collective-permute-done | bytes 262176 | tf_op jit(solution)/shard_map/ppermute | solution.py:181
  34.0 2.7 %collective-permute-start.8 = (bf16[512,256]{1,0:T(8,128)(2,1)S(1)}, bf16[512,256]{1,0:T(8,128)(2,1)S(1)}, u32[]{:S(2)}, u32[]{:S(2)}) collective-permute-start(bf16[512,256]{1,0:T(8,128)(2,1)S(1)} %collective-permute-done.4.refs_1_), channel_id=1, source_target_pairs={{0,28},{4,0},{8,4},{12,8},{16,12},{20,16},{24,20},{28,24},{1,29},{... | collective-permute-start | bytes 786440 | tf_op jit(solution)/shard_map/ppermute | solution.py:181
  36.7 3.8 %collective-permute-done.6.refs_2_ = bf16[512,256]{1,0:T(8,128)(2,1)S(1)} collective-permute-done((bf16[512,256]{1,0:T(8,128)(2,1)S(1)}, bf16[512,256]{1,0:T(8,128)(2,1)S(1)}, u32[]{:S(2)}, u32[]{:S(2)}) %collective-permute-start.6) | collective-permute-done | bytes 262176 | tf_op jit(solution)/shard_map/ppermute | solution.py:181
  41.8 2.7 %collective-permute-start.9 = (bf16[256,256]{1,0:T(8,128)(2,1)}, bf16[256,256]{1,0:T(8,128)(2,1)}, u32[]{:S(2)}, u32[]{:S(2)}) collective-permute-start(bf16[256,256]{1,0:T(8,128)(2,1)} %slice.48), channel_id=1, source_target_pairs={{0,28},{4,0},{8,4},{12,8},{16,12},{20,16},{24,20},{28,24},{1,29},{... | collective-permute-start | bytes 393224 | tf_op jit(solution)/shard_map/ppermute | solution.py:181
  44.4 3.0 %tile.5 = (f32[8,128,256]{2,1,0:T(8,128)S(1)}, f32[512,256]{1,0:T(8,128)S(1)}) custom-call(bf16[8,288,256]{2,1,0:T(8,128)(2,1)S(1)} %all-to-all-done.refs_0_, bf16[512,256]{1,0:T(8,128)(2,1)S(1)} %constant_dynamic-update-slice_fusion.refs_1_), custom_call_target="tpu_custom_call" | custom-call | flops 2684354560 | bytes 8388608 | tf_op jit(solution)/shard_map/tile/pallas_call | solution.py:160
  47.5 5.9 %tile.6 = (f32[8,128,256]{2,1,0:T(8,128)S(1)}, f32[512,256]{1,0:T(8,128)S(1)}, f32[512,256]{1,0:T(8,128)S(1)}) custom-call(bf16[8,288,256]{2,1,0:T(8,128)(2,1)S(1)} %all-to-all-done.refs_0_, bf16[512,256]{1,0:T(8,128)(2,1)S(1)} %collective-permute-done.8.refs_1_, bf16[512,256]{1,0:T(8,128)(2,1)S(1)} %collective-permute-done.6.refs_2_, ...), custom_call_target="tpu_custom_call" | custom-call | flops 5368709120 | bytes 8388608 | tf_op jit(solution)/shard_map/tile/pallas_call | solution.py:160
  53.8 1.5 %collective-permute-start.10 = (bf16[512,256]{1,0:T(8,128)(2,1)S(1)}, bf16[512,256]{1,0:T(8,128)(2,1)S(1)}, u32[]{:S(2)}, u32[]{:S(2)}) collective-permute-start(bf16[512,256]{1,0:T(8,128)(2,1)S(1)} %convert_element_type.50.refs_3_), channel_id=1, source_target_pairs={{0,4},{4,8},{8,12},{12,16},{16,20},{20,24},{24,28},{28,0},{1,5},{5... | collective-permute-start | bytes 786440 | tf_op jit(solution)/shard_map/ppermute | solution.py:181
  56.2 3.1 %tile.7 = (f32[8,128,256]{2,1,0:T(8,128)S(1)}, f32[512,256]{1,0:T(8,128)S(1)}) custom-call(bf16[8,288,256]{2,1,0:T(8,128)(2,1)S(1)} %all-to-all-done.refs_0_, bf16[512,256]{1,0:T(8,128)(2,1)S(1)} %pad_maximum_fusion.refs_1_, f32[8,128,256]{2,1,0:T(8,128)S(1)} %get-tuple-element.25.refs_2_, bf16[512,256]{1,0:T(8,128)(2,1)S(1)} %convert_element_type.50.refs_3_), custom_call_target="tpu_custom_call" | custom-call | flops 2684354560 | bytes 8388608 | tf_op jit(solution)/shard_map/tile/pallas_call | solution.py:160
  59.3 3.5 %collective-permute-start.11 = (bf16[512,256]{1,0:T(8,128)(2,1)S(1)}, bf16[512,256]{1,0:T(8,128)(2,1)S(1)}, u32[]{:S(2)}, u32[]{:S(2)}) collective-permute-start(bf16[512,256]{1,0:T(8,128)(2,1)S(1)} %convert_element_type.51.refs_4_), channel_id=1, source_target_pairs={{0,16},{4,20},{8,24},{12,28},{16,0},{20,4},{24,8},{28,12},{1,17},{... | collective-permute-start | bytes 786440 | tf_op jit(solution)/shard_map/ppermute | solution.py:181
  62.8 5.9 %tile.8 = (f32[8,128,256]{2,1,0:T(8,128)S(1)}, f32[512,256]{1,0:T(8,128)S(1)}, f32[512,256]{1,0:T(8,128)S(1)}) custom-call(bf16[8,288,256]{2,1,0:T(8,128)(2,1)S(1)} %all-to-all-done.refs_0_, bf16[512,256]{1,0:T(8,128)(2,1)S(1)} %collective-permute-done.4.refs_1_, bf16[512,256]{1,0:T(8,128)(2,1)S(1)} %collective-permute-done.5.refs_2_, ...), custom_call_target="tpu_custom_call" | custom-call | flops 5368709120 | bytes 8388608 | tf_op jit(solution)/shard_map/tile/pallas_call | solution.py:160
  68.9 2.7 %collective-permute-start.15 = (bf16[512,256]{1,0:T(8,128)(2,1)S(1)}, bf16[512,256]{1,0:T(8,128)(2,1)S(1)}, u32[]{:S(2)}, u32[]{:S(2)}) collective-permute-start(bf16[512,256]{1,0:T(8,128)(2,1)S(1)} %add_convert_fusion.1), channel_id=1, source_target_pairs={{0,28},{4,0},{8,4},{12,8},{16,12},{20,16},{24,20},{28,24},{1,29},{... | collective-permute-start | bytes 786440 | tf_op jit(solution)/shard_map/ppermute | solution.py:181
  71.7 6.6 %tile.9 = (bf16[8,128,256]{2,1,0:T(8,128)(2,1)}, f32[512,256]{1,0:T(8,128)S(1)}, f32[512,256]{1,0:T(8,128)S(1)}) custom-call(bf16[8,288,256]{2,1,0:T(8,128)(2,1)S(1)} %all-to-all-done.refs_0_, bf16[512,256]{1,0:T(8,128)(2,1)S(1)} %collective-permute-done.2.refs_1_, bf16[512,256]{1,0:T(8,128)(2,1)S(1)} %collective-permute-done.3.refs_2_, ...), custom_call_target="tpu_custom_call" | custom-call | flops 5368709120 | bytes 8388608 | tf_op jit(solution)/shard_map/tile/pallas_call | solution.py:160
  79.2 2.2 %collective-permute-start.13 = (bf16[512,256]{1,0:T(8,128)(2,1)S(1)}, bf16[512,256]{1,0:T(8,128)(2,1)S(1)}, u32[]{:S(2)}, u32[]{:S(2)}) collective-permute-start(bf16[512,256]{1,0:T(8,128)(2,1)S(1)} %add_convert_fusion.2), channel_id=1, source_target_pairs={{0,4},{4,8},{8,12},{12,16},{16,20},{20,24},{24,28},{28,0},{1,5},{5... | collective-permute-start | bytes 786440 | tf_op jit(solution)/shard_map/ppermute | solution.py:181
  82.1 4.3 %all-to-all-start.1 = ((bf16[8,128,256]{2,1,0:T(8,128)(2,1)}), bf16[8,128,256]{2,1,0:T(8,128)(2,1)S(1)}, u32[]{:S(2)}, u32[]{:S(2)}) async-start(bf16[8,128,256]{2,1,0:T(8,128)(2,1)} %get-tuple-element.31), calls=%async_computation.1 | async-start | bytes 1048576 | tf_op jit(solution)/shard_map/all_to_all | solution.py:221
  88.1 1.7 %collective-permute-start.17 = (bf16[256,256]{1,0:T(8,128)(2,1)S(1)}, bf16[256,256]{1,0:T(8,128)(2,1)S(1)}, u32[]{:S(2)}, u32[]{:S(2)}) collective-permute-start(bf16[256,256]{1,0:T(8,128)(2,1)S(1)} %slice.83), channel_id=1, source_target_pairs={{0,32},{32,0},{1,33},{33,1},{2,34},{34,2},{3,35},{35,3},{4,36},{36... | collective-permute-start | bytes 393224 | tf_op jit(solution)/shard_map/ppermute | solution.py:181
  89.8 4.2 %all-to-all-done.1 = bf16[8,128,256]{2,1,0:T(8,128)(2,1)S(1)} async-done(((bf16[8,128,256]{2,1,0:T(8,128)(2,1)}), bf16[8,128,256]{2,1,0:T(8,128)(2,1)S(1)}, u32[]{:S(2)}, u32[]{:S(2)}) %all-to-all-start.1) | async-done | bytes 524320 | tf_op jit(solution)/shard_map/all_to_all | solution.py:221
  94.3 7.5 %collective-permute-start.18 = (bf16[3,128,128]{2,1,0:T(8,128)(2,1)S(1)}, bf16[3,128,128]{2,1,0:T(8,128)(2,1)S(1)}, u32[]{:S(2)}, u32[]{:S(2)}) collective-permute-start(bf16[3,128,128]{2,1,0:T(8,128)(2,1)S(1)} %slice.54), channel_id=1, source_target_pairs={{0,1},{1,0},{2,3},{3,2},{4,5},{5,4},{6,7},{7,6},{8,9},{9,8},{10,11... | collective-permute-start | bytes 294920 | tf_op jit(solution)/shard_map/ppermute | solution.py:181
  (51 shorter events, 12.7 us)
Async XLA Ops:
  2.5 4.4 %collective-permute-start = (bf16[272,256]{1,0:T(8,128)(2,1)}, bf16[272,256]{1,0:T(8,128)(2,1)S(1)}, u32[]{:S(2)}, u32[]{:S(2)}) collective-permute-start(bf16[272,256]{1,0:T(8,128)(2,1)} %get-tuple-element.21), channel_id=1, source_target_pairs={{0,1},{1,0},{2,3},{3,2},{4,5},{5,4},{6,7},{7,6},{8,9},{9,8},{10,11... | collective-permute-start | bytes 417800 | tf_op jit(solution)/shard_map/ppermute | solution.py:181
  6.9 0.7 copy-start
  9.7 6.4 %collective-permute-start.1 = (bf16[256,256]{1,0:T(8,128)(2,1)}, bf16[256,256]{1,0:T(8,128)(2,1)S(1)}, u32[]{:S(2)}, u32[]{:S(2)}) collective-permute-start(bf16[256,256]{1,0:T(8,128)(2,1)} %get-tuple-element.23), channel_id=1, source_target_pairs={{0,32},{32,0},{1,33},{33,1},{2,34},{34,2},{3,35},{35,3},{4,36},{36... | collective-permute-start | bytes 393224 | tf_op jit(solution)/shard_map/ppermute | solution.py:181
  10.7 4.4 %copy-start.1 = (bf16[256,256]{1,0:T(8,128)(2,1)S(1)}, bf16[256,256]{1,0:T(8,128)(2,1)}, u32[]{:S(2)}) copy-start(bf16[256,256]{1,0:T(8,128)(2,1)} %get-tuple-element.23) | copy-start | bytes 393220
  10.7 33.8 %all-to-all-start = ((bf16[8,288,256]{2,1,0:T(8,128)(2,1)}), bf16[8,288,256]{2,1,0:T(8,128)(2,1)S(1)}, u32[]{:S(2)}, u32[]{:S(2)}) async-start(bf16[8,288,256]{2,1,0:T(8,128)(2,1)} %get-tuple-element.22), calls=%async_computation | async-start | bytes 2359296 | tf_op jit(solution)/shard_map/all_to_all | solution.py:194
  16.1 10.4 %collective-permute-start.3 = (bf16[512,256]{1,0:T(8,128)(2,1)S(1)}, bf16[512,256]{1,0:T(8,128)(2,1)S(1)}, u32[]{:S(2)}, u32[]{:S(2)}) collective-permute-start(bf16[512,256]{1,0:T(8,128)(2,1)S(1)} %constant_dynamic-update-slice_fusion.refs_1_), channel_id=1, source_target_pairs={{0,4},{4,8},{8,12},{12,16},{16,20},{20,24},{24,28},{28,0},{1,5},{5... | collective-permute-start | bytes 786440 | tf_op jit(solution)/shard_map/ppermute | solution.py:181
  16.8 9.7 %collective-permute-start.2 = (bf16[512,256]{1,0:T(8,128)(2,1)S(1)}, bf16[512,256]{1,0:T(8,128)(2,1)S(1)}, u32[]{:S(2)}, u32[]{:S(2)}) collective-permute-start(bf16[512,256]{1,0:T(8,128)(2,1)S(1)} %constant_dynamic-update-slice_fusion.refs_1_), channel_id=1, source_target_pairs={{0,28},{4,0},{8,4},{12,8},{16,12},{20,16},{24,20},{28,24},{1,29},{... | collective-permute-start | bytes 786440 | tf_op jit(solution)/shard_map/ppermute | solution.py:181
  26.5 7.5 %collective-permute-start.5 = (bf16[512,256]{1,0:T(8,128)(2,1)S(1)}, bf16[512,256]{1,0:T(8,128)(2,1)S(1)}, u32[]{:S(2)}, u32[]{:S(2)}) collective-permute-start(bf16[512,256]{1,0:T(8,128)(2,1)S(1)} %collective-permute-done.3.refs_2_), channel_id=1, source_target_pairs={{0,4},{4,8},{8,12},{12,16},{16,20},{20,24},{24,28},{28,0},{1,5},{5... | collective-permute-start | bytes 786440 | tf_op jit(solution)/shard_map/ppermute | solution.py:181
  26.5 7.5 %collective-permute-start.4 = (bf16[512,256]{1,0:T(8,128)(2,1)S(1)}, bf16[512,256]{1,0:T(8,128)(2,1)S(1)}, u32[]{:S(2)}, u32[]{:S(2)}) collective-permute-start(bf16[512,256]{1,0:T(8,128)(2,1)S(1)} %collective-permute-done.2.refs_1_), channel_id=1, source_target_pairs={{0,28},{4,0},{8,4},{12,8},{16,12},{20,16},{24,20},{28,24},{1,29},{... | collective-permute-start | bytes 786440 | tf_op jit(solution)/shard_map/ppermute | solution.py:181
  34.0 6.4 %collective-permute-start.6 = (bf16[512,256]{1,0:T(8,128)(2,1)S(1)}, bf16[512,256]{1,0:T(8,128)(2,1)S(1)}, u32[]{:S(2)}, u32[]{:S(2)}) collective-permute-start(bf16[512,256]{1,0:T(8,128)(2,1)S(1)} %collective-permute-done.5.refs_2_), channel_id=1, source_target_pairs={{0,4},{4,8},{8,12},{12,16},{16,20},{20,24},{24,28},{28,0},{1,5},{5... | collective-permute-start | bytes 786440 | tf_op jit(solution)/shard_map/ppermute | solution.py:181
  34.0 7.1 %collective-permute-start.8 = (bf16[512,256]{1,0:T(8,128)(2,1)S(1)}, bf16[512,256]{1,0:T(8,128)(2,1)S(1)}, u32[]{:S(2)}, u32[]{:S(2)}) collective-permute-start(bf16[512,256]{1,0:T(8,128)(2,1)S(1)} %collective-permute-done.4.refs_1_), channel_id=1, source_target_pairs={{0,28},{4,0},{8,4},{12,8},{16,12},{20,16},{24,20},{28,24},{1,29},{... | collective-permute-start | bytes 786440 | tf_op jit(solution)/shard_map/ppermute | solution.py:181
  41.1 14.1 %collective-permute-start.7 = (bf16[256,256]{1,0:T(8,128)(2,1)}, bf16[256,256]{1,0:T(8,128)(2,1)}, u32[]{:S(2)}, u32[]{:S(2)}) collective-permute-start(bf16[256,256]{1,0:T(8,128)(2,1)} %slice.47), channel_id=1, source_target_pairs={{0,4},{4,8},{8,12},{12,16},{16,20},{20,24},{24,28},{28,0},{1,5},{5... | collective-permute-start | bytes 393224 | tf_op jit(solution)/shard_map/ppermute | solution.py:181
  41.8 13.5 %collective-permute-start.9 = (bf16[256,256]{1,0:T(8,128)(2,1)}, bf16[256,256]{1,0:T(8,128)(2,1)}, u32[]{:S(2)}, u32[]{:S(2)}) collective-permute-start(bf16[256,256]{1,0:T(8,128)(2,1)} %slice.48), channel_id=1, source_target_pairs={{0,28},{4,0},{8,4},{12,8},{16,12},{20,16},{24,20},{28,24},{1,29},{... | collective-permute-start | bytes 393224 | tf_op jit(solution)/shard_map/ppermute | solution.py:181
  53.5 15.4 %collective-permute-start.14 = (bf16[512,256]{1,0:T(8,128)(2,1)S(1)}, bf16[512,256]{1,0:T(8,128)(2,1)S(1)}, u32[]{:S(2)}, u32[]{:S(2)}) collective-permute-start(bf16[512,256]{1,0:T(8,128)(2,1)S(1)} %convert_element_type.59), channel_id=1, source_target_pairs={{0,28},{4,0},{8,4},{12,8},{16,12},{20,16},{24,20},{28,24},{1,29},{... | collective-permute-start | bytes 786440 | tf_op jit(solution)/shard_map/ppermute | solution.py:181
  53.8 14.9 %collective-permute-start.10 = (bf16[512,256]{1,0:T(8,128)(2,1)S(1)}, bf16[512,256]{1,0:T(8,128)(2,1)S(1)}, u32[]{:S(2)}, u32[]{:S(2)}) collective-permute-start(bf16[512,256]{1,0:T(8,128)(2,1)S(1)} %convert_element_type.50.refs_3_), channel_id=1, source_target_pairs={{0,4},{4,8},{8,12},{12,16},{16,20},{20,24},{24,28},{28,0},{1,5},{5... | collective-permute-start | bytes 786440 | tf_op jit(solution)/shard_map/ppermute | solution.py:181
  59.3 27.2 %collective-permute-start.11 = (bf16[512,256]{1,0:T(8,128)(2,1)S(1)}, bf16[512,256]{1,0:T(8,128)(2,1)S(1)}, u32[]{:S(2)}, u32[]{:S(2)}) collective-permute-start(bf16[512,256]{1,0:T(8,128)(2,1)S(1)} %convert_element_type.51.refs_4_), channel_id=1, source_target_pairs={{0,16},{4,20},{8,24},{12,28},{16,0},{20,4},{24,8},{28,12},{1,17},{... | collective-permute-start | bytes 786440 | tf_op jit(solution)/shard_map/ppermute | solution.py:181
  68.8 10.4 %collective-permute-start.12 = (bf16[512,256]{1,0:T(8,128)(2,1)S(1)}, bf16[512,256]{1,0:T(8,128)(2,1)S(1)}, u32[]{:S(2)}, u32[]{:S(2)}) collective-permute-start(bf16[512,256]{1,0:T(8,128)(2,1)S(1)} %add_convert_fusion.3.refs_4_), channel_id=1, source_target_pairs={{0,4},{4,8},{8,12},{12,16},{16,20},{20,24},{24,28},{28,0},{1,5},{5... | collective-permute-start | bytes 786440 | tf_op jit(solution)/shard_map/ppermute | solution.py:181
  68.9 12.5 %collective-permute-start.15 = (bf16[512,256]{1,0:T(8,128)(2,1)S(1)}, bf16[512,256]{1,0:T(8,128)(2,1)S(1)}, u32[]{:S(2)}, u32[]{:S(2)}) collective-permute-start(bf16[512,256]{1,0:T(8,128)(2,1)S(1)} %add_convert_fusion.1), channel_id=1, source_target_pairs={{0,28},{4,0},{8,4},{12,8},{16,12},{20,16},{24,20},{28,24},{1,29},{... | collective-permute-start | bytes 786440 | tf_op jit(solution)/shard_map/ppermute | solution.py:181
  79.2 7.2 %collective-permute-start.13 = (bf16[512,256]{1,0:T(8,128)(2,1)S(1)}, bf16[512,256]{1,0:T(8,128)(2,1)S(1)}, u32[]{:S(2)}, u32[]{:S(2)}) collective-permute-start(bf16[512,256]{1,0:T(8,128)(2,1)S(1)} %add_convert_fusion.2), channel_id=1, source_target_pairs={{0,4},{4,8},{8,12},{12,16},{16,20},{20,24},{24,28},{28,0},{1,5},{5... | collective-permute-start | bytes 786440 | tf_op jit(solution)/shard_map/ppermute | solution.py:181
  81.5 6.5 %collective-permute-start.16 = (bf16[512,256]{1,0:T(8,128)(2,1)S(1)}, bf16[512,256]{1,0:T(8,128)(2,1)S(1)}, u32[]{:S(2)}, u32[]{:S(2)}) collective-permute-start(bf16[512,256]{1,0:T(8,128)(2,1)S(1)} %add_convert_fusion), channel_id=1, source_target_pairs={{0,28},{4,0},{8,4},{12,8},{16,12},{20,16},{24,20},{28,24},{1,29},{... | collective-permute-start | bytes 786440 | tf_op jit(solution)/shard_map/ppermute | solution.py:181
  82.1 11.9 %all-to-all-start.1 = ((bf16[8,128,256]{2,1,0:T(8,128)(2,1)}), bf16[8,128,256]{2,1,0:T(8,128)(2,1)S(1)}, u32[]{:S(2)}, u32[]{:S(2)}) async-start(bf16[8,128,256]{2,1,0:T(8,128)(2,1)} %get-tuple-element.31), calls=%async_computation.1 | async-start | bytes 1048576 | tf_op jit(solution)/shard_map/all_to_all | solution.py:221
  88.1 6.1 %collective-permute-start.17 = (bf16[256,256]{1,0:T(8,128)(2,1)S(1)}, bf16[256,256]{1,0:T(8,128)(2,1)S(1)}, u32[]{:S(2)}, u32[]{:S(2)}) collective-permute-start(bf16[256,256]{1,0:T(8,128)(2,1)S(1)} %slice.83), channel_id=1, source_target_pairs={{0,32},{32,0},{1,33},{33,1},{2,34},{34,2},{3,35},{35,3},{4,36},{36... | collective-permute-start | bytes 393224 | tf_op jit(solution)/shard_map/ppermute | solution.py:181
  94.3 8.5 %collective-permute-start.18 = (bf16[3,128,128]{2,1,0:T(8,128)(2,1)S(1)}, bf16[3,128,128]{2,1,0:T(8,128)(2,1)S(1)}, u32[]{:S(2)}, u32[]{:S(2)}) collective-permute-start(bf16[3,128,128]{2,1,0:T(8,128)(2,1)S(1)} %slice.54), channel_id=1, source_target_pairs={{0,1},{1,0},{2,3},{3,2},{4,5},{5,4},{6,7},{7,6},{8,9},{9,8},{10,11... | collective-permute-start | bytes 294920 | tf_op jit(solution)/shard_map/ppermute | solution.py:181

commit v12 on v11

--- a/solution.py
+++ b/solution.py
@@ -66,24 +66,19 @@
     )(core.reshape(1), *args)
 
 
-def spread_kernel(mine_ref, other_ref, out_ref, keys_ref):
+def spread_kernel(mine_ref, other_ref, _, out_ref):
     rows = HALF + STATS
     for n in range(out_ref.shape[0]):
         out_ref[n, :rows, :] = mine_ref[:rows, :]
         out_ref[n, rows:, :] = other_ref[:rows, :]
-    keys_ref[:HALF, :] = mine_ref[rows:, :]
-    keys_ref[HALF:, :] = other_ref[rows:, :]
 
 
 def spread_call(n, *args):
     return pl.pallas_call(
         spread_kernel,
-        in_specs=[pl.BlockSpec(memory_space=pltpu.VMEM)] * 2,
-        out_specs=[pl.BlockSpec(memory_space=pltpu.VMEM)] * 2,
-        out_shape=[
-            jax.ShapeDtypeStruct((n, 2 * (HALF + STATS), 2 * HEAD), BF16),
-            jax.ShapeDtypeStruct((ROWS, 2 * HEAD), BF16),
-        ],
+        in_specs=[pl.BlockSpec(memory_space=pltpu.VMEM)] * 3,
+        out_specs=pl.BlockSpec(memory_space=pltpu.VMEM),
+        out_shape=jax.ShapeDtypeStruct((n, 2 * (HALF + STATS), 2 * HEAD), BF16),
         name="spread",
     )(*args)
 
@@ -189,21 +184,25 @@
     )
     other = shift(send, "core", 1)
     peers = math.prod(lax.axis_size(a) for a in GROUP)
-    spread, key_pack = spread_call(peers, mine, other)
-    key_pair = jnp.concatenate([key_pack, shift(key_pack, "xh", 1)], axis=0)
+    key_pack = jnp.concatenate([mine[HALF + STATS :], other[HALF + STATS :]], axis=0)
+    partner = shift(key_pack, "xh", 1)
+    key_pair = jnp.concatenate([key_pack, partner], axis=0)
+    spread = spread_call(peers, mine, other, partner)
     gathered = lax.all_to_all(spread, GROUP, 0, 0, tiled=True)
     keys = {0: key_pair}
     for by in (1, 2, 3):
         keys[by] = shift(keys[by - 1], "z", 1)
         keys[-by] = shift(keys[1 - by], "z", -1)
+    total_q, own = tile_call(gathered, [keys[0]])
+    zero = jnp.minimum(jnp.abs(own[0, 0]), 0.0).astype(BF16)
     keys[4] = jnp.concatenate(
-        [shift(keys[3][:ROWS], "z", 1), shift(keys[-3][ROWS:], "z", -1)], axis=0
+        [shift(keys[3][:ROWS] + zero, "z", 1), shift(keys[-3][ROWS:] + zero, "z", -1)],
+        axis=0,
     )
 
     def low(x):
         return x.astype(BF16)
 
-    total_q, own = tile_call(gathered, [keys[0]])
     total_q, du, dd = tile_call(gathered, [keys[-3], keys[3]], total_q)
     up, down = low(du), low(dd)
     up_in, down_in = shift(up, "z", 1), shift(down, "z", -1)

time: 104 us -> 104 us (level)
  starting transfers between devices: 45.8 us -> 47.9 us
  waiting for transfers between devices: 24 us -> 22.3 us
    ppermute x19, starting transfers between devices: 37.1 us -> 39.6 us  [shift(): return lax.ppermute(x, axis, [(i, (i + by) % n) for i in range(n)])]
    ppermute x19, waiting for transfers between devices: 19.8 us -> 18.7 us  [shift(): return lax.ppermute(x, axis, [(i, (i + by) % n) for i in range(n)])]
  transfers between devices with their start and end apart: 21 -> 21, of which waited for: 9 -> 9; matrix products, arithmetic and copies ran while one was open for 3% -> 2% of each run, Pallas kernels for 24% -> 24%
where the time goes in v12:
time: 104 us
  starting transfers between devices  47.9 us (46%)
  Pallas kernels  28.5 us (27%)
  waiting for transfers between devices  22.3 us (21%)
  local copies, waits for them, and re-layouts  2.16 us (2%)
  between operations  1.56 us (2%)
  other arithmetic  1.32 us (1%)
    ppermute x19, starting transfers between devices, shift(): return lax.ppermute(x, axis, [(i, (i + by) % n) for i in range(n)])  39.6 us
    pallas_call x5, Pallas kernels, tile_call(): pl.pallas_call(functools.partial(tile_kernel, count, first, after is not...  24.5 us
    ppermute x19, waiting for transfers between devices, shift(): return lax.ppermute(x, axis, [(i, (i + by) % n) for i in range(n)])  18.7 us
    all_to_all x1, starting transfers between devices, local(): returned = lax.all_to_all(total_q, GROUP, 0, 0, tiled=True)  4.65 us
    all_to_all x1, starting transfers between devices, local(): gathered = lax.all_to_all(spread, GROUP, 0, 0, tiled=True)  3.69 us
    all_to_all x1, waiting for transfers between devices, local(): returned = lax.all_to_all(total_q, GROUP, 0, 0, tiled=True)  3.61 us
    pallas_call x1, Pallas kernels, spread_call(): pl.pallas_call(spread_kernel, in_specs=[pl.BlockSpec(memory_space=pltpu.V...  2.13 us
  transfers between devices with their start and end apart: 21, of which 9 were waited for; matrix products, arithmetic and copies ran while one was open for 2% of the time, Pallas kernels for 24%

profile of v12, /device:TPU:1, one launch (start us, length us, event | category | flops | bytes accessed | tf_op | source)
XLA Modules:
  0.0 103.8 jit_solution(17825440391486572497)
XLA Ops:
  0.6 1.8 %pack.1 = (bf16[272,256]{1,0:T(8,128)(2,1)}, bf16[272,256]{1,0:T(8,128)(2,1)}) custom-call(s32[1]{0:T(128)} %bitcast.core_ref, bf16[128,256]{1,0:T(8,128)(2,1)} %q_ref.1, bf16[128,256]{1,0:T(8,128)(2,1)} %k_ref.1, bf16[128,256]{1,0:T(8,128)(2,1)} %v_ref.1, bf16[128,256]{1,0:T(8,128)(2,1)} %o_ref.1, bf16[128,256]{1,0:T(8,128)(2,1)} %g_ref.1, f32[2,128]{1,0:T(2,128)} %lse_ref.1), custom_call_target="tpu_custom_call" | custom-call | tf_op jit(solution)/shard_map/pack/pallas_call | solution.py:59
  2.5 3.2 %collective-permute-start = (bf16[272,256]{1,0:T(8,128)(2,1)}, bf16[272,256]{1,0:T(8,128)(2,1)S(1)}, u32[]{:S(2)}, u32[]{:S(2)}) collective-permute-start(bf16[272,256]{1,0:T(8,128)(2,1)} %get-tuple-element.19), channel_id=1, source_target_pairs={{0,1},{1,0},{2,3},{3,2},{4,5},{5,4},{6,7},{7,6},{8,9},{9,8},{10,11... | collective-permute-start | bytes 417800 | tf_op jit(solution)/shard_map/ppermute | solution.py:176
  8.0 5.2 %collective-permute-done.1._ = bf16[256,256]{1,0:T(8,128)(2,1)S(1)} collective-permute-done((bf16[256,256]{1,0:T(8,128)(2,1)S(1)}, bf16[256,256]{1,0:T(8,128)(2,1)S(1)}, u32[]{:S(2)}, u32[]{:S(2)}) %collective-permute-start.1) | collective-permute-done | bytes 131104 | tf_op jit(solution)/shard_map/ppermute | solution.py:176
  13.9 2.1 %spread.1 = bf16[8,288,256]{2,1,0:T(8,128)(2,1)} custom-call(bf16[272,256]{1,0:T(8,128)(2,1)} %get-tuple-element.18.mine_ref, bf16[272,256]{1,0:T(8,128)(2,1)} %copy-done.2, bf16[256,256]{1,0:T(8,128)(2,1)} %copy-done), custom_call_target="tpu_custom_call" | custom-call | tf_op jit(solution)/shard_map/spread/pallas_call | solution.py:77
  16.0 3.7 %all-to-all-start = ((bf16[8,288,256]{2,1,0:T(8,128)(2,1)}), bf16[8,288,256]{2,1,0:T(8,128)(2,1)S(1)}, u32[]{:S(2)}, u32[]{:S(2)}) async-start(bf16[8,288,256]{2,1,0:T(8,128)(2,1)} %spread.1), calls=%async_computation | async-start | bytes 2359296 | tf_op jit(solution)/shard_map/all_to_all | solution.py:191
  21.3 4.0 %collective-permute-start.2 = (bf16[512,256]{1,0:T(8,128)(2,1)S(1)}, bf16[512,256]{1,0:T(8,128)(2,1)S(1)}, u32[]{:S(2)}, u32[]{:S(2)}) collective-permute-start(bf16[512,256]{1,0:T(8,128)(2,1)S(1)} %pad_maximum_fusion.refs_1_), channel_id=1, source_target_pairs={{0,28},{4,0},{8,4},{12,8},{16,12},{20,16},{24,20},{28,24},{1,29},{... | collective-permute-start | bytes 786440 | tf_op jit(solution)/shard_map/ppermute | solution.py:176
  25.3 5.0 %collective-permute-done.3.refs_2_ = bf16[512,256]{1,0:T(8,128)(2,1)S(1)} collective-permute-done((bf16[512,256]{1,0:T(8,128)(2,1)S(1)}, bf16[512,256]{1,0:T(8,128)(2,1)S(1)}, u32[]{:S(2)}, u32[]{:S(2)}) %collective-permute-start.3) | collective-permute-done | bytes 262176 | tf_op jit(solution)/shard_map/ppermute | solution.py:176
  30.4 2.7 %collective-permute-start.4 = (bf16[512,256]{1,0:T(8,128)(2,1)S(1)}, bf16[512,256]{1,0:T(8,128)(2,1)S(1)}, u32[]{:S(2)}, u32[]{:S(2)}) collective-permute-start(bf16[512,256]{1,0:T(8,128)(2,1)S(1)} %collective-permute-done.2.refs_1_), channel_id=1, source_target_pairs={{0,28},{4,0},{8,4},{12,8},{16,12},{20,16},{24,20},{28,24},{1,29},{... | collective-permute-start | bytes 786440 | tf_op jit(solution)/shard_map/ppermute | solution.py:176
  33.0 4.2 %collective-permute-done.5.refs_2_ = bf16[512,256]{1,0:T(8,128)(2,1)S(1)} collective-permute-done((bf16[512,256]{1,0:T(8,128)(2,1)S(1)}, bf16[512,256]{1,0:T(8,128)(2,1)S(1)}, u32[]{:S(2)}, u32[]{:S(2)}) %collective-permute-start.5) | collective-permute-done | bytes 262176 | tf_op jit(solution)/shard_map/ppermute | solution.py:176
  37.2 2.7 %collective-permute-start.8 = (bf16[512,256]{1,0:T(8,128)(2,1)S(1)}, bf16[512,256]{1,0:T(8,128)(2,1)S(1)}, u32[]{:S(2)}, u32[]{:S(2)}) collective-permute-start(bf16[512,256]{1,0:T(8,128)(2,1)S(1)} %collective-permute-done.4.refs_1_), channel_id=1, source_target_pairs={{0,28},{4,0},{8,4},{12,8},{16,12},{20,16},{24,20},{28,24},{1,29},{... | collective-permute-start | bytes 786440 | tf_op jit(solution)/shard_map/ppermute | solution.py:176
  39.9 3.0 %tile.5 = (f32[8,128,256]{2,1,0:T(8,128)S(1)}, f32[512,256]{1,0:T(8,128)S(1)}) custom-call(bf16[8,288,256]{2,1,0:T(8,128)(2,1)S(1)} %all-to-all-done.refs_0_, bf16[512,256]{1,0:T(8,128)(2,1)S(1)} %pad_maximum_fusion.refs_1_), custom_call_target="tpu_custom_call" | custom-call | flops 2684354560 | bytes 8388608 | tf_op jit(solution)/shard_map/tile/pallas_call | solution.py:155
  44.3 2.9 %collective-permute-start.9 = (bf16[256,256]{1,0:T(8,128)(2,1)S(1)}, bf16[256,256]{1,0:T(8,128)(2,1)S(1)}, u32[]{:S(2)}, u32[]{:S(2)}) collective-permute-start(bf16[256,256]{1,0:T(8,128)(2,1)S(1)} %slice_add_fusion.1), channel_id=1, source_target_pairs={{0,28},{4,0},{8,4},{12,8},{16,12},{20,16},{24,20},{28,24},{1,29},{... | collective-permute-start | bytes 393224 | tf_op jit(solution)/shard_map/ppermute | solution.py:176
  47.2 5.9 %tile.6 = (f32[8,128,256]{2,1,0:T(8,128)S(1)}, f32[512,256]{1,0:T(8,128)S(1)}, f32[512,256]{1,0:T(8,128)S(1)}) custom-call(bf16[8,288,256]{2,1,0:T(8,128)(2,1)S(1)} %all-to-all-done.refs_0_, bf16[512,256]{1,0:T(8,128)(2,1)S(1)} %collective-permute-done.8.refs_1_, bf16[512,256]{1,0:T(8,128)(2,1)S(1)} %collective-permute-done.6.refs_2_, ...), custom_call_target="tpu_custom_call" | custom-call | flops 5368709120 | bytes 8388608 | tf_op jit(solution)/shard_map/tile/pallas_call | solution.py:155
  54.8 3.1 %tile.7 = (f32[8,128,256]{2,1,0:T(8,128)S(1)}, f32[512,256]{1,0:T(8,128)S(1)}) custom-call(bf16[8,288,256]{2,1,0:T(8,128)(2,1)S(1)} %all-to-all-done.refs_0_, bf16[512,256]{1,0:T(8,128)(2,1)S(1)} %pad_maximum_fusion.1.refs_1_, f32[8,128,256]{2,1,0:T(8,128)S(1)} %get-tuple-element.22.refs_2_, bf16[512,256]{1,0:T(8,128)(2,1)S(1)} %convert_element_type.58.refs_3_), custom_call_target="tpu_custom_call" | custom-call | flops 2684354560 | bytes 8388608 | tf_op jit(solution)/shard_map/tile/pallas_call | solution.py:155
  57.9 3.7 %collective-permute-start.11 = (bf16[512,256]{1,0:T(8,128)(2,1)S(1)}, bf16[512,256]{1,0:T(8,128)(2,1)S(1)}, u32[]{:S(2)}, u32[]{:S(2)}) collective-permute-start(bf16[512,256]{1,0:T(8,128)(2,1)S(1)} %convert_element_type.59.refs_4_), channel_id=1, source_target_pairs={{0,16},{4,20},{8,24},{12,28},{16,0},{20,4},{24,8},{28,12},{1,17},{... | collective-permute-start | bytes 786440 | tf_op jit(solution)/shard_map/ppermute | solution.py:176
  61.5 5.9 %tile.8 = (f32[8,128,256]{2,1,0:T(8,128)S(1)}, f32[512,256]{1,0:T(8,128)S(1)}, f32[512,256]{1,0:T(8,128)S(1)}) custom-call(bf16[8,288,256]{2,1,0:T(8,128)(2,1)S(1)} %all-to-all-done.refs_0_, bf16[512,256]{1,0:T(8,128)(2,1)S(1)} %collective-permute-done.4.refs_1_, bf16[512,256]{1,0:T(8,128)(2,1)S(1)} %collective-permute-done.5.refs_2_, ...), custom_call_target="tpu_custom_call" | custom-call | flops 5368709120 | bytes 8388608 | tf_op jit(solution)/shard_map/tile/pallas_call | solution.py:155
  67.7 2.9 %collective-permute-start.15 = (bf16[512,256]{1,0:T(8,128)(2,1)S(1)}, bf16[512,256]{1,0:T(8,128)(2,1)S(1)}, u32[]{:S(2)}, u32[]{:S(2)}) collective-permute-start(bf16[512,256]{1,0:T(8,128)(2,1)S(1)} %add_convert_fusion.1), channel_id=1, source_target_pairs={{0,28},{4,0},{8,4},{12,8},{16,12},{20,16},{24,20},{28,24},{1,29},{... | collective-permute-start | bytes 786440 | tf_op jit(solution)/shard_map/ppermute | solution.py:176
  70.6 6.6 %tile.9 = (bf16[8,128,256]{2,1,0:T(8,128)(2,1)}, f32[512,256]{1,0:T(8,128)S(1)}, f32[512,256]{1,0:T(8,128)S(1)}) custom-call(bf16[8,288,256]{2,1,0:T(8,128)(2,1)S(1)} %all-to-all-done.refs_0_, bf16[512,256]{1,0:T(8,128)(2,1)S(1)} %collective-permute-done.2.refs_1_, bf16[512,256]{1,0:T(8,128)(2,1)S(1)} %collective-permute-done.3.refs_2_, ...), custom_call_target="tpu_custom_call" | custom-call | flops 5368709120 | bytes 8388608 | tf_op jit(solution)/shard_map/tile/pallas_call | solution.py:155
  77.3 1.6 %collective-permute-done.12 = bf16[512,256]{1,0:T(8,128)(2,1)S(1)} collective-permute-done((bf16[512,256]{1,0:T(8,128)(2,1)S(1)}, bf16[512,256]{1,0:T(8,128)(2,1)S(1)}, u32[]{:S(2)}, u32[]{:S(2)}) %collective-permute-start.12) | collective-permute-done | bytes 262176 | tf_op jit(solution)/shard_map/ppermute | solution.py:176
  78.9 2.3 %collective-permute-start.13 = (bf16[512,256]{1,0:T(8,128)(2,1)S(1)}, bf16[512,256]{1,0:T(8,128)(2,1)S(1)}, u32[]{:S(2)}, u32[]{:S(2)}) collective-permute-start(bf16[512,256]{1,0:T(8,128)(2,1)S(1)} %add_convert_fusion.2), channel_id=1, source_target_pairs={{0,4},{4,8},{8,12},{12,16},{16,20},{20,24},{24,28},{28,0},{1,5},{5... | collective-permute-start | bytes 786440 | tf_op jit(solution)/shard_map/ppermute | solution.py:176
  81.8 4.6 %all-to-all-start.1 = ((bf16[8,128,256]{2,1,0:T(8,128)(2,1)}), bf16[8,128,256]{2,1,0:T(8,128)(2,1)S(1)}, u32[]{:S(2)}, u32[]{:S(2)}) async-start(bf16[8,128,256]{2,1,0:T(8,128)(2,1)} %get-tuple-element.28), calls=%async_computation.1 | async-start | bytes 1048576 | tf_op jit(solution)/shard_map/all_to_all | solution.py:220
  87.8 2.5 %collective-permute-start.17 = (bf16[256,256]{1,0:T(8,128)(2,1)S(1)}, bf16[256,256]{1,0:T(8,128)(2,1)S(1)}, u32[]{:S(2)}, u32[]{:S(2)}) collective-permute-start(bf16[256,256]{1,0:T(8,128)(2,1)S(1)} %slice.98), channel_id=1, source_target_pairs={{0,32},{32,0},{1,33},{33,1},{2,34},{34,2},{3,35},{35,3},{4,36},{36... | collective-permute-start | bytes 393224 | tf_op jit(solution)/shard_map/ppermute | solution.py:176
  90.3 3.6 %all-to-all-done.1 = bf16[8,128,256]{2,1,0:T(8,128)(2,1)S(1)} async-done(((bf16[8,128,256]{2,1,0:T(8,128)(2,1)}), bf16[8,128,256]{2,1,0:T(8,128)(2,1)S(1)}, u32[]{:S(2)}, u32[]{:S(2)}) %all-to-all-start.1) | async-done | bytes 524320 | tf_op jit(solution)/shard_map/all_to_all | solution.py:220
  94.4 7.7 %collective-permute-start.18 = (bf16[3,128,128]{2,1,0:T(8,128)(2,1)S(1)}, bf16[3,128,128]{2,1,0:T(8,128)(2,1)S(1)}, u32[]{:S(2)}, u32[]{:S(2)}) collective-permute-start(bf16[3,128,128]{2,1,0:T(8,128)(2,1)S(1)} %slice.67), channel_id=1, source_target_pairs={{0,1},{1,0},{2,3},{3,2},{4,5},{5,4},{6,7},{7,6},{8,9},{9,8},{10,11... | collective-permute-start | bytes 294920 | tf_op jit(solution)/shard_map/ppermute | solution.py:176
  (56 shorter events, 11.1 us)
Async XLA Ops:
  2.5 4.4 %collective-permute-start = (bf16[272,256]{1,0:T(8,128)(2,1)}, bf16[272,256]{1,0:T(8,128)(2,1)S(1)}, u32[]{:S(2)}, u32[]{:S(2)}) collective-permute-start(bf16[272,256]{1,0:T(8,128)(2,1)} %get-tuple-element.19), channel_id=1, source_target_pairs={{0,1},{1,0},{2,3},{3,2},{4,5},{5,4},{6,7},{7,6},{8,9},{9,8},{10,11... | collective-permute-start | bytes 417800 | tf_op jit(solution)/shard_map/ppermute | solution.py:176
  6.9 6.3 %copy-start.2 = (bf16[272,256]{1,0:T(8,128)(2,1)}, bf16[272,256]{1,0:T(8,128)(2,1)S(1)}, u32[]{:S(2)}) copy-start(bf16[272,256]{1,0:T(8,128)(2,1)S(1)} %collective-permute-done.other_ref) | copy-start | bytes 417796
  6.9 6.3 %collective-permute-start.1 = (bf16[256,256]{1,0:T(8,128)(2,1)S(1)}, bf16[256,256]{1,0:T(8,128)(2,1)S(1)}, u32[]{:S(2)}, u32[]{:S(2)}) collective-permute-start(bf16[256,256]{1,0:T(8,128)(2,1)S(1)} %pad_maximum_fusion.3), channel_id=1, source_target_pairs={{0,32},{32,0},{1,33},{33,1},{2,34},{34,2},{3,35},{35,3},{4,36},{36... | collective-permute-start | bytes 393224 | tf_op jit(solution)/shard_map/ppermute | solution.py:176
  13.2 0.6 copy-start
  16.0 3.7 %copy-start.1 = (bf16[256,256]{1,0:T(8,128)(2,1)S(1)}, bf16[256,256]{1,0:T(8,128)(2,1)}, u32[]{:S(2)}) copy-start(bf16[256,256]{1,0:T(8,128)(2,1)} %copy-done) | copy-start | bytes 393220
  16.0 23.9 %all-to-all-start = ((bf16[8,288,256]{2,1,0:T(8,128)(2,1)}), bf16[8,288,256]{2,1,0:T(8,128)(2,1)S(1)}, u32[]{:S(2)}, u32[]{:S(2)}) async-start(bf16[8,288,256]{2,1,0:T(8,128)(2,1)} %spread.1), calls=%async_computation | async-start | bytes 2359296 | tf_op jit(solution)/shard_map/all_to_all | solution.py:191
  19.7 10.6 %collective-permute-start.3 = (bf16[512,256]{1,0:T(8,128)(2,1)S(1)}, bf16[512,256]{1,0:T(8,128)(2,1)S(1)}, u32[]{:S(2)}, u32[]{:S(2)}) collective-permute-start(bf16[512,256]{1,0:T(8,128)(2,1)S(1)} %pad_maximum_fusion.refs_1_), channel_id=1, source_target_pairs={{0,4},{4,8},{8,12},{12,16},{16,20},{20,24},{24,28},{28,0},{1,5},{5... | collective-permute-start | bytes 786440 | tf_op jit(solution)/shard_map/ppermute | solution.py:176
  21.3 9.1 %collective-permute-start.2 = (bf16[512,256]{1,0:T(8,128)(2,1)S(1)}, bf16[512,256]{1,0:T(8,128)(2,1)S(1)}, u32[]{:S(2)}, u32[]{:S(2)}) collective-permute-start(bf16[512,256]{1,0:T(8,128)(2,1)S(1)} %pad_maximum_fusion.refs_1_), channel_id=1, source_target_pairs={{0,28},{4,0},{8,4},{12,8},{16,12},{20,16},{24,20},{28,24},{1,29},{... | collective-permute-start | bytes 786440 | tf_op jit(solution)/shard_map/ppermute | solution.py:176
  30.3 6.9 %collective-permute-start.5 = (bf16[512,256]{1,0:T(8,128)(2,1)S(1)}, bf16[512,256]{1,0:T(8,128)(2,1)S(1)}, u32[]{:S(2)}, u32[]{:S(2)}) collective-permute-start(bf16[512,256]{1,0:T(8,128)(2,1)S(1)} %collective-permute-done.3.refs_2_), channel_id=1, source_target_pairs={{0,4},{4,8},{8,12},{12,16},{16,20},{20,24},{24,28},{28,0},{1,5},{5... | collective-permute-start | bytes 786440 | tf_op jit(solution)/shard_map/ppermute | solution.py:176
  30.4 6.9 %collective-permute-start.4 = (bf16[512,256]{1,0:T(8,128)(2,1)S(1)}, bf16[512,256]{1,0:T(8,128)(2,1)S(1)}, u32[]{:S(2)}, u32[]{:S(2)}) collective-permute-start(bf16[512,256]{1,0:T(8,128)(2,1)S(1)} %collective-permute-done.2.refs_1_), channel_id=1, source_target_pairs={{0,28},{4,0},{8,4},{12,8},{16,12},{20,16},{24,20},{28,24},{1,29},{... | collective-permute-start | bytes 786440 | tf_op jit(solution)/shard_map/ppermute | solution.py:176
  37.2 6.9 %collective-permute-start.6 = (bf16[512,256]{1,0:T(8,128)(2,1)S(1)}, bf16[512,256]{1,0:T(8,128)(2,1)S(1)}, u32[]{:S(2)}, u32[]{:S(2)}) collective-permute-start(bf16[512,256]{1,0:T(8,128)(2,1)S(1)} %collective-permute-done.5.refs_2_), channel_id=1, source_target_pairs={{0,4},{4,8},{8,12},{12,16},{16,20},{20,24},{24,28},{28,0},{1,5},{5... | collective-permute-start | bytes 786440 | tf_op jit(solution)/shard_map/ppermute | solution.py:176
  37.2 7.0 %collective-permute-start.8 = (bf16[512,256]{1,0:T(8,128)(2,1)S(1)}, bf16[512,256]{1,0:T(8,128)(2,1)S(1)}, u32[]{:S(2)}, u32[]{:S(2)}) collective-permute-start(bf16[512,256]{1,0:T(8,128)(2,1)S(1)} %collective-permute-done.4.refs_1_), channel_id=1, source_target_pairs={{0,28},{4,0},{8,4},{12,8},{16,12},{20,16},{24,20},{28,24},{1,29},{... | collective-permute-start | bytes 786440 | tf_op jit(solution)/shard_map/ppermute | solution.py:176
  44.2 10.6 %collective-permute-start.7 = (bf16[256,256]{1,0:T(8,128)(2,1)S(1)}, bf16[256,256]{1,0:T(8,128)(2,1)S(1)}, u32[]{:S(2)}, u32[]{:S(2)}) collective-permute-start(bf16[256,256]{1,0:T(8,128)(2,1)S(1)} %slice_add_fusion.2), channel_id=1, source_target_pairs={{0,4},{4,8},{8,12},{12,16},{16,20},{20,24},{24,28},{28,0},{1,5},{5... | collective-permute-start | bytes 393224 | tf_op jit(solution)/shard_map/ppermute | solution.py:176
  44.3 10.5 %collective-permute-start.9 = (bf16[256,256]{1,0:T(8,128)(2,1)S(1)}, bf16[256,256]{1,0:T(8,128)(2,1)S(1)}, u32[]{:S(2)}, u32[]{:S(2)}) collective-permute-start(bf16[256,256]{1,0:T(8,128)(2,1)S(1)} %slice_add_fusion.1), channel_id=1, source_target_pairs={{0,28},{4,0},{8,4},{12,8},{16,12},{20,16},{24,20},{28,24},{1,29},{... | collective-permute-start | bytes 393224 | tf_op jit(solution)/shard_map/ppermute | solution.py:176
  53.2 14.4 %collective-permute-start.14 = (bf16[512,256]{1,0:T(8,128)(2,1)S(1)}, bf16[512,256]{1,0:T(8,128)(2,1)S(1)}, u32[]{:S(2)}, u32[]{:S(2)}) collective-permute-start(bf16[512,256]{1,0:T(8,128)(2,1)S(1)} %convert_element_type.67), channel_id=1, source_target_pairs={{0,28},{4,0},{8,4},{12,8},{16,12},{20,16},{24,20},{28,24},{1,29},{... | collective-permute-start | bytes 786440 | tf_op jit(solution)/shard_map/ppermute | solution.py:176
  53.3 14.2 %collective-permute-start.10 = (bf16[512,256]{1,0:T(8,128)(2,1)S(1)}, bf16[512,256]{1,0:T(8,128)(2,1)S(1)}, u32[]{:S(2)}, u32[]{:S(2)}) collective-permute-start(bf16[512,256]{1,0:T(8,128)(2,1)S(1)} %convert_element_type.58.refs_3_), channel_id=1, source_target_pairs={{0,4},{4,8},{8,12},{12,16},{16,20},{20,24},{24,28},{28,0},{1,5},{5... | collective-permute-start | bytes 786440 | tf_op jit(solution)/shard_map/ppermute | solution.py:176
  57.9 28.5 %collective-permute-start.11 = (bf16[512,256]{1,0:T(8,128)(2,1)S(1)}, bf16[512,256]{1,0:T(8,128)(2,1)S(1)}, u32[]{:S(2)}, u32[]{:S(2)}) collective-permute-start(bf16[512,256]{1,0:T(8,128)(2,1)S(1)} %convert_element_type.59.refs_4_), channel_id=1, source_target_pairs={{0,16},{4,20},{8,24},{12,28},{16,0},{20,4},{24,8},{28,12},{1,17},{... | collective-permute-start | bytes 786440 | tf_op jit(solution)/shard_map/ppermute | solution.py:176
  67.5 11.3 %collective-permute-start.12 = (bf16[512,256]{1,0:T(8,128)(2,1)S(1)}, bf16[512,256]{1,0:T(8,128)(2,1)S(1)}, u32[]{:S(2)}, u32[]{:S(2)}) collective-permute-start(bf16[512,256]{1,0:T(8,128)(2,1)S(1)} %add_convert_fusion.3.refs_4_), channel_id=1, source_target_pairs={{0,4},{4,8},{8,12},{12,16},{16,20},{20,24},{24,28},{28,0},{1,5},{5... | collective-permute-start | bytes 786440 | tf_op jit(solution)/shard_map/ppermute | solution.py:176
  67.7 13.5 %collective-permute-start.15 = (bf16[512,256]{1,0:T(8,128)(2,1)S(1)}, bf16[512,256]{1,0:T(8,128)(2,1)S(1)}, u32[]{:S(2)}, u32[]{:S(2)}) collective-permute-start(bf16[512,256]{1,0:T(8,128)(2,1)S(1)} %add_convert_fusion.1), channel_id=1, source_target_pairs={{0,28},{4,0},{8,4},{12,8},{16,12},{20,16},{24,20},{28,24},{1,29},{... | collective-permute-start | bytes 786440 | tf_op jit(solution)/shard_map/ppermute | solution.py:176
  78.9 7.6 %collective-permute-start.13 = (bf16[512,256]{1,0:T(8,128)(2,1)S(1)}, bf16[512,256]{1,0:T(8,128)(2,1)S(1)}, u32[]{:S(2)}, u32[]{:S(2)}) collective-permute-start(bf16[512,256]{1,0:T(8,128)(2,1)S(1)} %add_convert_fusion.2), channel_id=1, source_target_pairs={{0,4},{4,8},{8,12},{12,16},{16,20},{20,24},{24,28},{28,0},{1,5},{5... | collective-permute-start | bytes 786440 | tf_op jit(solution)/shard_map/ppermute | solution.py:176
  81.2 6.4 %collective-permute-start.16 = (bf16[512,256]{1,0:T(8,128)(2,1)S(1)}, bf16[512,256]{1,0:T(8,128)(2,1)S(1)}, u32[]{:S(2)}, u32[]{:S(2)}) collective-permute-start(bf16[512,256]{1,0:T(8,128)(2,1)S(1)} %add_convert_fusion), channel_id=1, source_target_pairs={{0,28},{4,0},{8,4},{12,8},{16,12},{20,16},{24,20},{28,24},{1,29},{... | collective-permute-start | bytes 786440 | tf_op jit(solution)/shard_map/ppermute | solution.py:176
  81.8 12.2 %all-to-all-start.1 = ((bf16[8,128,256]{2,1,0:T(8,128)(2,1)}), bf16[8,128,256]{2,1,0:T(8,128)(2,1)S(1)}, u32[]{:S(2)}, u32[]{:S(2)}) async-start(bf16[8,128,256]{2,1,0:T(8,128)(2,1)} %get-tuple-element.28), calls=%async_computation.1 | async-start | bytes 1048576 | tf_op jit(solution)/shard_map/all_to_all | solution.py:220
  87.8 6.5 %collective-permute-start.17 = (bf16[256,256]{1,0:T(8,128)(2,1)S(1)}, bf16[256,256]{1,0:T(8,128)(2,1)S(1)}, u32[]{:S(2)}, u32[]{:S(2)}) collective-permute-start(bf16[256,256]{1,0:T(8,128)(2,1)S(1)} %slice.98), channel_id=1, source_target_pairs={{0,32},{32,0},{1,33},{33,1},{2,34},{34,2},{3,35},{35,3},{4,36},{36... | collective-permute-start | bytes 393224 | tf_op jit(solution)/shard_map/ppermute | solution.py:176
  94.4 8.7 %collective-permute-start.18 = (bf16[3,128,128]{2,1,0:T(8,128)(2,1)S(1)}, bf16[3,128,128]{2,1,0:T(8,128)(2,1)S(1)}, u32[]{:S(2)}, u32[]{:S(2)}) collective-permute-start(bf16[3,128,128]{2,1,0:T(8,128)(2,1)S(1)} %slice.67), channel_id=1, source_target_pairs={{0,1},{1,0},{2,3},{3,2},{4,5},{5,4},{6,7},{7,6},{8,9},{9,8},{10,11... | collective-permute-start | bytes 294920 | tf_op jit(solution)/shard_map/ppermute | solution.py:176

commit v13 on v10

--- a/solution.py
+++ b/solution.py
@@ -141,7 +141,7 @@
 def tile_call(qg, kv1, kv2, old, after, last):
     first = old is None
     groups, rows, width = qg.shape
-    chips = 4
+    chips = 2
     q_spec = pl.BlockSpec((chips, rows, width), lambda i: (i, 0, 0))
     keys = kv1.shape[0]
     kv_spec = pl.BlockSpec((keys, width), lambda i: (0, 0))

time: 101 us -> 103 us (1.020)
  Pallas kernels: 28.2 us -> 29.9 us
  starting transfers between devices: 43.8 us -> 45.1 us
  waiting for transfers between devices: 25.9 us -> 24.6 us
    ppermute x19, starting transfers between devices: 34.7 us -> 36.6 us  [shift(): return lax.ppermute(x, axis, [(i, (i + by) % n) for i in range(n)])]
    pallas_call x4, Pallas kernels: 24.3 us -> 26 us  [tile_call(): pl.pallas_call(functools.partial(tile_kernel, first, chips), grid=(groups...]
    ppermute x19, waiting for transfers between devices: 20.3 us -> 19.1 us  [shift(): return lax.ppermute(x, axis, [(i, (i + by) % n) for i in range(n)])]
  transfers between devices with their start and end apart: 21 -> 21, of which waited for: 8 -> 8; matrix products, arithmetic and copies ran while one was open for 1% -> 1% of each run, Pallas kernels for 24% -> 25%
where the time goes in v13:
time: 103 us
  starting transfers between devices  45.1 us (44%)
  Pallas kernels  29.9 us (29%)
  waiting for transfers between devices  24.6 us (24%)
  other arithmetic  1.27 us (1%)
    ppermute x19, starting transfers between devices, shift(): return lax.ppermute(x, axis, [(i, (i + by) % n) for i in range(n)])  36.6 us
    pallas_call x4, Pallas kernels, tile_call(): pl.pallas_call(functools.partial(tile_kernel, first, chips), grid=(groups...  26 us
    ppermute x19, waiting for transfers between devices, shift(): return lax.ppermute(x, axis, [(i, (i + by) % n) for i in range(n)])  19.1 us
    all_to_all x1, waiting for transfers between devices, local(): returned = lax.all_to_all(total_q, GROUP, 0, 0, tiled=True)  5.54 us
    all_to_all x1, starting transfers between devices, local(): gathered = lax.all_to_all(spread, GROUP, 0, 0, tiled=True)  4.35 us
    all_to_all x1, starting transfers between devices, local(): returned = lax.all_to_all(total_q, GROUP, 0, 0, tiled=True)  4.16 us
    pallas_call x1, Pallas kernels, spread_call(): pl.pallas_call(spread_kernel, in_specs=[pl.BlockSpec(memory_space=pltpu.V...  2.11 us
  transfers between devices with their start and end apart: 21, of which 8 were waited for; matrix products, arithmetic and copies ran while one was open for 1% of the time, Pallas kernels for 25%

profile of v13, /device:TPU:1, one launch (start us, length us, event | category | flops | bytes accessed | tf_op | source)
XLA Modules:
  0.0 102.7 jit_solution(2129708900097976980)
XLA Ops:
  0.6 1.8 %pack.1 = (bf16[144,256]{1,0:T(8,128)(2,1)}, bf16[128,256]{1,0:T(8,128)(2,1)}, bf16[272,256]{1,0:T(8,128)(2,1)}) custom-call(s32[1]{0:T(128)} %bitcast.core_ref, bf16[128,256]{1,0:T(8,128)(2,1)} %q_ref.1, bf16[128,256]{1,0:T(8,128)(2,1)} %k_ref.1, bf16[128,256]{1,0:T(8,128)(2,1)} %v_ref.1, bf16[128,256]{1,0:T(8,128)(2,1)} %o_ref.1, bf16[128,256]{1,0:T(8,128)(2,1)} %g_ref.1, ...), custom_call_target="tpu_custom_call" | custom-call | tf_op jit(solution)/shard_map/pack/pallas_call | solution.py:58
  2.4 3.2 %collective-permute-start = (bf16[272,256]{1,0:T(8,128)(2,1)}, bf16[272,256]{1,0:T(8,128)(2,1)S(1)}, u32[]{:S(2)}, u32[]{:S(2)}) collective-permute-start(bf16[272,256]{1,0:T(8,128)(2,1)} %get-tuple-element.22), channel_id=1, source_target_pairs={{0,1},{1,0},{2,3},{3,2},{4,5},{5,4},{6,7},{7,6},{8,9},{9,8},{10,11... | collective-permute-start | bytes 417800 | tf_op jit(solution)/shard_map/ppermute | solution.py:176
  7.5 2.1 %spread.1 = (bf16[8,288,256]{2,1,0:T(8,128)(2,1)}, bf16[256,256]{1,0:T(8,128)(2,1)}) custom-call(bf16[144,256]{1,0:T(8,128)(2,1)} %get-tuple-element.20.mine_ref, bf16[128,256]{1,0:T(8,128)(2,1)} %get-tuple-element.21.kv_ref, bf16[272,256]{1,0:T(8,128)(2,1)} %copy-done), custom_call_target="tpu_custom_call" | custom-call | tf_op jit(solution)/shard_map/spread/pallas_call | solution.py:82
  10.7 4.4 %all-to-all-start = ((bf16[8,288,256]{2,1,0:T(8,128)(2,1)}), bf16[8,288,256]{2,1,0:T(8,128)(2,1)S(1)}, u32[]{:S(2)}, u32[]{:S(2)}) async-start(bf16[8,288,256]{2,1,0:T(8,128)(2,1)} %get-tuple-element.23), calls=%async_computation | async-start | bytes 2359296 | tf_op jit(solution)/shard_map/all_to_all | solution.py:189
  16.8 4.0 %collective-permute-start.2 = (bf16[512,256]{1,0:T(8,128)(2,1)S(1)}, bf16[512,256]{1,0:T(8,128)(2,1)S(1)}, u32[]{:S(2)}, u32[]{:S(2)}) collective-permute-start(bf16[512,256]{1,0:T(8,128)(2,1)S(1)} %constant_dynamic-update-slice_fusion.refs_2_), channel_id=1, source_target_pairs={{0,28},{4,0},{8,4},{12,8},{16,12},{20,16},{24,20},{28,24},{1,29},{... | collective-permute-start | bytes 786440 | tf_op jit(solution)/shard_map/ppermute | solution.py:176
  20.8 5.7 %collective-permute-done.3.refs_2_ = bf16[512,256]{1,0:T(8,128)(2,1)S(1)} collective-permute-done((bf16[512,256]{1,0:T(8,128)(2,1)S(1)}, bf16[512,256]{1,0:T(8,128)(2,1)S(1)}, u32[]{:S(2)}, u32[]{:S(2)}) %collective-permute-start.3) | collective-permute-done | bytes 262176 | tf_op jit(solution)/shard_map/ppermute | solution.py:176
  26.5 2.7 %collective-permute-start.4 = (bf16[512,256]{1,0:T(8,128)(2,1)S(1)}, bf16[512,256]{1,0:T(8,128)(2,1)S(1)}, u32[]{:S(2)}, u32[]{:S(2)}) collective-permute-start(bf16[512,256]{1,0:T(8,128)(2,1)S(1)} %collective-permute-done.2.refs_1_), channel_id=1, source_target_pairs={{0,28},{4,0},{8,4},{12,8},{16,12},{20,16},{24,20},{28,24},{1,29},{... | collective-permute-start | bytes 786440 | tf_op jit(solution)/shard_map/ppermute | solution.py:176
  29.2 4.8 %collective-permute-done.5.refs_2_ = bf16[512,256]{1,0:T(8,128)(2,1)S(1)} collective-permute-done((bf16[512,256]{1,0:T(8,128)(2,1)S(1)}, bf16[512,256]{1,0:T(8,128)(2,1)S(1)}, u32[]{:S(2)}, u32[]{:S(2)}) %collective-permute-start.5) | collective-permute-done | bytes 262176 | tf_op jit(solution)/shard_map/ppermute | solution.py:176
  34.0 2.7 %collective-permute-start.8 = (bf16[512,256]{1,0:T(8,128)(2,1)S(1)}, bf16[512,256]{1,0:T(8,128)(2,1)S(1)}, u32[]{:S(2)}, u32[]{:S(2)}) collective-permute-start(bf16[512,256]{1,0:T(8,128)(2,1)S(1)} %collective-permute-done.4.refs_1_), channel_id=1, source_target_pairs={{0,28},{4,0},{8,4},{12,8},{16,12},{20,16},{24,20},{28,24},{1,29},{... | collective-permute-start | bytes 786440 | tf_op jit(solution)/shard_map/ppermute | solution.py:176
  36.6 3.8 %collective-permute-done.6.refs_2_ = bf16[512,256]{1,0:T(8,128)(2,1)S(1)} collective-permute-done((bf16[512,256]{1,0:T(8,128)(2,1)S(1)}, bf16[512,256]{1,0:T(8,128)(2,1)S(1)}, u32[]{:S(2)}, u32[]{:S(2)}) %collective-permute-start.6) | collective-permute-done | bytes 262176 | tf_op jit(solution)/shard_map/ppermute | solution.py:176
  40.5 2.7 %collective-permute-start.9 = (bf16[256,256]{1,0:T(8,128)(2,1)S(1)}, bf16[256,256]{1,0:T(8,128)(2,1)S(1)}, u32[]{:S(2)}, u32[]{:S(2)}) collective-permute-start(bf16[256,256]{1,0:T(8,128)(2,1)S(1)} %slice.48), channel_id=1, source_target_pairs={{0,28},{4,0},{8,4},{12,8},{16,12},{20,16},{24,20},{28,24},{1,29},{... | collective-permute-start | bytes 393224 | tf_op jit(solution)/shard_map/ppermute | solution.py:176
  43.3 6.3 %tile.4 = (f32[8,128,256]{2,1,0:T(8,128)S(1)}, f32[512,256]{1,0:T(8,128)S(1)}, f32[512,256]{1,0:T(8,128)S(1)}) custom-call(bf16[8,288,256]{2,1,0:T(8,128)(2,1)S(1)} %all-to-all-done.refs_0_, bf16[512,256]{1,0:T(8,128)(2,1)S(1)} %collective-permute-done.8.refs_1_, bf16[512,256]{1,0:T(8,128)(2,1)S(1)} %collective-permute-done.6.refs_2_), custom_call_target="tpu_custom_call" | custom-call | flops 5368709120 | bytes 8388608 | tf_op jit(solution)/shard_map/tile/pallas_call | solution.py:150
  49.7 1.4 %collective-permute-start.10 = (bf16[512,256]{1,0:T(8,128)(2,1)S(1)}, bf16[512,256]{1,0:T(8,128)(2,1)S(1)}, u32[]{:S(2)}, u32[]{:S(2)}) collective-permute-start(bf16[512,256]{1,0:T(8,128)(2,1)S(1)} %convert_element_type.50.refs_4_), channel_id=1, source_target_pairs={{0,4},{4,8},{8,12},{12,16},{16,20},{20,24},{24,28},{28,0},{1,5},{5... | collective-permute-start | bytes 786440 | tf_op jit(solution)/shard_map/ppermute | solution.py:176
  51.2 6.4 %tile.5 = (f32[8,128,256]{2,1,0:T(8,128)S(1)}, f32[512,256]{1,0:T(8,128)S(1)}, f32[512,256]{1,0:T(8,128)S(1)}) custom-call(bf16[8,288,256]{2,1,0:T(8,128)(2,1)S(1)} %all-to-all-done.refs_0_, bf16[512,256]{1,0:T(8,128)(2,1)S(1)} %pad_maximum_fusion.refs_1_, bf16[512,256]{1,0:T(8,128)(2,1)S(1)} %constant_dynamic-update-slice_fusion.refs_2_, ...), custom_call_target="tpu_custom_call" | custom-call | flops 5368709120 | bytes 8388608 | tf_op jit(solution)/shard_map/tile/pallas_call | solution.py:150
  57.6 3.5 %collective-permute-start.11 = (bf16[512,256]{1,0:T(8,128)(2,1)S(1)}, bf16[512,256]{1,0:T(8,128)(2,1)S(1)}, u32[]{:S(2)}, u32[]{:S(2)}) collective-permute-start(bf16[512,256]{1,0:T(8,128)(2,1)S(1)} %convert_element_type.51.refs_4_), channel_id=1, source_target_pairs={{0,16},{4,20},{8,24},{12,28},{16,0},{20,4},{24,8},{28,12},{1,17},{... | collective-permute-start | bytes 786440 | tf_op jit(solution)/shard_map/ppermute | solution.py:176
  61.1 6.4 %tile.6 = (f32[8,128,256]{2,1,0:T(8,128)S(1)}, f32[512,256]{1,0:T(8,128)S(1)}, f32[512,256]{1,0:T(8,128)S(1)}) custom-call(bf16[8,288,256]{2,1,0:T(8,128)(2,1)S(1)} %all-to-all-done.refs_0_, bf16[512,256]{1,0:T(8,128)(2,1)S(1)} %collective-permute-done.4.refs_1_, bf16[512,256]{1,0:T(8,128)(2,1)S(1)} %collective-permute-done.5.refs_2_, ...), custom_call_target="tpu_custom_call" | custom-call | flops 5368709120 | bytes 8388608 | tf_op jit(solution)/shard_map/tile/pallas_call | solution.py:150
  67.7 2.7 %collective-permute-start.15 = (bf16[512,256]{1,0:T(8,128)(2,1)S(1)}, bf16[512,256]{1,0:T(8,128)(2,1)S(1)}, u32[]{:S(2)}, u32[]{:S(2)}) collective-permute-start(bf16[512,256]{1,0:T(8,128)(2,1)S(1)} %add_convert_fusion.1), channel_id=1, source_target_pairs={{0,28},{4,0},{8,4},{12,8},{16,12},{20,16},{24,20},{28,24},{1,29},{... | collective-permute-start | bytes 786440 | tf_op jit(solution)/shard_map/ppermute | solution.py:176
  70.4 7.0 %tile.7 = (bf16[8,128,256]{2,1,0:T(8,128)(2,1)}, f32[512,256]{1,0:T(8,128)S(1)}, f32[512,256]{1,0:T(8,128)S(1)}) custom-call(bf16[8,288,256]{2,1,0:T(8,128)(2,1)S(1)} %all-to-all-done.refs_0_, bf16[512,256]{1,0:T(8,128)(2,1)S(1)} %collective-permute-done.2.refs_1_, bf16[512,256]{1,0:T(8,128)(2,1)S(1)} %collective-permute-done.3.refs_2_, ...), custom_call_target="tpu_custom_call" | custom-call | flops 5368709120 | bytes 8388608 | tf_op jit(solution)/shard_map/tile/pallas_call | solution.py:150
  77.4 1.6 %collective-permute-done.12 = bf16[512,256]{1,0:T(8,128)(2,1)S(1)} collective-permute-done((bf16[512,256]{1,0:T(8,128)(2,1)S(1)}, bf16[512,256]{1,0:T(8,128)(2,1)S(1)}, u32[]{:S(2)}, u32[]{:S(2)}) %collective-permute-start.12) | collective-permute-done | bytes 262176 | tf_op jit(solution)/shard_map/ppermute | solution.py:176
  79.3 2.7 %collective-permute-start.16 = (bf16[512,256]{1,0:T(8,128)(2,1)S(1)}, bf16[512,256]{1,0:T(8,128)(2,1)S(1)}, u32[]{:S(2)}, u32[]{:S(2)}) collective-permute-start(bf16[512,256]{1,0:T(8,128)(2,1)S(1)} %add_convert_fusion), channel_id=1, source_target_pairs={{0,28},{4,0},{8,4},{12,8},{16,12},{20,16},{24,20},{28,24},{1,29},{... | collective-permute-start | bytes 786440 | tf_op jit(solution)/shard_map/ppermute | solution.py:176
  82.0 4.2 %all-to-all-start.1 = ((bf16[8,128,256]{2,1,0:T(8,128)(2,1)}), bf16[8,128,256]{2,1,0:T(8,128)(2,1)S(1)}, u32[]{:S(2)}, u32[]{:S(2)}) async-start(bf16[8,128,256]{2,1,0:T(8,128)(2,1)} %get-tuple-element.31), calls=%async_computation.1 | async-start | bytes 1048576 | tf_op jit(solution)/shard_map/all_to_all | solution.py:213
  86.3 1.8 %collective-permute-start.17 = (bf16[256,256]{1,0:T(8,128)(2,1)S(1)}, bf16[256,256]{1,0:T(8,128)(2,1)S(1)}, u32[]{:S(2)}, u32[]{:S(2)}) collective-permute-start(bf16[256,256]{1,0:T(8,128)(2,1)S(1)} %slice.83), channel_id=1, source_target_pairs={{0,32},{32,0},{1,33},{33,1},{2,34},{34,2},{3,35},{35,3},{4,36},{36... | collective-permute-start | bytes 393224 | tf_op jit(solution)/shard_map/ppermute | solution.py:176
  88.2 5.5 %all-to-all-done.1 = bf16[8,128,256]{2,1,0:T(8,128)(2,1)S(1)} async-done(((bf16[8,128,256]{2,1,0:T(8,128)(2,1)}), bf16[8,128,256]{2,1,0:T(8,128)(2,1)S(1)}, u32[]{:S(2)}, u32[]{:S(2)}) %all-to-all-start.1) | async-done | bytes 524320 | tf_op jit(solution)/shard_map/all_to_all | solution.py:213
  94.0 7.0 %collective-permute-start.18 = (bf16[3,128,128]{2,1,0:T(8,128)(2,1)S(1)}, bf16[3,128,128]{2,1,0:T(8,128)(2,1)S(1)}, u32[]{:S(2)}, u32[]{:S(2)}) collective-permute-start(bf16[3,128,128]{2,1,0:T(8,128)(2,1)S(1)} %slice.54), channel_id=1, source_target_pairs={{0,1},{1,0},{2,3},{3,2},{4,5},{5,4},{6,7},{7,6},{8,9},{9,8},{10,11... | collective-permute-start | bytes 294920 | tf_op jit(solution)/shard_map/ppermute | solution.py:176
  (50 shorter events, 7.4 us)
Async XLA Ops:
  2.4 4.4 %collective-permute-start = (bf16[272,256]{1,0:T(8,128)(2,1)}, bf16[272,256]{1,0:T(8,128)(2,1)S(1)}, u32[]{:S(2)}, u32[]{:S(2)}) collective-permute-start(bf16[272,256]{1,0:T(8,128)(2,1)} %get-tuple-element.22), channel_id=1, source_target_pairs={{0,1},{1,0},{2,3},{3,2},{4,5},{5,4},{6,7},{7,6},{8,9},{9,8},{10,11... | collective-permute-start | bytes 417800 | tf_op jit(solution)/shard_map/ppermute | solution.py:176
  6.9 0.7 copy-start
  9.7 6.4 %collective-permute-start.1 = (bf16[256,256]{1,0:T(8,128)(2,1)}, bf16[256,256]{1,0:T(8,128)(2,1)S(1)}, u32[]{:S(2)}, u32[]{:S(2)}) collective-permute-start(bf16[256,256]{1,0:T(8,128)(2,1)} %get-tuple-element.24), channel_id=1, source_target_pairs={{0,32},{32,0},{1,33},{33,1},{2,34},{34,2},{3,35},{35,3},{4,36},{36... | collective-permute-start | bytes 393224 | tf_op jit(solution)/shard_map/ppermute | solution.py:176
  10.7 4.4 %copy-start.1 = (bf16[256,256]{1,0:T(8,128)(2,1)S(1)}, bf16[256,256]{1,0:T(8,128)(2,1)}, u32[]{:S(2)}) copy-start(bf16[256,256]{1,0:T(8,128)(2,1)} %get-tuple-element.24) | copy-start | bytes 393220
  10.7 32.6 %all-to-all-start = ((bf16[8,288,256]{2,1,0:T(8,128)(2,1)}), bf16[8,288,256]{2,1,0:T(8,128)(2,1)S(1)}, u32[]{:S(2)}, u32[]{:S(2)}) async-start(bf16[8,288,256]{2,1,0:T(8,128)(2,1)} %get-tuple-element.23), calls=%async_computation | async-start | bytes 2359296 | tf_op jit(solution)/shard_map/all_to_all | solution.py:189
  16.1 10.4 %collective-permute-start.3 = (bf16[512,256]{1,0:T(8,128)(2,1)S(1)}, bf16[512,256]{1,0:T(8,128)(2,1)S(1)}, u32[]{:S(2)}, u32[]{:S(2)}) collective-permute-start(bf16[512,256]{1,0:T(8,128)(2,1)S(1)} %constant_dynamic-update-slice_fusion.refs_2_), channel_id=1, source_target_pairs={{0,4},{4,8},{8,12},{12,16},{16,20},{20,24},{24,28},{28,0},{1,5},{5... | collective-permute-start | bytes 786440 | tf_op jit(solution)/shard_map/ppermute | solution.py:176
  16.8 9.7 %collective-permute-start.2 = (bf16[512,256]{1,0:T(8,128)(2,1)S(1)}, bf16[512,256]{1,0:T(8,128)(2,1)S(1)}, u32[]{:S(2)}, u32[]{:S(2)}) collective-permute-start(bf16[512,256]{1,0:T(8,128)(2,1)S(1)} %constant_dynamic-update-slice_fusion.refs_2_), channel_id=1, source_target_pairs={{0,28},{4,0},{8,4},{12,8},{16,12},{20,16},{24,20},{28,24},{1,29},{... | collective-permute-start | bytes 786440 | tf_op jit(solution)/shard_map/ppermute | solution.py:176
  26.5 7.5 %collective-permute-start.5 = (bf16[512,256]{1,0:T(8,128)(2,1)S(1)}, bf16[512,256]{1,0:T(8,128)(2,1)S(1)}, u32[]{:S(2)}, u32[]{:S(2)}) collective-permute-start(bf16[512,256]{1,0:T(8,128)(2,1)S(1)} %collective-permute-done.3.refs_2_), channel_id=1, source_target_pairs={{0,4},{4,8},{8,12},{12,16},{16,20},{20,24},{24,28},{28,0},{1,5},{5... | collective-permute-start | bytes 786440 | tf_op jit(solution)/shard_map/ppermute | solution.py:176
  26.5 7.5 %collective-permute-start.4 = (bf16[512,256]{1,0:T(8,128)(2,1)S(1)}, bf16[512,256]{1,0:T(8,128)(2,1)S(1)}, u32[]{:S(2)}, u32[]{:S(2)}) collective-permute-start(bf16[512,256]{1,0:T(8,128)(2,1)S(1)} %collective-permute-done.2.refs_1_), channel_id=1, source_target_pairs={{0,28},{4,0},{8,4},{12,8},{16,12},{20,16},{24,20},{28,24},{1,29},{... | collective-permute-start | bytes 786440 | tf_op jit(solution)/shard_map/ppermute | solution.py:176
  34.0 6.4 %collective-permute-start.6 = (bf16[512,256]{1,0:T(8,128)(2,1)S(1)}, bf16[512,256]{1,0:T(8,128)(2,1)S(1)}, u32[]{:S(2)}, u32[]{:S(2)}) collective-permute-start(bf16[512,256]{1,0:T(8,128)(2,1)S(1)} %collective-permute-done.5.refs_2_), channel_id=1, source_target_pairs={{0,4},{4,8},{8,12},{12,16},{16,20},{20,24},{24,28},{28,0},{1,5},{5... | collective-permute-start | bytes 786440 | tf_op jit(solution)/shard_map/ppermute | solution.py:176
  34.0 6.5 %collective-permute-start.8 = (bf16[512,256]{1,0:T(8,128)(2,1)S(1)}, bf16[512,256]{1,0:T(8,128)(2,1)S(1)}, u32[]{:S(2)}, u32[]{:S(2)}) collective-permute-start(bf16[512,256]{1,0:T(8,128)(2,1)S(1)} %collective-permute-done.4.refs_1_), channel_id=1, source_target_pairs={{0,28},{4,0},{8,4},{12,8},{16,12},{20,16},{24,20},{28,24},{1,29},{... | collective-permute-start | bytes 786440 | tf_op jit(solution)/shard_map/ppermute | solution.py:176
  40.4 10.8 %collective-permute-start.7 = (bf16[256,256]{1,0:T(8,128)(2,1)S(1)}, bf16[256,256]{1,0:T(8,128)(2,1)S(1)}, u32[]{:S(2)}, u32[]{:S(2)}) collective-permute-start(bf16[256,256]{1,0:T(8,128)(2,1)S(1)} %slice.47), channel_id=1, source_target_pairs={{0,4},{4,8},{8,12},{12,16},{16,20},{20,24},{24,28},{28,0},{1,5},{5... | collective-permute-start | bytes 393224 | tf_op jit(solution)/shard_map/ppermute | solution.py:176
  40.5 10.6 %collective-permute-start.9 = (bf16[256,256]{1,0:T(8,128)(2,1)S(1)}, bf16[256,256]{1,0:T(8,128)(2,1)S(1)}, u32[]{:S(2)}, u32[]{:S(2)}) collective-permute-start(bf16[256,256]{1,0:T(8,128)(2,1)S(1)} %slice.48), channel_id=1, source_target_pairs={{0,28},{4,0},{8,4},{12,8},{16,12},{20,16},{24,20},{28,24},{1,29},{... | collective-permute-start | bytes 393224 | tf_op jit(solution)/shard_map/ppermute | solution.py:176
  49.6 18.0 %collective-permute-start.14 = (bf16[512,256]{1,0:T(8,128)(2,1)S(1)}, bf16[512,256]{1,0:T(8,128)(2,1)S(1)}, u32[]{:S(2)}, u32[]{:S(2)}) collective-permute-start(bf16[512,256]{1,0:T(8,128)(2,1)S(1)} %convert_element_type.59), channel_id=1, source_target_pairs={{0,28},{4,0},{8,4},{12,8},{16,12},{20,16},{24,20},{28,24},{1,29},{... | collective-permute-start | bytes 786440 | tf_op jit(solution)/shard_map/ppermute | solution.py:176
  49.7 17.7 %collective-permute-start.10 = (bf16[512,256]{1,0:T(8,128)(2,1)S(1)}, bf16[512,256]{1,0:T(8,128)(2,1)S(1)}, u32[]{:S(2)}, u32[]{:S(2)}) collective-permute-start(bf16[512,256]{1,0:T(8,128)(2,1)S(1)} %convert_element_type.50.refs_4_), channel_id=1, source_target_pairs={{0,4},{4,8},{8,12},{12,16},{16,20},{20,24},{24,28},{28,0},{1,5},{5... | collective-permute-start | bytes 786440 | tf_op jit(solution)/shard_map/ppermute | solution.py:176
  57.6 28.6 %collective-permute-start.11 = (bf16[512,256]{1,0:T(8,128)(2,1)S(1)}, bf16[512,256]{1,0:T(8,128)(2,1)S(1)}, u32[]{:S(2)}, u32[]{:S(2)}) collective-permute-start(bf16[512,256]{1,0:T(8,128)(2,1)S(1)} %convert_element_type.51.refs_4_), channel_id=1, source_target_pairs={{0,16},{4,20},{8,24},{12,28},{16,0},{20,4},{24,8},{28,12},{1,17},{... | collective-permute-start | bytes 786440 | tf_op jit(solution)/shard_map/ppermute | solution.py:176
  67.5 11.5 %collective-permute-start.12 = (bf16[512,256]{1,0:T(8,128)(2,1)S(1)}, bf16[512,256]{1,0:T(8,128)(2,1)S(1)}, u32[]{:S(2)}, u32[]{:S(2)}) collective-permute-start(bf16[512,256]{1,0:T(8,128)(2,1)S(1)} %add_convert_fusion.3.refs_4_), channel_id=1, source_target_pairs={{0,4},{4,8},{8,12},{12,16},{16,20},{20,24},{24,28},{28,0},{1,5},{5... | collective-permute-start | bytes 786440 | tf_op jit(solution)/shard_map/ppermute | solution.py:176
  67.7 11.5 %collective-permute-start.15 = (bf16[512,256]{1,0:T(8,128)(2,1)S(1)}, bf16[512,256]{1,0:T(8,128)(2,1)S(1)}, u32[]{:S(2)}, u32[]{:S(2)}) collective-permute-start(bf16[512,256]{1,0:T(8,128)(2,1)S(1)} %add_convert_fusion.1), channel_id=1, source_target_pairs={{0,28},{4,0},{8,4},{12,8},{16,12},{20,16},{24,20},{28,24},{1,29},{... | collective-permute-start | bytes 786440 | tf_op jit(solution)/shard_map/ppermute | solution.py:176
  79.1 7.1 %collective-permute-start.13 = (bf16[512,256]{1,0:T(8,128)(2,1)S(1)}, bf16[512,256]{1,0:T(8,128)(2,1)S(1)}, u32[]{:S(2)}, u32[]{:S(2)}) collective-permute-start(bf16[512,256]{1,0:T(8,128)(2,1)S(1)} %add_convert_fusion.2), channel_id=1, source_target_pairs={{0,4},{4,8},{8,12},{12,16},{16,20},{20,24},{24,28},{28,0},{1,5},{5... | collective-permute-start | bytes 786440 | tf_op jit(solution)/shard_map/ppermute | solution.py:176
  79.3 6.9 %collective-permute-start.16 = (bf16[512,256]{1,0:T(8,128)(2,1)S(1)}, bf16[512,256]{1,0:T(8,128)(2,1)S(1)}, u32[]{:S(2)}, u32[]{:S(2)}) collective-permute-start(bf16[512,256]{1,0:T(8,128)(2,1)S(1)} %add_convert_fusion), channel_id=1, source_target_pairs={{0,28},{4,0},{8,4},{12,8},{16,12},{20,16},{24,20},{28,24},{1,29},{... | collective-permute-start | bytes 786440 | tf_op jit(solution)/shard_map/ppermute | solution.py:176
  82.0 11.7 %all-to-all-start.1 = ((bf16[8,128,256]{2,1,0:T(8,128)(2,1)}), bf16[8,128,256]{2,1,0:T(8,128)(2,1)S(1)}, u32[]{:S(2)}, u32[]{:S(2)}) async-start(bf16[8,128,256]{2,1,0:T(8,128)(2,1)} %get-tuple-element.31), calls=%async_computation.1 | async-start | bytes 1048576 | tf_op jit(solution)/shard_map/all_to_all | solution.py:213
  86.3 7.6 %collective-permute-start.17 = (bf16[256,256]{1,0:T(8,128)(2,1)S(1)}, bf16[256,256]{1,0:T(8,128)(2,1)S(1)}, u32[]{:S(2)}, u32[]{:S(2)}) collective-permute-start(bf16[256,256]{1,0:T(8,128)(2,1)S(1)} %slice.83), channel_id=1, source_target_pairs={{0,32},{32,0},{1,33},{33,1},{2,34},{34,2},{3,35},{35,3},{4,36},{36... | collective-permute-start | bytes 393224 | tf_op jit(solution)/shard_map/ppermute | solution.py:176
  94.0 8.0 %collective-permute-start.18 = (bf16[3,128,128]{2,1,0:T(8,128)(2,1)S(1)}, bf16[3,128,128]{2,1,0:T(8,128)(2,1)S(1)}, u32[]{:S(2)}, u32[]{:S(2)}) collective-permute-start(bf16[3,128,128]{2,1,0:T(8,128)(2,1)S(1)} %slice.54), channel_id=1, source_target_pairs={{0,1},{1,0},{2,3},{3,2},{4,5},{5,4},{6,7},{7,6},{8,9},{9,8},{10,11... | collective-permute-start | bytes 294920 | tf_op jit(solution)/shard_map/ppermute | solution.py:176
